TPU v7x, 32 devices: a whole 2x2x4 slice. The times are simulated.
32 devices in a mesh: groups: 2 (over y), shard: 8 (over z, x), replica: 2 (over core).
Axes of the slice: x: 2, y: 2, z: 4, core: 2. Of those that a mesh axis runs over, the one named last changes fastest.
Arguments:
- gradients: bfloat16 [2, 12, 768, 768], P('replica', 'groups', 'shard'), parts along dimension 1, may hold values from -5 to 5
- block_owner: int32 [12], P('groups'), parts along dimension 0, may hold values from 0 to 7, as said below
- left_gram: bfloat16 [16, 768, 768], P(('groups', 'shard'), 'replica'), parts along dimension 0, may hold values from -1 to 5
- right_gram: bfloat16 [16, 768, 768], P(('groups', 'shard'), 'replica'), parts along dimension 0, may hold values from -1 to 5
- left_root: bfloat16 [16, 768, 768], P(('groups', 'shard'), 'replica'), parts along dimension 0, may hold values from -1 to 3
- right_root: bfloat16 [16, 768, 768], P(('groups', 'shard'), None, 'replica'), parts along dimension 0, may hold values from -1 to 3
Outputs:
- left_new: bfloat16 [16, 768, 768], P(('groups', 'shard'), 'replica'), parts along dimension 0
- right_new: bfloat16 [16, 768, 768], P(('groups', 'shard'), 'replica'), parts along dimension 0
- update: bfloat16 [12, 768, 768], P('groups', 'shard', 'replica'), parts along dimension 0
There are 2 independent parts, one for each index of `groups`. A program takes and returns all parts, laid end to end along the dimension named above; each array names one. Nothing has to cross between parts.
Inputs may be any that keep to these rules, and one draw needn't show every extreme that they name: `block_owner`: the 6 owners are distinct.
All inputs are finite; a program needn't handle non-finite values.
Results may differ from a plain program's by a relative error of at most 0.0059.
Values may be sent and summed in bfloat16 or wider, within the bound.
No kernel may reach another device: no remote copies, remote signals or barrier semaphores. Data moves between devices by JAX's collectives and lax.ppermute only.
A program may use at most 64 MiB of HBM per device.

v0:
```python
import jax
import jax.numpy as jnp
from jax import lax
from jax.sharding import PartitionSpec as P


def per_device(gradients, block_owner, left_gram, right_gram, left_root, right_root):
    owners = lax.axis_size("shard")
    half_rows = left_gram.shape[1]
    full_width = left_gram.shape[2]
    first_row = lax.axis_index("replica") * half_rows
    owner_index = lax.broadcasted_iota(jnp.int32, (owners, block_owner.shape[0]), 0)
    owner_onehot = (owner_index == block_owner[None, :]).astype(jnp.bfloat16)
    outgoing = jnp.einsum(
        "ob,brc->orc", owner_onehot, gradients[0], preferred_element_type=jnp.float32
    )
    arrived = lax.all_to_all(
        outgoing.astype(jnp.bfloat16), "shard", split_axis=0, concat_axis=0, tiled=True
    )
    total = lax.psum(arrived.astype(jnp.float32).astype(jnp.bfloat16), "replica")
    summed_block = total.reshape(full_width, full_width)
    own_rows = lax.dynamic_slice_in_dim(summed_block, first_row, half_rows, 0)
    own_cols = lax.dynamic_slice_in_dim(summed_block, first_row, half_rows, 1)
    left_term = lax.dot_general(
        own_rows, summed_block, (((1,), (1,)), ((), ())), preferred_element_type=jnp.float32
    )
    right_term = lax.dot_general(
        own_cols, summed_block, (((0,), (0,)), ((), ())), preferred_element_type=jnp.float32
    )
    left_new = (0.99 * left_gram[0].astype(jnp.float32) + 0.01 * left_term).astype(jnp.bfloat16)
    right_new = (0.99 * right_gram[0].astype(jnp.float32) + 0.01 * right_term).astype(jnp.bfloat16)
    partial_side = jnp.dot(left_root[0], summed_block, preferred_element_type=jnp.float32).astype(
        jnp.bfloat16
    )
    left_side = lax.all_gather(partial_side, "replica", axis=0, tiled=True)
    both_sides = jnp.dot(left_side, right_root[0], preferred_element_type=jnp.float32)
    side_squares = lax.psum(jnp.sum(both_sides * both_sides), "replica")
    grad_squares = jnp.sum(jnp.square(summed_block.astype(jnp.float32)))
    graft = jnp.sqrt(grad_squares / (side_squares + 1e-06))
    scaled = (
        (both_sides * graft).astype(jnp.bfloat16).reshape(owners, full_width // owners, half_rows)
    )
    returned = lax.all_to_all(scaled, "shard", split_axis=0, concat_axis=0, tiled=True)
    update = jnp.take(returned, block_owner, axis=0)
    return (left_new[None], right_new[None], update)


def solution(mesh):
    return jax.shard_map(
        per_device,
        mesh=mesh,
        in_specs=(
            P("replica", "groups", "shard", None),
            P("groups"),
            P(("groups", "shard"), "replica", None),
            P(("groups", "shard"), "replica", None),
            P(("groups", "shard"), "replica", None),
            P(("groups", "shard"), None, "replica"),
        ),
        out_specs=(
            P(("groups", "shard"), "replica", None),
            P(("groups", "shard"), "replica", None),
            P("groups", "shard", "replica"),
        ),
        check_vma=False,
    )
```

profile of v0, /device:TPU:0, one launch (start us, length us, event | category | flops | bytes accessed | tf_op | source)
XLA Modules:
  0.0 117.0 jit_solution(16452629879528165062)
XLA Ops:
  7.2 0.0 copy-start
  7.2 0.0 all-reduce.2.cloned.1.call-start
  7.2 1.1 copy-done
  8.3 1.3 %convolution_convert_fusion = bf16[8,96,768]{2,0,1:T(8,128)(2,1)S(1)} fusion(bf16[6,96,768]{2,1,0:T(8,128)(2,1)S(1)} %bitcast.28, s32[6]{0:T(128)} %param.7), kind=kOutput, calls=%fused_computation.2 | convolution fusion | flops 7667760 | bytes 2064408 | tf_op jit(solution)/shard_map/ob,brc->orc/dot_general | solution.py:14
  9.6 0.2 copy.13
  9.8 36.1 %all_to_all.10 = bf16[8,96,768]{2,1,0:T(8,128)(2,1)} all-to-all(bf16[8,96,768]{2,1,0:T(8,128)(2,1)S(1)} %copy.13), channel_id=1, replica_groups=mesh['groups'=2,'shard'=8,'replica'=2] {'shard'}, dimensions={0} | all-to-all | bytes 2359296 | tf_op jit(solution)/shard_map/all_to_all | solution.py:17
  45.9 0.0 copy-start.3
  46.0 0.0 all-reduce.2.cloned.1.call-update
  46.0 0.0 all-gather.2.cloned.1.call-start
  46.0 18.6 %all-reduce.2.cloned.1.call-done = bf16[8,96,768]{2,1,0:T(8,128)(2,1)} async-done(((bf16[8,96,768]{2,1,0:T(8,128)(2,1)}), bf16[8,96,768]{2,1,0:T(8,128)(2,1)}) %all-reduce.2.cloned.1.call-update) | async-done | bytes 1179664 | tf_op jit(solution)/shard_map/psum | solution.py:20
  64.6 0.0 copy-done.3
  64.6 0.0 copy-start.1
  64.6 3.0 %fusion.6 = bf16[384,768]{0,1:T(8,128)(2,1)} fusion(bf16[768,768]{1,0:T(8,128)(2,1)} %bitcast.29, bf16[1,384,768]{2,1,0:T(8,128)(2,1)S(1)} %copy-done.3), kind=kOutput, calls=%fused_computation.12 | convolution fusion | flops 453279744 | bytes 2359296 | tf_op jit(solution)/shard_map/dot_general | solution.py:32
  67.6 0.0 all-gather.2.cloned.1.call-update
  67.6 0.0 copy-done.1
  67.7 1.2 %multiply_reduce_fusion = f32[]{:T(128)} fusion(bf16[8,96,768]{2,1,0:T(8,128)(2,1)S(1)} %copy-done.1), kind=kLoop, calls=%fused_computation.1 | loop fusion | flops 1769471 | bytes 1179652 | tf_op jit(solution)/shard_map/reduce_sum | solution.py:38
  68.9 9.3 %all-gather.2.cloned.1.call-done = bf16[768,768]{0,1:T(8,128)(2,1)} async-done(((bf16[384,768]{0,1:T(8,128)(2,1)}), bf16[768,768]{0,1:T(8,128)(2,1)}) %all-gather.2.cloned.1.call-update) | async-done | bytes 1179664 | tf_op jit(solution)/shard_map/all_gather | solution.py:35
  78.2 2.9 %multiply_reduce_fusion.1 = (f32[]{:T(128)}, f32[768,384]{1,0:T(8,128)S(1)}) fusion(bf16[768,768]{0,1:T(8,128)(2,1)} %all-gather.2.cloned.1.call-done, bf16[1,768,384]{2,1,0:T(8,128)(2,1)} %param.11), kind=kOutput, calls=%fused_computation.15 | convolution fusion | flops 453574656 | bytes 2949124 | tf_op jit(solution)/shard_map/dot_general | solution.py:36
  81.1 3.1 %psum.15 = f32[]{:T(128)} all-reduce(f32[]{:T(128)} %get-tuple-element.3), channel_id=1, replica_groups=mesh['groups'=2,'shard'=8,'replica'=2] {'replica'}, use_global_device_ids=true, to_apply=%region_3.0 | all-reduce | flops 1 | bytes 8 | tf_op jit(solution)/shard_map/psum | solution.py:37
  85.5 0.0 copy-start.2
  85.6 0.9 multiply_convert_fusion
  86.4 5.8 %all-to-all-start.1 = ((bf16[8,96,384]{2,1,0:T(8,128)(2,1)}), bf16[8,96,384]{2,1,0:T(8,128)(2,1)S(1)}, u32[]{:S(2)}, u32[]{:S(2)}) async-start(bf16[8,96,384]{2,1,0:T(8,128)(2,1)} %bitcast.10), calls=%async_computation.1 | async-start | bytes 1179648 | tf_op jit(solution)/shard_map/all_to_all | solution.py:43
  92.2 0.0 copy-done.2
  92.2 0.0 copy-start.4
  92.3 2.6 %fusion.5 = bf16[1,384,768]{2,1,0:T(8,128)(2,1)} fusion(bf16[768,768]{1,0:T(8,128)(2,1)S(1)} %bitcast.30, bf16[1,384,768]{2,1,0:T(8,128)(2,1)} %param.8, s32[]{:T(128)S(6)} %select_n.13), kind=kOutput, calls=%fused_computation.11 | convolution fusion | flops 454459392 | bytes 2949124 | tf_op jit(solution)/shard_map/dot_general | solution.py:24
  94.9 0.0 copy-done.4
  94.9 1.5 %fusion.4 = bf16[1,384,768]{2,1,0:T(8,128)(2,1)} fusion(bf16[768,768]{1,0:T(8,128)(2,1)S(1)} %bitcast.31, bf16[1,384,768]{2,1,0:T(8,128)(2,1)S(1)} %copy-done.4, s32[]{:T(128)S(6)} %select_n.13), kind=kOutput, calls=%fused_computation.10 | convolution fusion | flops 454459392 | bytes 2949124 | tf_op jit(solution)/shard_map/dot_general | solution.py:27
  96.4 12.2 %all-to-all-done.1 = bf16[8,96,384]{2,1,0:T(8,128)(2,1)S(1)} async-done(((bf16[8,96,384]{2,1,0:T(8,128)(2,1)}), bf16[8,96,384]{2,1,0:T(8,128)(2,1)S(1)}, u32[]{:S(2)}, u32[]{:S(2)}) %all-to-all-start.1) | async-done | bytes 589856 | tf_op jit(solution)/shard_map/all_to_all | solution.py:43
  108.6 0.6 gather_fusion
  109.2 0.9 broadcast_select_fusion
  (3 shorter events, 0.0 us)
Async XLA Ops:
  7.2 1.2 %copy-start = (bf16[1,6,96,768]{3,2,1,0:T(8,128)(2,1)S(1)}, bf16[1,6,96,768]{3,2,1,0:T(8,128)(2,1)}, u32[]{:S(2)}) copy-start(bf16[1,6,96,768]{3,2,1,0:T(8,128)(2,1)} %param.6) | copy-start | bytes 2654212
  7.2 57.4 %all-reduce.2.cloned.1.call-start = ((), (), s32[]{:S(2)}) async-start(), calls=%async_computation.2 | async-start | bytes 2359296 | tf_op jit(solution)/shard_map/psum | solution.py:20
  45.9 18.7 %copy-start.3 = (bf16[1,384,768]{2,1,0:T(8,128)(2,1)S(1)}, bf16[1,384,768]{2,1,0:T(8,128)(2,1)}, u32[]{:S(2)}) copy-start(bf16[1,384,768]{2,1,0:T(8,128)(2,1)} %param.10) | copy-start | bytes 1769476
  46.0 32.2 %all-gather.2.cloned.1.call-start = ((), (), s32[]{:S(2)}) async-start(), calls=%async_computation.3 | async-start | bytes 1769472 | tf_op jit(solution)/shard_map/all_gather | solution.py:35
  64.6 3.0 %copy-start.1 = (bf16[8,96,768]{2,1,0:T(8,128)(2,1)S(1)}, bf16[8,96,768]{2,1,0:T(8,128)(2,1)}, u32[]{:S(2)}) copy-start(bf16[8,96,768]{2,1,0:T(8,128)(2,1)} %all-reduce.2.cloned.1.call-done) | copy-start | bytes 3538948
  85.5 6.7 %copy-start.2 = (s32[6]{0:T(128)S(1)}, s32[6]{0:T(128)}, u32[]{:S(2)}) copy-start(s32[6]{0:T(128)} %param.7) | copy-start | bytes 76
  86.4 22.1 %all-to-all-start.1 = ((bf16[8,96,384]{2,1,0:T(8,128)(2,1)}), bf16[8,96,384]{2,1,0:T(8,128)(2,1)S(1)}, u32[]{:S(2)}, u32[]{:S(2)}) async-start(bf16[8,96,384]{2,1,0:T(8,128)(2,1)} %bitcast.10), calls=%async_computation.1 | async-start | bytes 1179648 | tf_op jit(solution)/shard_map/all_to_all | solution.py:43
  92.2 2.6 %copy-start.4 = (bf16[1,384,768]{2,1,0:T(8,128)(2,1)S(1)}, bf16[1,384,768]{2,1,0:T(8,128)(2,1)}, u32[]{:S(2)}) copy-start(bf16[1,384,768]{2,1,0:T(8,128)(2,1)} %param.9) | copy-start | bytes 1769476
Sparse Core Ops, SparseCore 0:
  46.1 18.4 all-reduce.1
  67.8 10.3 all-gather.1
where the time goes:
time: 117 us
  waiting for transfers between devices  40.2 us (34%)
  blocking collectives  39.2 us (34%)
  between operations  15.5 us (13%)
  matrix products  11.3 us (10%)
  starting transfers between devices  5.84 us (5%)
  other arithmetic  3 us (3%)
  local copies, waits for them, and re-layouts  1.99 us (2%)
    all_to_all x1, blocking collectives, per_device(): lax.all_to_all(outgoing.astype(jnp.bfloat16), 'shard', split_axis=0, conc...  36.1 us
    psum x1, waiting for transfers between devices, per_device(): lax.psum(arrived.astype(jnp.float32).astype(jnp.bfloat16), 'replica')  18.6 us
    all_to_all x1, waiting for transfers between devices, per_device(): lax.all_to_all(scaled, 'shard', split_axis=0, concat_axis=0, tiled=True)  12.2 us
    all_gather x1, waiting for transfers between devices, per_device(): left_side = lax.all_gather(partial_side, 'replica', axis=0, tiled=True)  9.32 us
    all_to_all x1, starting transfers between devices, per_device(): lax.all_to_all(scaled, 'shard', split_axis=0, concat_axis=0, tiled=True)  5.76 us
    psum x1, blocking collectives, per_device(): side_squares = lax.psum(jnp.sum(both_sides * both_sides), 'replica')  3.08 us
    dot_general x1, matrix products, per_device(): jnp.dot(left_root[0], summed_block, preferred_element_type=jnp.float32)  3 us
    dot_general x1, matrix products, per_device(): jnp.dot(left_side, right_root[0], preferred_element_type=jnp.float32)  2.93 us
  transfers between devices with their start and end apart: 3, of which 3 were waited for; matrix products, arithmetic and copies ran while one was open for 5% of the time, Pallas kernels for 0%

commit v1 on v0

--- a/solution.py
+++ b/solution.py
@@ -1,7 +1,15 @@
+import functools
+
 import jax
 import jax.numpy as jnp
 from jax import lax
+from jax.experimental import pallas as pl
+from jax.experimental.pallas import tpu as pltpu
 from jax.sharding import PartitionSpec as P
+
+VMEM = pl.BlockSpec(memory_space=pltpu.VMEM)
+SMEM = pl.BlockSpec(memory_space=pltpu.SMEM)
+PARAMS = pltpu.CompilerParams(vmem_limit_bytes=24 * 1024 * 1024)
 
 
 def per_device(gradients, block_owner, left_gram, right_gram, left_root, right_root):
@@ -45,9 +53,167 @@
     return (left_new[None], right_new[None], update)
 
 
+def pick_kernel(index_ref, mine_ref, theirs_ref, *out_refs):
+    for j, out_ref in enumerate(out_refs):
+        b = index_ref[j]
+        total = mine_ref[b].astype(jnp.float32) + theirs_ref[b].astype(jnp.float32)
+        out_ref[...] = total.astype(out_ref.dtype)
+
+
+def precondition_kernel(rounds, place_ref, *refs):
+    mine, theirs = refs[:rounds], refs[rounds:2 * rounds]
+    left_ref, own_ref, other_ref, summed_ref, both_ref, side_sq_ref, grad_sq_ref, side_ref = refs[2 * rounds:]
+    core, place = place_ref[0], place_ref[1]
+    slab = mine[0].shape[0]
+    half = rounds * slab
+    grad_sq = jnp.zeros((1, mine[0].shape[1]), jnp.float32)
+    for j in range(rounds):
+        for ref, side in ((mine[j], core), (theirs[j], 1 - core)):
+            row = pl.multiple_of(side * half + (place ^ j) * slab, slab)
+            block = ref[...]
+            summed_ref[pl.ds(row, slab), :] = block
+            wide = block.astype(jnp.float32)
+            grad_sq += jnp.sum(wide * wide, axis=0, keepdims=True)
+    grad_sq_ref[...] = jnp.sum(grad_sq, axis=1, keepdims=True)
+    side_ref[...] = jnp.dot(
+        left_ref[...], summed_ref[...], preferred_element_type=jnp.float32
+    ).astype(side_ref.dtype)
+    side_sq = jnp.zeros((1, 1), jnp.float32)
+    for ref, side in ((own_ref, core), (other_ref, 1 - core)):
+        both = jnp.dot(side_ref[...], ref[...], preferred_element_type=jnp.float32)
+        width = ref.shape[1]
+        both_ref[:, pl.ds(pl.multiple_of(side * width, 128), width)] = both
+        side_sq += jnp.sum(jnp.sum(both * both, axis=0, keepdims=True), axis=1, keepdims=True)
+    side_sq_ref[...] = side_sq
+
+
+def scale_kernel(rounds, place_ref, graft_ref, both_ref, *out_refs):
+    place, keep = place_ref[1], place_ref[2]
+    graft = graft_ref[0]
+    for j in range(rounds):
+        slab, width = out_refs[j].shape[1:]
+        row = pl.multiple_of((place ^ j) * slab, slab)
+        for k, side in ((0, keep), (1, 1 - keep)):
+            col = pl.multiple_of(side * width, 128)
+            piece = both_ref[pl.ds(row, slab), pl.ds(col, width)]
+            out_refs[j][k] = (piece * graft).astype(out_refs[j].dtype)
+
+
+def place_kernel(rounds, index_ref, *refs):
+    mine, theirs, out_ref = refs[:rounds], refs[rounds:2 * rounds], refs[2 * rounds]
+    for j in range(rounds):
+        for k, ref in ((0, mine[j]), (1, theirs[j])):
+            b = index_ref[2 * j + k]
+
+            @pl.when(b >= 0)
+            def _():
+                out_ref[b] = ref[...]
+
+
+def per_device_paired(gradients, block_owner, left_gram, right_gram, left_root, right_root):
+    owners = lax.axis_size("shard")
+    rounds = owners // 2
+    blocks, slab, width = gradients.shape[1:]
+    half_rows = left_gram.shape[1]
+    shard, core = lax.axis_index("shard"), lax.axis_index("replica")
+    side, place = shard // rounds, shard % rounds
+    swap = [(0, 1), (1, 0)]
+
+    def turn(j):
+        return [
+            ((h * rounds + l) * 2 + r, (r * rounds + (l ^ j)) * 2 + h)
+            for h in range(2) for l in range(rounds) for r in range(2) if j or h != r
+        ]
+
+    def other_core(x):
+        return lax.ppermute(x, "replica", swap)
+
+    def trade(x, j):
+        got = lax.ppermute(x, ("shard", "replica"), turn(j))
+        return got if j else jnp.where(side == core, x, got)
+
+    block_index = jnp.arange(blocks, dtype=jnp.int32)
+
+    def block_of(owner):
+        return jnp.max(jnp.where(block_owner == owner, block_index, -1))
+
+    gradient = gradients[0]
+    other_gradient = other_core(gradient)
+    sent_index = jnp.stack(
+        [jnp.maximum(block_of(core * rounds + (place ^ j)), 0) for j in range(rounds)]
+    )
+    outgoing = pl.pallas_call(
+        pick_kernel,
+        out_shape=[jax.ShapeDtypeStruct((slab, width), jnp.bfloat16)] * rounds,
+        in_specs=[SMEM, VMEM, VMEM],
+        out_specs=[VMEM] * rounds,
+        compiler_params=PARAMS,
+    )(sent_index, gradient, other_gradient)
+    mine = [trade(outgoing[j], j) for j in range(rounds)]
+    other_right = other_core(right_root[0])
+    theirs = [other_core(m) for m in mine]
+    place_info = jnp.stack([core, place, side]).astype(jnp.int32)
+    summed, both_sides, side_sq, grad_sq = pl.pallas_call(
+        functools.partial(precondition_kernel, rounds),
+        out_shape=[
+            jax.ShapeDtypeStruct((width, width), jnp.bfloat16),
+            jax.ShapeDtypeStruct((half_rows, width), jnp.float32),
+            jax.ShapeDtypeStruct((1, 1), jnp.float32),
+            jax.ShapeDtypeStruct((1, 1), jnp.float32),
+        ],
+        in_specs=[SMEM] + [VMEM] * (2 * rounds + 3),
+        out_specs=[VMEM] * 4,
+        scratch_shapes=[pltpu.VMEM((half_rows, width), jnp.bfloat16)],
+        compiler_params=PARAMS,
+    )(place_info, *mine, *theirs, left_root[0], right_root[0], other_right)
+    side_squares = side_sq + other_core(side_sq)
+    graft = jnp.sqrt(grad_sq / (side_squares + 1e-06))
+    scaled = pl.pallas_call(
+        functools.partial(scale_kernel, rounds),
+        out_shape=[jax.ShapeDtypeStruct((2, slab, width // 2), jnp.bfloat16)] * rounds,
+        in_specs=[SMEM, SMEM, VMEM],
+        out_specs=[VMEM] * rounds,
+        compiler_params=PARAMS,
+    )(place_info, graft.reshape(1), both_sides)
+    returned = [trade(scaled[j], j) for j in range(rounds)]
+    kept = [x[0] for x in returned]
+    passed = [other_core(x[1]) for x in returned]
+
+    present = block_of(shard) >= 0
+    share = jnp.where(present, 0.01, 0.0).astype(jnp.float32)
+    first_row = core * half_rows
+    own_rows = lax.dynamic_slice_in_dim(summed, first_row, half_rows, 0)
+    own_cols = lax.dynamic_slice_in_dim(summed, first_row, half_rows, 1)
+    left_term = lax.dot_general(
+        own_rows, summed, (((1,), (1,)), ((), ())), preferred_element_type=jnp.float32
+    )
+    right_term = lax.dot_general(
+        own_cols, summed, (((0,), (0,)), ((), ())), preferred_element_type=jnp.float32
+    )
+    left_new = (0.99 * left_gram[0].astype(jnp.float32) + share * left_term).astype(jnp.bfloat16)
+    right_new = (0.99 * right_gram[0].astype(jnp.float32) + share * right_term).astype(jnp.bfloat16)
+
+    placed_index = jnp.stack(
+        [
+            block_of(c * rounds + (place ^ j))
+            for j in range(rounds) for c in (core, 1 - core)
+        ]
+    )
+    update = pl.pallas_call(
+        functools.partial(place_kernel, rounds),
+        out_shape=jax.ShapeDtypeStruct((blocks, slab, width // 2), jnp.bfloat16),
+        in_specs=[SMEM] + [VMEM] * (2 * rounds),
+        out_specs=VMEM,
+        compiler_params=PARAMS,
+    )(placed_index, *kept, *passed)
+    return (left_new[None], right_new[None], update)
+
+
 def solution(mesh):
+    owners = mesh.shape["shard"]
+    paired = mesh.shape["replica"] == 2 and owners in (2, 4, 8, 16)
     return jax.shard_map(
-        per_device,
+        per_device_paired if paired else per_device,
         mesh=mesh,
         in_specs=(
             P("replica", "groups", "shard", None),

time: 117 us -> 59.7 us (0.51)
  blocking collectives: 39.2 us -> 0 us
  waiting for transfers between devices: 40.2 us -> 4.82 us
  starting transfers between devices: 5.84 us -> 32.5 us
  between operations: 15.5 us -> 5.93 us
  matrix products: 11.3 us -> 2.97 us
  Pallas kernels: 0 us -> 5.24 us
  local copies, waits for them, and re-layouts: 1.99 us -> 6.26 us
  other arithmetic: 3 us -> 1.66 us
    all_to_all x1 -> x0, blocking collectives: 36.1 us -> none  [per_device(): lax.all_to_all(outgoing.astype(jnp.bfloat16), 'shard', split_axis=0, conc...]
    ppermute x0 -> x19, starting transfers between devices: none -> 32.5 us  [the longest x11 23 us: other_core(): return lax.ppermute(x, 'replica', swap)]
    psum x1 -> x0, waiting for transfers between devices: 18.6 us -> none  [per_device(): lax.psum(arrived.astype(jnp.float32).astype(jnp.bfloat16), 'replica')]
    all_to_all x1 -> x0, waiting for transfers between devices: 12.2 us -> none  [per_device(): lax.all_to_all(scaled, 'shard', split_axis=0, concat_axis=0, tiled=True)]
    all_gather x1 -> x0, waiting for transfers between devices: 9.32 us -> none  [per_device(): left_side = lax.all_gather(partial_side, 'replica', axis=0, tiled=True)]
    dot_general x5 -> x2, matrix products: 11.3 us -> 2.97 us  [the longest x1 1.49 us: per_device_paired(): lax.dot_general(own_cols, summed, (((0,), (0,)), ((), ())), preferred_ele...]
    all_to_all x1 -> x0, starting transfers between devices: 5.76 us -> none  [per_device(): lax.all_to_all(scaled, 'shard', split_axis=0, concat_axis=0, tiled=True)]
    pallas_call x0 -> x4, Pallas kernels: none -> 5.24 us  [the longest x1 2.54 us: per_device_paired(): pl.pallas_call(functools.partial(precondition_kernel, rounds), out_shape=...]
  transfers between devices with their start and end apart: 3 -> 19, of which waited for: 3 -> 3; matrix products, arithmetic and copies ran while one was open for 5% -> 16% of each run, Pallas kernels for 0% -> 1%
where the time goes in v1:
time: 59.7 us; the launch traced here: 59.3 us
  starting transfers between devices  32.5 us (54%)
  local copies, waits for them, and re-layouts  6.26 us (10%)
  between operations  5.93 us (10%)
  Pallas kernels  5.24 us (9%)
  waiting for transfers between devices  4.82 us (8%)
  matrix products  2.97 us (5%)
  other arithmetic  1.66 us (3%)
    ppermute x11, starting transfers between devices, other_core(): return lax.ppermute(x, 'replica', swap)  23 us
    ppermute x8, starting transfers between devices, trade(): got = lax.ppermute(x, ('shard', 'replica'), turn(j))  9.42 us
    another operation x1, local copies, waits for them, and re-layouts, per_device_paired(): jnp.stack([block_of(c * rounds + (place ^ j)) for j in range(rounds) for...  5 us
    ppermute x8, waiting for transfers between devices, trade(): got = lax.ppermute(x, ('shard', 'replica'), turn(j))  3.41 us
    pallas_call x1, Pallas kernels, per_device_paired(): pl.pallas_call(functools.partial(precondition_kernel, rounds), out_shape=...  2.54 us
    dot_general x1, matrix products, per_device_paired(): lax.dot_general(own_cols, summed, (((0,), (0,)), ((), ())), preferred_ele...  1.49 us
    dot_general x1, matrix products, per_device_paired(): lax.dot_general(own_rows, summed, (((1,), (1,)), ((), ())), preferred_ele...  1.48 us
    reduce_max x1, other arithmetic, block_of(): return jnp.max(jnp.where(block_owner == owner, block_index, -1))  1.47 us
  transfers between devices with their start and end apart: 19, of which 3 were waited for; matrix products, arithmetic and copies ran while one was open for 16% of the time, Pallas kernels for 1%

profile of v1, /device:TPU:0, one launch (start us, length us, event | category | flops | bytes accessed | tf_op | source)
XLA Modules:
  0.0 59.3 jit_solution(3743344082125162264)
XLA Ops:
  0.6 0.5 collective-permute-start
  1.1 0.1 collective-permute-start.9
  1.2 1.5 %fusion.16 = (s32[]{:T(128)}, s32[]{:T(128)}, s32[]{:T(128)}, s32[]{:T(128)}, s32[]{:T(128)}, /*index=5*/s32[]{:T(128)}, s32[]{:T(128)}, s32[]{:T(128)}, s32[]{:T(128)}) fusion(s32[6]{0:T(128)} %param.7, s32[]{:T(128)S(6)} %add.60, s32[]{:T(128)S(6)} %add.58, s32[]{:T(128)S(6)} %add.57, s32[]{:T(128)S(6)} %add.53, s32[]{:T(128)S(6)} %add.52, s32[]{:T(128)S(6)} %add.51, ...), kind=kLoop, calls=%fused_computation.37 | loop fusion | flops 153 | bytes 96 | tf_op jit(solution)/shard_map/reduce_max | solution.py:138
  5.3 0.1 pad_add_fusion.1.index_ref
  5.3 0.0 collective-permute-done.theirs_ref
  5.3 1.2 %copy-done = bf16[1,6,96,768]{3,2,1,0:T(8,128)(2,1)S(1)} copy-done((bf16[1,6,96,768]{3,2,1,0:T(8,128)(2,1)S(1)}, bf16[1,6,96,768]{3,2,1,0:T(8,128)(2,1)}, u32[]{:S(2)}) %copy-start) | copy-done | bytes 884760
  6.5 0.7 %shard_map.85 = (bf16[96,768]{1,0:T(8,128)(2,1)S(1)}, bf16[96,768]{1,0:T(8,128)(2,1)S(1)}, bf16[96,768]{1,0:T(8,128)(2,1)S(1)}, bf16[96,768]{1,0:T(8,128)(2,1)S(1)}) custom-call(s32[4]{0:T(128)S(1)} %pad_add_fusion.1.index_ref, bf16[6,96,768]{2,1,0:T(8,128)(2,1)S(1)} %bitcast.46, bf16[6,96,768]{2,1,0:T(8,128)(2,1)S(1)} %collective-permute-done.theirs_ref), custom_call_target="tpu_custom_call" | custom-call | tf_op jit(solution)/shard_map/pallas_call | solution.py:145
  7.2 3.0 %collective-permute-start.2 = (bf16[96,768]{1,0:T(8,128)(2,1)S(1)}, bf16[96,768]{1,0:T(8,128)(2,1)S(1)}, u32[]{:S(2)}, u32[]{:S(2)}) collective-permute-start(bf16[96,768]{1,0:T(8,128)(2,1)S(1)} %get-tuple-element.16), channel_id=1, source_target_pairs={{0,2},{1,10},{2,0},{3,8},{4,6},{5,14},{6,4},{7,12},{8,3},{9,11},{1... | collective-permute-start | bytes 442376 | tf_op jit(solution)/shard_map/ppermute | solution.py:132
  10.2 1.6 %collective-permute-start.3 = (bf16[96,768]{1,0:T(8,128)(2,1)S(1)}, bf16[96,768]{1,0:T(8,128)(2,1)S(1)}, u32[]{:S(2)}, u32[]{:S(2)}) collective-permute-start(bf16[96,768]{1,0:T(8,128)(2,1)S(1)} %get-tuple-element.17), channel_id=1, source_target_pairs={{0,4},{1,12},{2,6},{3,14},{4,0},{5,8},{6,2},{7,10},{8,5},{9,13},{1... | collective-permute-start | bytes 442376 | tf_op jit(solution)/shard_map/ppermute | solution.py:132
  11.8 0.0 collective-permute-start.4
  11.8 0.7 %collective-permute-start.1 = (bf16[96,768]{1,0:T(8,128)(2,1)S(1)}, bf16[96,768]{1,0:T(8,128)(2,1)S(1)}, u32[]{:S(2)}, u32[]{:S(2)}) collective-permute-start(bf16[96,768]{1,0:T(8,128)(2,1)S(1)} %get-tuple-element.15), channel_id=1, source_target_pairs={{1,8},{3,10},{5,12},{7,14},{8,1},{10,3},{12,5},{14,7},{17,24},{19,... | collective-permute-start | bytes 442376 | tf_op jit(solution)/shard_map/ppermute | solution.py:132
  12.5 0.9 %collective-permute-done.2.refs_1_ = bf16[96,768]{1,0:T(8,128)(2,1)S(1)} collective-permute-done((bf16[96,768]{1,0:T(8,128)(2,1)S(1)}, bf16[96,768]{1,0:T(8,128)(2,1)S(1)}, u32[]{:S(2)}, u32[]{:S(2)}) %collective-permute-start.2) | collective-permute-done | bytes 147488 | tf_op jit(solution)/shard_map/ppermute | solution.py:132
  13.3 4.5 %collective-permute-start.6 = (bf16[96,768]{1,0:T(8,128)(2,1)S(1)}, bf16[96,768]{1,0:T(8,128)(2,1)S(1)}, u32[]{:S(2)}, u32[]{:S(2)}) collective-permute-start(bf16[96,768]{1,0:T(8,128)(2,1)S(1)} %collective-permute-done.2.refs_1_), channel_id=1, source_target_pairs={{0,1},{1,0},{2,3},{3,2},{4,5},{5,4},{6,7},{7,6},{8,9},{9,8},{10,11... | collective-permute-start | bytes 442376 | tf_op jit(solution)/shard_map/ppermute | solution.py:129
  17.9 0.0 collective-permute-done.3.refs_2_
  17.9 3.0 %collective-permute-start.7 = (bf16[96,768]{1,0:T(8,128)(2,1)S(1)}, bf16[96,768]{1,0:T(8,128)(2,1)S(1)}, u32[]{:S(2)}, u32[]{:S(2)}) collective-permute-start(bf16[96,768]{1,0:T(8,128)(2,1)S(1)} %collective-permute-done.3.refs_2_), channel_id=1, source_target_pairs={{0,1},{1,0},{2,3},{3,2},{4,5},{5,4},{6,7},{7,6},{8,9},{9,8},{10,11... | collective-permute-start | bytes 442376 | tf_op jit(solution)/shard_map/ppermute | solution.py:129
  20.9 0.0 collective-permute-done.4.refs_3_
  20.9 1.5 %collective-permute-start.8 = (bf16[96,768]{1,0:T(8,128)(2,1)S(1)}, bf16[96,768]{1,0:T(8,128)(2,1)S(1)}, u32[]{:S(2)}, u32[]{:S(2)}) collective-permute-start(bf16[96,768]{1,0:T(8,128)(2,1)S(1)} %collective-permute-done.4.refs_3_), channel_id=1, source_target_pairs={{0,1},{1,0},{2,3},{3,2},{4,5},{5,4},{6,7},{7,6},{8,9},{9,8},{10,11... | collective-permute-start | bytes 442376 | tf_op jit(solution)/shard_map/ppermute | solution.py:129
  22.4 0.0 collective-permute-done.1
  22.4 4.2 %collective-permute-start.5 = (bf16[96,768]{1,0:T(8,128)(2,1)S(1)}, bf16[96,768]{1,0:T(8,128)(2,1)S(1)}, u32[]{:S(2)}, u32[]{:S(2)}) collective-permute-start(bf16[96,768]{1,0:T(8,128)(2,1)S(1)} %broadcast_select_fusion.1.refs_0_), channel_id=1, source_target_pairs={{0,1},{1,0},{2,3},{3,2},{4,5},{5,4},{6,7},{7,6},{8,9},{9,8},{10,11... | collective-permute-start | bytes 442376 | tf_op jit(solution)/shard_map/ppermute | solution.py:129
  27.3 5.0 %stack.71.index_ref = s32[8]{0:T(128)S(1)} concatenate(s32[1]{0:T(128)} %bitcast.14, s32[1]{0:T(128)} %bitcast.15, s32[1]{0:T(128)} %bitcast.16, s32[1]{0:T(128)} %bitcast.17, s32[1]{0:T(128)} %bitcast.18, s32[1]{0:T(128)} %bitcast.19, s32[1]{0:T(128)} %bitcast.20, s32[1]{0:T(128)} %bitcast.21), dimensions={0} | concatenate | bytes 64 | tf_op jit(solution)/shard_map/stack | solution.py:196
  32.3 0.1 pad_add_fusion.place_ref
  32.3 0.0 collective-permute-done.9.refs_10_
  32.3 0.0 collective-permute-done.6.refs_5_
  32.3 0.0 collective-permute-done.7.refs_6_
  32.4 0.0 collective-permute-done.8.refs_7_
  32.4 0.0 collective-permute-done.5.refs_4_
  32.4 2.5 %shard_map.86 = (bf16[768,768]{1,0:T(8,128)(2,1)S(1)}, f32[384,768]{1,0:T(8,128)S(1)}, f32[1,1]{1,0:T(1,128)}, f32[1,1]{1,0:T(1,128)}) custom-call(s32[3]{0:T(128)S(1)} %pad_add_fusion.place_ref, bf16[96,768]{1,0:T(8,128)(2,1)S(1)} %broadcast_select_fusion.1.refs_0_, bf16[96,768]{1,0:T(8,128)(2,1)S(1)} %collective-permute-done.2.refs_1_, ...), custom_call_target="tpu_custom_call" | custom-call | tf_op jit(solution)/shard_map/pallas_call | solution.py:156
  34.9 0.0 collective-permute-start.10
  35.0 1.4 %collective-permute-done.10 = f32[1,1]{1,0:T(1,128)} collective-permute-done((f32[1,1]{1,0:T(1,128)}, f32[1,1]{1,0:T(1,128)}, u32[]{:S(2)}, u32[]{:S(2)}) %collective-permute-start.10) | collective-permute-done | bytes 36 | tf_op jit(solution)/shard_map/ppermute | solution.py:129
  38.2 0.6 %shard_map.87 = (bf16[2,96,384]{2,1,0:T(8,128)(2,1)S(1)}, bf16[2,96,384]{2,1,0:T(8,128)(2,1)S(1)}, bf16[2,96,384]{2,1,0:T(8,128)(2,1)S(1)}, bf16[2,96,384]{2,1,0:T(8,128)(2,1)S(1)}) custom-call(s32[3]{0:T(128)S(1)} %pad_add_fusion.place_ref, f32[1]{0:T(128)} %bitcast.22.graft_ref, f32[384,768]{1,0:T(8,128)S(1)} %get-tuple-element.22.both_ref), custom_call_target="tpu_custom_call" | custom-call | tf_op jit(solution)/shard_map/pallas_call | solution.py:171
  38.9 0.6 %collective-permute-start.12 = (bf16[2,96,384]{2,1,0:T(8,128)(2,1)S(1)}, bf16[2,96,384]{2,1,0:T(8,128)(2,1)S(1)}, u32[]{:S(2)}, u32[]{:S(2)}) collective-permute-start(bf16[2,96,384]{2,1,0:T(8,128)(2,1)S(1)} %get-tuple-element.24), channel_id=1, source_target_pairs={{0,2},{1,10},{2,0},{3,8},{4,6},{5,14},{6,4},{7,12},{8,3},{9,11},{1... | collective-permute-start | bytes 442376 | tf_op jit(solution)/shard_map/ppermute | solution.py:132
  39.5 1.5 %fusion.4 = bf16[1,384,768]{2,1,0:T(8,128)(2,1)} fusion(bf16[768,768]{1,0:T(8,128)(2,1)S(1)} %get-tuple-element.19, bf16[1,384,768]{2,1,0:T(8,128)(2,1)S(1)} %copy-done.3, s32[]{:T(128)S(6)} %select_n.77, f32[]{:T(128)S(6)} %select_n.68), kind=kOutput, calls=%fused_computation.6 | convolution fusion | flops 454459392 | bytes 2949128 | tf_op jit(solution)/shard_map/dot_general | solution.py:190
  41.0 0.4 collective-permute-start.13
  41.4 2.5 %collective-permute-start.14 = (bf16[2,96,384]{2,1,0:T(8,128)(2,1)S(1)}, bf16[2,96,384]{2,1,0:T(8,128)(2,1)S(1)}, u32[]{:S(2)}, u32[]{:S(2)}) collective-permute-start(bf16[2,96,384]{2,1,0:T(8,128)(2,1)S(1)} %get-tuple-element.26), channel_id=1, source_target_pairs={{0,6},{1,14},{2,4},{3,12},{4,2},{5,10},{6,0},{7,8},{8,7},{9,15},{1... | collective-permute-start | bytes 442376 | tf_op jit(solution)/shard_map/ppermute | solution.py:132
  43.9 0.7 %collective-permute-start.11 = (bf16[2,96,384]{2,1,0:T(8,128)(2,1)S(1)}, bf16[2,96,384]{2,1,0:T(8,128)(2,1)S(1)}, u32[]{:S(2)}, u32[]{:S(2)}) collective-permute-start(bf16[2,96,384]{2,1,0:T(8,128)(2,1)S(1)} %get-tuple-element.23), channel_id=1, source_target_pairs={{1,8},{3,10},{5,12},{7,14},{8,1},{10,3},{12,5},{14,7},{17,24},{19,... | collective-permute-start | bytes 442376 | tf_op jit(solution)/shard_map/ppermute | solution.py:132
  44.6 0.0 collective-permute-done.12
  44.6 3.9 %collective-permute-start.16 = (bf16[96,384]{1,0:T(8,128)(2,1)S(1)}, bf16[96,384]{1,0:T(8,128)(2,1)S(1)}, u32[]{:S(2)}, u32[]{:S(2)}) collective-permute-start(bf16[96,384]{1,0:T(8,128)(2,1)S(1)} %get-tuple-element.40), channel_id=1, source_target_pairs={{0,1},{1,0},{2,3},{3,2},{4,5},{5,4},{6,7},{7,6},{8,9},{9,8},{10,11... | collective-permute-start | bytes 221192 | tf_op jit(solution)/shard_map/ppermute | solution.py:129
  48.5 0.0 collective-permute-done.13
  48.5 2.2 %collective-permute-start.17 = (bf16[96,384]{1,0:T(8,128)(2,1)S(1)}, bf16[96,384]{1,0:T(8,128)(2,1)S(1)}, u32[]{:S(2)}, u32[]{:S(2)}) collective-permute-start(bf16[96,384]{1,0:T(8,128)(2,1)S(1)} %get-tuple-element.38), channel_id=1, source_target_pairs={{0,1},{1,0},{2,3},{3,2},{4,5},{5,4},{6,7},{7,6},{8,9},{9,8},{10,11... | collective-permute-start | bytes 221192 | tf_op jit(solution)/shard_map/ppermute | solution.py:129
  50.7 2.5 %collective-permute-done.14 = bf16[2,96,384]{2,1,0:T(8,128)(2,1)S(1)} collective-permute-done((bf16[2,96,384]{2,1,0:T(8,128)(2,1)S(1)}, bf16[2,96,384]{2,1,0:T(8,128)(2,1)S(1)}, u32[]{:S(2)}, u32[]{:S(2)}) %collective-permute-start.14) | collective-permute-done | bytes 147488 | tf_op jit(solution)/shard_map/ppermute | solution.py:132
  53.3 0.1 collective-permute-start.18
  53.4 0.0 collective-permute-done.11
  53.4 3.0 %collective-permute-start.15 = (bf16[96,384]{1,0:T(8,128)(2,1)S(1)}, bf16[96,384]{1,0:T(8,128)(2,1)S(1)}, u32[]{:S(2)}, u32[]{:S(2)}) collective-permute-start(bf16[96,384]{1,0:T(8,128)(2,1)S(1)} %get-tuple-element.42), channel_id=1, source_target_pairs={{0,1},{1,0},{2,3},{3,2},{4,5},{5,4},{6,7},{7,6},{8,9},{9,8},{10,11... | collective-permute-start | bytes 221192 | tf_op jit(solution)/shard_map/ppermute | solution.py:129
  56.4 1.5 %fusion.5 = bf16[1,384,768]{2,1,0:T(8,128)(2,1)} fusion(bf16[768,768]{1,0:T(8,128)(2,1)S(1)} %get-tuple-element.19, bf16[1,384,768]{2,1,0:T(8,128)(2,1)S(1)} %copy-done.4, s32[]{:T(128)S(6)} %select_n.77, f32[]{:T(128)S(6)} %select_n.68), kind=kOutput, calls=%fused_computation.7 | convolution fusion | flops 454459392 | bytes 2949128 | tf_op jit(solution)/shard_map/dot_general | solution.py:187
  57.9 0.0 collective-permute-done.16.refs_5_
  57.9 0.0 collective-permute-done.17.refs_6_
  57.9 0.0 collective-permute-done.18.refs_7_
  57.9 1.4 %shard_map.88 = bf16[6,96,384]{2,1,0:T(8,128)(2,1)} custom-call(s32[8]{0:T(128)S(1)} %stack.71.index_ref, bf16[96,384]{1,0:T(8,128)(2,1)S(1)} %get-tuple-element.43.refs_0_, bf16[96,384]{1,0:T(8,128)(2,1)S(1)} %get-tuple-element.41.refs_1_, bf16[96,384]{1,0:T(8,128)(2,1)S(1)} %get-tuple-element.39.refs_2_, bf16[96,384]{1,0:T(8,128)(2,1)S(1)} %get-tuple-element.37.refs_3_, ...), custom_call_target="tpu_custom_call" | custom-call | tf_op jit(solution)/shard_map/pallas_call | solution.py:202
  (16 shorter events, 0.1 us)
Async XLA Ops:
  0.6 4.7 %collective-permute-start = (bf16[6,96,768]{2,1,0:T(8,128)(2,1)}, bf16[6,96,768]{2,1,0:T(8,128)(2,1)S(1)}, u32[]{:S(2)}, u32[]{:S(2)}) collective-permute-start(bf16[6,96,768]{2,1,0:T(8,128)(2,1)} %bitcast.45), channel_id=1, source_target_pairs={{0,1},{1,0},{2,3},{3,2},{4,5},{5,4},{6,7},{7,6},{8,9},{9,8},{10,11... | collective-permute-start | bytes 2654216 | tf_op jit(solution)/shard_map/ppermute | solution.py:129
  1.1 31.2 %collective-permute-start.9 = (bf16[768,384]{1,0:T(8,128)(2,1)}, bf16[768,384]{1,0:T(8,128)(2,1)S(1)}, u32[]{:S(2)}, u32[]{:S(2)}) collective-permute-start(bf16[768,384]{1,0:T(8,128)(2,1)} %bitcast.48), channel_id=1, source_target_pairs={{0,1},{1,0},{2,3},{3,2},{4,5},{5,4},{6,7},{7,6},{8,9},{9,8},{10,11... | collective-permute-start | bytes 1769480 | tf_op jit(solution)/shard_map/ppermute | solution.py:129
  5.3 1.2 %copy-start = (bf16[1,6,96,768]{3,2,1,0:T(8,128)(2,1)S(1)}, bf16[1,6,96,768]{3,2,1,0:T(8,128)(2,1)}, u32[]{:S(2)}) copy-start(bf16[1,6,96,768]{3,2,1,0:T(8,128)(2,1)} %param.6) | copy-start | bytes 2654212
  6.5 25.9 %copy-start.1 = (bf16[1,384,768]{2,1,0:T(8,128)(2,1)S(1)}, bf16[1,384,768]{2,1,0:T(8,128)(2,1)}, u32[]{:S(2)}) copy-start(bf16[1,384,768]{2,1,0:T(8,128)(2,1)} %param.10) | copy-start | bytes 1769476
  6.5 25.9 %copy-start.2 = (bf16[1,768,384]{2,1,0:T(8,128)(2,1)S(1)}, bf16[1,768,384]{2,1,0:T(8,128)(2,1)}, u32[]{:S(2)}) copy-start(bf16[1,768,384]{2,1,0:T(8,128)(2,1)} %param.11) | copy-start | bytes 1769476
  7.2 6.1 %collective-permute-start.2 = (bf16[96,768]{1,0:T(8,128)(2,1)S(1)}, bf16[96,768]{1,0:T(8,128)(2,1)S(1)}, u32[]{:S(2)}, u32[]{:S(2)}) collective-permute-start(bf16[96,768]{1,0:T(8,128)(2,1)S(1)} %get-tuple-element.16), channel_id=1, source_target_pairs={{0,2},{1,10},{2,0},{3,8},{4,6},{5,14},{6,4},{7,12},{8,3},{9,11},{1... | collective-permute-start | bytes 442376 | tf_op jit(solution)/shard_map/ppermute | solution.py:132
  10.2 7.7 %collective-permute-start.3 = (bf16[96,768]{1,0:T(8,128)(2,1)S(1)}, bf16[96,768]{1,0:T(8,128)(2,1)S(1)}, u32[]{:S(2)}, u32[]{:S(2)}) collective-permute-start(bf16[96,768]{1,0:T(8,128)(2,1)S(1)} %get-tuple-element.17), channel_id=1, source_target_pairs={{0,4},{1,12},{2,6},{3,14},{4,0},{5,8},{6,2},{7,10},{8,5},{9,13},{1... | collective-permute-start | bytes 442376 | tf_op jit(solution)/shard_map/ppermute | solution.py:132
  11.8 9.1 %collective-permute-start.4 = (bf16[96,768]{1,0:T(8,128)(2,1)S(1)}, bf16[96,768]{1,0:T(8,128)(2,1)S(1)}, u32[]{:S(2)}, u32[]{:S(2)}) collective-permute-start(bf16[96,768]{1,0:T(8,128)(2,1)S(1)} %get-tuple-element.18), channel_id=1, source_target_pairs={{0,6},{1,14},{2,4},{3,12},{4,2},{5,10},{6,0},{7,8},{8,7},{9,15},{1... | collective-permute-start | bytes 442376 | tf_op jit(solution)/shard_map/ppermute | solution.py:132
  11.8 10.6 %collective-permute-start.1 = (bf16[96,768]{1,0:T(8,128)(2,1)S(1)}, bf16[96,768]{1,0:T(8,128)(2,1)S(1)}, u32[]{:S(2)}, u32[]{:S(2)}) collective-permute-start(bf16[96,768]{1,0:T(8,128)(2,1)S(1)} %get-tuple-element.15), channel_id=1, source_target_pairs={{1,8},{3,10},{5,12},{7,14},{8,1},{10,3},{12,5},{14,7},{17,24},{19,... | collective-permute-start | bytes 442376 | tf_op jit(solution)/shard_map/ppermute | solution.py:132
  13.3 19.0 %collective-permute-start.6 = (bf16[96,768]{1,0:T(8,128)(2,1)S(1)}, bf16[96,768]{1,0:T(8,128)(2,1)S(1)}, u32[]{:S(2)}, u32[]{:S(2)}) collective-permute-start(bf16[96,768]{1,0:T(8,128)(2,1)S(1)} %collective-permute-done.2.refs_1_), channel_id=1, source_target_pairs={{0,1},{1,0},{2,3},{3,2},{4,5},{5,4},{6,7},{7,6},{8,9},{9,8},{10,11... | collective-permute-start | bytes 442376 | tf_op jit(solution)/shard_map/ppermute | solution.py:129
  17.9 14.5 %collective-permute-start.7 = (bf16[96,768]{1,0:T(8,128)(2,1)S(1)}, bf16[96,768]{1,0:T(8,128)(2,1)S(1)}, u32[]{:S(2)}, u32[]{:S(2)}) collective-permute-start(bf16[96,768]{1,0:T(8,128)(2,1)S(1)} %collective-permute-done.3.refs_2_), channel_id=1, source_target_pairs={{0,1},{1,0},{2,3},{3,2},{4,5},{5,4},{6,7},{7,6},{8,9},{9,8},{10,11... | collective-permute-start | bytes 442376 | tf_op jit(solution)/shard_map/ppermute | solution.py:129
  20.9 11.5 %collective-permute-start.8 = (bf16[96,768]{1,0:T(8,128)(2,1)S(1)}, bf16[96,768]{1,0:T(8,128)(2,1)S(1)}, u32[]{:S(2)}, u32[]{:S(2)}) collective-permute-start(bf16[96,768]{1,0:T(8,128)(2,1)S(1)} %collective-permute-done.4.refs_3_), channel_id=1, source_target_pairs={{0,1},{1,0},{2,3},{3,2},{4,5},{5,4},{6,7},{7,6},{8,9},{9,8},{10,11... | collective-permute-start | bytes 442376 | tf_op jit(solution)/shard_map/ppermute | solution.py:129
  22.4 9.9 %collective-permute-start.5 = (bf16[96,768]{1,0:T(8,128)(2,1)S(1)}, bf16[96,768]{1,0:T(8,128)(2,1)S(1)}, u32[]{:S(2)}, u32[]{:S(2)}) collective-permute-start(bf16[96,768]{1,0:T(8,128)(2,1)S(1)} %broadcast_select_fusion.1.refs_0_), channel_id=1, source_target_pairs={{0,1},{1,0},{2,3},{3,2},{4,5},{5,4},{6,7},{7,6},{8,9},{9,8},{10,11... | collective-permute-start | bytes 442376 | tf_op jit(solution)/shard_map/ppermute | solution.py:129
  34.9 4.5 %copy-start.3 = (bf16[1,384,768]{2,1,0:T(8,128)(2,1)S(1)}, bf16[1,384,768]{2,1,0:T(8,128)(2,1)}, u32[]{:S(2)}) copy-start(bf16[1,384,768]{2,1,0:T(8,128)(2,1)} %param.9) | copy-start | bytes 1769476
  34.9 1.4 %collective-permute-start.10 = (f32[1,1]{1,0:T(1,128)}, f32[1,1]{1,0:T(1,128)}, u32[]{:S(2)}, u32[]{:S(2)}) collective-permute-start(f32[1,1]{1,0:T(1,128)} %get-tuple-element.21), channel_id=1, source_target_pairs={{0,1},{1,0},{2,3},{3,2},{4,5},{5,4},{6,7},{7,6},{8,9},{9,8},{10,11... | collective-permute-start | bytes 20 | tf_op jit(solution)/shard_map/ppermute | solution.py:129
  38.9 5.7 %collective-permute-start.12 = (bf16[2,96,384]{2,1,0:T(8,128)(2,1)S(1)}, bf16[2,96,384]{2,1,0:T(8,128)(2,1)S(1)}, u32[]{:S(2)}, u32[]{:S(2)}) collective-permute-start(bf16[2,96,384]{2,1,0:T(8,128)(2,1)S(1)} %get-tuple-element.24), channel_id=1, source_target_pairs={{0,2},{1,10},{2,0},{3,8},{4,6},{5,14},{6,4},{7,12},{8,3},{9,11},{1... | collective-permute-start | bytes 442376 | tf_op jit(solution)/shard_map/ppermute | solution.py:132
  41.0 15.5 %copy-start.4 = (bf16[1,384,768]{2,1,0:T(8,128)(2,1)S(1)}, bf16[1,384,768]{2,1,0:T(8,128)(2,1)}, u32[]{:S(2)}) copy-start(bf16[1,384,768]{2,1,0:T(8,128)(2,1)} %param.8) | copy-start | bytes 1769476
  41.0 7.6 %collective-permute-start.13 = (bf16[2,96,384]{2,1,0:T(8,128)(2,1)S(1)}, bf16[2,96,384]{2,1,0:T(8,128)(2,1)S(1)}, u32[]{:S(2)}, u32[]{:S(2)}) collective-permute-start(bf16[2,96,384]{2,1,0:T(8,128)(2,1)S(1)} %get-tuple-element.25), channel_id=1, source_target_pairs={{0,4},{1,12},{2,6},{3,14},{4,0},{5,8},{6,2},{7,10},{8,5},{9,13},{1... | collective-permute-start | bytes 442376 | tf_op jit(solution)/shard_map/ppermute | solution.py:132
  41.4 11.9 %collective-permute-start.14 = (bf16[2,96,384]{2,1,0:T(8,128)(2,1)S(1)}, bf16[2,96,384]{2,1,0:T(8,128)(2,1)S(1)}, u32[]{:S(2)}, u32[]{:S(2)}) collective-permute-start(bf16[2,96,384]{2,1,0:T(8,128)(2,1)S(1)} %get-tuple-element.26), channel_id=1, source_target_pairs={{0,6},{1,14},{2,4},{3,12},{4,2},{5,10},{6,0},{7,8},{8,7},{9,15},{1... | collective-permute-start | bytes 442376 | tf_op jit(solution)/shard_map/ppermute | solution.py:132
  43.9 9.4 %collective-permute-start.11 = (bf16[2,96,384]{2,1,0:T(8,128)(2,1)S(1)}, bf16[2,96,384]{2,1,0:T(8,128)(2,1)S(1)}, u32[]{:S(2)}, u32[]{:S(2)}) collective-permute-start(bf16[2,96,384]{2,1,0:T(8,128)(2,1)S(1)} %get-tuple-element.23), channel_id=1, source_target_pairs={{1,8},{3,10},{5,12},{7,14},{8,1},{10,3},{12,5},{14,7},{17,24},{19,... | collective-permute-start | bytes 442376 | tf_op jit(solution)/shard_map/ppermute | solution.py:132
  44.6 13.3 %collective-permute-start.16 = (bf16[96,384]{1,0:T(8,128)(2,1)S(1)}, bf16[96,384]{1,0:T(8,128)(2,1)S(1)}, u32[]{:S(2)}, u32[]{:S(2)}) collective-permute-start(bf16[96,384]{1,0:T(8,128)(2,1)S(1)} %get-tuple-element.40), channel_id=1, source_target_pairs={{0,1},{1,0},{2,3},{3,2},{4,5},{5,4},{6,7},{7,6},{8,9},{9,8},{10,11... | collective-permute-start | bytes 221192 | tf_op jit(solution)/shard_map/ppermute | solution.py:129
  48.5 9.4 %collective-permute-start.17 = (bf16[96,384]{1,0:T(8,128)(2,1)S(1)}, bf16[96,384]{1,0:T(8,128)(2,1)S(1)}, u32[]{:S(2)}, u32[]{:S(2)}) collective-permute-start(bf16[96,384]{1,0:T(8,128)(2,1)S(1)} %get-tuple-element.38), channel_id=1, source_target_pairs={{0,1},{1,0},{2,3},{3,2},{4,5},{5,4},{6,7},{7,6},{8,9},{9,8},{10,11... | collective-permute-start | bytes 221192 | tf_op jit(solution)/shard_map/ppermute | solution.py:129
  53.3 4.7 %collective-permute-start.18 = (bf16[96,384]{1,0:T(8,128)(2,1)S(1)}, bf16[96,384]{1,0:T(8,128)(2,1)S(1)}, u32[]{:S(2)}, u32[]{:S(2)}) collective-permute-start(bf16[96,384]{1,0:T(8,128)(2,1)S(1)} %get-tuple-element.36), channel_id=1, source_target_pairs={{0,1},{1,0},{2,3},{3,2},{4,5},{5,4},{6,7},{7,6},{8,9},{9,8},{10,11... | collective-permute-start | bytes 221192 | tf_op jit(solution)/shard_map/ppermute | solution.py:129
  53.4 4.5 %collective-permute-start.15 = (bf16[96,384]{1,0:T(8,128)(2,1)S(1)}, bf16[96,384]{1,0:T(8,128)(2,1)S(1)}, u32[]{:S(2)}, u32[]{:S(2)}) collective-permute-start(bf16[96,384]{1,0:T(8,128)(2,1)S(1)} %get-tuple-element.42), channel_id=1, source_target_pairs={{0,1},{1,0},{2,3},{3,2},{4,5},{5,4},{6,7},{7,6},{8,9},{9,8},{10,11... | collective-permute-start | bytes 221192 | tf_op jit(solution)/shard_map/ppermute | solution.py:129

commit v2 on v0

--- a/solution.py
+++ b/solution.py
@@ -1,7 +1,17 @@
+import functools
+
 import jax
 import jax.numpy as jnp
 from jax import lax
+from jax.experimental import pallas as pl
+from jax.experimental.pallas import tpu as pltpu
 from jax.sharding import PartitionSpec as P
+
+VMEM = pl.BlockSpec(memory_space=pltpu.VMEM)
+SMEM = pl.BlockSpec(memory_space=pltpu.SMEM)
+ANY = pl.BlockSpec(memory_space=pl.ANY)
+EARLY = 1
+PARAMS = pltpu.CompilerParams(vmem_limit_bytes=24 * 1024 * 1024)
 
 
 def per_device(gradients, block_owner, left_gram, right_gram, left_root, right_root):
@@ -45,9 +55,252 @@
     return (left_new[None], right_new[None], update)
 
 
+def device_place(rounds):
+    shard = lax.axis_index("shard")
+    return lax.div(shard, rounds), lax.rem(shard, rounds), lax.axis_index("replica")
+
+
+def block_of(owner_ref, owner):
+    block = jnp.int32(-1)
+    for b in range(owner_ref.shape[0]):
+        block = jnp.where(owner_ref[b] == owner, b, block)
+    return block
+
+
+def sent_block(owner_ref, rounds, j):
+    side, place, core = device_place(rounds)
+    return jnp.maximum(block_of(owner_ref, (side ^ core) * rounds + (place ^ j)), 0)
+
+
+def fetch_kernel(owner_ref, gradient_ref, out_ref, sem):
+    rounds = out_ref.shape[0]
+    copies = [
+        pltpu.make_async_copy(
+            gradient_ref.at[sent_block(owner_ref, rounds, j)], out_ref.at[j], sem.at[j]
+        )
+        for j in range(rounds)
+    ]
+    for copy in copies:
+        copy.start()
+    for copy in copies:
+        copy.wait()
+
+
+def pick_kernel(owner_ref, mine_ref, theirs_ref, *out_refs):
+    rounds = len(out_refs)
+    for j, out_ref in enumerate(out_refs):
+        other = theirs_ref[sent_block(owner_ref, rounds, j)]
+        total = mine_ref[j].astype(jnp.float32) + other.astype(jnp.float32)
+        out_ref[...] = total.astype(out_ref.dtype)
+
+
+def slab_for(ref, keep, row, slab, scale=None):
+    width = ref.shape[1] // 2
+    pieces = []
+    for side in (keep, 1 - keep):
+        piece = ref[pl.ds(row, slab), pl.ds(pl.multiple_of(side * width, 128), width)]
+        pieces.append(piece if scale is None else piece * scale)
+    return pieces
+
+
+def precondition_kernel(rounds, early, *refs):
+    mine, theirs = refs[:rounds], refs[rounds:2 * rounds]
+    left_ref, own_ref, other_ref, summed_ref, both_ref, side_sq_ref, grad_sq_ref = refs[
+        2 * rounds:2 * rounds + 7
+    ]
+    early_refs, side_ref = refs[2 * rounds + 7:-1], refs[-1]
+    side, place, core = device_place(rounds)
+    slab, full = mine[0].shape
+    half = rounds * slab
+    grad_sq = jnp.zeros((1, full), jnp.float32)
+    for j in range(rounds):
+        for ref, rows_side in ((mine[j], side ^ core), (theirs[j], side ^ (1 - core))):
+            row = pl.multiple_of(rows_side * half + (place ^ j) * slab, slab)
+            block = ref[...]
+            summed_ref[pl.ds(row, slab), :] = block
+            wide = block.astype(jnp.float32)
+            grad_sq += jnp.sum(wide * wide, axis=0, keepdims=True)
+    grad_sq_ref[...] = jnp.sum(grad_sq, axis=1, keepdims=True)
+    side_ref[...] = jnp.dot(
+        left_ref[...], summed_ref[...], preferred_element_type=jnp.float32
+    ).astype(side_ref.dtype)
+    side_sq = jnp.zeros((1, 1), jnp.float32)
+    for ref, columns_side in ((own_ref, core), (other_ref, 1 - core)):
+        both = jnp.dot(side_ref[...], ref[...], preferred_element_type=jnp.float32)
+        width = ref.shape[1]
+        both_ref[:, pl.ds(pl.multiple_of(columns_side * width, 128), width)] = both
+        side_sq += jnp.sum(jnp.sum(both * both, axis=0, keepdims=True), axis=1, keepdims=True)
+    side_sq_ref[...] = side_sq
+    for j, out_ref in zip(early, early_refs):
+        row = pl.multiple_of((place ^ j) * slab, slab)
+        for k, piece in enumerate(slab_for(both_ref, core, row, slab)):
+            out_ref[k] = piece.astype(out_ref.dtype)
+
+
+def scale_kernel(rounds, late, mine_sq_ref, theirs_sq_ref, grad_sq_ref, both_ref, graft_ref, *out_refs):
+    side, place, core = device_place(rounds)
+    slab = both_ref.shape[0] // rounds
+    side_sq = mine_sq_ref[...] + theirs_sq_ref[...]
+    graft = jnp.sqrt(grad_sq_ref[...] / (side_sq + 1e-06))
+    graft_ref[...] = jnp.broadcast_to(graft, graft_ref.shape)
+    for j, out_ref in zip(late, out_refs):
+        row = pl.multiple_of((place ^ j) * slab, slab)
+        for k, piece in enumerate(slab_for(both_ref, core, row, slab, graft)):
+            out_ref[k] = piece.astype(out_ref.dtype)
+
+
+def gram_kernel(owner_ref, summed_ref, left_ref, right_ref, after_ref, left_out, right_out):
+    half = left_ref.shape[0]
+    first = pl.multiple_of(lax.axis_index("replica") * half, 128)
+    present = block_of(owner_ref, lax.axis_index("shard")) >= 0
+    share = jnp.where(present, 0.01, 0.0).astype(jnp.float32)
+    summed = summed_ref[...]
+    left_term = lax.dot_general(
+        summed_ref[pl.ds(first, half), :], summed, (((1,), (1,)), ((), ())),
+        preferred_element_type=jnp.float32,
+    )
+    left_out[...] = (0.99 * left_ref[...].astype(jnp.float32) + share * left_term).astype(
+        left_out.dtype
+    )
+    right_term = lax.dot_general(
+        summed_ref[:, pl.ds(first, half)], summed, (((0,), (0,)), ((), ())),
+        preferred_element_type=jnp.float32,
+    )
+    right_out[...] = (0.99 * right_ref[...].astype(jnp.float32) + share * right_term).astype(
+        right_out.dtype
+    )
+
+
+def place_kernel(rounds, early, owner_ref, *refs):
+    slabs = (refs[:rounds], refs[rounds:2 * rounds])
+    grafts = refs[2 * rounds:2 * rounds + 2 * len(early)]
+    out_ref, scaled_ref, sem = refs[2 * rounds + 2 * len(early):]
+    side, place, core = device_place(rounds)
+    pending = []
+    for j in [j for j in range(rounds) if j not in early] + list(early):
+        for k in range(2):
+            owner = (side ^ core ^ k) * rounds + (place ^ j)
+            block = block_of(owner_ref, owner)
+            source = slabs[k][j].at[0] if k == 0 else slabs[k][j]
+            if j in early:
+                n = 2 * early.index(j) + k
+                ref = slabs[k][j]
+                value = ref[0] if k == 0 else ref[...]
+                scaled = value.astype(jnp.float32) * grafts[n][0:1, 0:1]
+                scaled_ref[n] = scaled.astype(scaled_ref.dtype)
+                source = scaled_ref.at[n]
+            copy = pltpu.make_async_copy(
+                source, out_ref.at[jnp.maximum(block, 0)], sem.at[2 * j + k]
+            )
+
+            @pl.when(block >= 0)
+            def _(copy=copy):
+                copy.start()
+
+            pending.append((block, copy))
+    for block, copy in pending:
+
+        @pl.when(block >= 0)
+        def _(copy=copy):
+            copy.wait()
+
+
+def per_device_paired(gradients, block_owner, left_gram, right_gram, left_root, right_root):
+    rounds = lax.axis_size("shard") // 2
+    blocks, slab, width = gradients.shape[1:]
+    half_rows = left_gram.shape[1]
+    order = [j for i in range((rounds + 1) // 2) for j in dict.fromkeys((i + rounds // 2, i))]
+    early, late = order[:EARLY], order[EARLY:]
+    places = [(h, l, r) for h in range(2) for l in range(rounds) for r in range(2)]
+
+    def device(h, l, r):
+        return (h * rounds + l) * 2 + r
+
+    def other_core(x):
+        return lax.ppermute(x, "replica", [(0, 1), (1, 0)])
+
+    def trade(x, j):
+        pairs = [(device(h, l, r), device(h ^ r, l ^ j, r)) for h, l, r in places]
+        return lax.ppermute(x, ("shard", "replica"), pairs)
+
+    def shape(dims, dtype=jnp.bfloat16):
+        return jax.ShapeDtypeStruct(dims, dtype)
+
+    def call(kernel, out_shape, in_specs, *args, **options):
+        return pl.pallas_call(
+            kernel, out_shape=out_shape, in_specs=in_specs, compiler_params=PARAMS, **options
+        )(*args)
+
+    other_gradient = other_core(gradients[0])
+    fetched = call(
+        fetch_kernel, shape((rounds, slab, width)), [SMEM, ANY], block_owner, gradients[0],
+        out_specs=VMEM, scratch_shapes=[pltpu.SemaphoreType.DMA((rounds,))],
+    )
+    outgoing = call(
+        pick_kernel, [shape((slab, width))] * rounds, [SMEM, VMEM, VMEM],
+        block_owner, fetched, other_gradient, out_specs=[VMEM] * rounds,
+    )
+    mine = {j: trade(outgoing[j], j) for j in order}
+    other_right = other_core(right_root[0])
+    left_rows = lax.ppermute(
+        left_root[0], ("shard", "replica"),
+        [(device(h, l, r), device(h, l, r ^ h)) for h, l, r in places],
+    )
+    theirs = {j: other_core(mine[j]) for j in order}
+    one = shape((1, 1), jnp.float32)
+    slab_shape = shape((2, slab, width // 2))
+    summed, both_sides, side_sq, grad_sq, *first = call(
+        functools.partial(precondition_kernel, rounds, early),
+        [shape((width, width)), shape((half_rows, width), jnp.float32), one, one]
+        + [slab_shape] * len(early),
+        [VMEM] * (2 * rounds + 3),
+        *[mine[j] for j in range(rounds)], *[theirs[j] for j in range(rounds)],
+        left_rows, right_root[0], other_right,
+        out_specs=[VMEM] * (4 + len(early)),
+        scratch_shapes=[pltpu.VMEM((half_rows, width), jnp.bfloat16)],
+    )
+    returned = {j: trade(x, j) for j, x in zip(early, first)}
+    graft, *rest = call(
+        functools.partial(scale_kernel, rounds, late),
+        [shape((8, 128), jnp.float32)] + [slab_shape] * len(late),
+        [VMEM] * 4, side_sq, other_core(side_sq), grad_sq, both_sides,
+        out_specs=[VMEM] * (1 + len(late)),
+    )
+    returned.update((j, trade(x, j)) for j, x in zip(late, rest))
+    grafts = []
+    for j in early:
+        came = trade(graft, j)
+        grafts += [came, other_core(came)]
+    passed = {j: other_core(returned[j][1]) for j in order}
+
+    left_new, right_new = call(
+        gram_kernel, [shape(left_gram.shape[1:]), shape(right_gram.shape[1:])],
+        [SMEM, VMEM, VMEM, VMEM, ANY],
+        block_owner, summed, left_gram[0], right_gram[0], returned[order[0]],
+        out_specs=[VMEM, VMEM],
+        cost_estimate=pl.CostEstimate(
+            flops=4 * half_rows * width * width, bytes_accessed=8 * half_rows * width,
+            transcendentals=0,
+        ),
+    )
+    update = call(
+        functools.partial(place_kernel, rounds, early), shape((blocks, slab, width // 2)),
+        [SMEM] + [VMEM] * (2 * rounds + len(grafts)), block_owner,
+        *[returned[j] for j in range(rounds)], *[passed[j] for j in range(rounds)], *grafts,
+        out_specs=ANY,
+        scratch_shapes=[
+            pltpu.VMEM((max(1, 2 * len(early)), slab, width // 2), jnp.bfloat16),
+            pltpu.SemaphoreType.DMA((2 * rounds,)),
+        ],
+    )
+    return (left_new[None], right_new[None], update)
+
+
 def solution(mesh):
+    owners = mesh.shape["shard"]
+    paired = mesh.shape["replica"] == 2 and owners in (2, 4, 8, 16)
     return jax.shard_map(
-        per_device,
+        per_device_paired if paired else per_device,
         mesh=mesh,
         in_specs=(
             P("replica", "groups", "shard", None),

time: 117 us -> 54.6 us (0.47)
  blocking collectives: 39.2 us -> 0 us
  waiting for transfers between devices: 40.2 us -> 1.99 us
  starting transfers between devices: 5.84 us -> 39.6 us
  between operations: 15.5 us -> 0.78 us
  matrix products: 11.3 us -> 0 us
  Pallas kernels: 0 us -> 10.1 us
  other arithmetic: 3 us -> 0 us
    ppermute x0 -> x22, starting transfers between devices: none -> 39.6 us  [the longest x12 25.2 us: other_core(): return lax.ppermute(x, 'replica', [(0, 1), (1, 0)])]
    all_to_all x1 -> x0, blocking collectives: 36.1 us -> none  [per_device(): lax.all_to_all(outgoing.astype(jnp.bfloat16), 'shard', split_axis=0, conc...]
    psum x1 -> x0, waiting for transfers between devices: 18.6 us -> none  [per_device(): lax.psum(arrived.astype(jnp.float32).astype(jnp.bfloat16), 'replica')]
    all_to_all x1 -> x0, waiting for transfers between devices: 12.2 us -> none  [per_device(): lax.all_to_all(scaled, 'shard', split_axis=0, concat_axis=0, tiled=True)]
    dot_general x5 -> x0, matrix products: 11.3 us -> none  [the longest x1 3 us: per_device(): jnp.dot(left_root[0], summed_block, preferred_element_type=jnp.float32)]
    pallas_call x0 -> x6, Pallas kernels: none -> 10.1 us  [call(): pl.pallas_call(kernel, out_shape=out_shape, in_specs=in_specs, compiler_p...]
    all_gather x1 -> x0, waiting for transfers between devices: 9.32 us -> none  [per_device(): left_side = lax.all_gather(partial_side, 'replica', axis=0, tiled=True)]
    all_to_all x1 -> x0, starting transfers between devices: 5.76 us -> none  [per_device(): lax.all_to_all(scaled, 'shard', split_axis=0, concat_axis=0, tiled=True)]
  transfers between devices with their start and end apart: 3 -> 22, of which waited for: 3 -> 2; matrix products, arithmetic and copies ran while one was open for 5% -> 0% of each run, Pallas kernels for 0% -> 12%
where the time goes in v2:
time: 54.6 us; the launch traced here: 54.3 us
  starting transfers between devices  39.6 us (73%)
  Pallas kernels  10.1 us (18%)
  waiting for transfers between devices  1.99 us (4%)
  local copies, waits for them, and re-layouts  1.87 us (3%)
  between operations  0.78 us (1%)
    ppermute x12, starting transfers between devices, other_core(): return lax.ppermute(x, 'replica', [(0, 1), (1, 0)])  25.2 us
    ppermute x9, starting transfers between devices, trade(): return lax.ppermute(x, ('shard', 'replica'), pairs)  12.7 us
    pallas_call x6, Pallas kernels, call(): pl.pallas_call(kernel, out_shape=out_shape, in_specs=in_specs, compiler_p...  10.1 us
    ppermute x12, waiting for transfers between devices, other_core(): return lax.ppermute(x, 'replica', [(0, 1), (1, 0)])  1.96 us
    unnamed x12, local copies, waits for them, and re-layouts  1.84 us
    ppermute x1, starting transfers between devices, per_device_paired(): lax.ppermute(left_root[0], ('shard', 'replica'), [(device(h, l, r), devic...  1.71 us
  transfers between devices with their start and end apart: 22, of which 2 were waited for; matrix products, arithmetic and copies ran while one was open for 0% of the time, Pallas kernels for 12%

profile of v2, /device:TPU:0, one launch (start us, length us, event | category | flops | bytes accessed | tf_op | source)
XLA Modules:
  0.0 54.3 jit_solution(5678842292394019331)
XLA Ops:
  0.6 0.5 collective-permute-start
  1.1 1.7 %collective-permute-start.9 = (bf16[384,768]{1,0:T(8,128)(2,1)}, bf16[384,768]{1,0:T(8,128)(2,1)S(1)}, u32[]{:S(2)}, u32[]{:S(2)}) collective-permute-start(bf16[384,768]{1,0:T(8,128)(2,1)} %bitcast.21), channel_id=1, source_target_pairs={{0,0},{1,1},{2,2},{3,3},{4,4},{5,5},{6,6},{7,7},{8,9},{9,8},{10,11... | collective-permute-start | bytes 1769480 | tf_op jit(solution)/shard_map/ppermute | solution.py:245
  2.9 0.1 collective-permute-start.10
  2.9 1.2 %copy-done = bf16[1,6,96,768]{3,2,1,0:T(8,128)(2,1)S(1)} copy-done((bf16[1,6,96,768]{3,2,1,0:T(8,128)(2,1)S(1)}, bf16[1,6,96,768]{3,2,1,0:T(8,128)(2,1)}, u32[]{:S(2)}) %copy-start) | copy-done | bytes 884760
  4.1 0.7 %copy-done.2 = s32[6]{0:T(128)S(1)} copy-done((s32[6]{0:T(128)S(1)}, s32[6]{0:T(128)}, u32[]{:S(2)}) %copy-start.2) | copy-done | bytes 48
  4.7 1.4 %shard_map.85.mine_ref = bf16[4,96,768]{2,1,0:T(8,128)(2,1)S(1)} custom-call(s32[6]{0:T(128)S(1)} %copy-done.2, bf16[6,96,768]{2,1,0:T(8,128)(2,1)S(1)} %bitcast.16), custom_call_target="tpu_custom_call" | custom-call | tf_op jit(solution)/shard_map/pallas_call | solution.py:230
  6.1 0.0 collective-permute-done.theirs_ref
  6.1 0.7 %shard_map.86 = (bf16[96,768]{1,0:T(8,128)(2,1)S(1)}, bf16[96,768]{1,0:T(8,128)(2,1)S(1)}, bf16[96,768]{1,0:T(8,128)(2,1)S(1)}, bf16[96,768]{1,0:T(8,128)(2,1)S(1)}) custom-call(s32[6]{0:T(128)S(1)} %copy-done.2, bf16[4,96,768]{2,1,0:T(8,128)(2,1)S(1)} %shard_map.85.mine_ref, bf16[6,96,768]{2,1,0:T(8,128)(2,1)S(1)} %collective-permute-done.theirs_ref), custom_call_target="tpu_custom_call" | custom-call | tf_op jit(solution)/shard_map/pallas_call | solution.py:230
  6.8 0.7 %collective-permute-start.1 = (bf16[96,768]{1,0:T(8,128)(2,1)S(1)}, bf16[96,768]{1,0:T(8,128)(2,1)S(1)}, u32[]{:S(2)}, u32[]{:S(2)}) collective-permute-start(bf16[96,768]{1,0:T(8,128)(2,1)S(1)} %get-tuple-element.18), channel_id=1, source_target_pairs={{0,0},{1,9},{2,2},{3,11},{4,4},{5,13},{6,6},{7,15},{8,8},{9,1},{10... | collective-permute-start | bytes 442376 | tf_op jit(solution)/shard_map/ppermute | solution.py:224
  7.5 3.0 %collective-permute-start.2 = (bf16[96,768]{1,0:T(8,128)(2,1)S(1)}, bf16[96,768]{1,0:T(8,128)(2,1)S(1)}, u32[]{:S(2)}, u32[]{:S(2)}) collective-permute-start(bf16[96,768]{1,0:T(8,128)(2,1)S(1)} %get-tuple-element.19), channel_id=1, source_target_pairs={{0,2},{1,11},{2,0},{3,9},{4,6},{5,15},{6,4},{7,13},{8,10},{9,3},{1... | collective-permute-start | bytes 442376 | tf_op jit(solution)/shard_map/ppermute | solution.py:224
  10.5 1.6 %collective-permute-start.3 = (bf16[96,768]{1,0:T(8,128)(2,1)S(1)}, bf16[96,768]{1,0:T(8,128)(2,1)S(1)}, u32[]{:S(2)}, u32[]{:S(2)}) collective-permute-start(bf16[96,768]{1,0:T(8,128)(2,1)S(1)} %get-tuple-element.20), channel_id=1, source_target_pairs={{0,4},{1,13},{2,6},{3,15},{4,0},{5,9},{6,2},{7,11},{8,12},{9,5},{1... | collective-permute-start | bytes 442376 | tf_op jit(solution)/shard_map/ppermute | solution.py:224
  12.1 0.0 collective-permute-done.9.refs_8_
  12.1 0.0 collective-permute-start.4
  12.1 0.0 collective-permute-done.1.refs_0_
  12.1 5.6 %collective-permute-start.5 = (bf16[96,768]{1,0:T(8,128)(2,1)S(1)}, bf16[96,768]{1,0:T(8,128)(2,1)S(1)}, u32[]{:S(2)}, u32[]{:S(2)}) collective-permute-start(bf16[96,768]{1,0:T(8,128)(2,1)S(1)} %collective-permute-done.1.refs_0_), channel_id=1, source_target_pairs={{0,1},{1,0},{2,3},{3,2},{4,5},{5,4},{6,7},{7,6},{8,9},{9,8},{10,11... | collective-permute-start | bytes 442376 | tf_op jit(solution)/shard_map/ppermute | solution.py:220
  17.7 0.0 collective-permute-done.2.refs_1_
  17.7 3.0 %collective-permute-start.6 = (bf16[96,768]{1,0:T(8,128)(2,1)S(1)}, bf16[96,768]{1,0:T(8,128)(2,1)S(1)}, u32[]{:S(2)}, u32[]{:S(2)}) collective-permute-start(bf16[96,768]{1,0:T(8,128)(2,1)S(1)} %collective-permute-done.2.refs_1_), channel_id=1, source_target_pairs={{0,1},{1,0},{2,3},{3,2},{4,5},{5,4},{6,7},{7,6},{8,9},{9,8},{10,11... | collective-permute-start | bytes 442376 | tf_op jit(solution)/shard_map/ppermute | solution.py:220
  20.7 0.0 collective-permute-done.3.refs_2_
  20.7 2.5 %collective-permute-start.7 = (bf16[96,768]{1,0:T(8,128)(2,1)S(1)}, bf16[96,768]{1,0:T(8,128)(2,1)S(1)}, u32[]{:S(2)}, u32[]{:S(2)}) collective-permute-start(bf16[96,768]{1,0:T(8,128)(2,1)S(1)} %collective-permute-done.3.refs_2_), channel_id=1, source_target_pairs={{0,1},{1,0},{2,3},{3,2},{4,5},{5,4},{6,7},{7,6},{8,9},{9,8},{10,11... | collective-permute-start | bytes 442376 | tf_op jit(solution)/shard_map/ppermute | solution.py:220
  23.3 0.0 collective-permute-done.4.refs_3_
  23.3 2.4 %collective-permute-start.8 = (bf16[96,768]{1,0:T(8,128)(2,1)S(1)}, bf16[96,768]{1,0:T(8,128)(2,1)S(1)}, u32[]{:S(2)}, u32[]{:S(2)}) collective-permute-start(bf16[96,768]{1,0:T(8,128)(2,1)S(1)} %collective-permute-done.4.refs_3_), channel_id=1, source_target_pairs={{0,1},{1,0},{2,3},{3,2},{4,5},{5,4},{6,7},{7,6},{8,9},{9,8},{10,11... | collective-permute-start | bytes 442376 | tf_op jit(solution)/shard_map/ppermute | solution.py:220
  25.7 0.0 collective-permute-done.10.refs_10_
  25.7 0.0 collective-permute-done.5.refs_4_
  25.7 0.0 collective-permute-done.6.refs_5_
  25.7 1.0 %collective-permute-done.8.refs_7_ = bf16[96,768]{1,0:T(8,128)(2,1)S(1)} collective-permute-done((bf16[96,768]{1,0:T(8,128)(2,1)S(1)}, bf16[96,768]{1,0:T(8,128)(2,1)S(1)}, u32[]{:S(2)}, u32[]{:S(2)}) %collective-permute-start.8) | collective-permute-done | bytes 147488 | tf_op jit(solution)/shard_map/ppermute | solution.py:220
  26.7 2.0 %shard_map.87 = (bf16[768,768]{1,0:T(8,128)(2,1)S(1)}, f32[384,768]{1,0:T(8,128)S(1)}, f32[1,1]{1,0:T(1,128)}, f32[1,1]{1,0:T(1,128)}, bf16[2,96,384]{2,1,0:T(8,128)(2,1)S(1)}) custom-call(bf16[96,768]{1,0:T(8,128)(2,1)S(1)} %collective-permute-done.1.refs_0_, bf16[96,768]{1,0:T(8,128)(2,1)S(1)} %collective-permute-done.2.refs_1_, ...), custom_call_target="tpu_custom_call" | custom-call | tf_op jit(solution)/shard_map/pallas_call | solution.py:230
  28.7 2.8 %collective-permute-start.11 = (bf16[2,96,384]{2,1,0:T(8,128)(2,1)S(1)}, bf16[2,96,384]{2,1,0:T(8,128)(2,1)S(1)}, u32[]{:S(2)}, u32[]{:S(2)}) collective-permute-start(bf16[2,96,384]{2,1,0:T(8,128)(2,1)S(1)} %get-tuple-element.23), channel_id=1, source_target_pairs={{0,4},{1,13},{2,6},{3,15},{4,0},{5,9},{6,2},{7,11},{8,12},{9,5},{1... | collective-permute-start | bytes 442376 | tf_op jit(solution)/shard_map/ppermute | solution.py:224
  31.6 0.4 collective-permute-start.12
  31.9 1.0 %collective-permute-done.12.theirs_sq_ref = f32[1,1]{1,0:T(1,128)} collective-permute-done((f32[1,1]{1,0:T(1,128)}, f32[1,1]{1,0:T(1,128)}, u32[]{:S(2)}, u32[]{:S(2)}) %collective-permute-start.12) | collective-permute-done | bytes 36 | tf_op jit(solution)/shard_map/ppermute | solution.py:220
  32.9 2.1 %shard_map.89 = (f32[8,128]{1,0:T(8,128)S(1)}, bf16[2,96,384]{2,1,0:T(8,128)(2,1)S(1)}, bf16[2,96,384]{2,1,0:T(8,128)(2,1)S(1)}, bf16[2,96,384]{2,1,0:T(8,128)(2,1)S(1)}) custom-call(f32[1,1]{1,0:T(1,128)} %get-tuple-element.26.mine_sq_ref, f32[1,1]{1,0:T(1,128)} %collective-permute-done.12.theirs_sq_ref, f32[1,1]{1,0:T(1,128)} %get-tuple-element.27.grad_sq_ref, ...), custom_call_target="tpu_custom_call" | custom-call | tf_op jit(solution)/shard_map/pallas_call | solution.py:230
  35.0 2.4 %collective-permute-start.20 = (f32[8,128]{1,0:T(8,128)S(1)}, f32[8,128]{1,0:T(8,128)S(1)}, u32[]{:S(2)}, u32[]{:S(2)}) collective-permute-start(f32[8,128]{1,0:T(8,128)S(1)} %get-tuple-element.32), channel_id=1, source_target_pairs={{0,4},{1,13},{2,6},{3,15},{4,0},{5,9},{6,2},{7,11},{8,12},{9,5},{1... | collective-permute-start | bytes 12296 | tf_op jit(solution)/shard_map/ppermute | solution.py:224
  37.4 0.7 %collective-permute-start.13 = (bf16[2,96,384]{2,1,0:T(8,128)(2,1)S(1)}, bf16[2,96,384]{2,1,0:T(8,128)(2,1)S(1)}, u32[]{:S(2)}, u32[]{:S(2)}) collective-permute-start(bf16[2,96,384]{2,1,0:T(8,128)(2,1)S(1)} %get-tuple-element.29), channel_id=1, source_target_pairs={{0,0},{1,9},{2,2},{3,11},{4,4},{5,13},{6,6},{7,15},{8,8},{9,1},{10... | collective-permute-start | bytes 442376 | tf_op jit(solution)/shard_map/ppermute | solution.py:224
  38.1 0.5 collective-permute-start.14
  38.6 1.0 %collective-permute-start.15 = (bf16[2,96,384]{2,1,0:T(8,128)(2,1)S(1)}, bf16[2,96,384]{2,1,0:T(8,128)(2,1)S(1)}, u32[]{:S(2)}, u32[]{:S(2)}) collective-permute-start(bf16[2,96,384]{2,1,0:T(8,128)(2,1)S(1)} %get-tuple-element.31), channel_id=1, source_target_pairs={{0,6},{1,15},{2,4},{3,13},{4,2},{5,11},{6,0},{7,9},{8,14},{9,7},{1... | collective-permute-start | bytes 442376 | tf_op jit(solution)/shard_map/ppermute | solution.py:224
  39.6 0.0 collective-permute-done.20.refs_8_
  39.6 4.3 %collective-permute-start.21 = (f32[8,128]{1,0:T(8,128)S(1)}, f32[8,128]{1,0:T(8,128)S(1)}, u32[]{:S(2)}, u32[]{:S(2)}) collective-permute-start(f32[8,128]{1,0:T(8,128)S(1)} %collective-permute-done.20.refs_8_), channel_id=1, source_target_pairs={{0,1},{1,0},{2,3},{3,2},{4,5},{5,4},{6,7},{7,6},{8,9},{9,8},{10,11... | collective-permute-start | bytes 12296 | tf_op jit(solution)/shard_map/ppermute | solution.py:220
  43.9 0.1 collective-permute-start.18
  44.0 3.0 %collective-permute-start.16 = (bf16[96,384]{1,0:T(8,128)(2,1)S(1)}, bf16[96,384]{1,0:T(8,128)(2,1)S(1)}, u32[]{:S(2)}, u32[]{:S(2)}) collective-permute-start(bf16[96,384]{1,0:T(8,128)(2,1)S(1)} %slice_bitcast_fusion.3), channel_id=1, source_target_pairs={{0,1},{1,0},{2,3},{3,2},{4,5},{5,4},{6,7},{7,6},{8,9},{9,8},{10,11... | collective-permute-start | bytes 221192 | tf_op jit(solution)/shard_map/ppermute | solution.py:220
  47.0 0.0 collective-permute-done.14.refs_1_
  47.0 3.3 %collective-permute-start.17 = (bf16[96,384]{1,0:T(8,128)(2,1)S(1)}, bf16[96,384]{1,0:T(8,128)(2,1)S(1)}, u32[]{:S(2)}, u32[]{:S(2)}) collective-permute-start(bf16[96,384]{1,0:T(8,128)(2,1)S(1)} %slice_bitcast_fusion.2), channel_id=1, source_target_pairs={{0,1},{1,0},{2,3},{3,2},{4,5},{5,4},{6,7},{7,6},{8,9},{9,8},{10,11... | collective-permute-start | bytes 221192 | tf_op jit(solution)/shard_map/ppermute | solution.py:220
  50.3 0.0 collective-permute-done.15.refs_3_
  50.3 0.1 collective-permute-start.19
  50.4 2.5 %shard_map.88 = (bf16[384,768]{1,0:T(8,128)(2,1)}, bf16[384,768]{1,0:T(8,128)(2,1)}) custom-call(s32[6]{0:T(128)S(1)} %copy-done.3, bf16[768,768]{1,0:T(8,128)(2,1)S(1)} %get-tuple-element.22.summed_ref, bf16[384,768]{1,0:T(8,128)(2,1)S(1)} %bitcast.19, bf16[384,768]{1,0:T(8,128)(2,1)S(1)} %bitcast.20, ...), custom_call_target="tpu_custom_call" | custom-call | flops 905969664 | bytes 2359296 | tf_op jit(solution)/shard_map/pallas_call | solution.py:230
  52.9 0.0 collective-permute-done.21.refs_9_
  52.9 0.0 collective-permute-done.18.refs_6_
  52.9 0.0 collective-permute-done.16.refs_4_
  52.9 0.0 collective-permute-done.19.refs_7_
  53.0 1.4 %shard_map.90 = bf16[6,96,384]{2,1,0:T(8,128)(2,1)} custom-call(s32[6]{0:T(128)S(1)} %copy-done.3, bf16[2,96,384]{2,1,0:T(8,128)(2,1)S(1)} %collective-permute-done.13.refs_0_, bf16[2,96,384]{2,1,0:T(8,128)(2,1)S(1)} %collective-permute-done.14.refs_1_, bf16[2,96,384]{2,1,0:T(8,128)(2,1)S(1)} %collective-permute-done.11.after_ref.refs_2_, ...), custom_call_target="tpu_custom_call" | custom-call | tf_op jit(solution)/shard_map/pallas_call | solution.py:230
  (18 shorter events, 0.1 us)
Async XLA Ops:
  0.6 5.5 %collective-permute-start = (bf16[6,96,768]{2,1,0:T(8,128)(2,1)}, bf16[6,96,768]{2,1,0:T(8,128)(2,1)S(1)}, u32[]{:S(2)}, u32[]{:S(2)}) collective-permute-start(bf16[6,96,768]{2,1,0:T(8,128)(2,1)} %bitcast.15), channel_id=1, source_target_pairs={{0,1},{1,0},{2,3},{3,2},{4,5},{5,4},{6,7},{7,6},{8,9},{9,8},{10,11... | collective-permute-start | bytes 2654216 | tf_op jit(solution)/shard_map/ppermute | solution.py:220
  1.1 11.0 %collective-permute-start.9 = (bf16[384,768]{1,0:T(8,128)(2,1)}, bf16[384,768]{1,0:T(8,128)(2,1)S(1)}, u32[]{:S(2)}, u32[]{:S(2)}) collective-permute-start(bf16[384,768]{1,0:T(8,128)(2,1)} %bitcast.21), channel_id=1, source_target_pairs={{0,0},{1,1},{2,2},{3,3},{4,4},{5,5},{6,6},{7,7},{8,9},{9,8},{10,11... | collective-permute-start | bytes 1769480 | tf_op jit(solution)/shard_map/ppermute | solution.py:245
  2.9 22.8 %collective-permute-start.10 = (bf16[768,384]{1,0:T(8,128)(2,1)}, bf16[768,384]{1,0:T(8,128)(2,1)S(1)}, u32[]{:S(2)}, u32[]{:S(2)}) collective-permute-start(bf16[768,384]{1,0:T(8,128)(2,1)} %bitcast.17), channel_id=1, source_target_pairs={{0,1},{1,0},{2,3},{3,2},{4,5},{5,4},{6,7},{7,6},{8,9},{9,8},{10,11... | collective-permute-start | bytes 1769480 | tf_op jit(solution)/shard_map/ppermute | solution.py:220
  2.9 1.2 %copy-start = (bf16[1,6,96,768]{3,2,1,0:T(8,128)(2,1)S(1)}, bf16[1,6,96,768]{3,2,1,0:T(8,128)(2,1)}, u32[]{:S(2)}) copy-start(bf16[1,6,96,768]{3,2,1,0:T(8,128)(2,1)} %param.6) | copy-start | bytes 2654212
  4.1 0.7 %copy-start.2 = (s32[6]{0:T(128)S(1)}, s32[6]{0:T(128)}, u32[]{:S(2)}) copy-start(s32[6]{0:T(128)} %owner_ref.7) | copy-start | bytes 76
  4.7 22.0 %copy-start.1 = (bf16[1,768,384]{2,1,0:T(8,128)(2,1)S(1)}, bf16[1,768,384]{2,1,0:T(8,128)(2,1)}, u32[]{:S(2)}) copy-start(bf16[1,768,384]{2,1,0:T(8,128)(2,1)} %param.11) | copy-start | bytes 1769476
  6.8 5.3 %collective-permute-start.1 = (bf16[96,768]{1,0:T(8,128)(2,1)S(1)}, bf16[96,768]{1,0:T(8,128)(2,1)S(1)}, u32[]{:S(2)}, u32[]{:S(2)}) collective-permute-start(bf16[96,768]{1,0:T(8,128)(2,1)S(1)} %get-tuple-element.18), channel_id=1, source_target_pairs={{0,0},{1,9},{2,2},{3,11},{4,4},{5,13},{6,6},{7,15},{8,8},{9,1},{10... | collective-permute-start | bytes 442376 | tf_op jit(solution)/shard_map/ppermute | solution.py:224
  7.5 10.2 %collective-permute-start.2 = (bf16[96,768]{1,0:T(8,128)(2,1)S(1)}, bf16[96,768]{1,0:T(8,128)(2,1)S(1)}, u32[]{:S(2)}, u32[]{:S(2)}) collective-permute-start(bf16[96,768]{1,0:T(8,128)(2,1)S(1)} %get-tuple-element.19), channel_id=1, source_target_pairs={{0,2},{1,11},{2,0},{3,9},{4,6},{5,15},{6,4},{7,13},{8,10},{9,3},{1... | collective-permute-start | bytes 442376 | tf_op jit(solution)/shard_map/ppermute | solution.py:224
  10.5 10.2 %collective-permute-start.3 = (bf16[96,768]{1,0:T(8,128)(2,1)S(1)}, bf16[96,768]{1,0:T(8,128)(2,1)S(1)}, u32[]{:S(2)}, u32[]{:S(2)}) collective-permute-start(bf16[96,768]{1,0:T(8,128)(2,1)S(1)} %get-tuple-element.20), channel_id=1, source_target_pairs={{0,4},{1,13},{2,6},{3,15},{4,0},{5,9},{6,2},{7,11},{8,12},{9,5},{1... | collective-permute-start | bytes 442376 | tf_op jit(solution)/shard_map/ppermute | solution.py:224
  12.1 11.2 %collective-permute-start.4 = (bf16[96,768]{1,0:T(8,128)(2,1)S(1)}, bf16[96,768]{1,0:T(8,128)(2,1)S(1)}, u32[]{:S(2)}, u32[]{:S(2)}) collective-permute-start(bf16[96,768]{1,0:T(8,128)(2,1)S(1)} %get-tuple-element.21), channel_id=1, source_target_pairs={{0,6},{1,15},{2,4},{3,13},{4,2},{5,11},{6,0},{7,9},{8,14},{9,7},{1... | collective-permute-start | bytes 442376 | tf_op jit(solution)/shard_map/ppermute | solution.py:224
  12.1 13.6 %collective-permute-start.5 = (bf16[96,768]{1,0:T(8,128)(2,1)S(1)}, bf16[96,768]{1,0:T(8,128)(2,1)S(1)}, u32[]{:S(2)}, u32[]{:S(2)}) collective-permute-start(bf16[96,768]{1,0:T(8,128)(2,1)S(1)} %collective-permute-done.1.refs_0_), channel_id=1, source_target_pairs={{0,1},{1,0},{2,3},{3,2},{4,5},{5,4},{6,7},{7,6},{8,9},{9,8},{10,11... | collective-permute-start | bytes 442376 | tf_op jit(solution)/shard_map/ppermute | solution.py:220
  17.7 8.0 %collective-permute-start.6 = (bf16[96,768]{1,0:T(8,128)(2,1)S(1)}, bf16[96,768]{1,0:T(8,128)(2,1)S(1)}, u32[]{:S(2)}, u32[]{:S(2)}) collective-permute-start(bf16[96,768]{1,0:T(8,128)(2,1)S(1)} %collective-permute-done.2.refs_1_), channel_id=1, source_target_pairs={{0,1},{1,0},{2,3},{3,2},{4,5},{5,4},{6,7},{7,6},{8,9},{9,8},{10,11... | collective-permute-start | bytes 442376 | tf_op jit(solution)/shard_map/ppermute | solution.py:220
  20.7 5.0 %collective-permute-start.7 = (bf16[96,768]{1,0:T(8,128)(2,1)S(1)}, bf16[96,768]{1,0:T(8,128)(2,1)S(1)}, u32[]{:S(2)}, u32[]{:S(2)}) collective-permute-start(bf16[96,768]{1,0:T(8,128)(2,1)S(1)} %collective-permute-done.3.refs_2_), channel_id=1, source_target_pairs={{0,1},{1,0},{2,3},{3,2},{4,5},{5,4},{6,7},{7,6},{8,9},{9,8},{10,11... | collective-permute-start | bytes 442376 | tf_op jit(solution)/shard_map/ppermute | solution.py:220
  23.3 3.4 %collective-permute-start.8 = (bf16[96,768]{1,0:T(8,128)(2,1)S(1)}, bf16[96,768]{1,0:T(8,128)(2,1)S(1)}, u32[]{:S(2)}, u32[]{:S(2)}) collective-permute-start(bf16[96,768]{1,0:T(8,128)(2,1)S(1)} %collective-permute-done.4.refs_3_), channel_id=1, source_target_pairs={{0,1},{1,0},{2,3},{3,2},{4,5},{5,4},{6,7},{7,6},{8,9},{9,8},{10,11... | collective-permute-start | bytes 442376 | tf_op jit(solution)/shard_map/ppermute | solution.py:220
  28.7 21.7 %copy-start.3 = (s32[6]{0:T(128)S(1)}, s32[6]{0:T(128)}, u32[]{:S(2)}) copy-start(s32[6]{0:T(128)} %owner_ref.7) | copy-start | bytes 76
  28.7 21.7 %copy-start.4 = (bf16[1,384,768]{2,1,0:T(8,128)(2,1)S(1)}, bf16[1,384,768]{2,1,0:T(8,128)(2,1)}, u32[]{:S(2)}) copy-start(bf16[1,384,768]{2,1,0:T(8,128)(2,1)} %param.8) | copy-start | bytes 1769476
  28.7 21.7 %copy-start.5 = (bf16[1,384,768]{2,1,0:T(8,128)(2,1)S(1)}, bf16[1,384,768]{2,1,0:T(8,128)(2,1)}, u32[]{:S(2)}) copy-start(bf16[1,384,768]{2,1,0:T(8,128)(2,1)} %param.9) | copy-start | bytes 1769476
  28.7 15.2 %collective-permute-start.11 = (bf16[2,96,384]{2,1,0:T(8,128)(2,1)S(1)}, bf16[2,96,384]{2,1,0:T(8,128)(2,1)S(1)}, u32[]{:S(2)}, u32[]{:S(2)}) collective-permute-start(bf16[2,96,384]{2,1,0:T(8,128)(2,1)S(1)} %get-tuple-element.23), channel_id=1, source_target_pairs={{0,4},{1,13},{2,6},{3,15},{4,0},{5,9},{6,2},{7,11},{8,12},{9,5},{1... | collective-permute-start | bytes 442376 | tf_op jit(solution)/shard_map/ppermute | solution.py:224
  31.6 1.3 %collective-permute-start.12 = (f32[1,1]{1,0:T(1,128)}, f32[1,1]{1,0:T(1,128)}, u32[]{:S(2)}, u32[]{:S(2)}) collective-permute-start(f32[1,1]{1,0:T(1,128)} %get-tuple-element.26.mine_sq_ref), channel_id=1, source_target_pairs={{0,1},{1,0},{2,3},{3,2},{4,5},{5,4},{6,7},{7,6},{8,9},{9,8},{10,11... | collective-permute-start | bytes 20 | tf_op jit(solution)/shard_map/ppermute | solution.py:220
  35.0 4.6 %collective-permute-start.20 = (f32[8,128]{1,0:T(8,128)S(1)}, f32[8,128]{1,0:T(8,128)S(1)}, u32[]{:S(2)}, u32[]{:S(2)}) collective-permute-start(f32[8,128]{1,0:T(8,128)S(1)} %get-tuple-element.32), channel_id=1, source_target_pairs={{0,4},{1,13},{2,6},{3,15},{4,0},{5,9},{6,2},{7,11},{8,12},{9,5},{1... | collective-permute-start | bytes 12296 | tf_op jit(solution)/shard_map/ppermute | solution.py:224
  37.4 6.6 %collective-permute-start.13 = (bf16[2,96,384]{2,1,0:T(8,128)(2,1)S(1)}, bf16[2,96,384]{2,1,0:T(8,128)(2,1)S(1)}, u32[]{:S(2)}, u32[]{:S(2)}) collective-permute-start(bf16[2,96,384]{2,1,0:T(8,128)(2,1)S(1)} %get-tuple-element.29), channel_id=1, source_target_pairs={{0,0},{1,9},{2,2},{3,11},{4,4},{5,13},{6,6},{7,15},{8,8},{9,1},{10... | collective-permute-start | bytes 442376 | tf_op jit(solution)/shard_map/ppermute | solution.py:224
  38.1 8.9 %collective-permute-start.14 = (bf16[2,96,384]{2,1,0:T(8,128)(2,1)S(1)}, bf16[2,96,384]{2,1,0:T(8,128)(2,1)S(1)}, u32[]{:S(2)}, u32[]{:S(2)}) collective-permute-start(bf16[2,96,384]{2,1,0:T(8,128)(2,1)S(1)} %get-tuple-element.30), channel_id=1, source_target_pairs={{0,2},{1,11},{2,0},{3,9},{4,6},{5,15},{6,4},{7,13},{8,10},{9,3},{1... | collective-permute-start | bytes 442376 | tf_op jit(solution)/shard_map/ppermute | solution.py:224
  38.6 11.7 %collective-permute-start.15 = (bf16[2,96,384]{2,1,0:T(8,128)(2,1)S(1)}, bf16[2,96,384]{2,1,0:T(8,128)(2,1)S(1)}, u32[]{:S(2)}, u32[]{:S(2)}) collective-permute-start(bf16[2,96,384]{2,1,0:T(8,128)(2,1)S(1)} %get-tuple-element.31), channel_id=1, source_target_pairs={{0,6},{1,15},{2,4},{3,13},{4,2},{5,11},{6,0},{7,9},{8,14},{9,7},{1... | collective-permute-start | bytes 442376 | tf_op jit(solution)/shard_map/ppermute | solution.py:224
  39.6 13.3 %collective-permute-start.21 = (f32[8,128]{1,0:T(8,128)S(1)}, f32[8,128]{1,0:T(8,128)S(1)}, u32[]{:S(2)}, u32[]{:S(2)}) collective-permute-start(f32[8,128]{1,0:T(8,128)S(1)} %collective-permute-done.20.refs_8_), channel_id=1, source_target_pairs={{0,1},{1,0},{2,3},{3,2},{4,5},{5,4},{6,7},{7,6},{8,9},{9,8},{10,11... | collective-permute-start | bytes 12296 | tf_op jit(solution)/shard_map/ppermute | solution.py:220
  43.9 9.0 %collective-permute-start.18 = (bf16[96,384]{1,0:T(8,128)(2,1)S(1)}, bf16[96,384]{1,0:T(8,128)(2,1)S(1)}, u32[]{:S(2)}, u32[]{:S(2)}) collective-permute-start(bf16[96,384]{1,0:T(8,128)(2,1)S(1)} %slice_bitcast_fusion.1), channel_id=1, source_target_pairs={{0,1},{1,0},{2,3},{3,2},{4,5},{5,4},{6,7},{7,6},{8,9},{9,8},{10,11... | collective-permute-start | bytes 221192 | tf_op jit(solution)/shard_map/ppermute | solution.py:220
  44.0 8.9 %collective-permute-start.16 = (bf16[96,384]{1,0:T(8,128)(2,1)S(1)}, bf16[96,384]{1,0:T(8,128)(2,1)S(1)}, u32[]{:S(2)}, u32[]{:S(2)}) collective-permute-start(bf16[96,384]{1,0:T(8,128)(2,1)S(1)} %slice_bitcast_fusion.3), channel_id=1, source_target_pairs={{0,1},{1,0},{2,3},{3,2},{4,5},{5,4},{6,7},{7,6},{8,9},{9,8},{10,11... | collective-permute-start | bytes 221192 | tf_op jit(solution)/shard_map/ppermute | solution.py:220
  47.0 5.9 %collective-permute-start.17 = (bf16[96,384]{1,0:T(8,128)(2,1)S(1)}, bf16[96,384]{1,0:T(8,128)(2,1)S(1)}, u32[]{:S(2)}, u32[]{:S(2)}) collective-permute-start(bf16[96,384]{1,0:T(8,128)(2,1)S(1)} %slice_bitcast_fusion.2), channel_id=1, source_target_pairs={{0,1},{1,0},{2,3},{3,2},{4,5},{5,4},{6,7},{7,6},{8,9},{9,8},{10,11... | collective-permute-start | bytes 221192 | tf_op jit(solution)/shard_map/ppermute | solution.py:220
  50.3 2.6 %collective-permute-start.19 = (bf16[96,384]{1,0:T(8,128)(2,1)S(1)}, bf16[96,384]{1,0:T(8,128)(2,1)S(1)}, u32[]{:S(2)}, u32[]{:S(2)}) collective-permute-start(bf16[96,384]{1,0:T(8,128)(2,1)S(1)} %slice_bitcast_fusion), channel_id=1, source_target_pairs={{0,1},{1,0},{2,3},{3,2},{4,5},{5,4},{6,7},{7,6},{8,9},{9,8},{10,11... | collective-permute-start | bytes 221192 | tf_op jit(solution)/shard_map/ppermute | solution.py:220

commit v3 on v2

--- a/solution.py
+++ b/solution.py
@@ -72,18 +72,10 @@
     return jnp.maximum(block_of(owner_ref, (side ^ core) * rounds + (place ^ j)), 0)
 
 
-def fetch_kernel(owner_ref, gradient_ref, out_ref, sem):
+def fetch_kernel(owner_ref, gradient_ref, out_ref):
     rounds = out_ref.shape[0]
-    copies = [
-        pltpu.make_async_copy(
-            gradient_ref.at[sent_block(owner_ref, rounds, j)], out_ref.at[j], sem.at[j]
-        )
-        for j in range(rounds)
-    ]
-    for copy in copies:
-        copy.start()
-    for copy in copies:
-        copy.wait()
+    for j in range(rounds):
+        out_ref[j] = gradient_ref[sent_block(owner_ref, rounds, j)]
 
 
 def pick_kernel(owner_ref, mine_ref, theirs_ref, *out_refs):
@@ -105,10 +97,9 @@
 
 def precondition_kernel(rounds, early, *refs):
     mine, theirs = refs[:rounds], refs[rounds:2 * rounds]
-    left_ref, own_ref, other_ref, summed_ref, both_ref, side_sq_ref, grad_sq_ref = refs[
-        2 * rounds:2 * rounds + 7
-    ]
-    early_refs, side_ref = refs[2 * rounds + 7:-1], refs[-1]
+    left_refs, right_refs = refs[2 * rounds:2 * rounds + 2], refs[2 * rounds + 2:2 * rounds + 4]
+    summed_ref, both_ref, side_sq_ref, grad_sq_ref = refs[2 * rounds + 4:2 * rounds + 8]
+    early_refs, side_ref = refs[2 * rounds + 8:-1], refs[-1]
     side, place, core = device_place(rounds)
     slab, full = mine[0].shape
     half = rounds * slab
@@ -120,17 +111,23 @@
             summed_ref[pl.ds(row, slab), :] = block
             wide = block.astype(jnp.float32)
             grad_sq += jnp.sum(wide * wide, axis=0, keepdims=True)
-    grad_sq_ref[...] = jnp.sum(grad_sq, axis=1, keepdims=True)
-    side_ref[...] = jnp.dot(
-        left_ref[...], summed_ref[...], preferred_element_type=jnp.float32
-    ).astype(side_ref.dtype)
+    total = jnp.sum(grad_sq, axis=1, keepdims=True)
+    grad_sq_ref[...] = jnp.broadcast_to(total, grad_sq_ref.shape)
+    for h, left_ref in enumerate(left_refs):
+
+        @pl.when(side == h)
+        def _(left_ref=left_ref):
+            side_ref[...] = jnp.dot(
+                left_ref[...], summed_ref[...], preferred_element_type=jnp.float32
+            ).astype(side_ref.dtype)
+
     side_sq = jnp.zeros((1, 1), jnp.float32)
-    for ref, columns_side in ((own_ref, core), (other_ref, 1 - core)):
+    for ref, columns_side in zip(right_refs, (core, 1 - core)):
         both = jnp.dot(side_ref[...], ref[...], preferred_element_type=jnp.float32)
         width = ref.shape[1]
         both_ref[:, pl.ds(pl.multiple_of(columns_side * width, 128), width)] = both
         side_sq += jnp.sum(jnp.sum(both * both, axis=0, keepdims=True), axis=1, keepdims=True)
-    side_sq_ref[...] = side_sq
+    side_sq_ref[...] = jnp.broadcast_to(side_sq, side_sq_ref.shape)
     for j, out_ref in zip(early, early_refs):
         row = pl.multiple_of((place ^ j) * slab, slab)
         for k, piece in enumerate(slab_for(both_ref, core, row, slab)):
@@ -141,8 +138,8 @@
     side, place, core = device_place(rounds)
     slab = both_ref.shape[0] // rounds
     side_sq = mine_sq_ref[...] + theirs_sq_ref[...]
-    graft = jnp.sqrt(grad_sq_ref[...] / (side_sq + 1e-06))
-    graft_ref[...] = jnp.broadcast_to(graft, graft_ref.shape)
+    graft_ref[...] = jnp.sqrt(grad_sq_ref[...] / (side_sq + 1e-06))
+    graft = graft_ref[0:1, 0:1]
     for j, out_ref in zip(late, out_refs):
         row = pl.multiple_of((place ^ j) * slab, slab)
         for k, piece in enumerate(slab_for(both_ref, core, row, slab, graft)):
@@ -233,8 +230,8 @@
 
     other_gradient = other_core(gradients[0])
     fetched = call(
-        fetch_kernel, shape((rounds, slab, width)), [SMEM, ANY], block_owner, gradients[0],
-        out_specs=VMEM, scratch_shapes=[pltpu.SemaphoreType.DMA((rounds,))],
+        fetch_kernel, shape((rounds, slab, width)), [SMEM, VMEM], block_owner, gradients[0],
+        out_specs=VMEM,
     )
     outgoing = call(
         pick_kernel, [shape((slab, width))] * rounds, [SMEM, VMEM, VMEM],
@@ -242,20 +239,17 @@
     )
     mine = {j: trade(outgoing[j], j) for j in order}
     other_right = other_core(right_root[0])
-    left_rows = lax.ppermute(
-        left_root[0], ("shard", "replica"),
-        [(device(h, l, r), device(h, l, r ^ h)) for h, l, r in places],
-    )
+    other_left = other_core(left_root[0])
     theirs = {j: other_core(mine[j]) for j in order}
-    one = shape((1, 1), jnp.float32)
+    one = shape((8, 128), jnp.float32)
     slab_shape = shape((2, slab, width // 2))
     summed, both_sides, side_sq, grad_sq, *first = call(
         functools.partial(precondition_kernel, rounds, early),
         [shape((width, width)), shape((half_rows, width), jnp.float32), one, one]
         + [slab_shape] * len(early),
-        [VMEM] * (2 * rounds + 3),
+        [VMEM] * (2 * rounds + 4),
         *[mine[j] for j in range(rounds)], *[theirs[j] for j in range(rounds)],
-        left_rows, right_root[0], other_right,
+        left_root[0], other_left, right_root[0], other_right,
         out_specs=[VMEM] * (4 + len(early)),
         scratch_shapes=[pltpu.VMEM((half_rows, width), jnp.bfloat16)],
     )
@@ -268,11 +262,11 @@
     )
     returned.update((j, trade(x, j)) for j, x in zip(late, rest))
     grafts = []
+    if early:
+        graft, returned[order[0]] = lax.optimization_barrier((graft, returned[order[0]]))
     for j in early:
         came = trade(graft, j)
         grafts += [came, other_core(came)]
-    passed = {j: other_core(returned[j][1]) for j in order}
-
     left_new, right_new = call(
         gram_kernel, [shape(left_gram.shape[1:]), shape(right_gram.shape[1:])],
         [SMEM, VMEM, VMEM, VMEM, ANY],
@@ -283,6 +277,10 @@
             transcendentals=0,
         ),
     )
+    left_new, right_new, returned[order[-1]] = lax.optimization_barrier(
+        (left_new, right_new, returned[order[-1]])
+    )
+    passed = {j: other_core(returned[j][1]) for j in order}
     update = call(
         functools.partial(place_kernel, rounds, early), shape((blocks, slab, width // 2)),
         [SMEM] + [VMEM] * (2 * rounds + len(grafts)), block_owner,

time: 54.6 us -> 50 us (0.916)
  starting transfers between devices: 39.6 us -> 35.9 us
  Pallas kernels: 10.1 us -> 7 us
  waiting for transfers between devices: 1.99 us -> 4.27 us
    ppermute x12 -> x13, starting transfers between devices: 25.2 us -> 21 us  [other_core(): return lax.ppermute(x, 'replica', [(0, 1), (1, 0)])]
    pallas_call x6, Pallas kernels: 10.1 us -> 7 us  [call(): pl.pallas_call(kernel, out_shape=out_shape, in_specs=in_specs, compiler_p...]
    ppermute x9, starting transfers between devices: 12.7 us -> 14.9 us  [trade(): return lax.ppermute(x, ('shard', 'replica'), pairs)]
    ppermute x1 -> x0, starting transfers between devices: 1.71 us -> none  [per_device_paired(): lax.ppermute(left_root[0], ('shard', 'replica'), [(device(h, l, r), devic...]
    ppermute x9, waiting for transfers between devices: 0.02 us -> 1.61 us  [trade(): return lax.ppermute(x, ('shard', 'replica'), pairs)]
    ppermute x12 -> x13, waiting for transfers between devices: 1.96 us -> 2.66 us  [other_core(): return lax.ppermute(x, 'replica', [(0, 1), (1, 0)])]
    unnamed x12 -> x14, local copies, waits for them, and re-layouts: 1.84 us -> 1.84 us
  transfers between devices with their start and end apart: 22 -> 22, of which waited for: 2 -> 4; matrix products, arithmetic and copies ran while one was open for 0% -> 0% of each run, Pallas kernels for 12% -> 8%
where the time goes in v3:
time: 50 us; the launch traced here: 49.8 us
  starting transfers between devices  35.9 us (72%)
  Pallas kernels  7 us (14%)
  waiting for transfers between devices  4.27 us (9%)
  local copies, waits for them, and re-layouts  1.87 us (4%)
  between operations  0.75 us (2%)
    ppermute x13, starting transfers between devices, other_core(): return lax.ppermute(x, 'replica', [(0, 1), (1, 0)])  21 us
    ppermute x9, starting transfers between devices, trade(): return lax.ppermute(x, ('shard', 'replica'), pairs)  14.9 us
    pallas_call x6, Pallas kernels, call(): pl.pallas_call(kernel, out_shape=out_shape, in_specs=in_specs, compiler_p...  7 us
    ppermute x13, waiting for transfers between devices, other_core(): return lax.ppermute(x, 'replica', [(0, 1), (1, 0)])  2.66 us
    unnamed x14, local copies, waits for them, and re-layouts  1.84 us
    ppermute x9, waiting for transfers between devices, trade(): return lax.ppermute(x, ('shard', 'replica'), pairs)  1.61 us
  transfers between devices with their start and end apart: 22, of which 4 were waited for; matrix products, arithmetic and copies ran while one was open for 0% of the time, Pallas kernels for 8%

profile of v3, /device:TPU:0, one launch (start us, length us, event | category | flops | bytes accessed | tf_op | source)
XLA Modules:
  0.0 49.8 jit_solution(5461507312845598054)
XLA Ops:
  0.6 0.5 %collective-permute-start = (bf16[6,96,768]{2,1,0:T(8,128)(2,1)}, bf16[6,96,768]{2,1,0:T(8,128)(2,1)S(1)}, u32[]{:S(2)}, u32[]{:S(2)}) collective-permute-start(bf16[6,96,768]{2,1,0:T(8,128)(2,1)} %bitcast.15), channel_id=1, source_target_pairs={{0,1},{1,0},{2,3},{3,2},{4,5},{5,4},{6,7},{7,6},{8,9},{9,8},{10,11... | collective-permute-start | bytes 2654216 | tf_op jit(solution)/shard_map/ppermute | solution.py:217
  1.1 0.1 collective-permute-start.9
  1.2 0.4 collective-permute-start.10
  1.7 1.2 %copy-done = bf16[1,6,96,768]{3,2,1,0:T(8,128)(2,1)S(1)} copy-done((bf16[1,6,96,768]{3,2,1,0:T(8,128)(2,1)S(1)}, bf16[1,6,96,768]{3,2,1,0:T(8,128)(2,1)}, u32[]{:S(2)}) %copy-start) | copy-done | bytes 884760
  2.8 0.7 %copy-done.3 = s32[6]{0:T(128)S(1)} copy-done((s32[6]{0:T(128)S(1)}, s32[6]{0:T(128)}, u32[]{:S(2)}) %copy-start.3) | copy-done | bytes 48
  3.5 0.6 %shard_map.85.mine_ref = bf16[4,96,768]{2,1,0:T(8,128)(2,1)S(1)} custom-call(s32[6]{0:T(128)S(1)} %copy-done.3, bf16[6,96,768]{2,1,0:T(8,128)(2,1)S(1)} %bitcast.16), custom_call_target="tpu_custom_call" | custom-call | tf_op jit(solution)/shard_map/pallas_call | solution.py:227
  4.1 0.0 collective-permute-done.theirs_ref
  4.1 0.7 %shard_map.86 = (bf16[96,768]{1,0:T(8,128)(2,1)S(1)}, bf16[96,768]{1,0:T(8,128)(2,1)S(1)}, bf16[96,768]{1,0:T(8,128)(2,1)S(1)}, bf16[96,768]{1,0:T(8,128)(2,1)S(1)}) custom-call(s32[6]{0:T(128)S(1)} %copy-done.3, bf16[4,96,768]{2,1,0:T(8,128)(2,1)S(1)} %shard_map.85.mine_ref, bf16[6,96,768]{2,1,0:T(8,128)(2,1)S(1)} %collective-permute-done.theirs_ref), custom_call_target="tpu_custom_call" | custom-call | tf_op jit(solution)/shard_map/pallas_call | solution.py:227
  4.8 0.7 %collective-permute-start.1 = (bf16[96,768]{1,0:T(8,128)(2,1)S(1)}, bf16[96,768]{1,0:T(8,128)(2,1)S(1)}, u32[]{:S(2)}, u32[]{:S(2)}) collective-permute-start(bf16[96,768]{1,0:T(8,128)(2,1)S(1)} %get-tuple-element.23), channel_id=1, source_target_pairs={{0,0},{1,9},{2,2},{3,11},{4,4},{5,13},{6,6},{7,15},{8,8},{9,1},{10... | collective-permute-start | bytes 442376 | tf_op jit(solution)/shard_map/ppermute | solution.py:221
  5.5 2.6 %collective-permute-start.2 = (bf16[96,768]{1,0:T(8,128)(2,1)S(1)}, bf16[96,768]{1,0:T(8,128)(2,1)S(1)}, u32[]{:S(2)}, u32[]{:S(2)}) collective-permute-start(bf16[96,768]{1,0:T(8,128)(2,1)S(1)} %get-tuple-element.24), channel_id=1, source_target_pairs={{0,2},{1,11},{2,0},{3,9},{4,6},{5,15},{6,4},{7,13},{8,10},{9,3},{1... | collective-permute-start | bytes 442376 | tf_op jit(solution)/shard_map/ppermute | solution.py:221
  8.1 1.6 %collective-permute-start.3 = (bf16[96,768]{1,0:T(8,128)(2,1)S(1)}, bf16[96,768]{1,0:T(8,128)(2,1)S(1)}, u32[]{:S(2)}, u32[]{:S(2)}) collective-permute-start(bf16[96,768]{1,0:T(8,128)(2,1)S(1)} %get-tuple-element.25), channel_id=1, source_target_pairs={{0,4},{1,13},{2,6},{3,15},{4,0},{5,9},{6,2},{7,11},{8,12},{9,5},{1... | collective-permute-start | bytes 442376 | tf_op jit(solution)/shard_map/ppermute | solution.py:221
  9.7 0.0 collective-permute-done.9.refs_9_
  9.7 0.0 collective-permute-start.4
  9.7 0.0 collective-permute-done.1.refs_0_
  9.7 5.3 %collective-permute-start.5 = (bf16[96,768]{1,0:T(8,128)(2,1)S(1)}, bf16[96,768]{1,0:T(8,128)(2,1)S(1)}, u32[]{:S(2)}, u32[]{:S(2)}) collective-permute-start(bf16[96,768]{1,0:T(8,128)(2,1)S(1)} %collective-permute-done.1.refs_0_), channel_id=1, source_target_pairs={{0,1},{1,0},{2,3},{3,2},{4,5},{5,4},{6,7},{7,6},{8,9},{9,8},{10,11... | collective-permute-start | bytes 442376 | tf_op jit(solution)/shard_map/ppermute | solution.py:217
  15.0 0.0 collective-permute-done.2.refs_1_
  15.0 3.0 %collective-permute-start.6 = (bf16[96,768]{1,0:T(8,128)(2,1)S(1)}, bf16[96,768]{1,0:T(8,128)(2,1)S(1)}, u32[]{:S(2)}, u32[]{:S(2)}) collective-permute-start(bf16[96,768]{1,0:T(8,128)(2,1)S(1)} %collective-permute-done.2.refs_1_), channel_id=1, source_target_pairs={{0,1},{1,0},{2,3},{3,2},{4,5},{5,4},{6,7},{7,6},{8,9},{9,8},{10,11... | collective-permute-start | bytes 442376 | tf_op jit(solution)/shard_map/ppermute | solution.py:217
  18.0 0.0 collective-permute-done.3.refs_2_
  18.0 2.6 %collective-permute-start.7 = (bf16[96,768]{1,0:T(8,128)(2,1)S(1)}, bf16[96,768]{1,0:T(8,128)(2,1)S(1)}, u32[]{:S(2)}, u32[]{:S(2)}) collective-permute-start(bf16[96,768]{1,0:T(8,128)(2,1)S(1)} %collective-permute-done.3.refs_2_), channel_id=1, source_target_pairs={{0,1},{1,0},{2,3},{3,2},{4,5},{5,4},{6,7},{7,6},{8,9},{9,8},{10,11... | collective-permute-start | bytes 442376 | tf_op jit(solution)/shard_map/ppermute | solution.py:217
  20.6 0.0 collective-permute-done.4.refs_3_
  20.6 2.4 %collective-permute-start.8 = (bf16[96,768]{1,0:T(8,128)(2,1)S(1)}, bf16[96,768]{1,0:T(8,128)(2,1)S(1)}, u32[]{:S(2)}, u32[]{:S(2)}) collective-permute-start(bf16[96,768]{1,0:T(8,128)(2,1)S(1)} %collective-permute-done.4.refs_3_), channel_id=1, source_target_pairs={{0,1},{1,0},{2,3},{3,2},{4,5},{5,4},{6,7},{7,6},{8,9},{9,8},{10,11... | collective-permute-start | bytes 442376 | tf_op jit(solution)/shard_map/ppermute | solution.py:217
  23.0 0.0 collective-permute-done.10.refs_11_
  23.0 0.0 collective-permute-done.5.refs_4_
  23.0 0.0 collective-permute-done.6.refs_5_
  23.0 0.0 collective-permute-done.7.refs_6_
  23.0 1.0 %collective-permute-done.8.refs_7_ = bf16[96,768]{1,0:T(8,128)(2,1)S(1)} collective-permute-done((bf16[96,768]{1,0:T(8,128)(2,1)S(1)}, bf16[96,768]{1,0:T(8,128)(2,1)S(1)}, u32[]{:S(2)}, u32[]{:S(2)}) %collective-permute-start.8) | collective-permute-done | bytes 147488 | tf_op jit(solution)/shard_map/ppermute | solution.py:217
  24.0 1.7 %shard_map.87 = (bf16[768,768]{1,0:T(8,128)(2,1)S(1)}, f32[384,768]{1,0:T(8,128)S(1)}, f32[8,128]{1,0:T(8,128)S(1)}, f32[8,128]{1,0:T(8,128)S(1)}, bf16[2,96,384]{2,1,0:T(8,128)(2,1)S(1)}) custom-call(bf16[96,768]{1,0:T(8,128)(2,1)S(1)} %collective-permute-done.1.refs_0_, bf16[96,768]{1,0:T(8,128)(2,1)S(1)} %collective-permute-done.2.refs_1_, ...), custom_call_target="tpu_custom_call" | custom-call | tf_op jit(solution)/shard_map/pallas_call | solution.py:227
  25.7 2.8 %collective-permute-start.12 = (bf16[2,96,384]{2,1,0:T(8,128)(2,1)S(1)}, bf16[2,96,384]{2,1,0:T(8,128)(2,1)S(1)}, u32[]{:S(2)}, u32[]{:S(2)}) collective-permute-start(bf16[2,96,384]{2,1,0:T(8,128)(2,1)S(1)} %get-tuple-element.32), channel_id=1, source_target_pairs={{0,4},{1,13},{2,6},{3,15},{4,0},{5,9},{6,2},{7,11},{8,12},{9,5},{1... | collective-permute-start | bytes 442376 | tf_op jit(solution)/shard_map/ppermute | solution.py:221
  28.5 0.4 collective-permute-start.11
  28.9 0.8 %collective-permute-done.11.theirs_sq_ref = f32[8,128]{1,0:T(8,128)S(1)} collective-permute-done((f32[8,128]{1,0:T(8,128)S(1)}, f32[8,128]{1,0:T(8,128)S(1)}, u32[]{:S(2)}, u32[]{:S(2)}) %collective-permute-start.11) | collective-permute-done | bytes 4128 | tf_op jit(solution)/shard_map/ppermute | solution.py:217
  29.7 0.1 shard_map.88
  29.9 1.0 %collective-permute-start.13 = (bf16[2,96,384]{2,1,0:T(8,128)(2,1)S(1)}, bf16[2,96,384]{2,1,0:T(8,128)(2,1)S(1)}, u32[]{:S(2)}, u32[]{:S(2)}) collective-permute-start(bf16[2,96,384]{2,1,0:T(8,128)(2,1)S(1)} %get-tuple-element.36), channel_id=1, source_target_pairs={{0,2},{1,11},{2,0},{3,9},{4,6},{5,15},{6,4},{7,13},{8,10},{9,3},{1... | collective-permute-start | bytes 442376 | tf_op jit(solution)/shard_map/ppermute | solution.py:221
  30.8 0.7 %collective-permute-start.14 = (bf16[2,96,384]{2,1,0:T(8,128)(2,1)S(1)}, bf16[2,96,384]{2,1,0:T(8,128)(2,1)S(1)}, u32[]{:S(2)}, u32[]{:S(2)}) collective-permute-start(bf16[2,96,384]{2,1,0:T(8,128)(2,1)S(1)} %get-tuple-element.39), channel_id=1, source_target_pairs={{0,0},{1,9},{2,2},{3,11},{4,4},{5,13},{6,6},{7,15},{8,8},{9,1},{10... | collective-permute-start | bytes 442376 | tf_op jit(solution)/shard_map/ppermute | solution.py:221
  31.5 2.9 %collective-permute-start.15 = (bf16[2,96,384]{2,1,0:T(8,128)(2,1)S(1)}, bf16[2,96,384]{2,1,0:T(8,128)(2,1)S(1)}, u32[]{:S(2)}, u32[]{:S(2)}) collective-permute-start(bf16[2,96,384]{2,1,0:T(8,128)(2,1)S(1)} %get-tuple-element.41), channel_id=1, source_target_pairs={{0,6},{1,15},{2,4},{3,13},{4,2},{5,11},{6,0},{7,9},{8,14},{9,7},{1... | collective-permute-start | bytes 442376 | tf_op jit(solution)/shard_map/ppermute | solution.py:221
  34.4 0.0 collective-permute-done.12.after_ref.refs_2_
  34.4 4.1 %collective-permute-start.18 = (bf16[96,384]{1,0:T(8,128)(2,1)S(1)}, bf16[96,384]{1,0:T(8,128)(2,1)S(1)}, u32[]{:S(2)}, u32[]{:S(2)}) collective-permute-start(bf16[96,384]{1,0:T(8,128)(2,1)S(1)} %slice_bitcast_fusion.2), channel_id=1, source_target_pairs={{0,1},{1,0},{2,3},{3,2},{4,5},{5,4},{6,7},{7,6},{8,9},{9,8},{10,11... | collective-permute-start | bytes 221192 | tf_op jit(solution)/shard_map/ppermute | solution.py:217
  38.6 2.5 %shard_map.89 = (bf16[384,768]{1,0:T(8,128)(2,1)}, bf16[384,768]{1,0:T(8,128)(2,1)}) custom-call(s32[6]{0:T(128)S(1)} %copy-done.4, bf16[768,768]{1,0:T(8,128)(2,1)S(1)} %get-tuple-element.27.summed_ref, bf16[384,768]{1,0:T(8,128)(2,1)S(1)} %bitcast.21, bf16[384,768]{1,0:T(8,128)(2,1)S(1)} %bitcast.22, ...), custom_call_target="tpu_custom_call" | custom-call | flops 905969664 | bytes 2359296 | tf_op jit(solution)/shard_map/pallas_call | solution.py:227
  41.1 0.0 collective-permute-done.14.refs_0_
  41.1 1.0 %collective-permute-start.16 = (bf16[96,384]{1,0:T(8,128)(2,1)S(1)}, bf16[96,384]{1,0:T(8,128)(2,1)S(1)}, u32[]{:S(2)}, u32[]{:S(2)}) collective-permute-start(bf16[96,384]{1,0:T(8,128)(2,1)S(1)} %slice_bitcast_fusion.1), channel_id=1, source_target_pairs={{0,1},{1,0},{2,3},{3,2},{4,5},{5,4},{6,7},{7,6},{8,9},{9,8},{10,11... | collective-permute-start | bytes 221192 | tf_op jit(solution)/shard_map/ppermute | solution.py:217
  42.1 0.6 %collective-permute-start.19 = (bf16[96,384]{1,0:T(8,128)(2,1)S(1)}, bf16[96,384]{1,0:T(8,128)(2,1)S(1)}, u32[]{:S(2)}, u32[]{:S(2)}) collective-permute-start(bf16[96,384]{1,0:T(8,128)(2,1)S(1)} %slice_bitcast_fusion), channel_id=1, source_target_pairs={{0,1},{1,0},{2,3},{3,2},{4,5},{5,4},{6,7},{7,6},{8,9},{9,8},{10,11... | collective-permute-start | bytes 221192 | tf_op jit(solution)/shard_map/ppermute | solution.py:217
  42.7 0.0 collective-permute-done.13.refs_1_
  42.7 0.1 collective-permute-start.17
  42.8 2.7 %collective-permute-start.20 = (f32[8,128]{1,0:T(8,128)S(1)}, f32[8,128]{1,0:T(8,128)S(1)}, u32[]{:S(2)}, u32[]{:S(2)}) collective-permute-start(f32[8,128]{1,0:T(8,128)S(1)} %get-tuple-element.42), channel_id=1, source_target_pairs={{0,4},{1,13},{2,6},{3,15},{4,0},{5,9},{6,2},{7,11},{8,12},{9,5},{1... | collective-permute-start | bytes 12296 | tf_op jit(solution)/shard_map/ppermute | solution.py:221
  45.5 1.6 %collective-permute-done.20.refs_8_ = f32[8,128]{1,0:T(8,128)S(1)} collective-permute-done((f32[8,128]{1,0:T(8,128)S(1)}, f32[8,128]{1,0:T(8,128)S(1)}, u32[]{:S(2)}, u32[]{:S(2)}) %collective-permute-start.20) | collective-permute-done | bytes 4128 | tf_op jit(solution)/shard_map/ppermute | solution.py:221
  47.1 0.5 collective-permute-start.21
  47.6 0.8 %collective-permute-done.21.refs_9_ = f32[8,128]{1,0:T(8,128)S(1)} collective-permute-done((f32[8,128]{1,0:T(8,128)S(1)}, f32[8,128]{1,0:T(8,128)S(1)}, u32[]{:S(2)}, u32[]{:S(2)}) %collective-permute-start.21) | collective-permute-done | bytes 4128 | tf_op jit(solution)/shard_map/ppermute | solution.py:217
  48.4 0.0 collective-permute-done.19.refs_7_
  48.4 1.4 %shard_map.90 = bf16[6,96,384]{2,1,0:T(8,128)(2,1)} custom-call(s32[6]{0:T(128)S(1)} %copy-done.4, bf16[2,96,384]{2,1,0:T(8,128)(2,1)S(1)} %collective-permute-done.14.refs_0_, bf16[2,96,384]{2,1,0:T(8,128)(2,1)S(1)} %collective-permute-done.13.refs_1_, bf16[2,96,384]{2,1,0:T(8,128)(2,1)S(1)} %collective-permute-done.12.after_ref.refs_2_, ...), custom_call_target="tpu_custom_call" | custom-call | tf_op jit(solution)/shard_map/pallas_call | solution.py:227
  (20 shorter events, 0.1 us)
Async XLA Ops:
  0.6 3.5 %collective-permute-start = (bf16[6,96,768]{2,1,0:T(8,128)(2,1)}, bf16[6,96,768]{2,1,0:T(8,128)(2,1)S(1)}, u32[]{:S(2)}, u32[]{:S(2)}) collective-permute-start(bf16[6,96,768]{2,1,0:T(8,128)(2,1)} %bitcast.15), channel_id=1, source_target_pairs={{0,1},{1,0},{2,3},{3,2},{4,5},{5,4},{6,7},{7,6},{8,9},{9,8},{10,11... | collective-permute-start | bytes 2654216 | tf_op jit(solution)/shard_map/ppermute | solution.py:217
  1.1 8.6 %collective-permute-start.9 = (bf16[384,768]{1,0:T(8,128)(2,1)}, bf16[384,768]{1,0:T(8,128)(2,1)S(1)}, u32[]{:S(2)}, u32[]{:S(2)}) collective-permute-start(bf16[384,768]{1,0:T(8,128)(2,1)} %bitcast.17), channel_id=1, source_target_pairs={{0,1},{1,0},{2,3},{3,2},{4,5},{5,4},{6,7},{7,6},{8,9},{9,8},{10,11... | collective-permute-start | bytes 1769480 | tf_op jit(solution)/shard_map/ppermute | solution.py:217
  1.2 21.8 %collective-permute-start.10 = (bf16[768,384]{1,0:T(8,128)(2,1)}, bf16[768,384]{1,0:T(8,128)(2,1)S(1)}, u32[]{:S(2)}, u32[]{:S(2)}) collective-permute-start(bf16[768,384]{1,0:T(8,128)(2,1)} %bitcast.19), channel_id=1, source_target_pairs={{0,1},{1,0},{2,3},{3,2},{4,5},{5,4},{6,7},{7,6},{8,9},{9,8},{10,11... | collective-permute-start | bytes 1769480 | tf_op jit(solution)/shard_map/ppermute | solution.py:217
  1.7 1.2 %copy-start = (bf16[1,6,96,768]{3,2,1,0:T(8,128)(2,1)S(1)}, bf16[1,6,96,768]{3,2,1,0:T(8,128)(2,1)}, u32[]{:S(2)}) copy-start(bf16[1,6,96,768]{3,2,1,0:T(8,128)(2,1)} %param.6) | copy-start | bytes 2654212
  2.8 0.7 %copy-start.3 = (s32[6]{0:T(128)S(1)}, s32[6]{0:T(128)}, u32[]{:S(2)}) copy-start(s32[6]{0:T(128)} %owner_ref.7) | copy-start | bytes 76
  3.5 20.5 %copy-start.1 = (bf16[1,384,768]{2,1,0:T(8,128)(2,1)S(1)}, bf16[1,384,768]{2,1,0:T(8,128)(2,1)}, u32[]{:S(2)}) copy-start(bf16[1,384,768]{2,1,0:T(8,128)(2,1)} %param.10) | copy-start | bytes 1769476
  3.5 20.5 %copy-start.2 = (bf16[1,768,384]{2,1,0:T(8,128)(2,1)S(1)}, bf16[1,768,384]{2,1,0:T(8,128)(2,1)}, u32[]{:S(2)}) copy-start(bf16[1,768,384]{2,1,0:T(8,128)(2,1)} %param.11) | copy-start | bytes 1769476
  4.8 4.9 %collective-permute-start.1 = (bf16[96,768]{1,0:T(8,128)(2,1)S(1)}, bf16[96,768]{1,0:T(8,128)(2,1)S(1)}, u32[]{:S(2)}, u32[]{:S(2)}) collective-permute-start(bf16[96,768]{1,0:T(8,128)(2,1)S(1)} %get-tuple-element.23), channel_id=1, source_target_pairs={{0,0},{1,9},{2,2},{3,11},{4,4},{5,13},{6,6},{7,15},{8,8},{9,1},{10... | collective-permute-start | bytes 442376 | tf_op jit(solution)/shard_map/ppermute | solution.py:221
  5.5 9.5 %collective-permute-start.2 = (bf16[96,768]{1,0:T(8,128)(2,1)S(1)}, bf16[96,768]{1,0:T(8,128)(2,1)S(1)}, u32[]{:S(2)}, u32[]{:S(2)}) collective-permute-start(bf16[96,768]{1,0:T(8,128)(2,1)S(1)} %get-tuple-element.24), channel_id=1, source_target_pairs={{0,2},{1,11},{2,0},{3,9},{4,6},{5,15},{6,4},{7,13},{8,10},{9,3},{1... | collective-permute-start | bytes 442376 | tf_op jit(solution)/shard_map/ppermute | solution.py:221
  8.1 9.9 %collective-permute-start.3 = (bf16[96,768]{1,0:T(8,128)(2,1)S(1)}, bf16[96,768]{1,0:T(8,128)(2,1)S(1)}, u32[]{:S(2)}, u32[]{:S(2)}) collective-permute-start(bf16[96,768]{1,0:T(8,128)(2,1)S(1)} %get-tuple-element.25), channel_id=1, source_target_pairs={{0,4},{1,13},{2,6},{3,15},{4,0},{5,9},{6,2},{7,11},{8,12},{9,5},{1... | collective-permute-start | bytes 442376 | tf_op jit(solution)/shard_map/ppermute | solution.py:221
  9.7 10.9 %collective-permute-start.4 = (bf16[96,768]{1,0:T(8,128)(2,1)S(1)}, bf16[96,768]{1,0:T(8,128)(2,1)S(1)}, u32[]{:S(2)}, u32[]{:S(2)}) collective-permute-start(bf16[96,768]{1,0:T(8,128)(2,1)S(1)} %get-tuple-element.26), channel_id=1, source_target_pairs={{0,6},{1,15},{2,4},{3,13},{4,2},{5,11},{6,0},{7,9},{8,14},{9,7},{1... | collective-permute-start | bytes 442376 | tf_op jit(solution)/shard_map/ppermute | solution.py:221
  9.7 13.3 %collective-permute-start.5 = (bf16[96,768]{1,0:T(8,128)(2,1)S(1)}, bf16[96,768]{1,0:T(8,128)(2,1)S(1)}, u32[]{:S(2)}, u32[]{:S(2)}) collective-permute-start(bf16[96,768]{1,0:T(8,128)(2,1)S(1)} %collective-permute-done.1.refs_0_), channel_id=1, source_target_pairs={{0,1},{1,0},{2,3},{3,2},{4,5},{5,4},{6,7},{7,6},{8,9},{9,8},{10,11... | collective-permute-start | bytes 442376 | tf_op jit(solution)/shard_map/ppermute | solution.py:217
  15.0 8.0 %collective-permute-start.6 = (bf16[96,768]{1,0:T(8,128)(2,1)S(1)}, bf16[96,768]{1,0:T(8,128)(2,1)S(1)}, u32[]{:S(2)}, u32[]{:S(2)}) collective-permute-start(bf16[96,768]{1,0:T(8,128)(2,1)S(1)} %collective-permute-done.2.refs_1_), channel_id=1, source_target_pairs={{0,1},{1,0},{2,3},{3,2},{4,5},{5,4},{6,7},{7,6},{8,9},{9,8},{10,11... | collective-permute-start | bytes 442376 | tf_op jit(solution)/shard_map/ppermute | solution.py:217
  18.0 5.0 %collective-permute-start.7 = (bf16[96,768]{1,0:T(8,128)(2,1)S(1)}, bf16[96,768]{1,0:T(8,128)(2,1)S(1)}, u32[]{:S(2)}, u32[]{:S(2)}) collective-permute-start(bf16[96,768]{1,0:T(8,128)(2,1)S(1)} %collective-permute-done.3.refs_2_), channel_id=1, source_target_pairs={{0,1},{1,0},{2,3},{3,2},{4,5},{5,4},{6,7},{7,6},{8,9},{9,8},{10,11... | collective-permute-start | bytes 442376 | tf_op jit(solution)/shard_map/ppermute | solution.py:217
  20.6 3.4 %collective-permute-start.8 = (bf16[96,768]{1,0:T(8,128)(2,1)S(1)}, bf16[96,768]{1,0:T(8,128)(2,1)S(1)}, u32[]{:S(2)}, u32[]{:S(2)}) collective-permute-start(bf16[96,768]{1,0:T(8,128)(2,1)S(1)} %collective-permute-done.4.refs_3_), channel_id=1, source_target_pairs={{0,1},{1,0},{2,3},{3,2},{4,5},{5,4},{6,7},{7,6},{8,9},{9,8},{10,11... | collective-permute-start | bytes 442376 | tf_op jit(solution)/shard_map/ppermute | solution.py:217
  25.7 12.9 %copy-start.4 = (s32[6]{0:T(128)S(1)}, s32[6]{0:T(128)}, u32[]{:S(2)}) copy-start(s32[6]{0:T(128)} %owner_ref.7) | copy-start | bytes 76
  25.7 12.9 %copy-start.5 = (bf16[1,384,768]{2,1,0:T(8,128)(2,1)S(1)}, bf16[1,384,768]{2,1,0:T(8,128)(2,1)}, u32[]{:S(2)}) copy-start(bf16[1,384,768]{2,1,0:T(8,128)(2,1)} %param.8) | copy-start | bytes 1769476
  25.7 12.9 %copy-start.6 = (bf16[1,384,768]{2,1,0:T(8,128)(2,1)S(1)}, bf16[1,384,768]{2,1,0:T(8,128)(2,1)}, u32[]{:S(2)}) copy-start(bf16[1,384,768]{2,1,0:T(8,128)(2,1)} %param.9) | copy-start | bytes 1769476
  25.7 8.7 %collective-permute-start.12 = (bf16[2,96,384]{2,1,0:T(8,128)(2,1)S(1)}, bf16[2,96,384]{2,1,0:T(8,128)(2,1)S(1)}, u32[]{:S(2)}, u32[]{:S(2)}) collective-permute-start(bf16[2,96,384]{2,1,0:T(8,128)(2,1)S(1)} %get-tuple-element.32), channel_id=1, source_target_pairs={{0,4},{1,13},{2,6},{3,15},{4,0},{5,9},{6,2},{7,11},{8,12},{9,5},{1... | collective-permute-start | bytes 442376 | tf_op jit(solution)/shard_map/ppermute | solution.py:221
  28.5 1.2 %collective-permute-start.11 = (f32[8,128]{1,0:T(8,128)S(1)}, f32[8,128]{1,0:T(8,128)S(1)}, u32[]{:S(2)}, u32[]{:S(2)}) collective-permute-start(f32[8,128]{1,0:T(8,128)S(1)} %get-tuple-element.28.mine_sq_ref), channel_id=1, source_target_pairs={{0,1},{1,0},{2,3},{3,2},{4,5},{5,4},{6,7},{7,6},{8,9},{9,8},{10,11... | collective-permute-start | bytes 12296 | tf_op jit(solution)/shard_map/ppermute | solution.py:217
  29.9 12.9 %collective-permute-start.13 = (bf16[2,96,384]{2,1,0:T(8,128)(2,1)S(1)}, bf16[2,96,384]{2,1,0:T(8,128)(2,1)S(1)}, u32[]{:S(2)}, u32[]{:S(2)}) collective-permute-start(bf16[2,96,384]{2,1,0:T(8,128)(2,1)S(1)} %get-tuple-element.36), channel_id=1, source_target_pairs={{0,2},{1,11},{2,0},{3,9},{4,6},{5,15},{6,4},{7,13},{8,10},{9,3},{1... | collective-permute-start | bytes 442376 | tf_op jit(solution)/shard_map/ppermute | solution.py:221
  30.8 10.2 %collective-permute-start.14 = (bf16[2,96,384]{2,1,0:T(8,128)(2,1)S(1)}, bf16[2,96,384]{2,1,0:T(8,128)(2,1)S(1)}, u32[]{:S(2)}, u32[]{:S(2)}) collective-permute-start(bf16[2,96,384]{2,1,0:T(8,128)(2,1)S(1)} %get-tuple-element.39), channel_id=1, source_target_pairs={{0,0},{1,9},{2,2},{3,11},{4,4},{5,13},{6,6},{7,15},{8,8},{9,1},{10... | collective-permute-start | bytes 442376 | tf_op jit(solution)/shard_map/ppermute | solution.py:221
  31.5 10.6 %collective-permute-start.15 = (bf16[2,96,384]{2,1,0:T(8,128)(2,1)S(1)}, bf16[2,96,384]{2,1,0:T(8,128)(2,1)S(1)}, u32[]{:S(2)}, u32[]{:S(2)}) collective-permute-start(bf16[2,96,384]{2,1,0:T(8,128)(2,1)S(1)} %get-tuple-element.41), channel_id=1, source_target_pairs={{0,6},{1,15},{2,4},{3,13},{4,2},{5,11},{6,0},{7,9},{8,14},{9,7},{1... | collective-permute-start | bytes 442376 | tf_op jit(solution)/shard_map/ppermute | solution.py:221
  34.4 14.0 %collective-permute-start.18 = (bf16[96,384]{1,0:T(8,128)(2,1)S(1)}, bf16[96,384]{1,0:T(8,128)(2,1)S(1)}, u32[]{:S(2)}, u32[]{:S(2)}) collective-permute-start(bf16[96,384]{1,0:T(8,128)(2,1)S(1)} %slice_bitcast_fusion.2), channel_id=1, source_target_pairs={{0,1},{1,0},{2,3},{3,2},{4,5},{5,4},{6,7},{7,6},{8,9},{9,8},{10,11... | collective-permute-start | bytes 221192 | tf_op jit(solution)/shard_map/ppermute | solution.py:217
  41.1 7.3 %collective-permute-start.16 = (bf16[96,384]{1,0:T(8,128)(2,1)S(1)}, bf16[96,384]{1,0:T(8,128)(2,1)S(1)}, u32[]{:S(2)}, u32[]{:S(2)}) collective-permute-start(bf16[96,384]{1,0:T(8,128)(2,1)S(1)} %slice_bitcast_fusion.1), channel_id=1, source_target_pairs={{0,1},{1,0},{2,3},{3,2},{4,5},{5,4},{6,7},{7,6},{8,9},{9,8},{10,11... | collective-permute-start | bytes 221192 | tf_op jit(solution)/shard_map/ppermute | solution.py:217
  42.1 6.3 %collective-permute-start.19 = (bf16[96,384]{1,0:T(8,128)(2,1)S(1)}, bf16[96,384]{1,0:T(8,128)(2,1)S(1)}, u32[]{:S(2)}, u32[]{:S(2)}) collective-permute-start(bf16[96,384]{1,0:T(8,128)(2,1)S(1)} %slice_bitcast_fusion), channel_id=1, source_target_pairs={{0,1},{1,0},{2,3},{3,2},{4,5},{5,4},{6,7},{7,6},{8,9},{9,8},{10,11... | collective-permute-start | bytes 221192 | tf_op jit(solution)/shard_map/ppermute | solution.py:217
  42.7 5.7 %collective-permute-start.17 = (bf16[96,384]{1,0:T(8,128)(2,1)S(1)}, bf16[96,384]{1,0:T(8,128)(2,1)S(1)}, u32[]{:S(2)}, u32[]{:S(2)}) collective-permute-start(bf16[96,384]{1,0:T(8,128)(2,1)S(1)} %slice_bitcast_fusion.3), channel_id=1, source_target_pairs={{0,1},{1,0},{2,3},{3,2},{4,5},{5,4},{6,7},{7,6},{8,9},{9,8},{10,11... | collective-permute-start | bytes 221192 | tf_op jit(solution)/shard_map/ppermute | solution.py:217
  42.8 4.3 %collective-permute-start.20 = (f32[8,128]{1,0:T(8,128)S(1)}, f32[8,128]{1,0:T(8,128)S(1)}, u32[]{:S(2)}, u32[]{:S(2)}) collective-permute-start(f32[8,128]{1,0:T(8,128)S(1)} %get-tuple-element.42), channel_id=1, source_target_pairs={{0,4},{1,13},{2,6},{3,15},{4,0},{5,9},{6,2},{7,11},{8,12},{9,5},{1... | collective-permute-start | bytes 12296 | tf_op jit(solution)/shard_map/ppermute | solution.py:221
  47.1 1.3 %collective-permute-start.21 = (f32[8,128]{1,0:T(8,128)S(1)}, f32[8,128]{1,0:T(8,128)S(1)}, u32[]{:S(2)}, u32[]{:S(2)}) collective-permute-start(f32[8,128]{1,0:T(8,128)S(1)} %collective-permute-done.20.refs_8_), channel_id=1, source_target_pairs={{0,1},{1,0},{2,3},{3,2},{4,5},{5,4},{6,7},{7,6},{8,9},{9,8},{10,11... | collective-permute-start | bytes 12296 | tf_op jit(solution)/shard_map/ppermute | solution.py:217

commit v4 on v3

--- a/solution.py
+++ b/solution.py
@@ -10,7 +10,7 @@
 VMEM = pl.BlockSpec(memory_space=pltpu.VMEM)
 SMEM = pl.BlockSpec(memory_space=pltpu.SMEM)
 ANY = pl.BlockSpec(memory_space=pl.ANY)
-EARLY = 1
+EARLY = 0
 PARAMS = pltpu.CompilerParams(vmem_limit_bytes=24 * 1024 * 1024)
 
 

time: 50 us -> 46.2 us (0.924)
  starting transfers between devices: 35.9 us -> 30.4 us
  waiting for transfers between devices: 4.27 us -> 5.58 us
  Pallas kernels: 7 us -> 7.51 us
    ppermute x9 -> x8, starting transfers between devices: 14.9 us -> 9.81 us  [trade(): return lax.ppermute(x, ('shard', 'replica'), pairs)]
    ppermute x9 -> x8, waiting for transfers between devices: 1.61 us -> 2.52 us  [trade(): return lax.ppermute(x, ('shard', 'replica'), pairs)]
    pallas_call x6, Pallas kernels: 7 us -> 7.51 us  [call(): pl.pallas_call(kernel, out_shape=out_shape, in_specs=in_specs, compiler_p...]
    ppermute x13 -> x12, starting transfers between devices: 21 us -> 20.5 us  [other_core(): return lax.ppermute(x, 'replica', [(0, 1), (1, 0)])]
    ppermute x13 -> x12, waiting for transfers between devices: 2.66 us -> 3.06 us  [other_core(): return lax.ppermute(x, 'replica', [(0, 1), (1, 0)])]
  transfers between devices with their start and end apart: 22 -> 20, of which waited for: 4 -> 5; matrix products, arithmetic and copies ran while one was open for 0% -> 0% of each run, Pallas kernels for 8% -> 8%
where the time goes in v4:
time: 46.2 us; the launch traced here: 46 us
  starting transfers between devices  30.4 us (66%)
  Pallas kernels  7.51 us (16%)
  waiting for transfers between devices  5.58 us (12%)
  local copies, waits for them, and re-layouts  1.87 us (4%)
  between operations  0.73 us (2%)
    ppermute x12, starting transfers between devices, other_core(): return lax.ppermute(x, 'replica', [(0, 1), (1, 0)])  20.5 us
    ppermute x8, starting transfers between devices, trade(): return lax.ppermute(x, ('shard', 'replica'), pairs)  9.81 us
    pallas_call x6, Pallas kernels, call(): pl.pallas_call(kernel, out_shape=out_shape, in_specs=in_specs, compiler_p...  7.51 us
    ppermute x12, waiting for transfers between devices, other_core(): return lax.ppermute(x, 'replica', [(0, 1), (1, 0)])  3.06 us
    ppermute x8, waiting for transfers between devices, trade(): return lax.ppermute(x, ('shard', 'replica'), pairs)  2.52 us
    unnamed x14, local copies, waits for them, and re-layouts  1.84 us
  transfers between devices with their start and end apart: 20, of which 5 were waited for; matrix products, arithmetic and copies ran while one was open for 0% of the time, Pallas kernels for 8%

profile of v4, /device:TPU:0, one launch (start us, length us, event | category | flops | bytes accessed | tf_op | source)
XLA Modules:
  0.0 46.0 jit_solution(16647602206628826696)
XLA Ops:
  0.6 0.5 %collective-permute-start = (bf16[6,96,768]{2,1,0:T(8,128)(2,1)}, bf16[6,96,768]{2,1,0:T(8,128)(2,1)S(1)}, u32[]{:S(2)}, u32[]{:S(2)}) collective-permute-start(bf16[6,96,768]{2,1,0:T(8,128)(2,1)} %bitcast.15), channel_id=1, source_target_pairs={{0,1},{1,0},{2,3},{3,2},{4,5},{5,4},{6,7},{7,6},{8,9},{9,8},{10,11... | collective-permute-start | bytes 2654216 | tf_op jit(solution)/shard_map/ppermute | solution.py:217
  1.1 0.1 collective-permute-start.9
  1.2 0.4 collective-permute-start.10
  1.7 1.2 %copy-done = bf16[1,6,96,768]{3,2,1,0:T(8,128)(2,1)S(1)} copy-done((bf16[1,6,96,768]{3,2,1,0:T(8,128)(2,1)S(1)}, bf16[1,6,96,768]{3,2,1,0:T(8,128)(2,1)}, u32[]{:S(2)}) %copy-start) | copy-done | bytes 884760
  2.8 0.7 %copy-done.3 = s32[6]{0:T(128)S(1)} copy-done((s32[6]{0:T(128)S(1)}, s32[6]{0:T(128)}, u32[]{:S(2)}) %copy-start.3) | copy-done | bytes 48
  3.5 0.6 %shard_map.85.mine_ref = bf16[4,96,768]{2,1,0:T(8,128)(2,1)S(1)} custom-call(s32[6]{0:T(128)S(1)} %copy-done.3, bf16[6,96,768]{2,1,0:T(8,128)(2,1)S(1)} %bitcast.16), custom_call_target="tpu_custom_call" | custom-call | tf_op jit(solution)/shard_map/pallas_call | solution.py:227
  4.1 0.0 collective-permute-done.theirs_ref
  4.1 0.7 %shard_map.86 = (bf16[96,768]{1,0:T(8,128)(2,1)S(1)}, bf16[96,768]{1,0:T(8,128)(2,1)S(1)}, bf16[96,768]{1,0:T(8,128)(2,1)S(1)}, bf16[96,768]{1,0:T(8,128)(2,1)S(1)}) custom-call(s32[6]{0:T(128)S(1)} %copy-done.3, bf16[4,96,768]{2,1,0:T(8,128)(2,1)S(1)} %shard_map.85.mine_ref, bf16[6,96,768]{2,1,0:T(8,128)(2,1)S(1)} %collective-permute-done.theirs_ref), custom_call_target="tpu_custom_call" | custom-call | tf_op jit(solution)/shard_map/pallas_call | solution.py:227
  4.8 0.7 %collective-permute-start.1 = (bf16[96,768]{1,0:T(8,128)(2,1)S(1)}, bf16[96,768]{1,0:T(8,128)(2,1)S(1)}, u32[]{:S(2)}, u32[]{:S(2)}) collective-permute-start(bf16[96,768]{1,0:T(8,128)(2,1)S(1)} %get-tuple-element.20), channel_id=1, source_target_pairs={{0,0},{1,9},{2,2},{3,11},{4,4},{5,13},{6,6},{7,15},{8,8},{9,1},{10... | collective-permute-start | bytes 442376 | tf_op jit(solution)/shard_map/ppermute | solution.py:221
  5.5 2.6 %collective-permute-start.2 = (bf16[96,768]{1,0:T(8,128)(2,1)S(1)}, bf16[96,768]{1,0:T(8,128)(2,1)S(1)}, u32[]{:S(2)}, u32[]{:S(2)}) collective-permute-start(bf16[96,768]{1,0:T(8,128)(2,1)S(1)} %get-tuple-element.21), channel_id=1, source_target_pairs={{0,2},{1,11},{2,0},{3,9},{4,6},{5,15},{6,4},{7,13},{8,10},{9,3},{1... | collective-permute-start | bytes 442376 | tf_op jit(solution)/shard_map/ppermute | solution.py:221
  8.1 1.6 %collective-permute-start.3 = (bf16[96,768]{1,0:T(8,128)(2,1)S(1)}, bf16[96,768]{1,0:T(8,128)(2,1)S(1)}, u32[]{:S(2)}, u32[]{:S(2)}) collective-permute-start(bf16[96,768]{1,0:T(8,128)(2,1)S(1)} %get-tuple-element.22), channel_id=1, source_target_pairs={{0,4},{1,13},{2,6},{3,15},{4,0},{5,9},{6,2},{7,11},{8,12},{9,5},{1... | collective-permute-start | bytes 442376 | tf_op jit(solution)/shard_map/ppermute | solution.py:221
  9.7 0.0 collective-permute-done.9.refs_9_
  9.7 0.0 collective-permute-start.4
  9.7 0.0 collective-permute-done.1.refs_0_
  9.7 5.3 %collective-permute-start.5 = (bf16[96,768]{1,0:T(8,128)(2,1)S(1)}, bf16[96,768]{1,0:T(8,128)(2,1)S(1)}, u32[]{:S(2)}, u32[]{:S(2)}) collective-permute-start(bf16[96,768]{1,0:T(8,128)(2,1)S(1)} %collective-permute-done.1.refs_0_), channel_id=1, source_target_pairs={{0,1},{1,0},{2,3},{3,2},{4,5},{5,4},{6,7},{7,6},{8,9},{9,8},{10,11... | collective-permute-start | bytes 442376 | tf_op jit(solution)/shard_map/ppermute | solution.py:217
  15.0 0.0 collective-permute-done.2.refs_1_
  15.0 3.0 %collective-permute-start.6 = (bf16[96,768]{1,0:T(8,128)(2,1)S(1)}, bf16[96,768]{1,0:T(8,128)(2,1)S(1)}, u32[]{:S(2)}, u32[]{:S(2)}) collective-permute-start(bf16[96,768]{1,0:T(8,128)(2,1)S(1)} %collective-permute-done.2.refs_1_), channel_id=1, source_target_pairs={{0,1},{1,0},{2,3},{3,2},{4,5},{5,4},{6,7},{7,6},{8,9},{9,8},{10,11... | collective-permute-start | bytes 442376 | tf_op jit(solution)/shard_map/ppermute | solution.py:217
  18.0 0.0 collective-permute-done.3.refs_2_
  18.0 2.6 %collective-permute-start.7 = (bf16[96,768]{1,0:T(8,128)(2,1)S(1)}, bf16[96,768]{1,0:T(8,128)(2,1)S(1)}, u32[]{:S(2)}, u32[]{:S(2)}) collective-permute-start(bf16[96,768]{1,0:T(8,128)(2,1)S(1)} %collective-permute-done.3.refs_2_), channel_id=1, source_target_pairs={{0,1},{1,0},{2,3},{3,2},{4,5},{5,4},{6,7},{7,6},{8,9},{9,8},{10,11... | collective-permute-start | bytes 442376 | tf_op jit(solution)/shard_map/ppermute | solution.py:217
  20.6 0.0 collective-permute-done.4.refs_3_
  20.6 2.4 %collective-permute-start.8 = (bf16[96,768]{1,0:T(8,128)(2,1)S(1)}, bf16[96,768]{1,0:T(8,128)(2,1)S(1)}, u32[]{:S(2)}, u32[]{:S(2)}) collective-permute-start(bf16[96,768]{1,0:T(8,128)(2,1)S(1)} %collective-permute-done.4.refs_3_), channel_id=1, source_target_pairs={{0,1},{1,0},{2,3},{3,2},{4,5},{5,4},{6,7},{7,6},{8,9},{9,8},{10,11... | collective-permute-start | bytes 442376 | tf_op jit(solution)/shard_map/ppermute | solution.py:217
  23.0 0.0 collective-permute-done.10.refs_11_
  23.0 0.0 collective-permute-done.5.refs_4_
  23.0 0.0 collective-permute-done.6.refs_5_
  23.0 0.0 collective-permute-done.7.refs_6_
  23.0 1.0 %collective-permute-done.8.refs_7_ = bf16[96,768]{1,0:T(8,128)(2,1)S(1)} collective-permute-done((bf16[96,768]{1,0:T(8,128)(2,1)S(1)}, bf16[96,768]{1,0:T(8,128)(2,1)S(1)}, u32[]{:S(2)}, u32[]{:S(2)}) %collective-permute-start.8) | collective-permute-done | bytes 147488 | tf_op jit(solution)/shard_map/ppermute | solution.py:217
  24.0 1.7 %shard_map.87 = (bf16[768,768]{1,0:T(8,128)(2,1)S(1)}, f32[384,768]{1,0:T(8,128)S(1)}, f32[8,128]{1,0:T(8,128)S(1)}, f32[8,128]{1,0:T(8,128)S(1)}) custom-call(bf16[96,768]{1,0:T(8,128)(2,1)S(1)} %collective-permute-done.1.refs_0_, bf16[96,768]{1,0:T(8,128)(2,1)S(1)} %collective-permute-done.2.refs_1_, bf16[96,768]{1,0:T(8,128)(2,1)S(1)} %collective-permute-done.3.refs_2_, ...), custom_call_target="tpu_custom_call" | custom-call | tf_op jit(solution)/shard_map/pallas_call | solution.py:227
  25.7 0.4 collective-permute-start.11
  26.1 0.8 %collective-permute-done.11.theirs_sq_ref = f32[8,128]{1,0:T(8,128)S(1)} collective-permute-done((f32[8,128]{1,0:T(8,128)S(1)}, f32[8,128]{1,0:T(8,128)S(1)}, u32[]{:S(2)}, u32[]{:S(2)}) %collective-permute-start.11) | collective-permute-done | bytes 4128 | tf_op jit(solution)/shard_map/ppermute | solution.py:217
  27.0 0.6 %shard_map.88 = (f32[8,128]{1,0:T(8,128)}, bf16[2,96,384]{2,1,0:T(8,128)(2,1)S(1)}, bf16[2,96,384]{2,1,0:T(8,128)(2,1)S(1)}, bf16[2,96,384]{2,1,0:T(8,128)(2,1)S(1)}, bf16[2,96,384]{2,1,0:T(8,128)(2,1)S(1)}) custom-call(f32[8,128]{1,0:T(8,128)S(1)} %get-tuple-element.25.mine_sq_ref, f32[8,128]{1,0:T(8,128)S(1)} %collective-permute-done.11.theirs_sq_ref, ...), custom_call_target="tpu_custom_call" | custom-call | tf_op jit(solution)/shard_map/pallas_call | solution.py:227
  27.6 2.7 %collective-permute-start.12 = (bf16[2,96,384]{2,1,0:T(8,128)(2,1)S(1)}, bf16[2,96,384]{2,1,0:T(8,128)(2,1)S(1)}, u32[]{:S(2)}, u32[]{:S(2)}) collective-permute-start(bf16[2,96,384]{2,1,0:T(8,128)(2,1)S(1)} %get-tuple-element.28), channel_id=1, source_target_pairs={{0,4},{1,13},{2,6},{3,15},{4,0},{5,9},{6,2},{7,11},{8,12},{9,5},{1... | collective-permute-start | bytes 442376 | tf_op jit(solution)/shard_map/ppermute | solution.py:221
  30.3 0.9 %collective-permute-start.13 = (bf16[2,96,384]{2,1,0:T(8,128)(2,1)S(1)}, bf16[2,96,384]{2,1,0:T(8,128)(2,1)S(1)}, u32[]{:S(2)}, u32[]{:S(2)}) collective-permute-start(bf16[2,96,384]{2,1,0:T(8,128)(2,1)S(1)} %get-tuple-element.31), channel_id=1, source_target_pairs={{0,2},{1,11},{2,0},{3,9},{4,6},{5,15},{6,4},{7,13},{8,10},{9,3},{1... | collective-permute-start | bytes 442376 | tf_op jit(solution)/shard_map/ppermute | solution.py:221
  31.3 0.7 %collective-permute-start.14 = (bf16[2,96,384]{2,1,0:T(8,128)(2,1)S(1)}, bf16[2,96,384]{2,1,0:T(8,128)(2,1)S(1)}, u32[]{:S(2)}, u32[]{:S(2)}) collective-permute-start(bf16[2,96,384]{2,1,0:T(8,128)(2,1)S(1)} %get-tuple-element.34), channel_id=1, source_target_pairs={{0,0},{1,9},{2,2},{3,11},{4,4},{5,13},{6,6},{7,15},{8,8},{9,1},{10... | collective-permute-start | bytes 442376 | tf_op jit(solution)/shard_map/ppermute | solution.py:221
  31.9 0.6 %collective-permute-start.15 = (bf16[2,96,384]{2,1,0:T(8,128)(2,1)S(1)}, bf16[2,96,384]{2,1,0:T(8,128)(2,1)S(1)}, u32[]{:S(2)}, u32[]{:S(2)}) collective-permute-start(bf16[2,96,384]{2,1,0:T(8,128)(2,1)S(1)} %get-tuple-element.36), channel_id=1, source_target_pairs={{0,6},{1,15},{2,4},{3,13},{4,2},{5,11},{6,0},{7,9},{8,14},{9,7},{1... | collective-permute-start | bytes 442376 | tf_op jit(solution)/shard_map/ppermute | solution.py:221
  32.5 2.5 %collective-permute-done.12.after_ref.refs_2_ = bf16[2,96,384]{2,1,0:T(8,128)(2,1)S(1)} collective-permute-done((bf16[2,96,384]{2,1,0:T(8,128)(2,1)S(1)}, bf16[2,96,384]{2,1,0:T(8,128)(2,1)S(1)}, u32[]{:S(2)}, u32[]{:S(2)}) %collective-permute-start.12) | collective-permute-done | bytes 147488 | tf_op jit(solution)/shard_map/ppermute | solution.py:221
  35.0 2.7 %collective-permute-start.18 = (bf16[96,384]{1,0:T(8,128)(2,1)S(1)}, bf16[96,384]{1,0:T(8,128)(2,1)S(1)}, u32[]{:S(2)}, u32[]{:S(2)}) collective-permute-start(bf16[96,384]{1,0:T(8,128)(2,1)S(1)} %slice_bitcast_fusion.1), channel_id=1, source_target_pairs={{0,1},{1,0},{2,3},{3,2},{4,5},{5,4},{6,7},{7,6},{8,9},{9,8},{10,11... | collective-permute-start | bytes 221192 | tf_op jit(solution)/shard_map/ppermute | solution.py:217
  37.8 2.5 %shard_map.89 = (bf16[384,768]{1,0:T(8,128)(2,1)}, bf16[384,768]{1,0:T(8,128)(2,1)}) custom-call(s32[6]{0:T(128)S(1)} %copy-done.4, bf16[768,768]{1,0:T(8,128)(2,1)S(1)} %get-tuple-element.24.summed_ref, bf16[384,768]{1,0:T(8,128)(2,1)S(1)} %bitcast.21, bf16[384,768]{1,0:T(8,128)(2,1)S(1)} %bitcast.22, ...), custom_call_target="tpu_custom_call" | custom-call | flops 905969664 | bytes 2359296 | tf_op jit(solution)/shard_map/pallas_call | solution.py:227
  40.3 0.0 collective-permute-done.13.refs_1_
  40.3 0.1 collective-permute-start.17
  40.4 0.0 collective-permute-done.14.refs_0_
  40.4 2.9 %collective-permute-start.16 = (bf16[96,384]{1,0:T(8,128)(2,1)S(1)}, bf16[96,384]{1,0:T(8,128)(2,1)S(1)}, u32[]{:S(2)}, u32[]{:S(2)}) collective-permute-start(bf16[96,384]{1,0:T(8,128)(2,1)S(1)} %slice_bitcast_fusion.2), channel_id=1, source_target_pairs={{0,1},{1,0},{2,3},{3,2},{4,5},{5,4},{6,7},{7,6},{8,9},{9,8},{10,11... | collective-permute-start | bytes 221192 | tf_op jit(solution)/shard_map/ppermute | solution.py:217
  43.3 0.0 collective-permute-done.15.refs_3_
  43.3 0.1 collective-permute-start.19
  43.4 0.0 collective-permute-done.18.refs_6_
  43.4 0.0 collective-permute-done.17.refs_5_
  43.4 0.8 %collective-permute-done.16.refs_4_ = bf16[96,384]{1,0:T(8,128)(2,1)S(1)} collective-permute-done((bf16[96,384]{1,0:T(8,128)(2,1)S(1)}, bf16[96,384]{1,0:T(8,128)(2,1)S(1)}, u32[]{:S(2)}, u32[]{:S(2)}) %collective-permute-start.16) | collective-permute-done | bytes 73760 | tf_op jit(solution)/shard_map/ppermute | solution.py:217
  44.2 0.4 collective-permute-done.19.refs_7_
  44.7 1.4 %shard_map.90 = bf16[6,96,384]{2,1,0:T(8,128)(2,1)} custom-call(s32[6]{0:T(128)S(1)} %copy-done.4, bf16[2,96,384]{2,1,0:T(8,128)(2,1)S(1)} %collective-permute-done.14.refs_0_, bf16[2,96,384]{2,1,0:T(8,128)(2,1)S(1)} %collective-permute-done.13.refs_1_, bf16[2,96,384]{2,1,0:T(8,128)(2,1)S(1)} %collective-permute-done.12.after_ref.refs_2_, ...), custom_call_target="tpu_custom_call" | custom-call | tf_op jit(solution)/shard_map/pallas_call | solution.py:227
  (16 shorter events, 0.1 us)
Async XLA Ops:
  0.6 3.5 %collective-permute-start = (bf16[6,96,768]{2,1,0:T(8,128)(2,1)}, bf16[6,96,768]{2,1,0:T(8,128)(2,1)S(1)}, u32[]{:S(2)}, u32[]{:S(2)}) collective-permute-start(bf16[6,96,768]{2,1,0:T(8,128)(2,1)} %bitcast.15), channel_id=1, source_target_pairs={{0,1},{1,0},{2,3},{3,2},{4,5},{5,4},{6,7},{7,6},{8,9},{9,8},{10,11... | collective-permute-start | bytes 2654216 | tf_op jit(solution)/shard_map/ppermute | solution.py:217
  1.1 8.6 %collective-permute-start.9 = (bf16[384,768]{1,0:T(8,128)(2,1)}, bf16[384,768]{1,0:T(8,128)(2,1)S(1)}, u32[]{:S(2)}, u32[]{:S(2)}) collective-permute-start(bf16[384,768]{1,0:T(8,128)(2,1)} %bitcast.17), channel_id=1, source_target_pairs={{0,1},{1,0},{2,3},{3,2},{4,5},{5,4},{6,7},{7,6},{8,9},{9,8},{10,11... | collective-permute-start | bytes 1769480 | tf_op jit(solution)/shard_map/ppermute | solution.py:217
  1.2 21.8 %collective-permute-start.10 = (bf16[768,384]{1,0:T(8,128)(2,1)}, bf16[768,384]{1,0:T(8,128)(2,1)S(1)}, u32[]{:S(2)}, u32[]{:S(2)}) collective-permute-start(bf16[768,384]{1,0:T(8,128)(2,1)} %bitcast.19), channel_id=1, source_target_pairs={{0,1},{1,0},{2,3},{3,2},{4,5},{5,4},{6,7},{7,6},{8,9},{9,8},{10,11... | collective-permute-start | bytes 1769480 | tf_op jit(solution)/shard_map/ppermute | solution.py:217
  1.7 1.2 %copy-start = (bf16[1,6,96,768]{3,2,1,0:T(8,128)(2,1)S(1)}, bf16[1,6,96,768]{3,2,1,0:T(8,128)(2,1)}, u32[]{:S(2)}) copy-start(bf16[1,6,96,768]{3,2,1,0:T(8,128)(2,1)} %param.6) | copy-start | bytes 2654212
  2.8 0.7 %copy-start.3 = (s32[6]{0:T(128)S(1)}, s32[6]{0:T(128)}, u32[]{:S(2)}) copy-start(s32[6]{0:T(128)} %owner_ref.7) | copy-start | bytes 76
  3.5 20.5 %copy-start.1 = (bf16[1,384,768]{2,1,0:T(8,128)(2,1)S(1)}, bf16[1,384,768]{2,1,0:T(8,128)(2,1)}, u32[]{:S(2)}) copy-start(bf16[1,384,768]{2,1,0:T(8,128)(2,1)} %param.10) | copy-start | bytes 1769476
  3.5 20.5 %copy-start.2 = (bf16[1,768,384]{2,1,0:T(8,128)(2,1)S(1)}, bf16[1,768,384]{2,1,0:T(8,128)(2,1)}, u32[]{:S(2)}) copy-start(bf16[1,768,384]{2,1,0:T(8,128)(2,1)} %param.11) | copy-start | bytes 1769476
  4.8 4.9 %collective-permute-start.1 = (bf16[96,768]{1,0:T(8,128)(2,1)S(1)}, bf16[96,768]{1,0:T(8,128)(2,1)S(1)}, u32[]{:S(2)}, u32[]{:S(2)}) collective-permute-start(bf16[96,768]{1,0:T(8,128)(2,1)S(1)} %get-tuple-element.20), channel_id=1, source_target_pairs={{0,0},{1,9},{2,2},{3,11},{4,4},{5,13},{6,6},{7,15},{8,8},{9,1},{10... | collective-permute-start | bytes 442376 | tf_op jit(solution)/shard_map/ppermute | solution.py:221
  5.5 9.5 %collective-permute-start.2 = (bf16[96,768]{1,0:T(8,128)(2,1)S(1)}, bf16[96,768]{1,0:T(8,128)(2,1)S(1)}, u32[]{:S(2)}, u32[]{:S(2)}) collective-permute-start(bf16[96,768]{1,0:T(8,128)(2,1)S(1)} %get-tuple-element.21), channel_id=1, source_target_pairs={{0,2},{1,11},{2,0},{3,9},{4,6},{5,15},{6,4},{7,13},{8,10},{9,3},{1... | collective-permute-start | bytes 442376 | tf_op jit(solution)/shard_map/ppermute | solution.py:221
  8.1 9.9 %collective-permute-start.3 = (bf16[96,768]{1,0:T(8,128)(2,1)S(1)}, bf16[96,768]{1,0:T(8,128)(2,1)S(1)}, u32[]{:S(2)}, u32[]{:S(2)}) collective-permute-start(bf16[96,768]{1,0:T(8,128)(2,1)S(1)} %get-tuple-element.22), channel_id=1, source_target_pairs={{0,4},{1,13},{2,6},{3,15},{4,0},{5,9},{6,2},{7,11},{8,12},{9,5},{1... | collective-permute-start | bytes 442376 | tf_op jit(solution)/shard_map/ppermute | solution.py:221
  9.7 10.9 %collective-permute-start.4 = (bf16[96,768]{1,0:T(8,128)(2,1)S(1)}, bf16[96,768]{1,0:T(8,128)(2,1)S(1)}, u32[]{:S(2)}, u32[]{:S(2)}) collective-permute-start(bf16[96,768]{1,0:T(8,128)(2,1)S(1)} %get-tuple-element.23), channel_id=1, source_target_pairs={{0,6},{1,15},{2,4},{3,13},{4,2},{5,11},{6,0},{7,9},{8,14},{9,7},{1... | collective-permute-start | bytes 442376 | tf_op jit(solution)/shard_map/ppermute | solution.py:221
  9.7 13.3 %collective-permute-start.5 = (bf16[96,768]{1,0:T(8,128)(2,1)S(1)}, bf16[96,768]{1,0:T(8,128)(2,1)S(1)}, u32[]{:S(2)}, u32[]{:S(2)}) collective-permute-start(bf16[96,768]{1,0:T(8,128)(2,1)S(1)} %collective-permute-done.1.refs_0_), channel_id=1, source_target_pairs={{0,1},{1,0},{2,3},{3,2},{4,5},{5,4},{6,7},{7,6},{8,9},{9,8},{10,11... | collective-permute-start | bytes 442376 | tf_op jit(solution)/shard_map/ppermute | solution.py:217
  15.0 8.0 %collective-permute-start.6 = (bf16[96,768]{1,0:T(8,128)(2,1)S(1)}, bf16[96,768]{1,0:T(8,128)(2,1)S(1)}, u32[]{:S(2)}, u32[]{:S(2)}) collective-permute-start(bf16[96,768]{1,0:T(8,128)(2,1)S(1)} %collective-permute-done.2.refs_1_), channel_id=1, source_target_pairs={{0,1},{1,0},{2,3},{3,2},{4,5},{5,4},{6,7},{7,6},{8,9},{9,8},{10,11... | collective-permute-start | bytes 442376 | tf_op jit(solution)/shard_map/ppermute | solution.py:217
  18.0 5.0 %collective-permute-start.7 = (bf16[96,768]{1,0:T(8,128)(2,1)S(1)}, bf16[96,768]{1,0:T(8,128)(2,1)S(1)}, u32[]{:S(2)}, u32[]{:S(2)}) collective-permute-start(bf16[96,768]{1,0:T(8,128)(2,1)S(1)} %collective-permute-done.3.refs_2_), channel_id=1, source_target_pairs={{0,1},{1,0},{2,3},{3,2},{4,5},{5,4},{6,7},{7,6},{8,9},{9,8},{10,11... | collective-permute-start | bytes 442376 | tf_op jit(solution)/shard_map/ppermute | solution.py:217
  20.6 3.4 %collective-permute-start.8 = (bf16[96,768]{1,0:T(8,128)(2,1)S(1)}, bf16[96,768]{1,0:T(8,128)(2,1)S(1)}, u32[]{:S(2)}, u32[]{:S(2)}) collective-permute-start(bf16[96,768]{1,0:T(8,128)(2,1)S(1)} %collective-permute-done.4.refs_3_), channel_id=1, source_target_pairs={{0,1},{1,0},{2,3},{3,2},{4,5},{5,4},{6,7},{7,6},{8,9},{9,8},{10,11... | collective-permute-start | bytes 442376 | tf_op jit(solution)/shard_map/ppermute | solution.py:217
  25.7 12.0 %copy-start.4 = (s32[6]{0:T(128)S(1)}, s32[6]{0:T(128)}, u32[]{:S(2)}) copy-start(s32[6]{0:T(128)} %owner_ref.7) | copy-start | bytes 76
  25.7 12.0 %copy-start.5 = (bf16[1,384,768]{2,1,0:T(8,128)(2,1)S(1)}, bf16[1,384,768]{2,1,0:T(8,128)(2,1)}, u32[]{:S(2)}) copy-start(bf16[1,384,768]{2,1,0:T(8,128)(2,1)} %param.8) | copy-start | bytes 1769476
  25.7 12.0 %copy-start.6 = (bf16[1,384,768]{2,1,0:T(8,128)(2,1)S(1)}, bf16[1,384,768]{2,1,0:T(8,128)(2,1)}, u32[]{:S(2)}) copy-start(bf16[1,384,768]{2,1,0:T(8,128)(2,1)} %param.9) | copy-start | bytes 1769476
  25.7 1.2 %collective-permute-start.11 = (f32[8,128]{1,0:T(8,128)S(1)}, f32[8,128]{1,0:T(8,128)S(1)}, u32[]{:S(2)}, u32[]{:S(2)}) collective-permute-start(f32[8,128]{1,0:T(8,128)S(1)} %get-tuple-element.25.mine_sq_ref), channel_id=1, source_target_pairs={{0,1},{1,0},{2,3},{3,2},{4,5},{5,4},{6,7},{7,6},{8,9},{9,8},{10,11... | collective-permute-start | bytes 12296 | tf_op jit(solution)/shard_map/ppermute | solution.py:217
  27.6 7.4 %collective-permute-start.12 = (bf16[2,96,384]{2,1,0:T(8,128)(2,1)S(1)}, bf16[2,96,384]{2,1,0:T(8,128)(2,1)S(1)}, u32[]{:S(2)}, u32[]{:S(2)}) collective-permute-start(bf16[2,96,384]{2,1,0:T(8,128)(2,1)S(1)} %get-tuple-element.28), channel_id=1, source_target_pairs={{0,4},{1,13},{2,6},{3,15},{4,0},{5,9},{6,2},{7,11},{8,12},{9,5},{1... | collective-permute-start | bytes 442376 | tf_op jit(solution)/shard_map/ppermute | solution.py:221
  30.3 9.9 %collective-permute-start.13 = (bf16[2,96,384]{2,1,0:T(8,128)(2,1)S(1)}, bf16[2,96,384]{2,1,0:T(8,128)(2,1)S(1)}, u32[]{:S(2)}, u32[]{:S(2)}) collective-permute-start(bf16[2,96,384]{2,1,0:T(8,128)(2,1)S(1)} %get-tuple-element.31), channel_id=1, source_target_pairs={{0,2},{1,11},{2,0},{3,9},{4,6},{5,15},{6,4},{7,13},{8,10},{9,3},{1... | collective-permute-start | bytes 442376 | tf_op jit(solution)/shard_map/ppermute | solution.py:221
  31.3 9.1 %collective-permute-start.14 = (bf16[2,96,384]{2,1,0:T(8,128)(2,1)S(1)}, bf16[2,96,384]{2,1,0:T(8,128)(2,1)S(1)}, u32[]{:S(2)}, u32[]{:S(2)}) collective-permute-start(bf16[2,96,384]{2,1,0:T(8,128)(2,1)S(1)} %get-tuple-element.34), channel_id=1, source_target_pairs={{0,0},{1,9},{2,2},{3,11},{4,4},{5,13},{6,6},{7,15},{8,8},{9,1},{10... | collective-permute-start | bytes 442376 | tf_op jit(solution)/shard_map/ppermute | solution.py:221
  31.9 11.4 %collective-permute-start.15 = (bf16[2,96,384]{2,1,0:T(8,128)(2,1)S(1)}, bf16[2,96,384]{2,1,0:T(8,128)(2,1)S(1)}, u32[]{:S(2)}, u32[]{:S(2)}) collective-permute-start(bf16[2,96,384]{2,1,0:T(8,128)(2,1)S(1)} %get-tuple-element.36), channel_id=1, source_target_pairs={{0,6},{1,15},{2,4},{3,13},{4,2},{5,11},{6,0},{7,9},{8,14},{9,7},{1... | collective-permute-start | bytes 442376 | tf_op jit(solution)/shard_map/ppermute | solution.py:221
  35.0 8.4 %collective-permute-start.18 = (bf16[96,384]{1,0:T(8,128)(2,1)S(1)}, bf16[96,384]{1,0:T(8,128)(2,1)S(1)}, u32[]{:S(2)}, u32[]{:S(2)}) collective-permute-start(bf16[96,384]{1,0:T(8,128)(2,1)S(1)} %slice_bitcast_fusion.1), channel_id=1, source_target_pairs={{0,1},{1,0},{2,3},{3,2},{4,5},{5,4},{6,7},{7,6},{8,9},{9,8},{10,11... | collective-permute-start | bytes 221192 | tf_op jit(solution)/shard_map/ppermute | solution.py:217
  40.3 3.2 %collective-permute-start.17 = (bf16[96,384]{1,0:T(8,128)(2,1)S(1)}, bf16[96,384]{1,0:T(8,128)(2,1)S(1)}, u32[]{:S(2)}, u32[]{:S(2)}) collective-permute-start(bf16[96,384]{1,0:T(8,128)(2,1)S(1)} %slice_bitcast_fusion.3), channel_id=1, source_target_pairs={{0,1},{1,0},{2,3},{3,2},{4,5},{5,4},{6,7},{7,6},{8,9},{9,8},{10,11... | collective-permute-start | bytes 221192 | tf_op jit(solution)/shard_map/ppermute | solution.py:217
  40.4 3.8 %collective-permute-start.16 = (bf16[96,384]{1,0:T(8,128)(2,1)S(1)}, bf16[96,384]{1,0:T(8,128)(2,1)S(1)}, u32[]{:S(2)}, u32[]{:S(2)}) collective-permute-start(bf16[96,384]{1,0:T(8,128)(2,1)S(1)} %slice_bitcast_fusion.2), channel_id=1, source_target_pairs={{0,1},{1,0},{2,3},{3,2},{4,5},{5,4},{6,7},{7,6},{8,9},{9,8},{10,11... | collective-permute-start | bytes 221192 | tf_op jit(solution)/shard_map/ppermute | solution.py:217
  43.3 1.3 %collective-permute-start.19 = (bf16[96,384]{1,0:T(8,128)(2,1)S(1)}, bf16[96,384]{1,0:T(8,128)(2,1)S(1)}, u32[]{:S(2)}, u32[]{:S(2)}) collective-permute-start(bf16[96,384]{1,0:T(8,128)(2,1)S(1)} %slice_bitcast_fusion), channel_id=1, source_target_pairs={{0,1},{1,0},{2,3},{3,2},{4,5},{5,4},{6,7},{7,6},{8,9},{9,8},{10,11... | collective-permute-start | bytes 221192 | tf_op jit(solution)/shard_map/ppermute | solution.py:217

commit v5 on v0

--- a/solution.py
+++ b/solution.py
@@ -1,7 +1,17 @@
+import functools
+
 import jax
 import jax.numpy as jnp
 from jax import lax
+from jax.experimental import pallas as pl
+from jax.experimental.pallas import tpu as pltpu
 from jax.sharding import PartitionSpec as P
+
+VMEM = pl.BlockSpec(memory_space=pltpu.VMEM)
+SMEM = pl.BlockSpec(memory_space=pltpu.SMEM)
+ANY = pl.BlockSpec(memory_space=pl.ANY)
+LIGHT = pl.CostEstimate(flops=0, bytes_accessed=0, transcendentals=0)
+PARAMS = pltpu.CompilerParams(vmem_limit_bytes=24 * 1024 * 1024)
 
 
 def per_device(gradients, block_owner, left_gram, right_gram, left_root, right_root):
@@ -45,9 +55,295 @@
     return (left_new[None], right_new[None], update)
 
 
+def codes_of(owners):
+    half, quarter = owners // 2, owners // 4
+    return (
+        [half + i for i in range(quarter)] + [i for i in reversed(range(quarter))],
+        [half + quarter + i for i in range(quarter)] + [quarter + i for i in range(quarter)],
+    )
+
+
+def partner(codes, k, other=False):
+    core = lax.axis_index("replica")
+    first = core == (1 if other else 0)
+    return lax.axis_index("shard") ^ jnp.where(first, codes[0][k], codes[1][k])
+
+
+def block_of(owner_ref, owner):
+    block = jnp.int32(-1)
+    for b in range(owner_ref.shape[0]):
+        block = jnp.where(owner_ref[b] == owner, b, block)
+    return block
+
+
+def sent_block(codes, owner_ref, k):
+    return jnp.maximum(block_of(owner_ref, partner(codes, k)), 0)
+
+
+def squares(value):
+    wide = value.astype(jnp.float32)
+    return jnp.sum(jnp.sum(wide * wide, axis=0, keepdims=True), axis=1, keepdims=True)
+
+
+def fetch_kernel(codes, owner_ref, gradient_ref, out_ref):
+    for k in range(out_ref.shape[0]):
+        out_ref[k] = gradient_ref[sent_block(codes, owner_ref, k)]
+
+
+def pick_kernel(codes, owner_ref, mine_ref, theirs_ref, *out_refs):
+    for k, out_ref in enumerate(out_refs):
+        other = theirs_ref[sent_block(codes, owner_ref, k)]
+        total = mine_ref[k].astype(jnp.float32) + other.astype(jnp.float32)
+        out_ref[...] = total.astype(out_ref.dtype)
+
+
+def order_kernel(codes, slots, own_ref, other_ref, *refs):
+    out_refs, rows_ref = refs[:-1], refs[-1]
+    half, full = own_ref.shape
+    rounds = len(codes[0])
+    slab = half // rounds
+    core = lax.axis_index("replica")
+    for k in range(rounds):
+        shard = partner(codes, k)
+        row = pl.multiple_of(lax.rem(shard, rounds) * slab, slab)
+        for ref, near in ((own_ref, True), (other_ref, False)):
+
+            @pl.when((lax.div(shard, rounds) == core) == near)
+            def _(ref=ref):
+                rows_ref[k * slab:(k + 1) * slab, :] = ref[pl.ds(row, slab), :]
+
+    for out_ref, group in zip(out_refs, slots):
+        column = lax.broadcasted_iota(jnp.int32, (1, len(group) * slab), 1)
+        source = column
+        for n, (k, other) in enumerate(group):
+            inside = (column >= n * slab) & (column < (n + 1) * slab)
+            shift = (partner(codes, k, other) - n) * slab
+            source = jnp.where(inside, column + shift, source)
+        row_index = lax.broadcasted_iota(jnp.int32, (full, len(group) * slab), 0)
+        choose = (row_index == source).astype(jnp.float32).astype(rows_ref.dtype)
+        out_ref[...] = jnp.dot(
+            rows_ref[...], choose, preferred_element_type=jnp.float32
+        ).astype(out_ref.dtype)
+
+
+def begin_kernel(left_ref, *refs):
+    *slabs, total_ref, grad_sq_ref, stacked_ref = refs
+    slab = slabs[0].shape[0]
+    for n, ref in enumerate(slabs):
+        stacked_ref[n * slab:(n + 1) * slab, :] = ref[...]
+    total_ref[...] = jnp.dot(
+        left_ref[...], stacked_ref[...], preferred_element_type=jnp.float32
+    )
+    grad_sq_ref[...] = jnp.broadcast_to(squares(stacked_ref[...]), grad_sq_ref.shape)
+
+
+def finish_kernel(early, left_ref, total_ref, begun_sq_ref, own_ref, other_ref, *refs):
+    *slabs, both_ref, side_sq_ref, grad_sq_ref = refs[:-2 - len(early)]
+    early_refs, stacked_ref, side_ref = refs[-2 - len(early):-2], refs[-2], refs[-1]
+    slab = slabs[0].shape[0]
+    for n, ref in enumerate(slabs):
+        stacked_ref[n * slab:(n + 1) * slab, :] = ref[...]
+    side = total_ref[...] + jnp.dot(
+        left_ref[...], stacked_ref[...], preferred_element_type=jnp.float32
+    )
+    side_ref[...] = side.astype(side_ref.dtype)
+    side_sq = jnp.zeros((1, 1), jnp.float32)
+    for n, ref in enumerate((own_ref, other_ref)):
+        both = jnp.dot(side_ref[...], ref[...], preferred_element_type=jnp.float32)
+        both_ref[n] = both
+        side_sq += squares(both)
+        for k, out_ref in zip(early, early_refs):
+            out_ref[n] = both[k * slab:(k + 1) * slab].astype(out_ref.dtype)
+    side_sq_ref[...] = jnp.broadcast_to(side_sq, side_sq_ref.shape)
+    grad_sq_ref[...] = begun_sq_ref[...] + squares(stacked_ref[...])
+
+
+def scale_kernel(late, mine_sq_ref, theirs_sq_ref, grad_sq_ref, both_ref, graft_ref, *out_refs):
+    side_sq = mine_sq_ref[...] + theirs_sq_ref[...]
+    graft_ref[...] = jnp.sqrt(grad_sq_ref[...] / (side_sq + 1e-06))
+    graft = graft_ref[0:1, 0:1]
+    for k, out_ref in zip(late, out_refs):
+        slab = out_ref.shape[1]
+        for n in range(2):
+            piece = both_ref[n, k * slab:(k + 1) * slab] * graft
+            out_ref[n] = piece.astype(out_ref.dtype)
+
+
+def gram_kernel(codes, owner_ref, left_ref, right_ref, after_ref, *refs):
+    rounds = len(codes[0])
+    slabs, (left_out, right_out, summed_ref) = refs[:2 * rounds], refs[2 * rounds:]
+    slab = slabs[0].shape[0]
+    for k in range(rounds):
+        for ref, other in ((slabs[k], False), (slabs[rounds + k], True)):
+            row = pl.multiple_of(partner(codes, k, other) * slab, slab)
+            summed_ref[pl.ds(row, slab), :] = ref[...]
+    half = left_ref.shape[0]
+    first = pl.multiple_of(lax.axis_index("replica") * half, 128)
+    present = block_of(owner_ref, lax.axis_index("shard")) >= 0
+    share = jnp.where(present, 0.01, 0.0).astype(jnp.float32)
+    summed = summed_ref[...]
+    left_term = lax.dot_general(
+        summed_ref[pl.ds(first, half), :], summed, (((1,), (1,)), ((), ())),
+        preferred_element_type=jnp.float32,
+    )
+    left_out[...] = (0.99 * left_ref[...].astype(jnp.float32) + share * left_term).astype(
+        left_out.dtype
+    )
+    right_term = lax.dot_general(
+        summed_ref[:, pl.ds(first, half)], summed, (((0,), (0,)), ((), ())),
+        preferred_element_type=jnp.float32,
+    )
+    right_out[...] = (0.99 * right_ref[...].astype(jnp.float32) + share * right_term).astype(
+        right_out.dtype
+    )
+
+
+def place_kernel(codes, early, owner_ref, *refs):
+    rounds = len(codes[0])
+    slabs = (refs[:rounds], refs[rounds:2 * rounds])
+    grafts = refs[2 * rounds:2 * rounds + 2 * len(early)]
+    out_ref, scaled_ref, sem = refs[2 * rounds + 2 * len(early):]
+    pending = []
+    for k in [k for k in range(rounds) if k not in early] + list(early):
+        for n in range(2):
+            block = block_of(owner_ref, partner(codes, k, n == 1))
+            source = slabs[n][k].at[0] if n == 0 else slabs[n][k]
+            if k in early:
+                m = 2 * early.index(k) + n
+                scaled = source[...].astype(jnp.float32) * grafts[m][0:1, 0:1]
+                scaled_ref[m] = scaled.astype(scaled_ref.dtype)
+                source = scaled_ref.at[m]
+            copy = pltpu.make_async_copy(
+                source, out_ref.at[jnp.maximum(block, 0)], sem.at[2 * k + n]
+            )
+
+            @pl.when(block >= 0)
+            def _(copy=copy):
+                copy.start()
+
+            pending.append((block, copy))
+    for block, copy in pending:
+
+        @pl.when(block >= 0)
+        def _(copy=copy):
+            copy.wait()
+
+
+def per_device_paired(gradients, block_owner, left_gram, right_gram, left_root, right_root):
+    owners = lax.axis_size("shard")
+    rounds = owners // 2
+    codes = codes_of(owners)
+    blocks, slab, width = gradients.shape[1:]
+    half_rows = left_gram.shape[1]
+    last = owners // 4 - 1
+    early = [0]
+    late = [k for k in range(rounds) if k not in early]
+    sooner = [(k, other) for k in range(rounds) if k != last for other in (False, True)]
+    slots = (sooner, [(last, False), (last, True)])
+
+    def other_core(x):
+        return lax.ppermute(x, "replica", [(0, 1), (1, 0)])
+
+    def trade(x, k):
+        pairs = [(s * 2 + r, (s ^ codes[r][k]) * 2 + r) for s in range(owners) for r in range(2)]
+        return lax.ppermute(x, ("shard", "replica"), pairs)
+
+    def shape(dims, dtype=jnp.bfloat16):
+        return jax.ShapeDtypeStruct(dims, dtype)
+
+    def call(kernel, out_shape, in_specs, *args, cost_estimate=LIGHT, **options):
+        return pl.pallas_call(
+            kernel, out_shape=out_shape, in_specs=in_specs, compiler_params=PARAMS,
+            cost_estimate=cost_estimate, **options
+        )(*args)
+
+    one = shape((8, 128), jnp.float32)
+    other_gradient = other_core(gradients[0])
+    fetched = call(
+        functools.partial(fetch_kernel, codes), shape((rounds, slab, width)), [SMEM, VMEM],
+        block_owner, gradients[0], out_specs=VMEM,
+    )
+    outgoing = call(
+        functools.partial(pick_kernel, codes), [shape((slab, width))] * rounds,
+        [SMEM, VMEM, VMEM], block_owner, fetched, other_gradient, out_specs=[VMEM] * rounds,
+    )
+    mine = [trade(outgoing[k], k) for k in range(rounds)]
+    other_right = other_core(right_root[0])
+    other_left = other_core(left_root[0])
+    left_sooner, left_last = call(
+        functools.partial(order_kernel, codes, slots),
+        [shape((half_rows, len(group) * slab)) for group in slots], [VMEM, VMEM],
+        left_root[0], other_left, out_specs=[VMEM, VMEM],
+        scratch_shapes=[pltpu.VMEM((half_rows, width), jnp.bfloat16)],
+    )
+    mine[last], left_sooner, left_last = lax.optimization_barrier(
+        (mine[last], left_sooner, left_last)
+    )
+    theirs = [other_core(x) for x in mine]
+    begun, begun_sq = call(
+        begin_kernel, [shape((half_rows, width), jnp.float32), one],
+        [VMEM] * (1 + len(sooner)), left_sooner,
+        *[(theirs if other else mine)[k] for k, other in sooner], out_specs=[VMEM, VMEM],
+        scratch_shapes=[pltpu.VMEM((len(sooner) * slab, width), jnp.bfloat16)],
+    )
+    slab_shape = shape((2, slab, width // 2))
+    both_sides, side_sq, grad_sq, *first = call(
+        functools.partial(finish_kernel, early),
+        [shape((2, half_rows, width // 2), jnp.float32), one, one] + [slab_shape] * len(early),
+        [VMEM] * 7, left_last, begun, begun_sq, right_root[0], other_right,
+        mine[last], theirs[last], out_specs=[VMEM] * (3 + len(early)),
+        scratch_shapes=[
+            pltpu.VMEM((2 * slab, width), jnp.bfloat16),
+            pltpu.VMEM((half_rows, width), jnp.bfloat16),
+        ],
+    )
+    returned = {k: trade(x, k) for k, x in zip(early, first)}
+    graft, *rest = call(
+        functools.partial(scale_kernel, late), [one] + [slab_shape] * len(late),
+        [VMEM] * 4, side_sq, other_core(side_sq), grad_sq, both_sides,
+        out_specs=[VMEM] * (1 + len(late)),
+    )
+    returned.update((k, trade(x, k)) for k, x in zip(late, rest))
+    grafts = []
+    for k in early:
+        graft, returned[k] = lax.optimization_barrier((graft, returned[k]))
+        came = trade(graft, k)
+        grafts += [came, other_core(came)]
+
+    left_new, right_new = call(
+        functools.partial(gram_kernel, codes),
+        [shape(left_gram.shape[1:]), shape(right_gram.shape[1:])],
+        [SMEM, VMEM, VMEM, ANY] + [VMEM] * (2 * rounds),
+        block_owner, left_gram[0], right_gram[0], grafts[0] if early else returned[0],
+        *mine, *theirs, out_specs=[VMEM, VMEM],
+        scratch_shapes=[pltpu.VMEM((width, width), jnp.bfloat16)],
+        cost_estimate=pl.CostEstimate(
+            flops=4 * half_rows * width * width, bytes_accessed=8 * half_rows * width,
+            transcendentals=0,
+        ),
+    )
+    left_new, right_new, returned[last] = lax.optimization_barrier(
+        (left_new, right_new, returned[last])
+    )
+    passed = [other_core(returned[k][1]) for k in range(rounds)]
+    update = call(
+        functools.partial(place_kernel, codes, early), shape((blocks, slab, width // 2)),
+        [SMEM] + [VMEM] * (2 * rounds + len(grafts)), block_owner,
+        *[returned[k] for k in range(rounds)], *passed, *grafts,
+        out_specs=ANY,
+        scratch_shapes=[
+            pltpu.VMEM((max(1, 2 * len(early)), slab, width // 2), jnp.bfloat16),
+            pltpu.SemaphoreType.DMA((2 * rounds,)),
+        ],
+    )
+    return (left_new[None], right_new[None], update)
+
+
 def solution(mesh):
+    owners = mesh.shape["shard"]
+    paired = mesh.shape["replica"] == 2 and owners in (4, 8, 16)
     return jax.shard_map(
-        per_device,
+        per_device_paired if paired else per_device,
         mesh=mesh,
         in_specs=(
             P("replica", "groups", "shard", None),

time: 117 us -> 49.8 us (0.43)
  blocking collectives: 39.2 us -> 0 us
  waiting for transfers between devices: 40.2 us -> 21.7 us
  between operations: 15.5 us -> 0.82 us
  starting transfers between devices: 5.84 us -> 17.3 us
  matrix products: 11.3 us -> 0 us
  Pallas kernels: 0 us -> 7.9 us
  other arithmetic: 3 us -> 0 us
    all_to_all x1 -> x0, blocking collectives: 36.1 us -> none  [per_device(): lax.all_to_all(outgoing.astype(jnp.bfloat16), 'shard', split_axis=0, conc...]
    ppermute x0 -> x22, waiting for transfers between devices: none -> 21.7 us  [the longest x9 19.4 us: trade(): return lax.ppermute(x, ('shard', 'replica'), pairs)]
    psum x1 -> x0, waiting for transfers between devices: 18.6 us -> none  [per_device(): lax.psum(arrived.astype(jnp.float32).astype(jnp.bfloat16), 'replica')]
    ppermute x0 -> x22, starting transfers between devices: none -> 17.3 us  [the longest x9 8.78 us: trade(): return lax.ppermute(x, ('shard', 'replica'), pairs)]
    all_to_all x1 -> x0, waiting for transfers between devices: 12.2 us -> none  [per_device(): lax.all_to_all(scaled, 'shard', split_axis=0, concat_axis=0, tiled=True)]
    dot_general x5 -> x0, matrix products: 11.3 us -> none  [the longest x1 3 us: per_device(): jnp.dot(left_root[0], summed_block, preferred_element_type=jnp.float32)]
    all_gather x1 -> x0, waiting for transfers between devices: 9.32 us -> none  [per_device(): left_side = lax.all_gather(partial_side, 'replica', axis=0, tiled=True)]
    pallas_call x0 -> x8, Pallas kernels: none -> 7.9 us  [call(): pl.pallas_call(kernel, out_shape=out_shape, in_specs=in_specs, compiler_p...]
  transfers between devices with their start and end apart: 3 -> 22, of which waited for: 3 -> 7; matrix products, arithmetic and copies ran while one was open for 5% -> 0% of each run, Pallas kernels for 0% -> 11%
where the time goes in v5:
time: 49.8 us; the launch traced here: 49.6 us
  waiting for transfers between devices  21.7 us (44%)
  starting transfers between devices  17.3 us (35%)
  Pallas kernels  7.9 us (16%)
  local copies, waits for them, and re-layouts  1.88 us (4%)
  between operations  0.82 us (2%)
    ppermute x9, waiting for transfers between devices, trade(): return lax.ppermute(x, ('shard', 'replica'), pairs)  19.4 us
    ppermute x9, starting transfers between devices, trade(): return lax.ppermute(x, ('shard', 'replica'), pairs)  8.78 us
    ppermute x13, starting transfers between devices, other_core(): return lax.ppermute(x, 'replica', [(0, 1), (1, 0)])  8.51 us
    pallas_call x8, Pallas kernels, call(): pl.pallas_call(kernel, out_shape=out_shape, in_specs=in_specs, compiler_p...  7.9 us
    ppermute x13, waiting for transfers between devices, other_core(): return lax.ppermute(x, 'replica', [(0, 1), (1, 0)])  2.36 us
    unnamed x14, local copies, waits for them, and re-layouts  1.84 us
  transfers between devices with their start and end apart: 22, of which 7 were waited for; matrix products, arithmetic and copies ran while one was open for 0% of the time, Pallas kernels for 11%

profile of v5, /device:TPU:0, one launch (start us, length us, event | category | flops | bytes accessed | tf_op | source)
XLA Modules:
  0.0 49.6 jit_solution(8134013126136734985)
XLA Ops:
  0.6 0.5 %collective-permute-start = (bf16[6,96,768]{2,1,0:T(8,128)(2,1)}, bf16[6,96,768]{2,1,0:T(8,128)(2,1)S(1)}, u32[]{:S(2)}, u32[]{:S(2)}) collective-permute-start(bf16[6,96,768]{2,1,0:T(8,128)(2,1)} %bitcast.15), channel_id=1, source_target_pairs={{0,1},{1,0},{2,3},{3,2},{4,5},{5,4},{6,7},{7,6},{8,9},{9,8},{10,11... | collective-permute-start | bytes 2654216 | tf_op jit(solution)/shard_map/ppermute | solution.py:245
  1.1 0.1 collective-permute-start.2
  1.2 0.4 collective-permute-start.9
  1.7 1.2 %copy-done = bf16[1,6,96,768]{3,2,1,0:T(8,128)(2,1)S(1)} copy-done((bf16[1,6,96,768]{3,2,1,0:T(8,128)(2,1)S(1)}, bf16[1,6,96,768]{3,2,1,0:T(8,128)(2,1)}, u32[]{:S(2)}) %copy-start) | copy-done | bytes 884760
  2.8 0.7 %copy-done.3 = s32[6]{0:T(128)S(1)} copy-done((s32[6]{0:T(128)S(1)}, s32[6]{0:T(128)}, u32[]{:S(2)}) %copy-start.3) | copy-done | bytes 48
  3.5 0.6 %shard_map.85.mine_ref = bf16[4,96,768]{2,1,0:T(8,128)(2,1)S(1)} custom-call(s32[6]{0:T(128)S(1)} %copy-done.3, bf16[6,96,768]{2,1,0:T(8,128)(2,1)S(1)} %bitcast.16), custom_call_target="tpu_custom_call" | custom-call | tf_op jit(solution)/shard_map/pallas_call | solution.py:255
  4.1 0.0 collective-permute-done.theirs_ref
  4.1 0.7 %shard_map.86 = (bf16[96,768]{1,0:T(8,128)(2,1)S(1)}, bf16[96,768]{1,0:T(8,128)(2,1)S(1)}, bf16[96,768]{1,0:T(8,128)(2,1)S(1)}, bf16[96,768]{1,0:T(8,128)(2,1)S(1)}) custom-call(s32[6]{0:T(128)S(1)} %copy-done.3, bf16[4,96,768]{2,1,0:T(8,128)(2,1)S(1)} %shard_map.85.mine_ref, bf16[6,96,768]{2,1,0:T(8,128)(2,1)S(1)} %collective-permute-done.theirs_ref), custom_call_target="tpu_custom_call" | custom-call | tf_op jit(solution)/shard_map/pallas_call | solution.py:255
  4.8 3.7 %collective-permute-start.3 = (bf16[96,768]{1,0:T(8,128)(2,1)S(1)}, bf16[96,768]{1,0:T(8,128)(2,1)S(1)}, u32[]{:S(2)}, u32[]{:S(2)}) collective-permute-start(bf16[96,768]{1,0:T(8,128)(2,1)S(1)} %get-tuple-element.34), channel_id=1, source_target_pairs={{0,8},{1,13},{2,10},{3,15},{4,12},{5,9},{6,14},{7,11},{8,0},{9,5},... | collective-permute-start | bytes 442376 | tf_op jit(solution)/shard_map/ppermute | solution.py:249
  8.5 1.5 %collective-permute-start.5 = (bf16[96,768]{1,0:T(8,128)(2,1)S(1)}, bf16[96,768]{1,0:T(8,128)(2,1)S(1)}, u32[]{:S(2)}, u32[]{:S(2)}) collective-permute-start(bf16[96,768]{1,0:T(8,128)(2,1)S(1)} %get-tuple-element.35), channel_id=1, source_target_pairs={{0,2},{1,5},{2,0},{3,7},{4,6},{5,1},{6,4},{7,3},{8,10},{9,13},{10,... | collective-permute-start | bytes 442376 | tf_op jit(solution)/shard_map/ppermute | solution.py:249
  10.0 0.7 %collective-permute-start.7 = (bf16[96,768]{1,0:T(8,128)(2,1)S(1)}, bf16[96,768]{1,0:T(8,128)(2,1)S(1)}, u32[]{:S(2)}, u32[]{:S(2)}) collective-permute-start(bf16[96,768]{1,0:T(8,128)(2,1)S(1)} %get-tuple-element.36), channel_id=1, source_target_pairs={{0,0},{1,7},{2,2},{3,5},{4,4},{5,3},{6,6},{7,1},{8,8},{9,15},{10,1... | collective-permute-start | bytes 442376 | tf_op jit(solution)/shard_map/ppermute | solution.py:249
  10.7 0.0 collective-permute-done.2.other_ref
  10.7 0.0 copy-start.2
  10.7 0.1 collective-permute-start.1
  10.8 0.8 %shard_map.87 = (bf16[384,576]{1,0:T(8,128)(2,1)S(1)}, bf16[384,192]{1,0:T(8,128)(2,1)S(1)}) custom-call(bf16[384,768]{1,0:T(8,128)(2,1)S(1)} %bitcast.18, bf16[384,768]{1,0:T(8,128)(2,1)S(1)} %collective-permute-done.2.other_ref), custom_call_target="tpu_custom_call" | custom-call | tf_op jit(solution)/shard_map/pallas_call | solution.py:255
  11.7 4.7 %collective-permute-done.3.refs_0_ = bf16[96,768]{1,0:T(8,128)(2,1)S(1)} collective-permute-done((bf16[96,768]{1,0:T(8,128)(2,1)S(1)}, bf16[96,768]{1,0:T(8,128)(2,1)S(1)}, u32[]{:S(2)}, u32[]{:S(2)}) %collective-permute-start.3) | collective-permute-done | bytes 147488 | tf_op jit(solution)/shard_map/ppermute | solution.py:249
  16.4 0.0 collective-permute-start.4
  16.4 0.0 collective-permute-done.5.refs_2_
  16.4 0.5 %collective-permute-start.6 = (bf16[96,768]{1,0:T(8,128)(2,1)S(1)}, bf16[96,768]{1,0:T(8,128)(2,1)S(1)}, u32[]{:S(2)}, u32[]{:S(2)}) collective-permute-start(bf16[96,768]{1,0:T(8,128)(2,1)S(1)} %collective-permute-done.5.refs_2_), channel_id=1, source_target_pairs={{0,1},{1,0},{2,3},{3,2},{4,5},{5,4},{6,7},{7,6},{8,9},{9,8},{10,11... | collective-permute-start | bytes 442376 | tf_op jit(solution)/shard_map/ppermute | solution.py:245
  16.9 0.0 collective-permute-done.7.refs_4_.refs_3_
  16.9 1.9 %collective-permute-start.8 = (bf16[96,768]{1,0:T(8,128)(2,1)S(1)}, bf16[96,768]{1,0:T(8,128)(2,1)S(1)}, u32[]{:S(2)}, u32[]{:S(2)}) collective-permute-start(bf16[96,768]{1,0:T(8,128)(2,1)S(1)} %collective-permute-done.7.refs_4_.refs_3_), channel_id=1, source_target_pairs={{0,1},{1,0},{2,3},{3,2},{4,5},{5,4},{6,7},{7,6},{8,9},{9,8},{10,11... | collective-permute-start | bytes 442376 | tf_op jit(solution)/shard_map/ppermute | solution.py:245
  18.8 4.6 %collective-permute-done.1.refs_0_.refs_1_ = bf16[96,768]{1,0:T(8,128)(2,1)S(1)} collective-permute-done((bf16[96,768]{1,0:T(8,128)(2,1)S(1)}, bf16[96,768]{1,0:T(8,128)(2,1)S(1)}, u32[]{:S(2)}, u32[]{:S(2)}) %collective-permute-start.1) | collective-permute-done | bytes 147488 | tf_op jit(solution)/shard_map/ppermute | solution.py:249
  23.4 0.0 collective-permute-start.10
  23.5 0.0 collective-permute-done.4.refs_1_.refs_4_
  23.5 0.0 collective-permute-done.6.refs_3_.refs_6_
  23.5 0.6 %shard_map.88 = (f32[384,768]{1,0:T(8,128)S(1)}, f32[8,128]{1,0:T(8,128)S(1)}) custom-call(bf16[384,576]{1,0:T(8,128)(2,1)S(1)} %get-tuple-element.33.left_ref, bf16[96,768]{1,0:T(8,128)(2,1)S(1)} %collective-permute-done.3.refs_0_, bf16[96,768]{1,0:T(8,128)(2,1)S(1)} %collective-permute-done.4.refs_1_.refs_4_, ...), custom_call_target="tpu_custom_call" | custom-call | tf_op jit(solution)/shard_map/pallas_call | solution.py:255
  24.1 0.7 %collective-permute-done.10.refs_1_.refs_5_ = bf16[96,768]{1,0:T(8,128)(2,1)S(1)} collective-permute-done((bf16[96,768]{1,0:T(8,128)(2,1)S(1)}, bf16[96,768]{1,0:T(8,128)(2,1)S(1)}, u32[]{:S(2)}, u32[]{:S(2)}) %collective-permute-start.10) | collective-permute-done | bytes 147488 | tf_op jit(solution)/shard_map/ppermute | solution.py:245
  24.8 1.0 %shard_map.89 = (f32[2,384,384]{2,1,0:T(8,128)S(1)}, f32[8,128]{1,0:T(8,128)S(1)}, f32[8,128]{1,0:T(8,128)S(1)}, bf16[2,96,384]{2,1,0:T(8,128)(2,1)S(1)}) custom-call(bf16[384,192]{1,0:T(8,128)(2,1)S(1)} %get-tuple-element.32.left_ref, f32[384,768]{1,0:T(8,128)S(1)} %get-tuple-element.37.total_ref, f32[8,128]{1,0:T(8,128)S(1)} %get-tuple-element.38.begun_sq_ref, ...), custom_call_target="tpu_custom_call" | custom-call | tf_op jit(solution)/shard_map/pallas_call | solution.py:255
  25.8 0.0 collective-permute-start.12
  25.9 2.7 %collective-permute-start.11 = (f32[8,128]{1,0:T(8,128)S(1)}, f32[8,128]{1,0:T(8,128)S(1)}, u32[]{:S(2)}, u32[]{:S(2)}) collective-permute-start(f32[8,128]{1,0:T(8,128)S(1)} %get-tuple-element.40.mine_sq_ref), channel_id=1, source_target_pairs={{0,1},{1,0},{2,3},{3,2},{4,5},{5,4},{6,7},{7,6},{8,9},{9,8},{10,11... | collective-permute-start | bytes 12296 | tf_op jit(solution)/shard_map/ppermute | solution.py:245
  28.6 0.8 %collective-permute-done.11.theirs_sq_ref = f32[8,128]{1,0:T(8,128)S(1)} collective-permute-done((f32[8,128]{1,0:T(8,128)S(1)}, f32[8,128]{1,0:T(8,128)S(1)}, u32[]{:S(2)}, u32[]{:S(2)}) %collective-permute-start.11) | collective-permute-done | bytes 4128 | tf_op jit(solution)/shard_map/ppermute | solution.py:245
  29.4 0.1 shard_map.90
  29.5 0.6 %collective-permute-start.14 = (bf16[2,96,384]{2,1,0:T(8,128)(2,1)S(1)}, bf16[2,96,384]{2,1,0:T(8,128)(2,1)S(1)}, u32[]{:S(2)}, u32[]{:S(2)}) collective-permute-start(bf16[2,96,384]{2,1,0:T(8,128)(2,1)S(1)} %get-tuple-element.48), channel_id=1, source_target_pairs={{0,10},{1,15},{2,8},{3,13},{4,14},{5,11},{6,12},{7,9},{8,2},{9,7},... | collective-permute-start | bytes 442376 | tf_op jit(solution)/shard_map/ppermute | solution.py:249
  30.1 1.5 %collective-permute-start.15 = (bf16[2,96,384]{2,1,0:T(8,128)(2,1)S(1)}, bf16[2,96,384]{2,1,0:T(8,128)(2,1)S(1)}, u32[]{:S(2)}, u32[]{:S(2)}) collective-permute-start(bf16[2,96,384]{2,1,0:T(8,128)(2,1)S(1)} %get-tuple-element.53), channel_id=1, source_target_pairs={{0,2},{1,5},{2,0},{3,7},{4,6},{5,1},{6,4},{7,3},{8,10},{9,13},{10,... | collective-permute-start | bytes 442376 | tf_op jit(solution)/shard_map/ppermute | solution.py:249
  31.6 0.7 %collective-permute-start.16 = (bf16[2,96,384]{2,1,0:T(8,128)(2,1)S(1)}, bf16[2,96,384]{2,1,0:T(8,128)(2,1)S(1)}, u32[]{:S(2)}, u32[]{:S(2)}) collective-permute-start(bf16[2,96,384]{2,1,0:T(8,128)(2,1)S(1)} %get-tuple-element.54), channel_id=1, source_target_pairs={{0,0},{1,7},{2,2},{3,5},{4,4},{5,3},{6,6},{7,1},{8,8},{9,15},{10,1... | collective-permute-start | bytes 442376 | tf_op jit(solution)/shard_map/ppermute | solution.py:249
  32.3 7.4 %collective-permute-done.12.refs_0_ = bf16[2,96,384]{2,1,0:T(8,128)(2,1)S(1)} collective-permute-done((bf16[2,96,384]{2,1,0:T(8,128)(2,1)S(1)}, bf16[2,96,384]{2,1,0:T(8,128)(2,1)S(1)}, u32[]{:S(2)}, u32[]{:S(2)}) %collective-permute-start.12) | collective-permute-done | bytes 147488 | tf_op jit(solution)/shard_map/ppermute | solution.py:249
  39.7 0.1 collective-permute-start.17
  39.8 0.6 %collective-permute-start.19 = (bf16[96,384]{1,0:T(8,128)(2,1)S(1)}, bf16[96,384]{1,0:T(8,128)(2,1)S(1)}, u32[]{:S(2)}, u32[]{:S(2)}) collective-permute-start(bf16[96,384]{1,0:T(8,128)(2,1)S(1)} %slice_bitcast_fusion.1), channel_id=1, source_target_pairs={{0,1},{1,0},{2,3},{3,2},{4,5},{5,4},{6,7},{7,6},{8,9},{9,8},{10,11... | collective-permute-start | bytes 221192 | tf_op jit(solution)/shard_map/ppermute | solution.py:245
  40.3 1.2 %collective-permute-start.20 = (bf16[96,384]{1,0:T(8,128)(2,1)S(1)}, bf16[96,384]{1,0:T(8,128)(2,1)S(1)}, u32[]{:S(2)}, u32[]{:S(2)}) collective-permute-start(bf16[96,384]{1,0:T(8,128)(2,1)S(1)} %slice_bitcast_fusion), channel_id=1, source_target_pairs={{0,1},{1,0},{2,3},{3,2},{4,5},{5,4},{6,7},{7,6},{8,9},{9,8},{10,11... | collective-permute-start | bytes 221192 | tf_op jit(solution)/shard_map/ppermute | solution.py:245
  41.5 2.6 %collective-permute-done.13.after_ref.refs_8_ = f32[8,128]{1,0:T(8,128)S(1)} collective-permute-done((f32[8,128]{1,0:T(8,128)S(1)}, f32[8,128]{1,0:T(8,128)S(1)}, u32[]{:S(2)}, u32[]{:S(2)}) %collective-permute-start.13) | collective-permute-done | bytes 4128 | tf_op jit(solution)/shard_map/ppermute | solution.py:249
  44.2 2.6 %shard_map.91 = (bf16[384,768]{1,0:T(8,128)(2,1)}, bf16[384,768]{1,0:T(8,128)(2,1)}) custom-call(s32[6]{0:T(128)S(1)} %copy-done.4, bf16[384,768]{1,0:T(8,128)(2,1)S(1)} %bitcast.21, bf16[384,768]{1,0:T(8,128)(2,1)S(1)} %bitcast.22, f32[8,128]{1,0:T(8,128)S(1)} %collective-permute-done.13.after_ref.refs_8_, ...), custom_call_target="tpu_custom_call" | custom-call | flops 905969664 | bytes 2359296 | tf_op jit(solution)/shard_map/pallas_call | solution.py:255
  46.8 0.0 collective-permute-done.14.refs_1_
  46.8 0.1 collective-permute-start.18
  46.9 0.5 %collective-permute-start.21 = (f32[8,128]{1,0:T(8,128)S(1)}, f32[8,128]{1,0:T(8,128)S(1)}, u32[]{:S(2)}, u32[]{:S(2)}) collective-permute-start(f32[8,128]{1,0:T(8,128)S(1)} %collective-permute-done.13.after_ref.refs_8_), channel_id=1, source_target_pairs={{0,1},{1,0},{2,3},{3,2},{4,5},{5,4},{6,7},{7,6},{8,9},{9,8},{10,11... | collective-permute-start | bytes 12296 | tf_op jit(solution)/shard_map/ppermute | solution.py:245
  47.4 0.8 %collective-permute-done.21.refs_9_ = f32[8,128]{1,0:T(8,128)S(1)} collective-permute-done((f32[8,128]{1,0:T(8,128)S(1)}, f32[8,128]{1,0:T(8,128)S(1)}, u32[]{:S(2)}, u32[]{:S(2)}) %collective-permute-start.21) | collective-permute-done | bytes 4128 | tf_op jit(solution)/shard_map/ppermute | solution.py:245
  48.2 0.0 collective-permute-done.20.refs_7_
  48.2 0.0 collective-permute-done.18.refs_5_
  48.2 1.4 %shard_map.92 = bf16[6,96,384]{2,1,0:T(8,128)(2,1)} custom-call(s32[6]{0:T(128)S(1)} %copy-done.4, bf16[2,96,384]{2,1,0:T(8,128)(2,1)S(1)} %collective-permute-done.12.refs_0_, bf16[2,96,384]{2,1,0:T(8,128)(2,1)S(1)} %collective-permute-done.14.refs_1_, bf16[2,96,384]{2,1,0:T(8,128)(2,1)S(1)} %collective-permute-done.15.refs_2_, ...), custom_call_target="tpu_custom_call" | custom-call | tf_op jit(solution)/shard_map/pallas_call | solution.py:255
  (22 shorter events, 0.1 us)
Async XLA Ops:
  0.6 3.5 %collective-permute-start = (bf16[6,96,768]{2,1,0:T(8,128)(2,1)}, bf16[6,96,768]{2,1,0:T(8,128)(2,1)S(1)}, u32[]{:S(2)}, u32[]{:S(2)}) collective-permute-start(bf16[6,96,768]{2,1,0:T(8,128)(2,1)} %bitcast.15), channel_id=1, source_target_pairs={{0,1},{1,0},{2,3},{3,2},{4,5},{5,4},{6,7},{7,6},{8,9},{9,8},{10,11... | collective-permute-start | bytes 2654216 | tf_op jit(solution)/shard_map/ppermute | solution.py:245
  1.1 9.5 %collective-permute-start.2 = (bf16[384,768]{1,0:T(8,128)(2,1)}, bf16[384,768]{1,0:T(8,128)(2,1)S(1)}, u32[]{:S(2)}, u32[]{:S(2)}) collective-permute-start(bf16[384,768]{1,0:T(8,128)(2,1)} %bitcast.17), channel_id=1, source_target_pairs={{0,1},{1,0},{2,3},{3,2},{4,5},{5,4},{6,7},{7,6},{8,9},{9,8},{10,11... | collective-permute-start | bytes 1769480 | tf_op jit(solution)/shard_map/ppermute | solution.py:245
  1.2 22.9 %collective-permute-start.9 = (bf16[768,384]{1,0:T(8,128)(2,1)}, bf16[768,384]{1,0:T(8,128)(2,1)S(1)}, u32[]{:S(2)}, u32[]{:S(2)}) collective-permute-start(bf16[768,384]{1,0:T(8,128)(2,1)} %bitcast.19), channel_id=1, source_target_pairs={{0,1},{1,0},{2,3},{3,2},{4,5},{5,4},{6,7},{7,6},{8,9},{9,8},{10,11... | collective-permute-start | bytes 1769480 | tf_op jit(solution)/shard_map/ppermute | solution.py:245
  1.7 1.2 %copy-start = (bf16[1,6,96,768]{3,2,1,0:T(8,128)(2,1)S(1)}, bf16[1,6,96,768]{3,2,1,0:T(8,128)(2,1)}, u32[]{:S(2)}) copy-start(bf16[1,6,96,768]{3,2,1,0:T(8,128)(2,1)} %param.6) | copy-start | bytes 2654212
  2.8 0.7 %copy-start.3 = (s32[6]{0:T(128)S(1)}, s32[6]{0:T(128)}, u32[]{:S(2)}) copy-start(s32[6]{0:T(128)} %owner_ref.7) | copy-start | bytes 76
  3.5 7.3 %copy-start.1 = (bf16[1,384,768]{2,1,0:T(8,128)(2,1)S(1)}, bf16[1,384,768]{2,1,0:T(8,128)(2,1)}, u32[]{:S(2)}) copy-start(bf16[1,384,768]{2,1,0:T(8,128)(2,1)} %param.10) | copy-start | bytes 1769476
  4.8 11.6 %collective-permute-start.3 = (bf16[96,768]{1,0:T(8,128)(2,1)S(1)}, bf16[96,768]{1,0:T(8,128)(2,1)S(1)}, u32[]{:S(2)}, u32[]{:S(2)}) collective-permute-start(bf16[96,768]{1,0:T(8,128)(2,1)S(1)} %get-tuple-element.34), channel_id=1, source_target_pairs={{0,8},{1,13},{2,10},{3,15},{4,12},{5,9},{6,14},{7,11},{8,0},{9,5},... | collective-permute-start | bytes 442376 | tf_op jit(solution)/shard_map/ppermute | solution.py:249
  8.5 7.9 %collective-permute-start.5 = (bf16[96,768]{1,0:T(8,128)(2,1)S(1)}, bf16[96,768]{1,0:T(8,128)(2,1)S(1)}, u32[]{:S(2)}, u32[]{:S(2)}) collective-permute-start(bf16[96,768]{1,0:T(8,128)(2,1)S(1)} %get-tuple-element.35), channel_id=1, source_target_pairs={{0,2},{1,5},{2,0},{3,7},{4,6},{5,1},{6,4},{7,3},{8,10},{9,13},{10,... | collective-permute-start | bytes 442376 | tf_op jit(solution)/shard_map/ppermute | solution.py:249
  10.0 6.9 %collective-permute-start.7 = (bf16[96,768]{1,0:T(8,128)(2,1)S(1)}, bf16[96,768]{1,0:T(8,128)(2,1)S(1)}, u32[]{:S(2)}, u32[]{:S(2)}) collective-permute-start(bf16[96,768]{1,0:T(8,128)(2,1)S(1)} %get-tuple-element.36), channel_id=1, source_target_pairs={{0,0},{1,7},{2,2},{3,5},{4,4},{5,3},{6,6},{7,1},{8,8},{9,15},{10,1... | collective-permute-start | bytes 442376 | tf_op jit(solution)/shard_map/ppermute | solution.py:249
  10.7 14.1 %copy-start.2 = (bf16[1,768,384]{2,1,0:T(8,128)(2,1)S(1)}, bf16[1,768,384]{2,1,0:T(8,128)(2,1)}, u32[]{:S(2)}) copy-start(bf16[1,768,384]{2,1,0:T(8,128)(2,1)} %param.11) | copy-start | bytes 1769476
  10.7 12.7 %collective-permute-start.1 = (bf16[96,768]{1,0:T(8,128)(2,1)S(1)}, bf16[96,768]{1,0:T(8,128)(2,1)S(1)}, u32[]{:S(2)}, u32[]{:S(2)}) collective-permute-start(bf16[96,768]{1,0:T(8,128)(2,1)S(1)} %get-tuple-element.29), channel_id=1, source_target_pairs={{0,10},{1,15},{2,8},{3,13},{4,14},{5,11},{6,12},{7,9},{8,2},{9,7},... | collective-permute-start | bytes 442376 | tf_op jit(solution)/shard_map/ppermute | solution.py:249
  16.4 7.1 %collective-permute-start.4 = (bf16[96,768]{1,0:T(8,128)(2,1)S(1)}, bf16[96,768]{1,0:T(8,128)(2,1)S(1)}, u32[]{:S(2)}, u32[]{:S(2)}) collective-permute-start(bf16[96,768]{1,0:T(8,128)(2,1)S(1)} %collective-permute-done.3.refs_0_), channel_id=1, source_target_pairs={{0,1},{1,0},{2,3},{3,2},{4,5},{5,4},{6,7},{7,6},{8,9},{9,8},{10,11... | collective-permute-start | bytes 442376 | tf_op jit(solution)/shard_map/ppermute | solution.py:245
  16.4 7.0 %collective-permute-start.6 = (bf16[96,768]{1,0:T(8,128)(2,1)S(1)}, bf16[96,768]{1,0:T(8,128)(2,1)S(1)}, u32[]{:S(2)}, u32[]{:S(2)}) collective-permute-start(bf16[96,768]{1,0:T(8,128)(2,1)S(1)} %collective-permute-done.5.refs_2_), channel_id=1, source_target_pairs={{0,1},{1,0},{2,3},{3,2},{4,5},{5,4},{6,7},{7,6},{8,9},{9,8},{10,11... | collective-permute-start | bytes 442376 | tf_op jit(solution)/shard_map/ppermute | solution.py:245
  16.9 6.5 %collective-permute-start.8 = (bf16[96,768]{1,0:T(8,128)(2,1)S(1)}, bf16[96,768]{1,0:T(8,128)(2,1)S(1)}, u32[]{:S(2)}, u32[]{:S(2)}) collective-permute-start(bf16[96,768]{1,0:T(8,128)(2,1)S(1)} %collective-permute-done.7.refs_4_.refs_3_), channel_id=1, source_target_pairs={{0,1},{1,0},{2,3},{3,2},{4,5},{5,4},{6,7},{7,6},{8,9},{9,8},{10,11... | collective-permute-start | bytes 442376 | tf_op jit(solution)/shard_map/ppermute | solution.py:245
  23.4 1.4 %collective-permute-start.10 = (bf16[96,768]{1,0:T(8,128)(2,1)S(1)}, bf16[96,768]{1,0:T(8,128)(2,1)S(1)}, u32[]{:S(2)}, u32[]{:S(2)}) collective-permute-start(bf16[96,768]{1,0:T(8,128)(2,1)S(1)} %collective-permute-done.1.refs_0_.refs_1_), channel_id=1, source_target_pairs={{0,1},{1,0},{2,3},{3,2},{4,5},{5,4},{6,7},{7,6},{8,9},{9,8},{10,11... | collective-permute-start | bytes 442376 | tf_op jit(solution)/shard_map/ppermute | solution.py:245
  25.8 18.3 %copy-start.4 = (s32[6]{0:T(128)S(1)}, s32[6]{0:T(128)}, u32[]{:S(2)}) copy-start(s32[6]{0:T(128)} %owner_ref.7) | copy-start | bytes 76
  25.8 18.3 %copy-start.5 = (bf16[1,384,768]{2,1,0:T(8,128)(2,1)S(1)}, bf16[1,384,768]{2,1,0:T(8,128)(2,1)}, u32[]{:S(2)}) copy-start(bf16[1,384,768]{2,1,0:T(8,128)(2,1)} %param.8) | copy-start | bytes 1769476
  25.8 18.3 %copy-start.6 = (bf16[1,384,768]{2,1,0:T(8,128)(2,1)S(1)}, bf16[1,384,768]{2,1,0:T(8,128)(2,1)}, u32[]{:S(2)}) copy-start(bf16[1,384,768]{2,1,0:T(8,128)(2,1)} %param.9) | copy-start | bytes 1769476
  25.8 13.8 %collective-permute-start.12 = (bf16[2,96,384]{2,1,0:T(8,128)(2,1)S(1)}, bf16[2,96,384]{2,1,0:T(8,128)(2,1)S(1)}, u32[]{:S(2)}, u32[]{:S(2)}) collective-permute-start(bf16[2,96,384]{2,1,0:T(8,128)(2,1)S(1)} %get-tuple-element.44), channel_id=1, source_target_pairs={{0,8},{1,13},{2,10},{3,15},{4,12},{5,9},{6,14},{7,11},{8,0},{9,5},... | collective-permute-start | bytes 442376 | tf_op jit(solution)/shard_map/ppermute | solution.py:249
  25.9 3.5 %collective-permute-start.11 = (f32[8,128]{1,0:T(8,128)S(1)}, f32[8,128]{1,0:T(8,128)S(1)}, u32[]{:S(2)}, u32[]{:S(2)}) collective-permute-start(f32[8,128]{1,0:T(8,128)S(1)} %get-tuple-element.40.mine_sq_ref), channel_id=1, source_target_pairs={{0,1},{1,0},{2,3},{3,2},{4,5},{5,4},{6,7},{7,6},{8,9},{9,8},{10,11... | collective-permute-start | bytes 12296 | tf_op jit(solution)/shard_map/ppermute | solution.py:245
  29.5 17.2 %collective-permute-start.14 = (bf16[2,96,384]{2,1,0:T(8,128)(2,1)S(1)}, bf16[2,96,384]{2,1,0:T(8,128)(2,1)S(1)}, u32[]{:S(2)}, u32[]{:S(2)}) collective-permute-start(bf16[2,96,384]{2,1,0:T(8,128)(2,1)S(1)} %get-tuple-element.48), channel_id=1, source_target_pairs={{0,10},{1,15},{2,8},{3,13},{4,14},{5,11},{6,12},{7,9},{8,2},{9,7},... | collective-permute-start | bytes 442376 | tf_op jit(solution)/shard_map/ppermute | solution.py:249
  30.1 9.6 %collective-permute-start.15 = (bf16[2,96,384]{2,1,0:T(8,128)(2,1)S(1)}, bf16[2,96,384]{2,1,0:T(8,128)(2,1)S(1)}, u32[]{:S(2)}, u32[]{:S(2)}) collective-permute-start(bf16[2,96,384]{2,1,0:T(8,128)(2,1)S(1)} %get-tuple-element.53), channel_id=1, source_target_pairs={{0,2},{1,5},{2,0},{3,7},{4,6},{5,1},{6,4},{7,3},{8,10},{9,13},{10,... | collective-permute-start | bytes 442376 | tf_op jit(solution)/shard_map/ppermute | solution.py:249
  31.6 8.7 %collective-permute-start.16 = (bf16[2,96,384]{2,1,0:T(8,128)(2,1)S(1)}, bf16[2,96,384]{2,1,0:T(8,128)(2,1)S(1)}, u32[]{:S(2)}, u32[]{:S(2)}) collective-permute-start(bf16[2,96,384]{2,1,0:T(8,128)(2,1)S(1)} %get-tuple-element.54), channel_id=1, source_target_pairs={{0,0},{1,7},{2,2},{3,5},{4,4},{5,3},{6,6},{7,1},{8,8},{9,15},{10,1... | collective-permute-start | bytes 442376 | tf_op jit(solution)/shard_map/ppermute | solution.py:249
  39.7 4.5 %collective-permute-start.13 = (f32[8,128]{1,0:T(8,128)S(1)}, f32[8,128]{1,0:T(8,128)S(1)}, u32[]{:S(2)}, u32[]{:S(2)}) collective-permute-start(f32[8,128]{1,0:T(8,128)S(1)} %get-tuple-element.45), channel_id=1, source_target_pairs={{0,8},{1,13},{2,10},{3,15},{4,12},{5,9},{6,14},{7,11},{8,0},{9,5},... | collective-permute-start | bytes 12296 | tf_op jit(solution)/shard_map/ppermute | solution.py:249
  39.7 8.5 %collective-permute-start.17 = (bf16[96,384]{1,0:T(8,128)(2,1)S(1)}, bf16[96,384]{1,0:T(8,128)(2,1)S(1)}, u32[]{:S(2)}, u32[]{:S(2)}) collective-permute-start(bf16[96,384]{1,0:T(8,128)(2,1)S(1)} %slice_bitcast_fusion.3), channel_id=1, source_target_pairs={{0,1},{1,0},{2,3},{3,2},{4,5},{5,4},{6,7},{7,6},{8,9},{9,8},{10,11... | collective-permute-start | bytes 221192 | tf_op jit(solution)/shard_map/ppermute | solution.py:245
  39.8 8.4 %collective-permute-start.19 = (bf16[96,384]{1,0:T(8,128)(2,1)S(1)}, bf16[96,384]{1,0:T(8,128)(2,1)S(1)}, u32[]{:S(2)}, u32[]{:S(2)}) collective-permute-start(bf16[96,384]{1,0:T(8,128)(2,1)S(1)} %slice_bitcast_fusion.1), channel_id=1, source_target_pairs={{0,1},{1,0},{2,3},{3,2},{4,5},{5,4},{6,7},{7,6},{8,9},{9,8},{10,11... | collective-permute-start | bytes 221192 | tf_op jit(solution)/shard_map/ppermute | solution.py:245
  40.3 7.8 %collective-permute-start.20 = (bf16[96,384]{1,0:T(8,128)(2,1)S(1)}, bf16[96,384]{1,0:T(8,128)(2,1)S(1)}, u32[]{:S(2)}, u32[]{:S(2)}) collective-permute-start(bf16[96,384]{1,0:T(8,128)(2,1)S(1)} %slice_bitcast_fusion), channel_id=1, source_target_pairs={{0,1},{1,0},{2,3},{3,2},{4,5},{5,4},{6,7},{7,6},{8,9},{9,8},{10,11... | collective-permute-start | bytes 221192 | tf_op jit(solution)/shard_map/ppermute | solution.py:245
  46.8 1.4 %collective-permute-start.18 = (bf16[96,384]{1,0:T(8,128)(2,1)S(1)}, bf16[96,384]{1,0:T(8,128)(2,1)S(1)}, u32[]{:S(2)}, u32[]{:S(2)}) collective-permute-start(bf16[96,384]{1,0:T(8,128)(2,1)S(1)} %slice_bitcast_fusion.2), channel_id=1, source_target_pairs={{0,1},{1,0},{2,3},{3,2},{4,5},{5,4},{6,7},{7,6},{8,9},{9,8},{10,11... | collective-permute-start | bytes 221192 | tf_op jit(solution)/shard_map/ppermute | solution.py:245
  46.9 1.3 %collective-permute-start.21 = (f32[8,128]{1,0:T(8,128)S(1)}, f32[8,128]{1,0:T(8,128)S(1)}, u32[]{:S(2)}, u32[]{:S(2)}) collective-permute-start(f32[8,128]{1,0:T(8,128)S(1)} %collective-permute-done.13.after_ref.refs_8_), channel_id=1, source_target_pairs={{0,1},{1,0},{2,3},{3,2},{4,5},{5,4},{6,7},{7,6},{8,9},{9,8},{10,11... | collective-permute-start | bytes 12296 | tf_op jit(solution)/shard_map/ppermute | solution.py:245

commit v6 on v5

--- a/solution.py
+++ b/solution.py
@@ -236,10 +236,9 @@
     blocks, slab, width = gradients.shape[1:]
     half_rows = left_gram.shape[1]
     last = owners // 4 - 1
-    early = [0]
+    early = []
     late = [k for k in range(rounds) if k not in early]
-    sooner = [(k, other) for k in range(rounds) if k != last for other in (False, True)]
-    slots = (sooner, [(last, False), (last, True)])
+    slots = [[(k, other) for k in range(rounds)] for other in (False, True)]
 
     def other_core(x):
         return lax.ppermute(x, "replica", [(0, 1), (1, 0)])
@@ -270,32 +269,26 @@
     mine = [trade(outgoing[k], k) for k in range(rounds)]
     other_right = other_core(right_root[0])
     other_left = other_core(left_root[0])
-    left_sooner, left_last = call(
+    left_mine, left_theirs = call(
         functools.partial(order_kernel, codes, slots),
         [shape((half_rows, len(group) * slab)) for group in slots], [VMEM, VMEM],
         left_root[0], other_left, out_specs=[VMEM, VMEM],
         scratch_shapes=[pltpu.VMEM((half_rows, width), jnp.bfloat16)],
     )
-    mine[last], left_sooner, left_last = lax.optimization_barrier(
-        (mine[last], left_sooner, left_last)
-    )
+    left_mine, left_theirs, *mine = lax.optimization_barrier((left_mine, left_theirs, *mine))
     theirs = [other_core(x) for x in mine]
     begun, begun_sq = call(
         begin_kernel, [shape((half_rows, width), jnp.float32), one],
-        [VMEM] * (1 + len(sooner)), left_sooner,
-        *[(theirs if other else mine)[k] for k, other in sooner], out_specs=[VMEM, VMEM],
-        scratch_shapes=[pltpu.VMEM((len(sooner) * slab, width), jnp.bfloat16)],
+        [VMEM] * (1 + rounds), left_mine, *mine, out_specs=[VMEM, VMEM],
+        scratch_shapes=[pltpu.VMEM((half_rows, width), jnp.bfloat16)],
     )
     slab_shape = shape((2, slab, width // 2))
     both_sides, side_sq, grad_sq, *first = call(
         functools.partial(finish_kernel, early),
         [shape((2, half_rows, width // 2), jnp.float32), one, one] + [slab_shape] * len(early),
-        [VMEM] * 7, left_last, begun, begun_sq, right_root[0], other_right,
-        mine[last], theirs[last], out_specs=[VMEM] * (3 + len(early)),
-        scratch_shapes=[
-            pltpu.VMEM((2 * slab, width), jnp.bfloat16),
-            pltpu.VMEM((half_rows, width), jnp.bfloat16),
-        ],
+        [VMEM] * (5 + rounds), left_theirs, begun, begun_sq, right_root[0], other_right,
+        *theirs, out_specs=[VMEM] * (3 + len(early)),
+        scratch_shapes=[pltpu.VMEM((half_rows, width), jnp.bfloat16)] * 2,
     )
     returned = {k: trade(x, k) for k, x in zip(early, first)}
     graft, *rest = call(
@@ -306,7 +299,7 @@
     returned.update((k, trade(x, k)) for k, x in zip(late, rest))
     grafts = []
     for k in early:
-        graft, returned[k] = lax.optimization_barrier((graft, returned[k]))
+        graft, returned[last + 1] = lax.optimization_barrier((graft, returned[last + 1]))
         came = trade(graft, k)
         grafts += [came, other_core(came)]
 
@@ -314,7 +307,7 @@
         functools.partial(gram_kernel, codes),
         [shape(left_gram.shape[1:]), shape(right_gram.shape[1:])],
         [SMEM, VMEM, VMEM, ANY] + [VMEM] * (2 * rounds),
-        block_owner, left_gram[0], right_gram[0], grafts[0] if early else returned[0],
+        block_owner, left_gram[0], right_gram[0], returned[0],
         *mine, *theirs, out_specs=[VMEM, VMEM],
         scratch_shapes=[pltpu.VMEM((width, width), jnp.bfloat16)],
         cost_estimate=pl.CostEstimate(
@@ -322,9 +315,10 @@
             transcendentals=0,
         ),
     )
-    left_new, right_new, returned[last] = lax.optimization_barrier(
-        (left_new, right_new, returned[last])
-    )
+    left_new, right_new, *rest = lax.optimization_barrier(
+        (left_new, right_new, *[returned[k] for k in range(1, rounds)])
+    )
+    returned.update(enumerate(rest, 1))
     passed = [other_core(returned[k][1]) for k in range(rounds)]
     update = call(
         functools.partial(place_kernel, codes, early), shape((blocks, slab, width // 2)),

time: 49.8 us -> 48.3 us (0.970)
  starting transfers between devices: 17.3 us -> 14.5 us
  waiting for transfers between devices: 21.7 us -> 22.5 us
  Pallas kernels: 7.9 us -> 8.41 us
    ppermute x13 -> x12, starting transfers between devices: 8.51 us -> 3.49 us  [other_core(): return lax.ppermute(x, 'replica', [(0, 1), (1, 0)])]
    ppermute x9 -> x8, starting transfers between devices: 8.78 us -> 11 us  [trade(): return lax.ppermute(x, ('shard', 'replica'), pairs)]
    ppermute x9 -> x8, waiting for transfers between devices: 19.4 us -> 20.2 us  [trade(): return lax.ppermute(x, ('shard', 'replica'), pairs)]
    pallas_call x8, Pallas kernels: 7.9 us -> 8.41 us  [call(): pl.pallas_call(kernel, out_shape=out_shape, in_specs=in_specs, compiler_p...]
    ppermute x13 -> x12, waiting for transfers between devices: 2.36 us -> 2.37 us  [other_core(): return lax.ppermute(x, 'replica', [(0, 1), (1, 0)])]
  transfers between devices with their start and end apart: 22 -> 20, of which waited for: 7 -> 10; matrix products, arithmetic and copies ran while one was open for 0% -> 0% of each run, Pallas kernels for 11% -> 11%
where the time goes in v6:
time: 48.3 us; the launch traced here: 48.1 us
  waiting for transfers between devices  22.5 us (47%)
  starting transfers between devices  14.5 us (30%)
  Pallas kernels  8.41 us (17%)
  local copies, waits for them, and re-layouts  1.88 us (4%)
  between operations  0.8 us (2%)
    ppermute x8, waiting for transfers between devices, trade(): return lax.ppermute(x, ('shard', 'replica'), pairs)  20.2 us
    ppermute x8, starting transfers between devices, trade(): return lax.ppermute(x, ('shard', 'replica'), pairs)  11 us
    pallas_call x8, Pallas kernels, call(): pl.pallas_call(kernel, out_shape=out_shape, in_specs=in_specs, compiler_p...  8.41 us
    ppermute x12, starting transfers between devices, other_core(): return lax.ppermute(x, 'replica', [(0, 1), (1, 0)])  3.49 us
    ppermute x12, waiting for transfers between devices, other_core(): return lax.ppermute(x, 'replica', [(0, 1), (1, 0)])  2.37 us
    unnamed x14, local copies, waits for them, and re-layouts  1.84 us
  transfers between devices with their start and end apart: 20, of which 10 were waited for; matrix products, arithmetic and copies ran while one was open for 0% of the time, Pallas kernels for 11%

profile of v6, /device:TPU:0, one launch (start us, length us, event | category | flops | bytes accessed | tf_op | source)
XLA Modules:
  0.0 48.1 jit_solution(2294890129388470076)
XLA Ops:
  0.6 0.5 %collective-permute-start.1 = (bf16[6,96,768]{2,1,0:T(8,128)(2,1)}, bf16[6,96,768]{2,1,0:T(8,128)(2,1)S(1)}, u32[]{:S(2)}, u32[]{:S(2)}) collective-permute-start(bf16[6,96,768]{2,1,0:T(8,128)(2,1)} %bitcast.15), channel_id=1, source_target_pairs={{0,1},{1,0},{2,3},{3,2},{4,5},{5,4},{6,7},{7,6},{8,9},{9,8},{10,11... | collective-permute-start | bytes 2654216 | tf_op jit(solution)/shard_map/ppermute | solution.py:244
  1.1 0.1 collective-permute-start
  1.2 0.4 collective-permute-start.6
  1.7 1.2 %copy-done = bf16[1,6,96,768]{3,2,1,0:T(8,128)(2,1)S(1)} copy-done((bf16[1,6,96,768]{3,2,1,0:T(8,128)(2,1)S(1)}, bf16[1,6,96,768]{3,2,1,0:T(8,128)(2,1)}, u32[]{:S(2)}) %copy-start) | copy-done | bytes 884760
  2.8 0.7 %copy-done.3 = s32[6]{0:T(128)S(1)} copy-done((s32[6]{0:T(128)S(1)}, s32[6]{0:T(128)}, u32[]{:S(2)}) %copy-start.3) | copy-done | bytes 48
  3.5 0.6 %shard_map.86.mine_ref = bf16[4,96,768]{2,1,0:T(8,128)(2,1)S(1)} custom-call(s32[6]{0:T(128)S(1)} %copy-done.3, bf16[6,96,768]{2,1,0:T(8,128)(2,1)S(1)} %bitcast.16), custom_call_target="tpu_custom_call" | custom-call | tf_op jit(solution)/shard_map/pallas_call | solution.py:254
  4.1 0.0 collective-permute-done.1.theirs_ref
  4.1 0.7 %shard_map.87 = (bf16[96,768]{1,0:T(8,128)(2,1)S(1)}, bf16[96,768]{1,0:T(8,128)(2,1)S(1)}, bf16[96,768]{1,0:T(8,128)(2,1)S(1)}, bf16[96,768]{1,0:T(8,128)(2,1)S(1)}) custom-call(s32[6]{0:T(128)S(1)} %copy-done.3, bf16[4,96,768]{2,1,0:T(8,128)(2,1)S(1)} %shard_map.86.mine_ref, bf16[6,96,768]{2,1,0:T(8,128)(2,1)S(1)} %collective-permute-done.1.theirs_ref), custom_call_target="tpu_custom_call" | custom-call | tf_op jit(solution)/shard_map/pallas_call | solution.py:254
  4.8 0.0 copy-start.1
  4.8 3.7 %collective-permute-start.2 = (bf16[96,768]{1,0:T(8,128)(2,1)S(1)}, bf16[96,768]{1,0:T(8,128)(2,1)S(1)}, u32[]{:S(2)}, u32[]{:S(2)}) collective-permute-start(bf16[96,768]{1,0:T(8,128)(2,1)S(1)} %get-tuple-element.33), channel_id=1, source_target_pairs={{0,8},{1,13},{2,10},{3,15},{4,12},{5,9},{6,14},{7,11},{8,0},{9,5},... | collective-permute-start | bytes 442376 | tf_op jit(solution)/shard_map/ppermute | solution.py:248
  8.5 1.3 %collective-permute-start.3 = (bf16[96,768]{1,0:T(8,128)(2,1)S(1)}, bf16[96,768]{1,0:T(8,128)(2,1)S(1)}, u32[]{:S(2)}, u32[]{:S(2)}) collective-permute-start(bf16[96,768]{1,0:T(8,128)(2,1)S(1)} %get-tuple-element.34), channel_id=1, source_target_pairs={{0,10},{1,15},{2,8},{3,13},{4,14},{5,11},{6,12},{7,9},{8,2},{9,7},... | collective-permute-start | bytes 442376 | tf_op jit(solution)/shard_map/ppermute | solution.py:248
  9.8 0.3 collective-permute-start.4
  10.1 0.0 collective-permute-done.other_ref
  10.1 0.7 %collective-permute-start.5 = (bf16[96,768]{1,0:T(8,128)(2,1)S(1)}, bf16[96,768]{1,0:T(8,128)(2,1)S(1)}, u32[]{:S(2)}, u32[]{:S(2)}) collective-permute-start(bf16[96,768]{1,0:T(8,128)(2,1)S(1)} %get-tuple-element.36), channel_id=1, source_target_pairs={{0,0},{1,7},{2,2},{3,5},{4,4},{5,3},{6,6},{7,1},{8,8},{9,15},{10,1... | collective-permute-start | bytes 442376 | tf_op jit(solution)/shard_map/ppermute | solution.py:248
  10.8 0.9 %shard_map.85 = (bf16[384,384]{1,0:T(8,128)(2,1)S(1)}, bf16[384,384]{1,0:T(8,128)(2,1)S(1)}) custom-call(bf16[384,768]{1,0:T(8,128)(2,1)S(1)} %bitcast.20, bf16[384,768]{1,0:T(8,128)(2,1)S(1)} %collective-permute-done.other_ref), custom_call_target="tpu_custom_call" | custom-call | tf_op jit(solution)/shard_map/pallas_call | solution.py:254
  11.7 7.9 %collective-permute-done.2.refs_0_ = bf16[96,768]{1,0:T(8,128)(2,1)S(1)} collective-permute-done((bf16[96,768]{1,0:T(8,128)(2,1)S(1)}, bf16[96,768]{1,0:T(8,128)(2,1)S(1)}, u32[]{:S(2)}, u32[]{:S(2)}) %collective-permute-start.2) | collective-permute-done | bytes 147488 | tf_op jit(solution)/shard_map/ppermute | solution.py:248
  19.6 4.0 %collective-permute-done.3.refs_1_ = bf16[96,768]{1,0:T(8,128)(2,1)S(1)} collective-permute-done((bf16[96,768]{1,0:T(8,128)(2,1)S(1)}, bf16[96,768]{1,0:T(8,128)(2,1)S(1)}, u32[]{:S(2)}, u32[]{:S(2)}) %collective-permute-start.3) | collective-permute-done | bytes 147488 | tf_op jit(solution)/shard_map/ppermute | solution.py:248
  23.6 0.0 collective-permute-done.4.refs_2_
  23.6 0.0 collective-permute-done.5.refs_3_
  23.6 0.0 collective-permute-start.7
  23.6 0.5 %collective-permute-start.8 = (bf16[96,768]{1,0:T(8,128)(2,1)S(1)}, bf16[96,768]{1,0:T(8,128)(2,1)S(1)}, u32[]{:S(2)}, u32[]{:S(2)}) collective-permute-start(bf16[96,768]{1,0:T(8,128)(2,1)S(1)} %collective-permute-done.3.refs_1_), channel_id=1, source_target_pairs={{0,1},{1,0},{2,3},{3,2},{4,5},{5,4},{6,7},{7,6},{8,9},{9,8},{10,11... | collective-permute-start | bytes 442376 | tf_op jit(solution)/shard_map/ppermute | solution.py:244
  24.1 0.1 collective-permute-start.9
  24.2 0.4 collective-permute-start.10
  24.6 0.5 shard_map.88
  25.1 0.0 collective-permute-done.6.other_ref
  25.1 0.0 collective-permute-done.7.refs_0_.refs_4_
  25.1 0.1 collective-permute-done.8.refs_1_.refs_5_
  25.2 0.3 collective-permute-done.9.refs_2_.refs_6_
  25.5 0.2 collective-permute-done.10.refs_3_.refs_7_
  25.7 1.2 %shard_map.89 = (f32[2,384,384]{2,1,0:T(8,128)S(1)}, f32[8,128]{1,0:T(8,128)S(1)}, f32[8,128]{1,0:T(8,128)S(1)}) custom-call(bf16[384,384]{1,0:T(8,128)(2,1)S(1)} %get-tuple-element.37.left_ref, f32[384,768]{1,0:T(8,128)S(1)} %get-tuple-element.43.total_ref, f32[8,128]{1,0:T(8,128)S(1)} %get-tuple-element.44.begun_sq_ref, bf16[768,384]{1,0:T(8,128)(2,1)S(1)} %bitcast.18, ...), custom_call_target="tpu_custom_call" | custom-call | tf_op jit(solution)/shard_map/pallas_call | solution.py:254
  26.9 0.3 collective-permute-start.11
  27.2 0.9 %collective-permute-done.11.theirs_sq_ref = f32[8,128]{1,0:T(8,128)S(1)} collective-permute-done((f32[8,128]{1,0:T(8,128)S(1)}, f32[8,128]{1,0:T(8,128)S(1)}, u32[]{:S(2)}, u32[]{:S(2)}) %collective-permute-start.11) | collective-permute-done | bytes 4128 | tf_op jit(solution)/shard_map/ppermute | solution.py:244
  28.1 0.6 %shard_map.90 = (f32[8,128]{1,0:T(8,128)}, bf16[2,96,384]{2,1,0:T(8,128)(2,1)S(1)}, bf16[2,96,384]{2,1,0:T(8,128)(2,1)S(1)}, bf16[2,96,384]{2,1,0:T(8,128)(2,1)S(1)}, bf16[2,96,384]{2,1,0:T(8,128)(2,1)S(1)}) custom-call(f32[8,128]{1,0:T(8,128)S(1)} %get-tuple-element.45.mine_sq_ref, f32[8,128]{1,0:T(8,128)S(1)} %collective-permute-done.11.theirs_sq_ref, ...), custom_call_target="tpu_custom_call" | custom-call | tf_op jit(solution)/shard_map/pallas_call | solution.py:254
  28.7 0.0 collective-permute-start.12
  28.7 2.9 %collective-permute-start.13 = (bf16[2,96,384]{2,1,0:T(8,128)(2,1)S(1)}, bf16[2,96,384]{2,1,0:T(8,128)(2,1)S(1)}, u32[]{:S(2)}, u32[]{:S(2)}) collective-permute-start(bf16[2,96,384]{2,1,0:T(8,128)(2,1)S(1)} %get-tuple-element.51), channel_id=1, source_target_pairs={{0,10},{1,15},{2,8},{3,13},{4,14},{5,11},{6,12},{7,9},{8,2},{9,7},... | collective-permute-start | bytes 442376 | tf_op jit(solution)/shard_map/ppermute | solution.py:248
  31.6 1.5 %collective-permute-start.14 = (bf16[2,96,384]{2,1,0:T(8,128)(2,1)S(1)}, bf16[2,96,384]{2,1,0:T(8,128)(2,1)S(1)}, u32[]{:S(2)}, u32[]{:S(2)}) collective-permute-start(bf16[2,96,384]{2,1,0:T(8,128)(2,1)S(1)} %get-tuple-element.52), channel_id=1, source_target_pairs={{0,2},{1,5},{2,0},{3,7},{4,6},{5,1},{6,4},{7,3},{8,10},{9,13},{10,... | collective-permute-start | bytes 442376 | tf_op jit(solution)/shard_map/ppermute | solution.py:248
  33.1 0.7 %collective-permute-start.15 = (bf16[2,96,384]{2,1,0:T(8,128)(2,1)S(1)}, bf16[2,96,384]{2,1,0:T(8,128)(2,1)S(1)}, u32[]{:S(2)}, u32[]{:S(2)}) collective-permute-start(bf16[2,96,384]{2,1,0:T(8,128)(2,1)S(1)} %get-tuple-element.53), channel_id=1, source_target_pairs={{0,0},{1,7},{2,2},{3,5},{4,4},{5,3},{6,6},{7,1},{8,8},{9,15},{10,1... | collective-permute-start | bytes 442376 | tf_op jit(solution)/shard_map/ppermute | solution.py:248
  33.7 8.3 %collective-permute-done.12.after_ref.refs_0_ = bf16[2,96,384]{2,1,0:T(8,128)(2,1)S(1)} collective-permute-done((bf16[2,96,384]{2,1,0:T(8,128)(2,1)S(1)}, bf16[2,96,384]{2,1,0:T(8,128)(2,1)S(1)}, u32[]{:S(2)}, u32[]{:S(2)}) %collective-permute-start.12) | collective-permute-done | bytes 147488 | tf_op jit(solution)/shard_map/ppermute | solution.py:248
  42.0 0.1 collective-permute-start.16
  42.1 2.6 %shard_map.91 = (bf16[384,768]{1,0:T(8,128)(2,1)}, bf16[384,768]{1,0:T(8,128)(2,1)}) custom-call(s32[6]{0:T(128)S(1)} %copy-done.4, bf16[384,768]{1,0:T(8,128)(2,1)S(1)} %bitcast.21, bf16[384,768]{1,0:T(8,128)(2,1)S(1)} %bitcast.22, bf16[2,96,384]{2,1,0:T(8,128)(2,1)S(1)} %collective-permute-done.12.after_ref.refs_0_, ...), custom_call_target="tpu_custom_call" | custom-call | flops 905969664 | bytes 2359296 | tf_op jit(solution)/shard_map/pallas_call | solution.py:254
  44.7 0.0 collective-permute-done.13.refs_1_
  44.8 0.5 %collective-permute-start.19 = (bf16[96,384]{1,0:T(8,128)(2,1)S(1)}, bf16[96,384]{1,0:T(8,128)(2,1)S(1)}, u32[]{:S(2)}, u32[]{:S(2)}) collective-permute-start(bf16[96,384]{1,0:T(8,128)(2,1)S(1)} %slice_bitcast_fusion.1), channel_id=1, source_target_pairs={{0,1},{1,0},{2,3},{3,2},{4,5},{5,4},{6,7},{7,6},{8,9},{9,8},{10,11... | collective-permute-start | bytes 221192 | tf_op jit(solution)/shard_map/ppermute | solution.py:244
  45.3 0.1 collective-permute-start.18
  45.4 0.4 collective-permute-start.17
  45.8 0.4 collective-permute-done.19.refs_7_
  46.2 0.4 collective-permute-done.18.refs_6_
  46.6 0.2 collective-permute-done.17.refs_5_
  46.7 1.4 %shard_map.92 = bf16[6,96,384]{2,1,0:T(8,128)(2,1)} custom-call(s32[6]{0:T(128)S(1)} %copy-done.4, bf16[2,96,384]{2,1,0:T(8,128)(2,1)S(1)} %collective-permute-done.12.after_ref.refs_0_, bf16[2,96,384]{2,1,0:T(8,128)(2,1)S(1)} %collective-permute-done.13.refs_1_, bf16[2,96,384]{2,1,0:T(8,128)(2,1)S(1)} %collective-permute-done.14.refs_2_, ...), custom_call_target="tpu_custom_call" | custom-call | tf_op jit(solution)/shard_map/pallas_call | solution.py:254
  (18 shorter events, 0.1 us)
Async XLA Ops:
  0.6 3.5 %collective-permute-start.1 = (bf16[6,96,768]{2,1,0:T(8,128)(2,1)}, bf16[6,96,768]{2,1,0:T(8,128)(2,1)S(1)}, u32[]{:S(2)}, u32[]{:S(2)}) collective-permute-start(bf16[6,96,768]{2,1,0:T(8,128)(2,1)} %bitcast.15), channel_id=1, source_target_pairs={{0,1},{1,0},{2,3},{3,2},{4,5},{5,4},{6,7},{7,6},{8,9},{9,8},{10,11... | collective-permute-start | bytes 2654216 | tf_op jit(solution)/shard_map/ppermute | solution.py:244
  1.1 8.9 %collective-permute-start = (bf16[384,768]{1,0:T(8,128)(2,1)}, bf16[384,768]{1,0:T(8,128)(2,1)S(1)}, u32[]{:S(2)}, u32[]{:S(2)}) collective-permute-start(bf16[384,768]{1,0:T(8,128)(2,1)} %bitcast.19), channel_id=1, source_target_pairs={{0,1},{1,0},{2,3},{3,2},{4,5},{5,4},{6,7},{7,6},{8,9},{9,8},{10,11... | collective-permute-start | bytes 1769480 | tf_op jit(solution)/shard_map/ppermute | solution.py:244
  1.2 23.8 %collective-permute-start.6 = (bf16[768,384]{1,0:T(8,128)(2,1)}, bf16[768,384]{1,0:T(8,128)(2,1)S(1)}, u32[]{:S(2)}, u32[]{:S(2)}) collective-permute-start(bf16[768,384]{1,0:T(8,128)(2,1)} %bitcast.17), channel_id=1, source_target_pairs={{0,1},{1,0},{2,3},{3,2},{4,5},{5,4},{6,7},{7,6},{8,9},{9,8},{10,11... | collective-permute-start | bytes 1769480 | tf_op jit(solution)/shard_map/ppermute | solution.py:244
  1.7 1.2 %copy-start = (bf16[1,6,96,768]{3,2,1,0:T(8,128)(2,1)S(1)}, bf16[1,6,96,768]{3,2,1,0:T(8,128)(2,1)}, u32[]{:S(2)}) copy-start(bf16[1,6,96,768]{3,2,1,0:T(8,128)(2,1)} %param.6) | copy-start | bytes 2654212
  2.8 0.7 %copy-start.3 = (s32[6]{0:T(128)S(1)}, s32[6]{0:T(128)}, u32[]{:S(2)}) copy-start(s32[6]{0:T(128)} %owner_ref.7) | copy-start | bytes 76
  3.5 7.3 %copy-start.2 = (bf16[1,384,768]{2,1,0:T(8,128)(2,1)S(1)}, bf16[1,384,768]{2,1,0:T(8,128)(2,1)}, u32[]{:S(2)}) copy-start(bf16[1,384,768]{2,1,0:T(8,128)(2,1)} %param.10) | copy-start | bytes 1769476
  4.8 20.9 %copy-start.1 = (bf16[1,768,384]{2,1,0:T(8,128)(2,1)S(1)}, bf16[1,768,384]{2,1,0:T(8,128)(2,1)}, u32[]{:S(2)}) copy-start(bf16[1,768,384]{2,1,0:T(8,128)(2,1)} %param.11) | copy-start | bytes 1769476
  4.8 14.7 %collective-permute-start.2 = (bf16[96,768]{1,0:T(8,128)(2,1)S(1)}, bf16[96,768]{1,0:T(8,128)(2,1)S(1)}, u32[]{:S(2)}, u32[]{:S(2)}) collective-permute-start(bf16[96,768]{1,0:T(8,128)(2,1)S(1)} %get-tuple-element.33), channel_id=1, source_target_pairs={{0,8},{1,13},{2,10},{3,15},{4,12},{5,9},{6,14},{7,11},{8,0},{9,5},... | collective-permute-start | bytes 442376 | tf_op jit(solution)/shard_map/ppermute | solution.py:248
  8.5 15.0 %collective-permute-start.3 = (bf16[96,768]{1,0:T(8,128)(2,1)S(1)}, bf16[96,768]{1,0:T(8,128)(2,1)S(1)}, u32[]{:S(2)}, u32[]{:S(2)}) collective-permute-start(bf16[96,768]{1,0:T(8,128)(2,1)S(1)} %get-tuple-element.34), channel_id=1, source_target_pairs={{0,10},{1,15},{2,8},{3,13},{4,14},{5,11},{6,12},{7,9},{8,2},{9,7},... | collective-permute-start | bytes 442376 | tf_op jit(solution)/shard_map/ppermute | solution.py:248
  9.8 13.8 %collective-permute-start.4 = (bf16[96,768]{1,0:T(8,128)(2,1)S(1)}, bf16[96,768]{1,0:T(8,128)(2,1)S(1)}, u32[]{:S(2)}, u32[]{:S(2)}) collective-permute-start(bf16[96,768]{1,0:T(8,128)(2,1)S(1)} %get-tuple-element.35), channel_id=1, source_target_pairs={{0,2},{1,5},{2,0},{3,7},{4,6},{5,1},{6,4},{7,3},{8,10},{9,13},{10,... | collective-permute-start | bytes 442376 | tf_op jit(solution)/shard_map/ppermute | solution.py:248
  10.1 13.5 %collective-permute-start.5 = (bf16[96,768]{1,0:T(8,128)(2,1)S(1)}, bf16[96,768]{1,0:T(8,128)(2,1)S(1)}, u32[]{:S(2)}, u32[]{:S(2)}) collective-permute-start(bf16[96,768]{1,0:T(8,128)(2,1)S(1)} %get-tuple-element.36), channel_id=1, source_target_pairs={{0,0},{1,7},{2,2},{3,5},{4,4},{5,3},{6,6},{7,1},{8,8},{9,15},{10,1... | collective-permute-start | bytes 442376 | tf_op jit(solution)/shard_map/ppermute | solution.py:248
  23.6 1.5 %collective-permute-start.7 = (bf16[96,768]{1,0:T(8,128)(2,1)S(1)}, bf16[96,768]{1,0:T(8,128)(2,1)S(1)}, u32[]{:S(2)}, u32[]{:S(2)}) collective-permute-start(bf16[96,768]{1,0:T(8,128)(2,1)S(1)} %collective-permute-done.2.refs_0_), channel_id=1, source_target_pairs={{0,1},{1,0},{2,3},{3,2},{4,5},{5,4},{6,7},{7,6},{8,9},{9,8},{10,11... | collective-permute-start | bytes 442376 | tf_op jit(solution)/shard_map/ppermute | solution.py:244
  23.6 1.6 %collective-permute-start.8 = (bf16[96,768]{1,0:T(8,128)(2,1)S(1)}, bf16[96,768]{1,0:T(8,128)(2,1)S(1)}, u32[]{:S(2)}, u32[]{:S(2)}) collective-permute-start(bf16[96,768]{1,0:T(8,128)(2,1)S(1)} %collective-permute-done.3.refs_1_), channel_id=1, source_target_pairs={{0,1},{1,0},{2,3},{3,2},{4,5},{5,4},{6,7},{7,6},{8,9},{9,8},{10,11... | collective-permute-start | bytes 442376 | tf_op jit(solution)/shard_map/ppermute | solution.py:244
  24.1 1.4 %collective-permute-start.9 = (bf16[96,768]{1,0:T(8,128)(2,1)S(1)}, bf16[96,768]{1,0:T(8,128)(2,1)S(1)}, u32[]{:S(2)}, u32[]{:S(2)}) collective-permute-start(bf16[96,768]{1,0:T(8,128)(2,1)S(1)} %collective-permute-done.4.refs_2_), channel_id=1, source_target_pairs={{0,1},{1,0},{2,3},{3,2},{4,5},{5,4},{6,7},{7,6},{8,9},{9,8},{10,11... | collective-permute-start | bytes 442376 | tf_op jit(solution)/shard_map/ppermute | solution.py:244
  24.2 1.5 %collective-permute-start.10 = (bf16[96,768]{1,0:T(8,128)(2,1)S(1)}, bf16[96,768]{1,0:T(8,128)(2,1)S(1)}, u32[]{:S(2)}, u32[]{:S(2)}) collective-permute-start(bf16[96,768]{1,0:T(8,128)(2,1)S(1)} %collective-permute-done.5.refs_3_), channel_id=1, source_target_pairs={{0,1},{1,0},{2,3},{3,2},{4,5},{5,4},{6,7},{7,6},{8,9},{9,8},{10,11... | collective-permute-start | bytes 442376 | tf_op jit(solution)/shard_map/ppermute | solution.py:244
  26.8 15.2 %copy-start.4 = (s32[6]{0:T(128)S(1)}, s32[6]{0:T(128)}, u32[]{:S(2)}) copy-start(s32[6]{0:T(128)} %owner_ref.7) | copy-start | bytes 76
  26.8 15.2 %copy-start.5 = (bf16[1,384,768]{2,1,0:T(8,128)(2,1)S(1)}, bf16[1,384,768]{2,1,0:T(8,128)(2,1)}, u32[]{:S(2)}) copy-start(bf16[1,384,768]{2,1,0:T(8,128)(2,1)} %param.8) | copy-start | bytes 1769476
  26.8 15.2 %copy-start.6 = (bf16[1,384,768]{2,1,0:T(8,128)(2,1)S(1)}, bf16[1,384,768]{2,1,0:T(8,128)(2,1)}, u32[]{:S(2)}) copy-start(bf16[1,384,768]{2,1,0:T(8,128)(2,1)} %param.9) | copy-start | bytes 1769476
  26.9 1.2 %collective-permute-start.11 = (f32[8,128]{1,0:T(8,128)S(1)}, f32[8,128]{1,0:T(8,128)S(1)}, u32[]{:S(2)}, u32[]{:S(2)}) collective-permute-start(f32[8,128]{1,0:T(8,128)S(1)} %get-tuple-element.45.mine_sq_ref), channel_id=1, source_target_pairs={{0,1},{1,0},{2,3},{3,2},{4,5},{5,4},{6,7},{7,6},{8,9},{9,8},{10,11... | collective-permute-start | bytes 12296 | tf_op jit(solution)/shard_map/ppermute | solution.py:244
  28.7 13.3 %collective-permute-start.12 = (bf16[2,96,384]{2,1,0:T(8,128)(2,1)S(1)}, bf16[2,96,384]{2,1,0:T(8,128)(2,1)S(1)}, u32[]{:S(2)}, u32[]{:S(2)}) collective-permute-start(bf16[2,96,384]{2,1,0:T(8,128)(2,1)S(1)} %get-tuple-element.48), channel_id=1, source_target_pairs={{0,8},{1,13},{2,10},{3,15},{4,12},{5,9},{6,14},{7,11},{8,0},{9,5},... | collective-permute-start | bytes 442376 | tf_op jit(solution)/shard_map/ppermute | solution.py:248
  28.7 16.0 %collective-permute-start.13 = (bf16[2,96,384]{2,1,0:T(8,128)(2,1)S(1)}, bf16[2,96,384]{2,1,0:T(8,128)(2,1)S(1)}, u32[]{:S(2)}, u32[]{:S(2)}) collective-permute-start(bf16[2,96,384]{2,1,0:T(8,128)(2,1)S(1)} %get-tuple-element.51), channel_id=1, source_target_pairs={{0,10},{1,15},{2,8},{3,13},{4,14},{5,11},{6,12},{7,9},{8,2},{9,7},... | collective-permute-start | bytes 442376 | tf_op jit(solution)/shard_map/ppermute | solution.py:248
  31.6 13.1 %collective-permute-start.14 = (bf16[2,96,384]{2,1,0:T(8,128)(2,1)S(1)}, bf16[2,96,384]{2,1,0:T(8,128)(2,1)S(1)}, u32[]{:S(2)}, u32[]{:S(2)}) collective-permute-start(bf16[2,96,384]{2,1,0:T(8,128)(2,1)S(1)} %get-tuple-element.52), channel_id=1, source_target_pairs={{0,2},{1,5},{2,0},{3,7},{4,6},{5,1},{6,4},{7,3},{8,10},{9,13},{10,... | collective-permute-start | bytes 442376 | tf_op jit(solution)/shard_map/ppermute | solution.py:248
  33.1 11.7 %collective-permute-start.15 = (bf16[2,96,384]{2,1,0:T(8,128)(2,1)S(1)}, bf16[2,96,384]{2,1,0:T(8,128)(2,1)S(1)}, u32[]{:S(2)}, u32[]{:S(2)}) collective-permute-start(bf16[2,96,384]{2,1,0:T(8,128)(2,1)S(1)} %get-tuple-element.53), channel_id=1, source_target_pairs={{0,0},{1,7},{2,2},{3,5},{4,4},{5,3},{6,6},{7,1},{8,8},{9,15},{10,1... | collective-permute-start | bytes 442376 | tf_op jit(solution)/shard_map/ppermute | solution.py:248
  42.0 3.8 %collective-permute-start.16 = (bf16[96,384]{1,0:T(8,128)(2,1)S(1)}, bf16[96,384]{1,0:T(8,128)(2,1)S(1)}, u32[]{:S(2)}, u32[]{:S(2)}) collective-permute-start(bf16[96,384]{1,0:T(8,128)(2,1)S(1)} %slice_bitcast_fusion), channel_id=1, source_target_pairs={{0,1},{1,0},{2,3},{3,2},{4,5},{5,4},{6,7},{7,6},{8,9},{9,8},{10,11... | collective-permute-start | bytes 221192 | tf_op jit(solution)/shard_map/ppermute | solution.py:244
  44.8 1.4 %collective-permute-start.19 = (bf16[96,384]{1,0:T(8,128)(2,1)S(1)}, bf16[96,384]{1,0:T(8,128)(2,1)S(1)}, u32[]{:S(2)}, u32[]{:S(2)}) collective-permute-start(bf16[96,384]{1,0:T(8,128)(2,1)S(1)} %slice_bitcast_fusion.1), channel_id=1, source_target_pairs={{0,1},{1,0},{2,3},{3,2},{4,5},{5,4},{6,7},{7,6},{8,9},{9,8},{10,11... | collective-permute-start | bytes 221192 | tf_op jit(solution)/shard_map/ppermute | solution.py:244
  45.3 1.3 %collective-permute-start.18 = (bf16[96,384]{1,0:T(8,128)(2,1)S(1)}, bf16[96,384]{1,0:T(8,128)(2,1)S(1)}, u32[]{:S(2)}, u32[]{:S(2)}) collective-permute-start(bf16[96,384]{1,0:T(8,128)(2,1)S(1)} %slice_bitcast_fusion.2), channel_id=1, source_target_pairs={{0,1},{1,0},{2,3},{3,2},{4,5},{5,4},{6,7},{7,6},{8,9},{9,8},{10,11... | collective-permute-start | bytes 221192 | tf_op jit(solution)/shard_map/ppermute | solution.py:244
  45.4 1.3 %collective-permute-start.17 = (bf16[96,384]{1,0:T(8,128)(2,1)S(1)}, bf16[96,384]{1,0:T(8,128)(2,1)S(1)}, u32[]{:S(2)}, u32[]{:S(2)}) collective-permute-start(bf16[96,384]{1,0:T(8,128)(2,1)S(1)} %slice_bitcast_fusion.3), channel_id=1, source_target_pairs={{0,1},{1,0},{2,3},{3,2},{4,5},{5,4},{6,7},{7,6},{8,9},{9,8},{10,11... | collective-permute-start | bytes 221192 | tf_op jit(solution)/shard_map/ppermute | solution.py:244

commit v7 on v5

--- a/solution.py
+++ b/solution.py
@@ -11,6 +11,7 @@
 SMEM = pl.BlockSpec(memory_space=pltpu.SMEM)
 ANY = pl.BlockSpec(memory_space=pl.ANY)
 LIGHT = pl.CostEstimate(flops=0, bytes_accessed=0, transcendentals=0)
+ORDER = {2: (1, 0), 4: (2, 1, 0, 3)}
 PARAMS = pltpu.CompilerParams(vmem_limit_bytes=24 * 1024 * 1024)
 
 
@@ -56,11 +57,8 @@
 
 
 def codes_of(owners):
-    half, quarter = owners // 2, owners // 4
-    return (
-        [half + i for i in range(quarter)] + [i for i in reversed(range(quarter))],
-        [half + quarter + i for i in range(quarter)] + [quarter + i for i in range(quarter)],
-    )
+    near = ORDER[owners // 2]
+    return near, tuple(owners // 2 + code for code in near)
 
 
 def partner(codes, k, other=False):
@@ -103,14 +101,14 @@
     rounds = len(codes[0])
     slab = half // rounds
     core = lax.axis_index("replica")
-    for k in range(rounds):
-        shard = partner(codes, k)
+    for n in range(2 * rounds):
+        shard = partner(codes, n % rounds, n >= rounds)
         row = pl.multiple_of(lax.rem(shard, rounds) * slab, slab)
         for ref, near in ((own_ref, True), (other_ref, False)):
 
             @pl.when((lax.div(shard, rounds) == core) == near)
             def _(ref=ref):
-                rows_ref[k * slab:(k + 1) * slab, :] = ref[pl.ds(row, slab), :]
+                rows_ref[n * slab:(n + 1) * slab, :] = ref[pl.ds(row, slab), :]
 
     for out_ref, group in zip(out_refs, slots):
         column = lax.broadcasted_iota(jnp.int32, (1, len(group) * slab), 1)
@@ -137,36 +135,23 @@
     grad_sq_ref[...] = jnp.broadcast_to(squares(stacked_ref[...]), grad_sq_ref.shape)
 
 
-def finish_kernel(early, left_ref, total_ref, begun_sq_ref, own_ref, other_ref, *refs):
-    *slabs, both_ref, side_sq_ref, grad_sq_ref = refs[:-2 - len(early)]
-    early_refs, stacked_ref, side_ref = refs[-2 - len(early):-2], refs[-2], refs[-1]
-    slab = slabs[0].shape[0]
-    for n, ref in enumerate(slabs):
-        stacked_ref[n * slab:(n + 1) * slab, :] = ref[...]
-    side = total_ref[...] + jnp.dot(
-        left_ref[...], stacked_ref[...], preferred_element_type=jnp.float32
-    )
+def finish_kernel(left_ref, total_ref, begun_sq_ref, own_ref, other_ref, slab_ref, *refs):
+    *whole_refs, keep_ref, pass_ref, side_ref, both_ref = refs
+    last = slab_ref[...]
+    side = total_ref[...] + jnp.dot(left_ref[...], last, preferred_element_type=jnp.float32)
     side_ref[...] = side.astype(side_ref.dtype)
+    grad_sq = begun_sq_ref[0:1, 0:1] + squares(last)
+    half, slab = own_ref.shape[1], slab_ref.shape[0]
     side_sq = jnp.zeros((1, 1), jnp.float32)
     for n, ref in enumerate((own_ref, other_ref)):
         both = jnp.dot(side_ref[...], ref[...], preferred_element_type=jnp.float32)
-        both_ref[n] = both
+        both_ref[n] = both[:half]
         side_sq += squares(both)
-        for k, out_ref in zip(early, early_refs):
-            out_ref[n] = both[k * slab:(k + 1) * slab].astype(out_ref.dtype)
-    side_sq_ref[...] = jnp.broadcast_to(side_sq, side_sq_ref.shape)
-    grad_sq_ref[...] = begun_sq_ref[...] + squares(stacked_ref[...])
-
-
-def scale_kernel(late, mine_sq_ref, theirs_sq_ref, grad_sq_ref, both_ref, graft_ref, *out_refs):
-    side_sq = mine_sq_ref[...] + theirs_sq_ref[...]
-    graft_ref[...] = jnp.sqrt(grad_sq_ref[...] / (side_sq + 1e-06))
-    graft = graft_ref[0:1, 0:1]
-    for k, out_ref in zip(late, out_refs):
-        slab = out_ref.shape[1]
-        for n in range(2):
-            piece = both_ref[n, k * slab:(k + 1) * slab] * graft
-            out_ref[n] = piece.astype(out_ref.dtype)
+    graft = jnp.sqrt(grad_sq / (side_sq + 1e-06))
+    for k, out_ref in enumerate(whole_refs):
+        out_ref[...] = (both_ref[:, k * slab:(k + 1) * slab] * graft).astype(out_ref.dtype)
+    for n, out_ref in enumerate((keep_ref, pass_ref)):
+        out_ref[...] = (both_ref[n, half - slab:] * graft).astype(out_ref.dtype)
 
 
 def gram_kernel(codes, owner_ref, left_ref, right_ref, after_ref, *refs):
@@ -198,21 +183,16 @@
     )
 
 
-def place_kernel(codes, early, owner_ref, *refs):
+def place_kernel(codes, owner_ref, *refs):
     rounds = len(codes[0])
-    slabs = (refs[:rounds], refs[rounds:2 * rounds])
-    grafts = refs[2 * rounds:2 * rounds + 2 * len(early)]
-    out_ref, scaled_ref, sem = refs[2 * rounds + 2 * len(early):]
+    slabs, (out_ref, sem) = refs[:2 * rounds], refs[2 * rounds:]
     pending = []
-    for k in [k for k in range(rounds) if k not in early] + list(early):
+    for k in range(rounds):
         for n in range(2):
             block = block_of(owner_ref, partner(codes, k, n == 1))
-            source = slabs[n][k].at[0] if n == 0 else slabs[n][k]
-            if k in early:
-                m = 2 * early.index(k) + n
-                scaled = source[...].astype(jnp.float32) * grafts[m][0:1, 0:1]
-                scaled_ref[m] = scaled.astype(scaled_ref.dtype)
-                source = scaled_ref.at[m]
+            source = slabs[n * rounds + k]
+            if len(source.shape) == 3:
+                source = source.at[0]
             copy = pltpu.make_async_copy(
                 source, out_ref.at[jnp.maximum(block, 0)], sem.at[2 * k + n]
             )
@@ -232,20 +212,20 @@
 def per_device_paired(gradients, block_owner, left_gram, right_gram, left_root, right_root):
     owners = lax.axis_size("shard")
     rounds = owners // 2
+    last = rounds - 1
     codes = codes_of(owners)
     blocks, slab, width = gradients.shape[1:]
     half_rows = left_gram.shape[1]
-    last = owners // 4 - 1
-    early = [0]
-    late = [k for k in range(rounds) if k not in early]
-    sooner = [(k, other) for k in range(rounds) if k != last for other in (False, True)]
-    slots = (sooner, [(last, False), (last, True)])
+    slots = [(k, other) for k in range(rounds) for other in (False, True)]
+    slots = (slots[:-1], slots[-1:])
 
     def other_core(x):
         return lax.ppermute(x, "replica", [(0, 1), (1, 0)])
 
-    def trade(x, k):
-        pairs = [(s * 2 + r, (s ^ codes[r][k]) * 2 + r) for s in range(owners) for r in range(2)]
+    def trade(x, k, turn=0):
+        pairs = [
+            (s * 2 + r, (s ^ codes[r][k]) * 2 + (r ^ turn)) for s in range(owners) for r in range(2)
+        ]
         return lax.ppermute(x, ("shard", "replica"), pairs)
 
     def shape(dims, dtype=jnp.bfloat16):
@@ -257,7 +237,6 @@
             cost_estimate=cost_estimate, **options
         )(*args)
 
-    one = shape((8, 128), jnp.float32)
     other_gradient = other_core(gradients[0])
     fetched = call(
         functools.partial(fetch_kernel, codes), shape((rounds, slab, width)), [SMEM, VMEM],
@@ -268,80 +247,61 @@
         [SMEM, VMEM, VMEM], block_owner, fetched, other_gradient, out_specs=[VMEM] * rounds,
     )
     mine = [trade(outgoing[k], k) for k in range(rounds)]
-    other_right = other_core(right_root[0])
-    other_left = other_core(left_root[0])
+    other_left, other_right = other_core(left_root[0]), other_core(right_root[0])
     left_sooner, left_last = call(
         functools.partial(order_kernel, codes, slots),
-        [shape((half_rows, len(group) * slab)) for group in slots], [VMEM, VMEM],
+        [shape((2 * half_rows, len(group) * slab)) for group in slots], [VMEM, VMEM],
         left_root[0], other_left, out_specs=[VMEM, VMEM],
-        scratch_shapes=[pltpu.VMEM((half_rows, width), jnp.bfloat16)],
-    )
-    mine[last], left_sooner, left_last = lax.optimization_barrier(
-        (mine[last], left_sooner, left_last)
-    )
+        scratch_shapes=[pltpu.VMEM((2 * half_rows, width), jnp.bfloat16)],
+    )
+    mine[0], left_sooner, left_last = lax.optimization_barrier((mine[0], left_sooner, left_last))
     theirs = [other_core(x) for x in mine]
+    sooner = [(theirs if other else mine)[k] for k, other in slots[0]]
     begun, begun_sq = call(
-        begin_kernel, [shape((half_rows, width), jnp.float32), one],
-        [VMEM] * (1 + len(sooner)), left_sooner,
-        *[(theirs if other else mine)[k] for k, other in sooner], out_specs=[VMEM, VMEM],
+        begin_kernel,
+        [shape((2 * half_rows, width), jnp.float32), shape((8, 128), jnp.float32)],
+        [VMEM] * (1 + len(sooner)), left_sooner, *sooner, out_specs=[VMEM, VMEM],
         scratch_shapes=[pltpu.VMEM((len(sooner) * slab, width), jnp.bfloat16)],
     )
-    slab_shape = shape((2, slab, width // 2))
-    both_sides, side_sq, grad_sq, *first = call(
-        functools.partial(finish_kernel, early),
-        [shape((2, half_rows, width // 2), jnp.float32), one, one] + [slab_shape] * len(early),
-        [VMEM] * 7, left_last, begun, begun_sq, right_root[0], other_right,
-        mine[last], theirs[last], out_specs=[VMEM] * (3 + len(early)),
+    *whole, keep, cross = call(
+        finish_kernel,
+        [shape((2, slab, width // 2))] * last + [shape((slab, width // 2))] * 2, [VMEM] * 6,
+        left_last, begun, begun_sq, right_root[0], other_right, theirs[last],
+        out_specs=[VMEM] * (last + 2),
         scratch_shapes=[
-            pltpu.VMEM((2 * slab, width), jnp.bfloat16),
-            pltpu.VMEM((half_rows, width), jnp.bfloat16),
+            pltpu.VMEM((2 * half_rows, width), jnp.bfloat16),
+            pltpu.VMEM((2, half_rows, width // 2), jnp.float32),
         ],
     )
-    returned = {k: trade(x, k) for k, x in zip(early, first)}
-    graft, *rest = call(
-        functools.partial(scale_kernel, late), [one] + [slab_shape] * len(late),
-        [VMEM] * 4, side_sq, other_core(side_sq), grad_sq, both_sides,
-        out_specs=[VMEM] * (1 + len(late)),
-    )
-    returned.update((k, trade(x, k)) for k, x in zip(late, rest))
-    grafts = []
-    for k in early:
-        graft, returned[k] = lax.optimization_barrier((graft, returned[k]))
-        came = trade(graft, k)
-        grafts += [came, other_core(came)]
-
+    returned = [trade(x, k) for k, x in enumerate(whole)] + [trade(keep, last)]
+    crossed = trade(cross, last, turn=1)
     left_new, right_new = call(
         functools.partial(gram_kernel, codes),
         [shape(left_gram.shape[1:]), shape(right_gram.shape[1:])],
         [SMEM, VMEM, VMEM, ANY] + [VMEM] * (2 * rounds),
-        block_owner, left_gram[0], right_gram[0], grafts[0] if early else returned[0],
-        *mine, *theirs, out_specs=[VMEM, VMEM],
+        block_owner, left_gram[0], right_gram[0], returned[0], *mine, *theirs,
+        out_specs=[VMEM, VMEM],
         scratch_shapes=[pltpu.VMEM((width, width), jnp.bfloat16)],
         cost_estimate=pl.CostEstimate(
             flops=4 * half_rows * width * width, bytes_accessed=8 * half_rows * width,
             transcendentals=0,
         ),
     )
-    left_new, right_new, returned[last] = lax.optimization_barrier(
-        (left_new, right_new, returned[last])
-    )
-    passed = [other_core(returned[k][1]) for k in range(rounds)]
+    left_new, right_new, *returned[1:last] = lax.optimization_barrier(
+        (left_new, right_new, *returned[1:last])
+    )
+    passed = [other_core(x[1]) for x in returned[:last]] + [crossed]
     update = call(
-        functools.partial(place_kernel, codes, early), shape((blocks, slab, width // 2)),
-        [SMEM] + [VMEM] * (2 * rounds + len(grafts)), block_owner,
-        *[returned[k] for k in range(rounds)], *passed, *grafts,
-        out_specs=ANY,
-        scratch_shapes=[
-            pltpu.VMEM((max(1, 2 * len(early)), slab, width // 2), jnp.bfloat16),
-            pltpu.SemaphoreType.DMA((2 * rounds,)),
-        ],
+        functools.partial(place_kernel, codes), shape((blocks, slab, width // 2)),
+        [SMEM] + [ANY] * (2 * rounds), block_owner, *returned, *passed,
+        out_specs=ANY, scratch_shapes=[pltpu.SemaphoreType.DMA((2 * rounds,))],
     )
     return (left_new[None], right_new[None], update)
 
 
 def solution(mesh):
     owners = mesh.shape["shard"]
-    paired = mesh.shape["replica"] == 2 and owners in (4, 8, 16)
+    paired = mesh.shape["replica"] == 2 and owners // 2 in ORDER
     return jax.shard_map(
         per_device_paired if paired else per_device,
         mesh=mesh,

time: 49.8 us -> 43.9 us (0.88)
  waiting for transfers between devices: 21.7 us -> 1.63 us
  starting transfers between devices: 17.3 us -> 29.6 us
  Pallas kernels: 7.9 us -> 9.81 us
    ppermute x9, waiting for transfers between devices: 19.4 us -> 0.02 us  [trade(): return lax.ppermute(x, ('shard', 'replica'), pairs)]
    ppermute x13 -> x10, starting transfers between devices: 8.51 us -> 16 us  [other_core(): return lax.ppermute(x, 'replica', [(0, 1), (1, 0)])]
    ppermute x9, starting transfers between devices: 8.78 us -> 13.6 us  [trade(): return lax.ppermute(x, ('shard', 'replica'), pairs)]
    pallas_call x8 -> x7, Pallas kernels: 7.9 us -> 9.81 us  [call(): pl.pallas_call(kernel, out_shape=out_shape, in_specs=in_specs, compiler_p...]
    ppermute x13 -> x10, waiting for transfers between devices: 2.36 us -> 1.61 us  [other_core(): return lax.ppermute(x, 'replica', [(0, 1), (1, 0)])]
  transfers between devices with their start and end apart: 22 -> 19, of which waited for: 7 -> 4; matrix products, arithmetic and copies ran while one was open for 0% -> 0% of each run, Pallas kernels for 11% -> 15%
where the time goes in v7:
time: 43.9 us; the launch traced here: 43.7 us
  starting transfers between devices  29.6 us (67%)
  Pallas kernels  9.81 us (22%)
  local copies, waits for them, and re-layouts  1.88 us (4%)
  waiting for transfers between devices  1.63 us (4%)
  between operations  0.8 us (2%)
    ppermute x10, starting transfers between devices, other_core(): return lax.ppermute(x, 'replica', [(0, 1), (1, 0)])  16 us
    ppermute x9, starting transfers between devices, trade(): return lax.ppermute(x, ('shard', 'replica'), pairs)  13.6 us
    pallas_call x7, Pallas kernels, call(): pl.pallas_call(kernel, out_shape=out_shape, in_specs=in_specs, compiler_p...  9.81 us
    unnamed x14, local copies, waits for them, and re-layouts  1.85 us
    ppermute x10, waiting for transfers between devices, other_core(): return lax.ppermute(x, 'replica', [(0, 1), (1, 0)])  1.61 us
  transfers between devices with their start and end apart: 19, of which 4 were waited for; matrix products, arithmetic and copies ran while one was open for 0% of the time, Pallas kernels for 15%

profile of v7, /device:TPU:0, one launch (start us, length us, event | category | flops | bytes accessed | tf_op | source)
XLA Modules:
  0.0 43.7 jit_solution(15224020483809514807)
XLA Ops:
  0.6 0.5 %collective-permute-start = (bf16[6,96,768]{2,1,0:T(8,128)(2,1)}, bf16[6,96,768]{2,1,0:T(8,128)(2,1)S(1)}, u32[]{:S(2)}, u32[]{:S(2)}) collective-permute-start(bf16[6,96,768]{2,1,0:T(8,128)(2,1)} %bitcast.13), channel_id=1, source_target_pairs={{0,1},{1,0},{2,3},{3,2},{4,5},{5,4},{6,7},{7,6},{8,9},{9,8},{10,11... | collective-permute-start | bytes 2654216 | tf_op jit(solution)/shard_map/ppermute | solution.py:223
  1.1 0.1 collective-permute-start.2
  1.2 0.4 collective-permute-start.9
  1.7 1.2 %copy-done = bf16[1,6,96,768]{3,2,1,0:T(8,128)(2,1)S(1)} copy-done((bf16[1,6,96,768]{3,2,1,0:T(8,128)(2,1)S(1)}, bf16[1,6,96,768]{3,2,1,0:T(8,128)(2,1)}, u32[]{:S(2)}) %copy-start) | copy-done | bytes 884760
  2.8 0.7 %copy-done.3 = s32[6]{0:T(128)S(1)} copy-done((s32[6]{0:T(128)S(1)}, s32[6]{0:T(128)}, u32[]{:S(2)}) %copy-start.3) | copy-done | bytes 48
  3.5 0.6 %shard_map.85.mine_ref = bf16[4,96,768]{2,1,0:T(8,128)(2,1)S(1)} custom-call(s32[6]{0:T(128)S(1)} %copy-done.3, bf16[6,96,768]{2,1,0:T(8,128)(2,1)S(1)} %bitcast.14), custom_call_target="tpu_custom_call" | custom-call | tf_op jit(solution)/shard_map/pallas_call | solution.py:235
  4.1 0.0 copy-start.2
  4.1 0.0 collective-permute-done.theirs_ref
  4.1 0.7 %shard_map.86 = (bf16[96,768]{1,0:T(8,128)(2,1)S(1)}, bf16[96,768]{1,0:T(8,128)(2,1)S(1)}, bf16[96,768]{1,0:T(8,128)(2,1)S(1)}, bf16[96,768]{1,0:T(8,128)(2,1)S(1)}) custom-call(s32[6]{0:T(128)S(1)} %copy-done.3, bf16[4,96,768]{2,1,0:T(8,128)(2,1)S(1)} %shard_map.85.mine_ref, bf16[6,96,768]{2,1,0:T(8,128)(2,1)S(1)} %collective-permute-done.theirs_ref), custom_call_target="tpu_custom_call" | custom-call | tf_op jit(solution)/shard_map/pallas_call | solution.py:235
  4.8 2.7 %collective-permute-start.1 = (bf16[96,768]{1,0:T(8,128)(2,1)S(1)}, bf16[96,768]{1,0:T(8,128)(2,1)S(1)}, u32[]{:S(2)}, u32[]{:S(2)}) collective-permute-start(bf16[96,768]{1,0:T(8,128)(2,1)S(1)} %get-tuple-element.25), channel_id=1, source_target_pairs={{0,4},{1,13},{2,6},{3,15},{4,0},{5,9},{6,2},{7,11},{8,12},{9,5},{1... | collective-permute-start | bytes 442376 | tf_op jit(solution)/shard_map/ppermute | solution.py:229
  7.5 1.5 %collective-permute-start.4 = (bf16[96,768]{1,0:T(8,128)(2,1)S(1)}, bf16[96,768]{1,0:T(8,128)(2,1)S(1)}, u32[]{:S(2)}, u32[]{:S(2)}) collective-permute-start(bf16[96,768]{1,0:T(8,128)(2,1)S(1)} %get-tuple-element.31), channel_id=1, source_target_pairs={{0,2},{1,11},{2,0},{3,9},{4,6},{5,15},{6,4},{7,13},{8,10},{9,3},{1... | collective-permute-start | bytes 442376 | tf_op jit(solution)/shard_map/ppermute | solution.py:229
  9.0 0.7 %collective-permute-start.6 = (bf16[96,768]{1,0:T(8,128)(2,1)S(1)}, bf16[96,768]{1,0:T(8,128)(2,1)S(1)}, u32[]{:S(2)}, u32[]{:S(2)}) collective-permute-start(bf16[96,768]{1,0:T(8,128)(2,1)S(1)} %get-tuple-element.32), channel_id=1, source_target_pairs={{0,0},{1,9},{2,2},{3,11},{4,4},{5,13},{6,6},{7,15},{8,8},{9,1},{10... | collective-permute-start | bytes 442376 | tf_op jit(solution)/shard_map/ppermute | solution.py:229
  9.7 0.0 collective-permute-done.2.other_ref
  9.7 0.1 collective-permute-start.8
  9.8 1.6 %shard_map.87 = (bf16[768,672]{1,0:T(8,128)(2,1)S(1)}, bf16[768,96]{1,0:T(8,128)(2,1)S(1)}) custom-call(bf16[384,768]{1,0:T(8,128)(2,1)S(1)} %bitcast.16, bf16[384,768]{1,0:T(8,128)(2,1)S(1)} %collective-permute-done.2.other_ref), custom_call_target="tpu_custom_call" | custom-call | tf_op jit(solution)/shard_map/pallas_call | solution.py:235
  11.4 0.0 collective-permute-done.1.refs_0_
  11.4 5.3 %collective-permute-start.3 = (bf16[96,768]{1,0:T(8,128)(2,1)S(1)}, bf16[96,768]{1,0:T(8,128)(2,1)S(1)}, u32[]{:S(2)}, u32[]{:S(2)}) collective-permute-start(bf16[96,768]{1,0:T(8,128)(2,1)S(1)} %collective-permute-done.1.refs_0_), channel_id=1, source_target_pairs={{0,1},{1,0},{2,3},{3,2},{4,5},{5,4},{6,7},{7,6},{8,9},{9,8},{10,11... | collective-permute-start | bytes 442376 | tf_op jit(solution)/shard_map/ppermute | solution.py:223
  16.7 0.0 collective-permute-done.4.refs_2_.refs_1_
  16.7 1.1 %collective-permute-start.5 = (bf16[96,768]{1,0:T(8,128)(2,1)S(1)}, bf16[96,768]{1,0:T(8,128)(2,1)S(1)}, u32[]{:S(2)}, u32[]{:S(2)}) collective-permute-start(bf16[96,768]{1,0:T(8,128)(2,1)S(1)} %collective-permute-done.4.refs_2_.refs_1_), channel_id=1, source_target_pairs={{0,1},{1,0},{2,3},{3,2},{4,5},{5,4},{6,7},{7,6},{8,9},{9,8},{10,11... | collective-permute-start | bytes 442376 | tf_op jit(solution)/shard_map/ppermute | solution.py:223
  17.8 0.0 collective-permute-done.6.refs_4_.refs_2_
  17.8 3.6 %collective-permute-start.7 = (bf16[96,768]{1,0:T(8,128)(2,1)S(1)}, bf16[96,768]{1,0:T(8,128)(2,1)S(1)}, u32[]{:S(2)}, u32[]{:S(2)}) collective-permute-start(bf16[96,768]{1,0:T(8,128)(2,1)S(1)} %collective-permute-done.6.refs_4_.refs_2_), channel_id=1, source_target_pairs={{0,1},{1,0},{2,3},{3,2},{4,5},{5,4},{6,7},{7,6},{8,9},{9,8},{10,11... | collective-permute-start | bytes 442376 | tf_op jit(solution)/shard_map/ppermute | solution.py:223
  21.5 0.0 collective-permute-done.8.refs_6_.refs_3_
  21.5 0.3 collective-permute-start.10
  21.8 0.0 collective-permute-done.3.refs_1_.refs_4_
  21.8 0.0 collective-permute-done.5.refs_3_.refs_5_
  21.8 0.7 %collective-permute-done.7.refs_5_.refs_6_ = bf16[96,768]{1,0:T(8,128)(2,1)S(1)} collective-permute-done((bf16[96,768]{1,0:T(8,128)(2,1)S(1)}, bf16[96,768]{1,0:T(8,128)(2,1)S(1)}, u32[]{:S(2)}, u32[]{:S(2)}) %collective-permute-start.7) | collective-permute-done | bytes 147488 | tf_op jit(solution)/shard_map/ppermute | solution.py:223
  22.5 1.1 %shard_map.88 = (f32[768,768]{1,0:T(8,128)S(1)}, f32[8,128]{1,0:T(8,128)S(1)}) custom-call(bf16[768,672]{1,0:T(8,128)(2,1)S(1)} %get-tuple-element.29.left_ref, bf16[96,768]{1,0:T(8,128)(2,1)S(1)} %collective-permute-done.1.refs_0_, bf16[96,768]{1,0:T(8,128)(2,1)S(1)} %collective-permute-done.3.refs_1_.refs_4_, ...), custom_call_target="tpu_custom_call" | custom-call | tf_op jit(solution)/shard_map/pallas_call | solution.py:235
  23.6 0.0 copy-start.4
  23.6 0.0 copy-start.5
  23.6 0.0 copy-start.6
  23.6 0.0 collective-permute-done.10.slab_ref.refs_7_
  23.6 1.9 %shard_map.89 = (bf16[2,96,384]{2,1,0:T(8,128)(2,1)S(1)}, bf16[2,96,384]{2,1,0:T(8,128)(2,1)S(1)}, bf16[2,96,384]{2,1,0:T(8,128)(2,1)S(1)}, bf16[96,384]{1,0:T(8,128)(2,1)S(1)}, bf16[96,384]{1,0:T(8,128)(2,1)S(1)}) custom-call(bf16[768,96]{1,0:T(8,128)(2,1)S(1)} %get-tuple-element.28.left_ref, f32[768,768]{1,0:T(8,128)S(1)} %get-tuple-element.34.total_ref, ...), custom_call_target="tpu_custom_call" | custom-call | tf_op jit(solution)/shard_map/pallas_call | solution.py:235
  25.5 1.7 %collective-permute-start.11 = (bf16[2,96,384]{2,1,0:T(8,128)(2,1)S(1)}, bf16[2,96,384]{2,1,0:T(8,128)(2,1)S(1)}, u32[]{:S(2)}, u32[]{:S(2)}) collective-permute-start(bf16[2,96,384]{2,1,0:T(8,128)(2,1)S(1)} %get-tuple-element.36), channel_id=1, source_target_pairs={{0,4},{1,13},{2,6},{3,15},{4,0},{5,9},{6,2},{7,11},{8,12},{9,5},{1... | collective-permute-start | bytes 442376 | tf_op jit(solution)/shard_map/ppermute | solution.py:229
  27.2 1.0 %collective-permute-start.12 = (bf16[2,96,384]{2,1,0:T(8,128)(2,1)S(1)}, bf16[2,96,384]{2,1,0:T(8,128)(2,1)S(1)}, u32[]{:S(2)}, u32[]{:S(2)}) collective-permute-start(bf16[2,96,384]{2,1,0:T(8,128)(2,1)S(1)} %get-tuple-element.39), channel_id=1, source_target_pairs={{0,2},{1,11},{2,0},{3,9},{4,6},{5,15},{6,4},{7,13},{8,10},{9,3},{1... | collective-permute-start | bytes 442376 | tf_op jit(solution)/shard_map/ppermute | solution.py:229
  28.2 0.7 %collective-permute-start.13 = (bf16[2,96,384]{2,1,0:T(8,128)(2,1)S(1)}, bf16[2,96,384]{2,1,0:T(8,128)(2,1)S(1)}, u32[]{:S(2)}, u32[]{:S(2)}) collective-permute-start(bf16[2,96,384]{2,1,0:T(8,128)(2,1)S(1)} %get-tuple-element.40), channel_id=1, source_target_pairs={{0,0},{1,9},{2,2},{3,11},{4,4},{5,13},{6,6},{7,15},{8,8},{9,1},{10... | collective-permute-start | bytes 442376 | tf_op jit(solution)/shard_map/ppermute | solution.py:229
  28.9 0.9 %collective-permute-start.14 = (bf16[96,384]{1,0:T(8,128)(2,1)S(1)}, bf16[96,384]{1,0:T(8,128)(2,1)S(1)}, u32[]{:S(2)}, u32[]{:S(2)}) collective-permute-start(bf16[96,384]{1,0:T(8,128)(2,1)S(1)} %get-tuple-element.45), channel_id=1, source_target_pairs={{0,6},{1,15},{2,4},{3,13},{4,2},{5,11},{6,0},{7,9},{8,14},{9,7},{1... | collective-permute-start | bytes 221192 | tf_op jit(solution)/shard_map/ppermute | solution.py:229
  29.8 4.3 %collective-permute-start.18 = (bf16[96,384]{1,0:T(8,128)(2,1)S(1)}, bf16[96,384]{1,0:T(8,128)(2,1)S(1)}, u32[]{:S(2)}, u32[]{:S(2)}) collective-permute-start(bf16[96,384]{1,0:T(8,128)(2,1)S(1)} %get-tuple-element.46), channel_id=1, source_target_pairs={{0,7},{1,14},{2,5},{3,12},{4,3},{5,10},{6,1},{7,8},{8,15},{9,6},{1... | collective-permute-start | bytes 221192 | tf_op jit(solution)/shard_map/ppermute | solution.py:229
  34.2 0.0 collective-permute-done.11.after_ref.refs_0_
  34.2 2.6 %shard_map.90 = (bf16[384,768]{1,0:T(8,128)(2,1)}, bf16[384,768]{1,0:T(8,128)(2,1)}) custom-call(s32[6]{0:T(128)S(1)} %copy-done.4, bf16[384,768]{1,0:T(8,128)(2,1)S(1)} %bitcast.19, bf16[384,768]{1,0:T(8,128)(2,1)S(1)} %bitcast.20, bf16[2,96,384]{2,1,0:T(8,128)(2,1)S(1)} %collective-permute-done.11.after_ref.refs_0_, ...), custom_call_target="tpu_custom_call" | custom-call | flops 905969664 | bytes 2359296 | tf_op jit(solution)/shard_map/pallas_call | solution.py:235
  36.8 0.0 collective-permute-done.12.refs_1_
  36.8 0.0 collective-permute-done.13.refs_2_
  36.8 4.0 %collective-permute-start.16 = (bf16[96,384]{1,0:T(8,128)(2,1)S(1)}, bf16[96,384]{1,0:T(8,128)(2,1)S(1)}, u32[]{:S(2)}, u32[]{:S(2)}) collective-permute-start(bf16[96,384]{1,0:T(8,128)(2,1)S(1)} %slice_bitcast_fusion.2), channel_id=1, source_target_pairs={{0,1},{1,0},{2,3},{3,2},{4,5},{5,4},{6,7},{7,6},{8,9},{9,8},{10,11... | collective-permute-start | bytes 221192 | tf_op jit(solution)/shard_map/ppermute | solution.py:223
  40.8 0.1 collective-permute-start.17
  40.8 0.6 %collective-permute-start.15 = (bf16[96,384]{1,0:T(8,128)(2,1)S(1)}, bf16[96,384]{1,0:T(8,128)(2,1)S(1)}, u32[]{:S(2)}, u32[]{:S(2)}) collective-permute-start(bf16[96,384]{1,0:T(8,128)(2,1)S(1)} %slice_bitcast_fusion), channel_id=1, source_target_pairs={{0,1},{1,0},{2,3},{3,2},{4,5},{5,4},{6,7},{7,6},{8,9},{9,8},{10,11... | collective-permute-start | bytes 221192 | tf_op jit(solution)/shard_map/ppermute | solution.py:223
  41.4 0.2 collective-permute-done.16.refs_5_
  41.7 0.4 collective-permute-done.17.refs_6_
  42.1 0.2 collective-permute-done.15.refs_4_
  42.3 1.4 %shard_map.91 = bf16[6,96,384]{2,1,0:T(8,128)(2,1)} custom-call(s32[6]{0:T(128)S(1)} %copy-done.4, bf16[2,96,384]{2,1,0:T(8,128)(2,1)S(1)} %collective-permute-done.11.after_ref.refs_0_, bf16[2,96,384]{2,1,0:T(8,128)(2,1)S(1)} %collective-permute-done.12.refs_1_, bf16[2,96,384]{2,1,0:T(8,128)(2,1)S(1)} %collective-permute-done.13.refs_2_, ...), custom_call_target="tpu_custom_call" | custom-call | tf_op jit(solution)/shard_map/pallas_call | solution.py:235
  (14 shorter events, 0.0 us)
Async XLA Ops:
  0.6 3.5 %collective-permute-start = (bf16[6,96,768]{2,1,0:T(8,128)(2,1)}, bf16[6,96,768]{2,1,0:T(8,128)(2,1)S(1)}, u32[]{:S(2)}, u32[]{:S(2)}) collective-permute-start(bf16[6,96,768]{2,1,0:T(8,128)(2,1)} %bitcast.13), channel_id=1, source_target_pairs={{0,1},{1,0},{2,3},{3,2},{4,5},{5,4},{6,7},{7,6},{8,9},{9,8},{10,11... | collective-permute-start | bytes 2654216 | tf_op jit(solution)/shard_map/ppermute | solution.py:223
  1.1 8.5 %collective-permute-start.2 = (bf16[384,768]{1,0:T(8,128)(2,1)}, bf16[384,768]{1,0:T(8,128)(2,1)S(1)}, u32[]{:S(2)}, u32[]{:S(2)}) collective-permute-start(bf16[384,768]{1,0:T(8,128)(2,1)} %bitcast.15), channel_id=1, source_target_pairs={{0,1},{1,0},{2,3},{3,2},{4,5},{5,4},{6,7},{7,6},{8,9},{9,8},{10,11... | collective-permute-start | bytes 1769480 | tf_op jit(solution)/shard_map/ppermute | solution.py:223
  1.2 22.4 %collective-permute-start.9 = (bf16[768,384]{1,0:T(8,128)(2,1)}, bf16[768,384]{1,0:T(8,128)(2,1)S(1)}, u32[]{:S(2)}, u32[]{:S(2)}) collective-permute-start(bf16[768,384]{1,0:T(8,128)(2,1)} %bitcast.17), channel_id=1, source_target_pairs={{0,1},{1,0},{2,3},{3,2},{4,5},{5,4},{6,7},{7,6},{8,9},{9,8},{10,11... | collective-permute-start | bytes 1769480 | tf_op jit(solution)/shard_map/ppermute | solution.py:223
  1.7 1.2 %copy-start = (bf16[1,6,96,768]{3,2,1,0:T(8,128)(2,1)S(1)}, bf16[1,6,96,768]{3,2,1,0:T(8,128)(2,1)}, u32[]{:S(2)}) copy-start(bf16[1,6,96,768]{3,2,1,0:T(8,128)(2,1)} %param.6) | copy-start | bytes 2654212
  2.8 0.7 %copy-start.3 = (s32[6]{0:T(128)S(1)}, s32[6]{0:T(128)}, u32[]{:S(2)}) copy-start(s32[6]{0:T(128)} %owner_ref.7) | copy-start | bytes 76
  3.5 6.3 %copy-start.1 = (bf16[1,384,768]{2,1,0:T(8,128)(2,1)S(1)}, bf16[1,384,768]{2,1,0:T(8,128)(2,1)}, u32[]{:S(2)}) copy-start(bf16[1,384,768]{2,1,0:T(8,128)(2,1)} %param.10) | copy-start | bytes 1769476
  4.1 19.5 %copy-start.2 = (bf16[1,768,384]{2,1,0:T(8,128)(2,1)S(1)}, bf16[1,768,384]{2,1,0:T(8,128)(2,1)}, u32[]{:S(2)}) copy-start(bf16[1,768,384]{2,1,0:T(8,128)(2,1)} %param.11) | copy-start | bytes 1769476
  4.8 6.6 %collective-permute-start.1 = (bf16[96,768]{1,0:T(8,128)(2,1)S(1)}, bf16[96,768]{1,0:T(8,128)(2,1)S(1)}, u32[]{:S(2)}, u32[]{:S(2)}) collective-permute-start(bf16[96,768]{1,0:T(8,128)(2,1)S(1)} %get-tuple-element.25), channel_id=1, source_target_pairs={{0,4},{1,13},{2,6},{3,15},{4,0},{5,9},{6,2},{7,11},{8,12},{9,5},{1... | collective-permute-start | bytes 442376 | tf_op jit(solution)/shard_map/ppermute | solution.py:229
  7.5 9.1 %collective-permute-start.4 = (bf16[96,768]{1,0:T(8,128)(2,1)S(1)}, bf16[96,768]{1,0:T(8,128)(2,1)S(1)}, u32[]{:S(2)}, u32[]{:S(2)}) collective-permute-start(bf16[96,768]{1,0:T(8,128)(2,1)S(1)} %get-tuple-element.31), channel_id=1, source_target_pairs={{0,2},{1,11},{2,0},{3,9},{4,6},{5,15},{6,4},{7,13},{8,10},{9,3},{1... | collective-permute-start | bytes 442376 | tf_op jit(solution)/shard_map/ppermute | solution.py:229
  9.0 8.8 %collective-permute-start.6 = (bf16[96,768]{1,0:T(8,128)(2,1)S(1)}, bf16[96,768]{1,0:T(8,128)(2,1)S(1)}, u32[]{:S(2)}, u32[]{:S(2)}) collective-permute-start(bf16[96,768]{1,0:T(8,128)(2,1)S(1)} %get-tuple-element.32), channel_id=1, source_target_pairs={{0,0},{1,9},{2,2},{3,11},{4,4},{5,13},{6,6},{7,15},{8,8},{9,1},{10... | collective-permute-start | bytes 442376 | tf_op jit(solution)/shard_map/ppermute | solution.py:229
  9.7 11.8 %collective-permute-start.8 = (bf16[96,768]{1,0:T(8,128)(2,1)S(1)}, bf16[96,768]{1,0:T(8,128)(2,1)S(1)}, u32[]{:S(2)}, u32[]{:S(2)}) collective-permute-start(bf16[96,768]{1,0:T(8,128)(2,1)S(1)} %get-tuple-element.33), channel_id=1, source_target_pairs={{0,6},{1,15},{2,4},{3,13},{4,2},{5,11},{6,0},{7,9},{8,14},{9,7},{1... | collective-permute-start | bytes 442376 | tf_op jit(solution)/shard_map/ppermute | solution.py:229
  11.4 10.4 %collective-permute-start.3 = (bf16[96,768]{1,0:T(8,128)(2,1)S(1)}, bf16[96,768]{1,0:T(8,128)(2,1)S(1)}, u32[]{:S(2)}, u32[]{:S(2)}) collective-permute-start(bf16[96,768]{1,0:T(8,128)(2,1)S(1)} %collective-permute-done.1.refs_0_), channel_id=1, source_target_pairs={{0,1},{1,0},{2,3},{3,2},{4,5},{5,4},{6,7},{7,6},{8,9},{9,8},{10,11... | collective-permute-start | bytes 442376 | tf_op jit(solution)/shard_map/ppermute | solution.py:223
  16.7 5.1 %collective-permute-start.5 = (bf16[96,768]{1,0:T(8,128)(2,1)S(1)}, bf16[96,768]{1,0:T(8,128)(2,1)S(1)}, u32[]{:S(2)}, u32[]{:S(2)}) collective-permute-start(bf16[96,768]{1,0:T(8,128)(2,1)S(1)} %collective-permute-done.4.refs_2_.refs_1_), channel_id=1, source_target_pairs={{0,1},{1,0},{2,3},{3,2},{4,5},{5,4},{6,7},{7,6},{8,9},{9,8},{10,11... | collective-permute-start | bytes 442376 | tf_op jit(solution)/shard_map/ppermute | solution.py:223
  17.8 4.7 %collective-permute-start.7 = (bf16[96,768]{1,0:T(8,128)(2,1)S(1)}, bf16[96,768]{1,0:T(8,128)(2,1)S(1)}, u32[]{:S(2)}, u32[]{:S(2)}) collective-permute-start(bf16[96,768]{1,0:T(8,128)(2,1)S(1)} %collective-permute-done.6.refs_4_.refs_2_), channel_id=1, source_target_pairs={{0,1},{1,0},{2,3},{3,2},{4,5},{5,4},{6,7},{7,6},{8,9},{9,8},{10,11... | collective-permute-start | bytes 442376 | tf_op jit(solution)/shard_map/ppermute | solution.py:223
  21.5 2.1 %collective-permute-start.10 = (bf16[96,768]{1,0:T(8,128)(2,1)S(1)}, bf16[96,768]{1,0:T(8,128)(2,1)S(1)}, u32[]{:S(2)}, u32[]{:S(2)}) collective-permute-start(bf16[96,768]{1,0:T(8,128)(2,1)S(1)} %collective-permute-done.8.refs_6_.refs_3_), channel_id=1, source_target_pairs={{0,1},{1,0},{2,3},{3,2},{4,5},{5,4},{6,7},{7,6},{8,9},{9,8},{10,11... | collective-permute-start | bytes 442376 | tf_op jit(solution)/shard_map/ppermute | solution.py:223
  23.6 10.6 %copy-start.4 = (s32[6]{0:T(128)S(1)}, s32[6]{0:T(128)}, u32[]{:S(2)}) copy-start(s32[6]{0:T(128)} %owner_ref.7) | copy-start | bytes 76
  23.6 10.6 %copy-start.5 = (bf16[1,384,768]{2,1,0:T(8,128)(2,1)S(1)}, bf16[1,384,768]{2,1,0:T(8,128)(2,1)}, u32[]{:S(2)}) copy-start(bf16[1,384,768]{2,1,0:T(8,128)(2,1)} %param.8) | copy-start | bytes 1769476
  23.6 10.6 %copy-start.6 = (bf16[1,384,768]{2,1,0:T(8,128)(2,1)S(1)}, bf16[1,384,768]{2,1,0:T(8,128)(2,1)}, u32[]{:S(2)}) copy-start(bf16[1,384,768]{2,1,0:T(8,128)(2,1)} %param.9) | copy-start | bytes 1769476
  25.5 8.6 %collective-permute-start.11 = (bf16[2,96,384]{2,1,0:T(8,128)(2,1)S(1)}, bf16[2,96,384]{2,1,0:T(8,128)(2,1)S(1)}, u32[]{:S(2)}, u32[]{:S(2)}) collective-permute-start(bf16[2,96,384]{2,1,0:T(8,128)(2,1)S(1)} %get-tuple-element.36), channel_id=1, source_target_pairs={{0,4},{1,13},{2,6},{3,15},{4,0},{5,9},{6,2},{7,11},{8,12},{9,5},{1... | collective-permute-start | bytes 442376 | tf_op jit(solution)/shard_map/ppermute | solution.py:229
  27.2 9.5 %collective-permute-start.12 = (bf16[2,96,384]{2,1,0:T(8,128)(2,1)S(1)}, bf16[2,96,384]{2,1,0:T(8,128)(2,1)S(1)}, u32[]{:S(2)}, u32[]{:S(2)}) collective-permute-start(bf16[2,96,384]{2,1,0:T(8,128)(2,1)S(1)} %get-tuple-element.39), channel_id=1, source_target_pairs={{0,2},{1,11},{2,0},{3,9},{4,6},{5,15},{6,4},{7,13},{8,10},{9,3},{1... | collective-permute-start | bytes 442376 | tf_op jit(solution)/shard_map/ppermute | solution.py:229
  28.2 8.5 %collective-permute-start.13 = (bf16[2,96,384]{2,1,0:T(8,128)(2,1)S(1)}, bf16[2,96,384]{2,1,0:T(8,128)(2,1)S(1)}, u32[]{:S(2)}, u32[]{:S(2)}) collective-permute-start(bf16[2,96,384]{2,1,0:T(8,128)(2,1)S(1)} %get-tuple-element.40), channel_id=1, source_target_pairs={{0,0},{1,9},{2,2},{3,11},{4,4},{5,13},{6,6},{7,15},{8,8},{9,1},{10... | collective-permute-start | bytes 442376 | tf_op jit(solution)/shard_map/ppermute | solution.py:229
  28.9 12.5 %collective-permute-start.14 = (bf16[96,384]{1,0:T(8,128)(2,1)S(1)}, bf16[96,384]{1,0:T(8,128)(2,1)S(1)}, u32[]{:S(2)}, u32[]{:S(2)}) collective-permute-start(bf16[96,384]{1,0:T(8,128)(2,1)S(1)} %get-tuple-element.45), channel_id=1, source_target_pairs={{0,6},{1,15},{2,4},{3,13},{4,2},{5,11},{6,0},{7,9},{8,14},{9,7},{1... | collective-permute-start | bytes 221192 | tf_op jit(solution)/shard_map/ppermute | solution.py:229
  29.8 11.6 %collective-permute-start.18 = (bf16[96,384]{1,0:T(8,128)(2,1)S(1)}, bf16[96,384]{1,0:T(8,128)(2,1)S(1)}, u32[]{:S(2)}, u32[]{:S(2)}) collective-permute-start(bf16[96,384]{1,0:T(8,128)(2,1)S(1)} %get-tuple-element.46), channel_id=1, source_target_pairs={{0,7},{1,14},{2,5},{3,12},{4,3},{5,10},{6,1},{7,8},{8,15},{9,6},{1... | collective-permute-start | bytes 221192 | tf_op jit(solution)/shard_map/ppermute | solution.py:229
  36.8 4.9 %collective-permute-start.16 = (bf16[96,384]{1,0:T(8,128)(2,1)S(1)}, bf16[96,384]{1,0:T(8,128)(2,1)S(1)}, u32[]{:S(2)}, u32[]{:S(2)}) collective-permute-start(bf16[96,384]{1,0:T(8,128)(2,1)S(1)} %slice_bitcast_fusion.2), channel_id=1, source_target_pairs={{0,1},{1,0},{2,3},{3,2},{4,5},{5,4},{6,7},{7,6},{8,9},{9,8},{10,11... | collective-permute-start | bytes 221192 | tf_op jit(solution)/shard_map/ppermute | solution.py:223
  40.8 1.3 %collective-permute-start.17 = (bf16[96,384]{1,0:T(8,128)(2,1)S(1)}, bf16[96,384]{1,0:T(8,128)(2,1)S(1)}, u32[]{:S(2)}, u32[]{:S(2)}) collective-permute-start(bf16[96,384]{1,0:T(8,128)(2,1)S(1)} %slice_bitcast_fusion.1), channel_id=1, source_target_pairs={{0,1},{1,0},{2,3},{3,2},{4,5},{5,4},{6,7},{7,6},{8,9},{9,8},{10,11... | collective-permute-start | bytes 221192 | tf_op jit(solution)/shard_map/ppermute | solution.py:223
  40.8 1.5 %collective-permute-start.15 = (bf16[96,384]{1,0:T(8,128)(2,1)S(1)}, bf16[96,384]{1,0:T(8,128)(2,1)S(1)}, u32[]{:S(2)}, u32[]{:S(2)}) collective-permute-start(bf16[96,384]{1,0:T(8,128)(2,1)S(1)} %slice_bitcast_fusion), channel_id=1, source_target_pairs={{0,1},{1,0},{2,3},{3,2},{4,5},{5,4},{6,7},{7,6},{8,9},{9,8},{10,11... | collective-permute-start | bytes 221192 | tf_op jit(solution)/shard_map/ppermute | solution.py:223

commit v8 on v7

--- a/solution.py
+++ b/solution.py
@@ -83,15 +83,14 @@
     return jnp.sum(jnp.sum(wide * wide, axis=0, keepdims=True), axis=1, keepdims=True)
 
 
-def fetch_kernel(codes, owner_ref, gradient_ref, out_ref):
-    for k in range(out_ref.shape[0]):
-        out_ref[k] = gradient_ref[sent_block(codes, owner_ref, k)]
+def fetch_kernel(gradient_ref, out_ref):
+    out_ref[...] = gradient_ref[...]
 
 
 def pick_kernel(codes, owner_ref, mine_ref, theirs_ref, *out_refs):
     for k, out_ref in enumerate(out_refs):
-        other = theirs_ref[sent_block(codes, owner_ref, k)]
-        total = mine_ref[k].astype(jnp.float32) + other.astype(jnp.float32)
+        b = sent_block(codes, owner_ref, k)
+        total = mine_ref[b].astype(jnp.float32) + theirs_ref[b].astype(jnp.float32)
         out_ref[...] = total.astype(out_ref.dtype)
 
 
@@ -135,13 +134,17 @@
     grad_sq_ref[...] = jnp.broadcast_to(squares(stacked_ref[...]), grad_sq_ref.shape)
 
 
-def finish_kernel(left_ref, total_ref, begun_sq_ref, own_ref, other_ref, slab_ref, *refs):
-    *whole_refs, keep_ref, pass_ref, side_ref, both_ref = refs
-    last = slab_ref[...]
+def finish_kernel(count, left_ref, total_ref, begun_sq_ref, own_ref, other_ref, *refs):
+    slabs = refs[:count]
+    *whole_refs, keep_ref, pass_ref, stacked_ref, side_ref, both_ref = refs[count:]
+    slab = slabs[0].shape[0]
+    for n, ref in enumerate(slabs):
+        stacked_ref[n * slab:(n + 1) * slab, :] = ref[...]
+    last = stacked_ref[...]
     side = total_ref[...] + jnp.dot(left_ref[...], last, preferred_element_type=jnp.float32)
     side_ref[...] = side.astype(side_ref.dtype)
     grad_sq = begun_sq_ref[0:1, 0:1] + squares(last)
-    half, slab = own_ref.shape[1], slab_ref.shape[0]
+    half = own_ref.shape[1]
     side_sq = jnp.zeros((1, 1), jnp.float32)
     for n, ref in enumerate((own_ref, other_ref)):
         both = jnp.dot(side_ref[...], ref[...], preferred_element_type=jnp.float32)
@@ -217,7 +220,8 @@
     blocks, slab, width = gradients.shape[1:]
     half_rows = left_gram.shape[1]
     slots = [(k, other) for k in range(rounds) for other in (False, True)]
-    slots = (slots[:-1], slots[-1:])
+    after = [(k, True) for k in range(max(last - 1, 0), rounds)]
+    slots = ([x for x in slots if x not in after], after)
 
     def other_core(x):
         return lax.ppermute(x, "replica", [(0, 1), (1, 0)])
@@ -231,18 +235,18 @@
     def shape(dims, dtype=jnp.bfloat16):
         return jax.ShapeDtypeStruct(dims, dtype)
 
-    def call(kernel, out_shape, in_specs, *args, cost_estimate=LIGHT, **options):
+    def call(kernel, out_shape, in_specs, *args, params=PARAMS, cost_estimate=LIGHT, **options):
         return pl.pallas_call(
-            kernel, out_shape=out_shape, in_specs=in_specs, compiler_params=PARAMS,
+            kernel, out_shape=out_shape, in_specs=in_specs, compiler_params=params,
             cost_estimate=cost_estimate, **options
         )(*args)
 
     other_gradient = other_core(gradients[0])
+    block_owner = other_core(block_owner)
     fetched = call(
-        functools.partial(fetch_kernel, codes), shape((rounds, slab, width)), [SMEM, VMEM],
-        block_owner, gradients[0], out_specs=VMEM,
-    )
-    outgoing = call(
+        fetch_kernel, shape((blocks, slab, width)), [VMEM], gradients[0], out_specs=VMEM
+    )
+    *outgoing, = call(
         functools.partial(pick_kernel, codes), [shape((slab, width))] * rounds,
         [SMEM, VMEM, VMEM], block_owner, fetched, other_gradient, out_specs=[VMEM] * rounds,
     )
@@ -264,11 +268,13 @@
         scratch_shapes=[pltpu.VMEM((len(sooner) * slab, width), jnp.bfloat16)],
     )
     *whole, keep, cross = call(
-        finish_kernel,
-        [shape((2, slab, width // 2))] * last + [shape((slab, width // 2))] * 2, [VMEM] * 6,
-        left_last, begun, begun_sq, right_root[0], other_right, theirs[last],
+        functools.partial(finish_kernel, len(after)),
+        [shape((2, slab, width // 2))] * last + [shape((slab, width // 2))] * 2,
+        [VMEM] * (5 + len(after)),
+        left_last, begun, begun_sq, right_root[0], other_right, *[theirs[k] for k, _ in after],
         out_specs=[VMEM] * (last + 2),
         scratch_shapes=[
+            pltpu.VMEM((len(after) * slab, width), jnp.bfloat16),
             pltpu.VMEM((2 * half_rows, width), jnp.bfloat16),
             pltpu.VMEM((2, half_rows, width // 2), jnp.float32),
         ],
@@ -287,9 +293,7 @@
             transcendentals=0,
         ),
     )
-    left_new, right_new, *returned[1:last] = lax.optimization_barrier(
-        (left_new, right_new, *returned[1:last])
-    )
+    left_new, right_new, returned[1] = lax.optimization_barrier((left_new, right_new, returned[1]))
     passed = [other_core(x[1]) for x in returned[:last]] + [crossed]
     update = call(
         functools.partial(place_kernel, codes), shape((blocks, slab, width // 2)),

time: 43.9 us -> 43.9 us (level)
  waiting for transfers between devices: 1.63 us -> 3.06 us
  local copies, waits for them, and re-layouts: 1.88 us -> 1.22 us
  Pallas kernels: 9.81 us -> 9.29 us
    ppermute x10 -> x11, waiting for transfers between devices: 1.61 us -> 3.04 us  [other_core(): return lax.ppermute(x, 'replica', [(0, 1), (1, 0)])]
    ppermute x10 -> x11, starting transfers between devices: 16 us -> 14.8 us  [other_core(): return lax.ppermute(x, 'replica', [(0, 1), (1, 0)])]
    ppermute x9, starting transfers between devices: 13.6 us -> 14.5 us  [trade(): return lax.ppermute(x, ('shard', 'replica'), pairs)]
    unnamed x14 -> x10, local copies, waits for them, and re-layouts: 1.85 us -> 1.19 us
    pallas_call x7, Pallas kernels: 9.81 us -> 9.29 us  [call(): pl.pallas_call(kernel, out_shape=out_shape, in_specs=in_specs, compiler_p...]
  transfers between devices with their start and end apart: 19 -> 20, of which waited for: 4 -> 3; matrix products, arithmetic and copies ran while one was open for 0% -> 0% of each run, Pallas kernels for 15% -> 14%
where the time goes in v8:
time: 43.9 us; the launch traced here: 43.7 us
  starting transfers between devices  29.3 us (67%)
  Pallas kernels  9.29 us (21%)
  waiting for transfers between devices  3.06 us (7%)
  local copies, waits for them, and re-layouts  1.22 us (3%)
  between operations  0.79 us (2%)
    ppermute x11, starting transfers between devices, other_core(): return lax.ppermute(x, 'replica', [(0, 1), (1, 0)])  14.8 us
    ppermute x9, starting transfers between devices, trade(): return lax.ppermute(x, ('shard', 'replica'), pairs)  14.5 us
    pallas_call x7, Pallas kernels, call(): pl.pallas_call(kernel, out_shape=out_shape, in_specs=in_specs, compiler_p...  9.29 us
    ppermute x11, waiting for transfers between devices, other_core(): return lax.ppermute(x, 'replica', [(0, 1), (1, 0)])  3.04 us
    unnamed x10, local copies, waits for them, and re-layouts  1.19 us
  transfers between devices with their start and end apart: 20, of which 3 were waited for; matrix products, arithmetic and copies ran while one was open for 0% of the time, Pallas kernels for 14%

profile of v8, /device:TPU:0, one launch (start us, length us, event | category | flops | bytes accessed | tf_op | source)
XLA Modules:
  0.0 43.7 jit_solution(14510415167815818384)
XLA Ops:
  0.6 0.5 %collective-permute-start.1 = (bf16[6,96,768]{2,1,0:T(8,128)(2,1)}, bf16[6,96,768]{2,1,0:T(8,128)(2,1)S(1)}, u32[]{:S(2)}, u32[]{:S(2)}) collective-permute-start(bf16[6,96,768]{2,1,0:T(8,128)(2,1)} %bitcast.13), channel_id=1, source_target_pairs={{0,1},{1,0},{2,3},{3,2},{4,5},{5,4},{6,7},{7,6},{8,9},{9,8},{10,11... | collective-permute-start | bytes 2654216 | tf_op jit(solution)/shard_map/ppermute | solution.py:227
  1.1 0.1 collective-permute-start.3
  1.2 0.4 collective-permute-start.9
  1.7 0.1 collective-permute-start
  1.7 1.2 %copy-done = bf16[1,6,96,768]{3,2,1,0:T(8,128)(2,1)S(1)} copy-done((bf16[1,6,96,768]{3,2,1,0:T(8,128)(2,1)S(1)}, bf16[1,6,96,768]{3,2,1,0:T(8,128)(2,1)}, u32[]{:S(2)}) %copy-start) | copy-done | bytes 884760
  2.9 0.1 shard_map.85.mine_ref
  3.0 0.0 copy-start.1
  3.0 2.1 %collective-permute-done.owner_ref = s32[6]{0:T(128)S(1)} collective-permute-done((s32[6]{0:T(128)}, s32[6]{0:T(128)S(1)}, u32[]{:S(2)}, u32[]{:S(2)}) %collective-permute-start) | collective-permute-done | bytes 56 | tf_op jit(solution)/shard_map/ppermute | solution.py:227
  5.1 0.0 collective-permute-done.1.theirs_ref
  5.1 0.7 %shard_map.86 = (bf16[96,768]{1,0:T(8,128)(2,1)S(1)}, bf16[96,768]{1,0:T(8,128)(2,1)S(1)}, bf16[96,768]{1,0:T(8,128)(2,1)S(1)}, bf16[96,768]{1,0:T(8,128)(2,1)S(1)}) custom-call(s32[6]{0:T(128)S(1)} %collective-permute-done.owner_ref, bf16[6,96,768]{2,1,0:T(8,128)(2,1)S(1)} %shard_map.85.mine_ref, bf16[6,96,768]{2,1,0:T(8,128)(2,1)S(1)} %collective-permute-done.1.theirs_ref), custom_call_target="tpu_custom_call" | custom-call | tf_op jit(solution)/shard_map/pallas_call | solution.py:239
  5.8 3.0 %collective-permute-start.2 = (bf16[96,768]{1,0:T(8,128)(2,1)S(1)}, bf16[96,768]{1,0:T(8,128)(2,1)S(1)}, u32[]{:S(2)}, u32[]{:S(2)}) collective-permute-start(bf16[96,768]{1,0:T(8,128)(2,1)S(1)} %get-tuple-element.24), channel_id=1, source_target_pairs={{0,4},{1,13},{2,6},{3,15},{4,0},{5,9},{6,2},{7,11},{8,12},{9,5},{1... | collective-permute-start | bytes 442376 | tf_op jit(solution)/shard_map/ppermute | solution.py:233
  8.8 1.5 %collective-permute-start.5 = (bf16[96,768]{1,0:T(8,128)(2,1)S(1)}, bf16[96,768]{1,0:T(8,128)(2,1)S(1)}, u32[]{:S(2)}, u32[]{:S(2)}) collective-permute-start(bf16[96,768]{1,0:T(8,128)(2,1)S(1)} %get-tuple-element.30), channel_id=1, source_target_pairs={{0,2},{1,11},{2,0},{3,9},{4,6},{5,15},{6,4},{7,13},{8,10},{9,3},{1... | collective-permute-start | bytes 442376 | tf_op jit(solution)/shard_map/ppermute | solution.py:233
  10.3 0.7 %collective-permute-start.7 = (bf16[96,768]{1,0:T(8,128)(2,1)S(1)}, bf16[96,768]{1,0:T(8,128)(2,1)S(1)}, u32[]{:S(2)}, u32[]{:S(2)}) collective-permute-start(bf16[96,768]{1,0:T(8,128)(2,1)S(1)} %get-tuple-element.31), channel_id=1, source_target_pairs={{0,0},{1,9},{2,2},{3,11},{4,4},{5,13},{6,6},{7,15},{8,8},{9,1},{10... | collective-permute-start | bytes 442376 | tf_op jit(solution)/shard_map/ppermute | solution.py:233
  11.0 0.0 collective-permute-done.3.other_ref
  11.0 0.1 collective-permute-start.8
  11.1 1.6 %shard_map.87 = (bf16[768,576]{1,0:T(8,128)(2,1)S(1)}, bf16[768,192]{1,0:T(8,128)(2,1)S(1)}) custom-call(bf16[384,768]{1,0:T(8,128)(2,1)S(1)} %bitcast.18, bf16[384,768]{1,0:T(8,128)(2,1)S(1)} %collective-permute-done.3.other_ref), custom_call_target="tpu_custom_call" | custom-call | tf_op jit(solution)/shard_map/pallas_call | solution.py:239
  12.7 0.0 collective-permute-done.2.refs_0_
  12.7 5.0 %collective-permute-start.4 = (bf16[96,768]{1,0:T(8,128)(2,1)S(1)}, bf16[96,768]{1,0:T(8,128)(2,1)S(1)}, u32[]{:S(2)}, u32[]{:S(2)}) collective-permute-start(bf16[96,768]{1,0:T(8,128)(2,1)S(1)} %collective-permute-done.2.refs_0_), channel_id=1, source_target_pairs={{0,1},{1,0},{2,3},{3,2},{4,5},{5,4},{6,7},{7,6},{8,9},{9,8},{10,11... | collective-permute-start | bytes 442376 | tf_op jit(solution)/shard_map/ppermute | solution.py:227
  17.7 0.0 collective-permute-done.5.refs_2_.refs_1_
  17.7 1.1 %collective-permute-start.6 = (bf16[96,768]{1,0:T(8,128)(2,1)S(1)}, bf16[96,768]{1,0:T(8,128)(2,1)S(1)}, u32[]{:S(2)}, u32[]{:S(2)}) collective-permute-start(bf16[96,768]{1,0:T(8,128)(2,1)S(1)} %collective-permute-done.5.refs_2_.refs_1_), channel_id=1, source_target_pairs={{0,1},{1,0},{2,3},{3,2},{4,5},{5,4},{6,7},{7,6},{8,9},{9,8},{10,11... | collective-permute-start | bytes 442376 | tf_op jit(solution)/shard_map/ppermute | solution.py:227
  18.8 0.0 collective-permute-done.7.refs_4_.refs_2_
  18.8 3.5 %collective-permute-start.10 = (bf16[96,768]{1,0:T(8,128)(2,1)S(1)}, bf16[96,768]{1,0:T(8,128)(2,1)S(1)}, u32[]{:S(2)}, u32[]{:S(2)}) collective-permute-start(bf16[96,768]{1,0:T(8,128)(2,1)S(1)} %collective-permute-done.7.refs_4_.refs_2_), channel_id=1, source_target_pairs={{0,1},{1,0},{2,3},{3,2},{4,5},{5,4},{6,7},{7,6},{8,9},{9,8},{10,11... | collective-permute-start | bytes 442376 | tf_op jit(solution)/shard_map/ppermute | solution.py:227
  22.4 0.0 collective-permute-done.8.refs_5_.refs_3_
  22.4 0.4 collective-permute-start.11
  22.8 0.0 collective-permute-done.4.refs_1_.refs_4_
  22.8 0.0 collective-permute-done.6.refs_3_.refs_5_
  22.8 1.1 %shard_map.88 = (f32[768,768]{1,0:T(8,128)S(1)}, f32[8,128]{1,0:T(8,128)S(1)}) custom-call(bf16[768,576]{1,0:T(8,128)(2,1)S(1)} %get-tuple-element.28.left_ref, bf16[96,768]{1,0:T(8,128)(2,1)S(1)} %collective-permute-done.2.refs_0_, bf16[96,768]{1,0:T(8,128)(2,1)S(1)} %collective-permute-done.4.refs_1_.refs_4_, ...), custom_call_target="tpu_custom_call" | custom-call | tf_op jit(solution)/shard_map/pallas_call | solution.py:239
  23.9 0.0 copy-start.3
  23.9 0.0 copy-start.4
  23.9 0.0 collective-permute-done.9.other_ref
  23.9 0.0 collective-permute-done.10.refs_0_.refs_6_
  23.9 0.0 collective-permute-done.11.refs_1_.refs_7_
  23.9 1.9 %shard_map.89 = (bf16[2,96,384]{2,1,0:T(8,128)(2,1)S(1)}, bf16[2,96,384]{2,1,0:T(8,128)(2,1)S(1)}, bf16[2,96,384]{2,1,0:T(8,128)(2,1)S(1)}, bf16[96,384]{1,0:T(8,128)(2,1)S(1)}, bf16[96,384]{1,0:T(8,128)(2,1)S(1)}) custom-call(bf16[768,192]{1,0:T(8,128)(2,1)S(1)} %get-tuple-element.27.left_ref, f32[768,768]{1,0:T(8,128)S(1)} %get-tuple-element.33.total_ref, ...), custom_call_target="tpu_custom_call" | custom-call | tf_op jit(solution)/shard_map/pallas_call | solution.py:239
  25.9 2.2 %collective-permute-start.12 = (bf16[2,96,384]{2,1,0:T(8,128)(2,1)S(1)}, bf16[2,96,384]{2,1,0:T(8,128)(2,1)S(1)}, u32[]{:S(2)}, u32[]{:S(2)}) collective-permute-start(bf16[2,96,384]{2,1,0:T(8,128)(2,1)S(1)} %get-tuple-element.35), channel_id=1, source_target_pairs={{0,4},{1,13},{2,6},{3,15},{4,0},{5,9},{6,2},{7,11},{8,12},{9,5},{1... | collective-permute-start | bytes 442376 | tf_op jit(solution)/shard_map/ppermute | solution.py:233
  28.1 1.0 %collective-permute-start.13 = (bf16[2,96,384]{2,1,0:T(8,128)(2,1)S(1)}, bf16[2,96,384]{2,1,0:T(8,128)(2,1)S(1)}, u32[]{:S(2)}, u32[]{:S(2)}) collective-permute-start(bf16[2,96,384]{2,1,0:T(8,128)(2,1)S(1)} %get-tuple-element.38), channel_id=1, source_target_pairs={{0,2},{1,11},{2,0},{3,9},{4,6},{5,15},{6,4},{7,13},{8,10},{9,3},{1... | collective-permute-start | bytes 442376 | tf_op jit(solution)/shard_map/ppermute | solution.py:233
  29.1 0.7 %collective-permute-start.14 = (bf16[2,96,384]{2,1,0:T(8,128)(2,1)S(1)}, bf16[2,96,384]{2,1,0:T(8,128)(2,1)S(1)}, u32[]{:S(2)}, u32[]{:S(2)}) collective-permute-start(bf16[2,96,384]{2,1,0:T(8,128)(2,1)S(1)} %get-tuple-element.42), channel_id=1, source_target_pairs={{0,0},{1,9},{2,2},{3,11},{4,4},{5,13},{6,6},{7,15},{8,8},{9,1},{10... | collective-permute-start | bytes 442376 | tf_op jit(solution)/shard_map/ppermute | solution.py:233
  29.8 0.6 %collective-permute-start.15 = (bf16[96,384]{1,0:T(8,128)(2,1)S(1)}, bf16[96,384]{1,0:T(8,128)(2,1)S(1)}, u32[]{:S(2)}, u32[]{:S(2)}) collective-permute-start(bf16[96,384]{1,0:T(8,128)(2,1)S(1)} %get-tuple-element.43), channel_id=1, source_target_pairs={{0,6},{1,15},{2,4},{3,13},{4,2},{5,11},{6,0},{7,9},{8,14},{9,7},{1... | collective-permute-start | bytes 221192 | tf_op jit(solution)/shard_map/ppermute | solution.py:233
  30.4 4.7 %collective-permute-start.19 = (bf16[96,384]{1,0:T(8,128)(2,1)S(1)}, bf16[96,384]{1,0:T(8,128)(2,1)S(1)}, u32[]{:S(2)}, u32[]{:S(2)}) collective-permute-start(bf16[96,384]{1,0:T(8,128)(2,1)S(1)} %get-tuple-element.44), channel_id=1, source_target_pairs={{0,7},{1,14},{2,5},{3,12},{4,3},{5,10},{6,1},{7,8},{8,15},{9,6},{1... | collective-permute-start | bytes 221192 | tf_op jit(solution)/shard_map/ppermute | solution.py:233
  35.1 2.6 %shard_map.90 = (bf16[384,768]{1,0:T(8,128)(2,1)}, bf16[384,768]{1,0:T(8,128)(2,1)}) custom-call(s32[6]{0:T(128)S(1)} %collective-permute-done.owner_ref, bf16[384,768]{1,0:T(8,128)(2,1)S(1)} %bitcast.19, bf16[384,768]{1,0:T(8,128)(2,1)S(1)} %bitcast.20, bf16[2,96,384]{2,1,0:T(8,128)(2,1)S(1)} %collective-permute-done.12.after_ref.refs_0_, ...), custom_call_target="tpu_custom_call" | custom-call | flops 905969664 | bytes 2359296 | tf_op jit(solution)/shard_map/pallas_call | solution.py:239
  37.7 2.7 %collective-permute-start.17 = (bf16[96,384]{1,0:T(8,128)(2,1)S(1)}, bf16[96,384]{1,0:T(8,128)(2,1)S(1)}, u32[]{:S(2)}, u32[]{:S(2)}) collective-permute-start(bf16[96,384]{1,0:T(8,128)(2,1)S(1)} %slice_bitcast_fusion.2), channel_id=1, source_target_pairs={{0,1},{1,0},{2,3},{3,2},{4,5},{5,4},{6,7},{7,6},{8,9},{9,8},{10,11... | collective-permute-start | bytes 221192 | tf_op jit(solution)/shard_map/ppermute | solution.py:227
  40.4 0.1 collective-permute-start.16
  40.5 0.8 %collective-permute-start.18 = (bf16[96,384]{1,0:T(8,128)(2,1)S(1)}, bf16[96,384]{1,0:T(8,128)(2,1)S(1)}, u32[]{:S(2)}, u32[]{:S(2)}) collective-permute-start(bf16[96,384]{1,0:T(8,128)(2,1)S(1)} %slice_bitcast_fusion), channel_id=1, source_target_pairs={{0,1},{1,0},{2,3},{3,2},{4,5},{5,4},{6,7},{7,6},{8,9},{9,8},{10,11... | collective-permute-start | bytes 221192 | tf_op jit(solution)/shard_map/ppermute | solution.py:227
  41.4 0.0 collective-permute-done.15.refs_3_
  41.4 0.0 collective-permute-done.19.refs_7_
  41.4 0.0 collective-permute-done.17.refs_5_
  41.4 0.4 collective-permute-done.16.refs_4_
  41.8 0.5 %collective-permute-done.18.refs_6_ = bf16[96,384]{1,0:T(8,128)(2,1)S(1)} collective-permute-done((bf16[96,384]{1,0:T(8,128)(2,1)S(1)}, bf16[96,384]{1,0:T(8,128)(2,1)S(1)}, u32[]{:S(2)}, u32[]{:S(2)}) %collective-permute-start.18) | collective-permute-done | bytes 73760 | tf_op jit(solution)/shard_map/ppermute | solution.py:227
  42.3 1.4 %shard_map.91 = bf16[6,96,384]{2,1,0:T(8,128)(2,1)} custom-call(s32[6]{0:T(128)S(1)} %collective-permute-done.owner_ref, bf16[2,96,384]{2,1,0:T(8,128)(2,1)S(1)} %collective-permute-done.12.after_ref.refs_0_, bf16[2,96,384]{2,1,0:T(8,128)(2,1)S(1)} %collective-permute-done.13.refs_1_, bf16[2,96,384]{2,1,0:T(8,128)(2,1)S(1)} %collective-permute-done.14.refs_2_, ...), custom_call_target="tpu_custom_call" | custom-call | tf_op jit(solution)/shard_map/pallas_call | solution.py:239
  (12 shorter events, 0.0 us)
Async XLA Ops:
  0.6 4.5 %collective-permute-start.1 = (bf16[6,96,768]{2,1,0:T(8,128)(2,1)}, bf16[6,96,768]{2,1,0:T(8,128)(2,1)S(1)}, u32[]{:S(2)}, u32[]{:S(2)}) collective-permute-start(bf16[6,96,768]{2,1,0:T(8,128)(2,1)} %bitcast.13), channel_id=1, source_target_pairs={{0,1},{1,0},{2,3},{3,2},{4,5},{5,4},{6,7},{7,6},{8,9},{9,8},{10,11... | collective-permute-start | bytes 2654216 | tf_op jit(solution)/shard_map/ppermute | solution.py:227
  1.1 9.8 %collective-permute-start.3 = (bf16[384,768]{1,0:T(8,128)(2,1)}, bf16[384,768]{1,0:T(8,128)(2,1)S(1)}, u32[]{:S(2)}, u32[]{:S(2)}) collective-permute-start(bf16[384,768]{1,0:T(8,128)(2,1)} %bitcast.17), channel_id=1, source_target_pairs={{0,1},{1,0},{2,3},{3,2},{4,5},{5,4},{6,7},{7,6},{8,9},{9,8},{10,11... | collective-permute-start | bytes 1769480 | tf_op jit(solution)/shard_map/ppermute | solution.py:227
  1.2 22.7 %collective-permute-start.9 = (bf16[768,384]{1,0:T(8,128)(2,1)}, bf16[768,384]{1,0:T(8,128)(2,1)S(1)}, u32[]{:S(2)}, u32[]{:S(2)}) collective-permute-start(bf16[768,384]{1,0:T(8,128)(2,1)} %bitcast.15), channel_id=1, source_target_pairs={{0,1},{1,0},{2,3},{3,2},{4,5},{5,4},{6,7},{7,6},{8,9},{9,8},{10,11... | collective-permute-start | bytes 1769480 | tf_op jit(solution)/shard_map/ppermute | solution.py:227
  1.7 3.4 %collective-permute-start = (s32[6]{0:T(128)}, s32[6]{0:T(128)S(1)}, u32[]{:S(2)}, u32[]{:S(2)}) collective-permute-start(s32[6]{0:T(128)} %param.7), channel_id=1, source_target_pairs={{0,1},{1,0},{2,3},{3,2},{4,5},{5,4},{6,7},{7,6},{8,9},{9,8},{10,11... | collective-permute-start | bytes 80 | tf_op jit(solution)/shard_map/ppermute | solution.py:227
  1.7 1.2 %copy-start = (bf16[1,6,96,768]{3,2,1,0:T(8,128)(2,1)S(1)}, bf16[1,6,96,768]{3,2,1,0:T(8,128)(2,1)}, u32[]{:S(2)}) copy-start(bf16[1,6,96,768]{3,2,1,0:T(8,128)(2,1)} %param.6) | copy-start | bytes 2654212
  2.9 8.2 %copy-start.2 = (bf16[1,384,768]{2,1,0:T(8,128)(2,1)S(1)}, bf16[1,384,768]{2,1,0:T(8,128)(2,1)}, u32[]{:S(2)}) copy-start(bf16[1,384,768]{2,1,0:T(8,128)(2,1)} %param.10) | copy-start | bytes 1769476
  3.0 21.0 %copy-start.1 = (bf16[1,768,384]{2,1,0:T(8,128)(2,1)S(1)}, bf16[1,768,384]{2,1,0:T(8,128)(2,1)}, u32[]{:S(2)}) copy-start(bf16[1,768,384]{2,1,0:T(8,128)(2,1)} %param.11) | copy-start | bytes 1769476
  5.8 6.9 %collective-permute-start.2 = (bf16[96,768]{1,0:T(8,128)(2,1)S(1)}, bf16[96,768]{1,0:T(8,128)(2,1)S(1)}, u32[]{:S(2)}, u32[]{:S(2)}) collective-permute-start(bf16[96,768]{1,0:T(8,128)(2,1)S(1)} %get-tuple-element.24), channel_id=1, source_target_pairs={{0,4},{1,13},{2,6},{3,15},{4,0},{5,9},{6,2},{7,11},{8,12},{9,5},{1... | collective-permute-start | bytes 442376 | tf_op jit(solution)/shard_map/ppermute | solution.py:233
  8.8 8.9 %collective-permute-start.5 = (bf16[96,768]{1,0:T(8,128)(2,1)S(1)}, bf16[96,768]{1,0:T(8,128)(2,1)S(1)}, u32[]{:S(2)}, u32[]{:S(2)}) collective-permute-start(bf16[96,768]{1,0:T(8,128)(2,1)S(1)} %get-tuple-element.30), channel_id=1, source_target_pairs={{0,2},{1,11},{2,0},{3,9},{4,6},{5,15},{6,4},{7,13},{8,10},{9,3},{1... | collective-permute-start | bytes 442376 | tf_op jit(solution)/shard_map/ppermute | solution.py:233
  10.3 8.5 %collective-permute-start.7 = (bf16[96,768]{1,0:T(8,128)(2,1)S(1)}, bf16[96,768]{1,0:T(8,128)(2,1)S(1)}, u32[]{:S(2)}, u32[]{:S(2)}) collective-permute-start(bf16[96,768]{1,0:T(8,128)(2,1)S(1)} %get-tuple-element.31), channel_id=1, source_target_pairs={{0,0},{1,9},{2,2},{3,11},{4,4},{5,13},{6,6},{7,15},{8,8},{9,1},{10... | collective-permute-start | bytes 442376 | tf_op jit(solution)/shard_map/ppermute | solution.py:233
  11.0 11.4 %collective-permute-start.8 = (bf16[96,768]{1,0:T(8,128)(2,1)S(1)}, bf16[96,768]{1,0:T(8,128)(2,1)S(1)}, u32[]{:S(2)}, u32[]{:S(2)}) collective-permute-start(bf16[96,768]{1,0:T(8,128)(2,1)S(1)} %get-tuple-element.32), channel_id=1, source_target_pairs={{0,6},{1,15},{2,4},{3,13},{4,2},{5,11},{6,0},{7,9},{8,14},{9,7},{1... | collective-permute-start | bytes 442376 | tf_op jit(solution)/shard_map/ppermute | solution.py:233
  12.7 10.1 %collective-permute-start.4 = (bf16[96,768]{1,0:T(8,128)(2,1)S(1)}, bf16[96,768]{1,0:T(8,128)(2,1)S(1)}, u32[]{:S(2)}, u32[]{:S(2)}) collective-permute-start(bf16[96,768]{1,0:T(8,128)(2,1)S(1)} %collective-permute-done.2.refs_0_), channel_id=1, source_target_pairs={{0,1},{1,0},{2,3},{3,2},{4,5},{5,4},{6,7},{7,6},{8,9},{9,8},{10,11... | collective-permute-start | bytes 442376 | tf_op jit(solution)/shard_map/ppermute | solution.py:227
  17.7 5.1 %collective-permute-start.6 = (bf16[96,768]{1,0:T(8,128)(2,1)S(1)}, bf16[96,768]{1,0:T(8,128)(2,1)S(1)}, u32[]{:S(2)}, u32[]{:S(2)}) collective-permute-start(bf16[96,768]{1,0:T(8,128)(2,1)S(1)} %collective-permute-done.5.refs_2_.refs_1_), channel_id=1, source_target_pairs={{0,1},{1,0},{2,3},{3,2},{4,5},{5,4},{6,7},{7,6},{8,9},{9,8},{10,11... | collective-permute-start | bytes 442376 | tf_op jit(solution)/shard_map/ppermute | solution.py:227
  18.8 5.1 %collective-permute-start.10 = (bf16[96,768]{1,0:T(8,128)(2,1)S(1)}, bf16[96,768]{1,0:T(8,128)(2,1)S(1)}, u32[]{:S(2)}, u32[]{:S(2)}) collective-permute-start(bf16[96,768]{1,0:T(8,128)(2,1)S(1)} %collective-permute-done.7.refs_4_.refs_2_), channel_id=1, source_target_pairs={{0,1},{1,0},{2,3},{3,2},{4,5},{5,4},{6,7},{7,6},{8,9},{9,8},{10,11... | collective-permute-start | bytes 442376 | tf_op jit(solution)/shard_map/ppermute | solution.py:227
  22.4 1.6 %collective-permute-start.11 = (bf16[96,768]{1,0:T(8,128)(2,1)S(1)}, bf16[96,768]{1,0:T(8,128)(2,1)S(1)}, u32[]{:S(2)}, u32[]{:S(2)}) collective-permute-start(bf16[96,768]{1,0:T(8,128)(2,1)S(1)} %collective-permute-done.8.refs_5_.refs_3_), channel_id=1, source_target_pairs={{0,1},{1,0},{2,3},{3,2},{4,5},{5,4},{6,7},{7,6},{8,9},{9,8},{10,11... | collective-permute-start | bytes 442376 | tf_op jit(solution)/shard_map/ppermute | solution.py:227
  23.9 11.2 %copy-start.3 = (bf16[1,384,768]{2,1,0:T(8,128)(2,1)S(1)}, bf16[1,384,768]{2,1,0:T(8,128)(2,1)}, u32[]{:S(2)}) copy-start(bf16[1,384,768]{2,1,0:T(8,128)(2,1)} %param.8) | copy-start | bytes 1769476
  23.9 11.2 %copy-start.4 = (bf16[1,384,768]{2,1,0:T(8,128)(2,1)S(1)}, bf16[1,384,768]{2,1,0:T(8,128)(2,1)}, u32[]{:S(2)}) copy-start(bf16[1,384,768]{2,1,0:T(8,128)(2,1)} %param.9) | copy-start | bytes 1769476
  25.9 9.2 %collective-permute-start.12 = (bf16[2,96,384]{2,1,0:T(8,128)(2,1)S(1)}, bf16[2,96,384]{2,1,0:T(8,128)(2,1)S(1)}, u32[]{:S(2)}, u32[]{:S(2)}) collective-permute-start(bf16[2,96,384]{2,1,0:T(8,128)(2,1)S(1)} %get-tuple-element.35), channel_id=1, source_target_pairs={{0,4},{1,13},{2,6},{3,15},{4,0},{5,9},{6,2},{7,11},{8,12},{9,5},{1... | collective-permute-start | bytes 442376 | tf_op jit(solution)/shard_map/ppermute | solution.py:233
  28.1 9.6 %collective-permute-start.13 = (bf16[2,96,384]{2,1,0:T(8,128)(2,1)S(1)}, bf16[2,96,384]{2,1,0:T(8,128)(2,1)S(1)}, u32[]{:S(2)}, u32[]{:S(2)}) collective-permute-start(bf16[2,96,384]{2,1,0:T(8,128)(2,1)S(1)} %get-tuple-element.38), channel_id=1, source_target_pairs={{0,2},{1,11},{2,0},{3,9},{4,6},{5,15},{6,4},{7,13},{8,10},{9,3},{1... | collective-permute-start | bytes 442376 | tf_op jit(solution)/shard_map/ppermute | solution.py:233
  29.1 11.4 %collective-permute-start.14 = (bf16[2,96,384]{2,1,0:T(8,128)(2,1)S(1)}, bf16[2,96,384]{2,1,0:T(8,128)(2,1)S(1)}, u32[]{:S(2)}, u32[]{:S(2)}) collective-permute-start(bf16[2,96,384]{2,1,0:T(8,128)(2,1)S(1)} %get-tuple-element.42), channel_id=1, source_target_pairs={{0,0},{1,9},{2,2},{3,11},{4,4},{5,13},{6,6},{7,15},{8,8},{9,1},{10... | collective-permute-start | bytes 442376 | tf_op jit(solution)/shard_map/ppermute | solution.py:233
  29.8 11.6 %collective-permute-start.15 = (bf16[96,384]{1,0:T(8,128)(2,1)S(1)}, bf16[96,384]{1,0:T(8,128)(2,1)S(1)}, u32[]{:S(2)}, u32[]{:S(2)}) collective-permute-start(bf16[96,384]{1,0:T(8,128)(2,1)S(1)} %get-tuple-element.43), channel_id=1, source_target_pairs={{0,6},{1,15},{2,4},{3,13},{4,2},{5,11},{6,0},{7,9},{8,14},{9,7},{1... | collective-permute-start | bytes 221192 | tf_op jit(solution)/shard_map/ppermute | solution.py:233
  30.4 11.0 %collective-permute-start.19 = (bf16[96,384]{1,0:T(8,128)(2,1)S(1)}, bf16[96,384]{1,0:T(8,128)(2,1)S(1)}, u32[]{:S(2)}, u32[]{:S(2)}) collective-permute-start(bf16[96,384]{1,0:T(8,128)(2,1)S(1)} %get-tuple-element.44), channel_id=1, source_target_pairs={{0,7},{1,14},{2,5},{3,12},{4,3},{5,10},{6,1},{7,8},{8,15},{9,6},{1... | collective-permute-start | bytes 221192 | tf_op jit(solution)/shard_map/ppermute | solution.py:233
  37.7 3.7 %collective-permute-start.17 = (bf16[96,384]{1,0:T(8,128)(2,1)S(1)}, bf16[96,384]{1,0:T(8,128)(2,1)S(1)}, u32[]{:S(2)}, u32[]{:S(2)}) collective-permute-start(bf16[96,384]{1,0:T(8,128)(2,1)S(1)} %slice_bitcast_fusion.2), channel_id=1, source_target_pairs={{0,1},{1,0},{2,3},{3,2},{4,5},{5,4},{6,7},{7,6},{8,9},{9,8},{10,11... | collective-permute-start | bytes 221192 | tf_op jit(solution)/shard_map/ppermute | solution.py:227
  40.4 1.3 %collective-permute-start.16 = (bf16[96,384]{1,0:T(8,128)(2,1)S(1)}, bf16[96,384]{1,0:T(8,128)(2,1)S(1)}, u32[]{:S(2)}, u32[]{:S(2)}) collective-permute-start(bf16[96,384]{1,0:T(8,128)(2,1)S(1)} %slice_bitcast_fusion.1), channel_id=1, source_target_pairs={{0,1},{1,0},{2,3},{3,2},{4,5},{5,4},{6,7},{7,6},{8,9},{9,8},{10,11... | collective-permute-start | bytes 221192 | tf_op jit(solution)/shard_map/ppermute | solution.py:227
  40.5 1.8 %collective-permute-start.18 = (bf16[96,384]{1,0:T(8,128)(2,1)S(1)}, bf16[96,384]{1,0:T(8,128)(2,1)S(1)}, u32[]{:S(2)}, u32[]{:S(2)}) collective-permute-start(bf16[96,384]{1,0:T(8,128)(2,1)S(1)} %slice_bitcast_fusion), channel_id=1, source_target_pairs={{0,1},{1,0},{2,3},{3,2},{4,5},{5,4},{6,7},{7,6},{8,9},{9,8},{10,11... | collective-permute-start | bytes 221192 | tf_op jit(solution)/shard_map/ppermute | solution.py:227

commit v9 on v8

--- a/solution.py
+++ b/solution.py
@@ -83,7 +83,7 @@
     return jnp.sum(jnp.sum(wide * wide, axis=0, keepdims=True), axis=1, keepdims=True)
 
 
-def fetch_kernel(gradient_ref, out_ref):
+def fetch_kernel(gradient_ref, after_ref, out_ref):
     out_ref[...] = gradient_ref[...]
 
 
@@ -220,7 +220,7 @@
     blocks, slab, width = gradients.shape[1:]
     half_rows = left_gram.shape[1]
     slots = [(k, other) for k in range(rounds) for other in (False, True)]
-    after = [(k, True) for k in range(max(last - 1, 0), rounds)]
+    after = [(k, True) for k in reversed(range(max(last - 1, 0), rounds))]
     slots = ([x for x in slots if x not in after], after)
 
     def other_core(x):
@@ -242,9 +242,9 @@
         )(*args)
 
     other_gradient = other_core(gradients[0])
-    block_owner = other_core(block_owner)
     fetched = call(
-        fetch_kernel, shape((blocks, slab, width)), [VMEM], gradients[0], out_specs=VMEM
+        fetch_kernel, shape((blocks, slab, width)), [VMEM, ANY], gradients[0], block_owner,
+        out_specs=VMEM,
     )
     *outgoing, = call(
         functools.partial(pick_kernel, codes), [shape((slab, width))] * rounds,

time: 43.9 us -> 42.4 us (0.966)
  waiting for transfers between devices: 3.06 us -> 0.94 us
  local copies, waits for them, and re-layouts: 1.22 us -> 1.88 us
    ppermute x11 -> x10, waiting for transfers between devices: 3.04 us -> 0.92 us  [other_core(): return lax.ppermute(x, 'replica', [(0, 1), (1, 0)])]
    unnamed x10 -> x14, local copies, waits for them, and re-layouts: 1.19 us -> 1.85 us
    ppermute x11 -> x10, starting transfers between devices: 14.8 us -> 14.9 us  [other_core(): return lax.ppermute(x, 'replica', [(0, 1), (1, 0)])]
  transfers between devices with their start and end apart: 20 -> 19, of which waited for: 3 -> 2; matrix products, arithmetic and copies ran while one was open for 0% -> 0% of each run, Pallas kernels for 14% -> 14%
where the time goes in v9:
time: 42.4 us; the launch traced here: 42.2 us
  starting transfers between devices  29.2 us (69%)
  Pallas kernels  9.3 us (22%)
  local copies, waits for them, and re-layouts  1.88 us (4%)
  waiting for transfers between devices  0.94 us (2%)
  between operations  0.81 us (2%)
    ppermute x10, starting transfers between devices, other_core(): return lax.ppermute(x, 'replica', [(0, 1), (1, 0)])  14.9 us
    ppermute x9, starting transfers between devices, trade(): return lax.ppermute(x, ('shard', 'replica'), pairs)  14.3 us
    pallas_call x7, Pallas kernels, call(): pl.pallas_call(kernel, out_shape=out_shape, in_specs=in_specs, compiler_p...  9.3 us
    unnamed x14, local copies, waits for them, and re-layouts  1.85 us
    ppermute x10, waiting for transfers between devices, other_core(): return lax.ppermute(x, 'replica', [(0, 1), (1, 0)])  0.92 us
  transfers between devices with their start and end apart: 19, of which 2 were waited for; matrix products, arithmetic and copies ran while one was open for 0% of the time, Pallas kernels for 14%

profile of v9, /device:TPU:0, one launch (start us, length us, event | category | flops | bytes accessed | tf_op | source)
XLA Modules:
  0.0 42.2 jit_solution(5156282634884761889)
XLA Ops:
  0.6 0.5 %collective-permute-start = (bf16[6,96,768]{2,1,0:T(8,128)(2,1)}, bf16[6,96,768]{2,1,0:T(8,128)(2,1)S(1)}, u32[]{:S(2)}, u32[]{:S(2)}) collective-permute-start(bf16[6,96,768]{2,1,0:T(8,128)(2,1)} %bitcast.13), channel_id=1, source_target_pairs={{0,1},{1,0},{2,3},{3,2},{4,5},{5,4},{6,7},{7,6},{8,9},{9,8},{10,11... | collective-permute-start | bytes 2654216 | tf_op jit(solution)/shard_map/ppermute | solution.py:227
  1.1 0.1 collective-permute-start.2
  1.2 0.4 %collective-permute-start.8 = (bf16[768,384]{1,0:T(8,128)(2,1)}, bf16[768,384]{1,0:T(8,128)(2,1)S(1)}, u32[]{:S(2)}, u32[]{:S(2)}) collective-permute-start(bf16[768,384]{1,0:T(8,128)(2,1)} %bitcast.15), channel_id=1, source_target_pairs={{0,1},{1,0},{2,3},{3,2},{4,5},{5,4},{6,7},{7,6},{8,9},{9,8},{10,11... | collective-permute-start | bytes 1769480 | tf_op jit(solution)/shard_map/ppermute | solution.py:227
  1.7 1.2 %copy-done = bf16[1,6,96,768]{3,2,1,0:T(8,128)(2,1)S(1)} copy-done((bf16[1,6,96,768]{3,2,1,0:T(8,128)(2,1)S(1)}, bf16[1,6,96,768]{3,2,1,0:T(8,128)(2,1)}, u32[]{:S(2)}) %copy-start) | copy-done | bytes 884760
  2.8 0.7 %copy-done.3 = s32[6]{0:T(128)S(1)} copy-done((s32[6]{0:T(128)S(1)}, s32[6]{0:T(128)}, u32[]{:S(2)}) %copy-start.3) | copy-done | bytes 48
  3.5 0.1 shard_map.85.mine_ref
  3.5 0.0 copy-start.1
  3.6 0.0 collective-permute-done.theirs_ref
  3.6 0.7 %shard_map.86 = (bf16[96,768]{1,0:T(8,128)(2,1)S(1)}, bf16[96,768]{1,0:T(8,128)(2,1)S(1)}, bf16[96,768]{1,0:T(8,128)(2,1)S(1)}, bf16[96,768]{1,0:T(8,128)(2,1)S(1)}) custom-call(s32[6]{0:T(128)S(1)} %copy-done.3, bf16[6,96,768]{2,1,0:T(8,128)(2,1)S(1)} %shard_map.85.mine_ref, bf16[6,96,768]{2,1,0:T(8,128)(2,1)S(1)} %collective-permute-done.theirs_ref), custom_call_target="tpu_custom_call" | custom-call | tf_op jit(solution)/shard_map/pallas_call | solution.py:239
  4.3 2.9 %collective-permute-start.1 = (bf16[96,768]{1,0:T(8,128)(2,1)S(1)}, bf16[96,768]{1,0:T(8,128)(2,1)S(1)}, u32[]{:S(2)}, u32[]{:S(2)}) collective-permute-start(bf16[96,768]{1,0:T(8,128)(2,1)S(1)} %get-tuple-element.24), channel_id=1, source_target_pairs={{0,4},{1,13},{2,6},{3,15},{4,0},{5,9},{6,2},{7,11},{8,12},{9,5},{1... | collective-permute-start | bytes 442376 | tf_op jit(solution)/shard_map/ppermute | solution.py:233
  7.1 1.5 %collective-permute-start.4 = (bf16[96,768]{1,0:T(8,128)(2,1)S(1)}, bf16[96,768]{1,0:T(8,128)(2,1)S(1)}, u32[]{:S(2)}, u32[]{:S(2)}) collective-permute-start(bf16[96,768]{1,0:T(8,128)(2,1)S(1)} %get-tuple-element.30), channel_id=1, source_target_pairs={{0,2},{1,11},{2,0},{3,9},{4,6},{5,15},{6,4},{7,13},{8,10},{9,3},{1... | collective-permute-start | bytes 442376 | tf_op jit(solution)/shard_map/ppermute | solution.py:233
  8.6 0.7 %collective-permute-start.6 = (bf16[96,768]{1,0:T(8,128)(2,1)S(1)}, bf16[96,768]{1,0:T(8,128)(2,1)S(1)}, u32[]{:S(2)}, u32[]{:S(2)}) collective-permute-start(bf16[96,768]{1,0:T(8,128)(2,1)S(1)} %get-tuple-element.31), channel_id=1, source_target_pairs={{0,0},{1,9},{2,2},{3,11},{4,4},{5,13},{6,6},{7,15},{8,8},{9,1},{10... | collective-permute-start | bytes 442376 | tf_op jit(solution)/shard_map/ppermute | solution.py:233
  9.3 0.0 collective-permute-done.2.other_ref
  9.3 0.1 collective-permute-start.7
  9.4 1.6 %shard_map.87 = (bf16[768,576]{1,0:T(8,128)(2,1)S(1)}, bf16[768,192]{1,0:T(8,128)(2,1)S(1)}) custom-call(bf16[384,768]{1,0:T(8,128)(2,1)S(1)} %bitcast.18, bf16[384,768]{1,0:T(8,128)(2,1)S(1)} %collective-permute-done.2.other_ref), custom_call_target="tpu_custom_call" | custom-call | tf_op jit(solution)/shard_map/pallas_call | solution.py:239
  11.0 0.0 collective-permute-done.1.refs_0_
  11.0 5.1 %collective-permute-start.3 = (bf16[96,768]{1,0:T(8,128)(2,1)S(1)}, bf16[96,768]{1,0:T(8,128)(2,1)S(1)}, u32[]{:S(2)}, u32[]{:S(2)}) collective-permute-start(bf16[96,768]{1,0:T(8,128)(2,1)S(1)} %collective-permute-done.1.refs_0_), channel_id=1, source_target_pairs={{0,1},{1,0},{2,3},{3,2},{4,5},{5,4},{6,7},{7,6},{8,9},{9,8},{10,11... | collective-permute-start | bytes 442376 | tf_op jit(solution)/shard_map/ppermute | solution.py:227
  16.1 0.0 collective-permute-done.4.refs_2_.refs_1_
  16.1 1.1 %collective-permute-start.5 = (bf16[96,768]{1,0:T(8,128)(2,1)S(1)}, bf16[96,768]{1,0:T(8,128)(2,1)S(1)}, u32[]{:S(2)}, u32[]{:S(2)}) collective-permute-start(bf16[96,768]{1,0:T(8,128)(2,1)S(1)} %collective-permute-done.4.refs_2_.refs_1_), channel_id=1, source_target_pairs={{0,1},{1,0},{2,3},{3,2},{4,5},{5,4},{6,7},{7,6},{8,9},{9,8},{10,11... | collective-permute-start | bytes 442376 | tf_op jit(solution)/shard_map/ppermute | solution.py:227
  17.2 0.0 collective-permute-done.6.refs_4_.refs_2_
  17.2 3.6 %collective-permute-start.10 = (bf16[96,768]{1,0:T(8,128)(2,1)S(1)}, bf16[96,768]{1,0:T(8,128)(2,1)S(1)}, u32[]{:S(2)}, u32[]{:S(2)}) collective-permute-start(bf16[96,768]{1,0:T(8,128)(2,1)S(1)} %collective-permute-done.6.refs_4_.refs_2_), channel_id=1, source_target_pairs={{0,1},{1,0},{2,3},{3,2},{4,5},{5,4},{6,7},{7,6},{8,9},{9,8},{10,11... | collective-permute-start | bytes 442376 | tf_op jit(solution)/shard_map/ppermute | solution.py:227
  20.8 0.4 collective-permute-start.9
  21.2 0.0 collective-permute-done.3.refs_1_.refs_4_
  21.2 0.0 collective-permute-done.5.refs_3_.refs_5_
  21.2 1.1 %shard_map.88 = (f32[768,768]{1,0:T(8,128)S(1)}, f32[8,128]{1,0:T(8,128)S(1)}) custom-call(bf16[768,576]{1,0:T(8,128)(2,1)S(1)} %get-tuple-element.28.left_ref, bf16[96,768]{1,0:T(8,128)(2,1)S(1)} %collective-permute-done.1.refs_0_, bf16[96,768]{1,0:T(8,128)(2,1)S(1)} %collective-permute-done.3.refs_1_.refs_4_, ...), custom_call_target="tpu_custom_call" | custom-call | tf_op jit(solution)/shard_map/pallas_call | solution.py:239
  22.3 0.0 copy-start.4
  22.3 0.0 copy-start.5
  22.4 0.0 copy-start.6
  22.4 0.0 collective-permute-done.8.other_ref
  22.4 0.0 collective-permute-done.10.refs_1_.refs_6_
  22.4 1.9 %shard_map.89 = (bf16[2,96,384]{2,1,0:T(8,128)(2,1)S(1)}, bf16[2,96,384]{2,1,0:T(8,128)(2,1)S(1)}, bf16[2,96,384]{2,1,0:T(8,128)(2,1)S(1)}, bf16[96,384]{1,0:T(8,128)(2,1)S(1)}, bf16[96,384]{1,0:T(8,128)(2,1)S(1)}) custom-call(bf16[768,192]{1,0:T(8,128)(2,1)S(1)} %get-tuple-element.27.left_ref, f32[768,768]{1,0:T(8,128)S(1)} %get-tuple-element.33.total_ref, ...), custom_call_target="tpu_custom_call" | custom-call | tf_op jit(solution)/shard_map/pallas_call | solution.py:239
  24.3 2.3 %collective-permute-start.11 = (bf16[2,96,384]{2,1,0:T(8,128)(2,1)S(1)}, bf16[2,96,384]{2,1,0:T(8,128)(2,1)S(1)}, u32[]{:S(2)}, u32[]{:S(2)}) collective-permute-start(bf16[2,96,384]{2,1,0:T(8,128)(2,1)S(1)} %get-tuple-element.35), channel_id=1, source_target_pairs={{0,4},{1,13},{2,6},{3,15},{4,0},{5,9},{6,2},{7,11},{8,12},{9,5},{1... | collective-permute-start | bytes 442376 | tf_op jit(solution)/shard_map/ppermute | solution.py:233
  26.6 1.0 %collective-permute-start.12 = (bf16[2,96,384]{2,1,0:T(8,128)(2,1)S(1)}, bf16[2,96,384]{2,1,0:T(8,128)(2,1)S(1)}, u32[]{:S(2)}, u32[]{:S(2)}) collective-permute-start(bf16[2,96,384]{2,1,0:T(8,128)(2,1)S(1)} %get-tuple-element.38), channel_id=1, source_target_pairs={{0,2},{1,11},{2,0},{3,9},{4,6},{5,15},{6,4},{7,13},{8,10},{9,3},{1... | collective-permute-start | bytes 442376 | tf_op jit(solution)/shard_map/ppermute | solution.py:233
  27.6 0.7 %collective-permute-start.13 = (bf16[2,96,384]{2,1,0:T(8,128)(2,1)S(1)}, bf16[2,96,384]{2,1,0:T(8,128)(2,1)S(1)}, u32[]{:S(2)}, u32[]{:S(2)}) collective-permute-start(bf16[2,96,384]{2,1,0:T(8,128)(2,1)S(1)} %get-tuple-element.42), channel_id=1, source_target_pairs={{0,0},{1,9},{2,2},{3,11},{4,4},{5,13},{6,6},{7,15},{8,8},{9,1},{10... | collective-permute-start | bytes 442376 | tf_op jit(solution)/shard_map/ppermute | solution.py:233
  28.3 0.6 %collective-permute-start.14 = (bf16[96,384]{1,0:T(8,128)(2,1)S(1)}, bf16[96,384]{1,0:T(8,128)(2,1)S(1)}, u32[]{:S(2)}, u32[]{:S(2)}) collective-permute-start(bf16[96,384]{1,0:T(8,128)(2,1)S(1)} %get-tuple-element.43), channel_id=1, source_target_pairs={{0,6},{1,15},{2,4},{3,13},{4,2},{5,11},{6,0},{7,9},{8,14},{9,7},{1... | collective-permute-start | bytes 221192 | tf_op jit(solution)/shard_map/ppermute | solution.py:233
  28.9 4.7 %collective-permute-start.18 = (bf16[96,384]{1,0:T(8,128)(2,1)S(1)}, bf16[96,384]{1,0:T(8,128)(2,1)S(1)}, u32[]{:S(2)}, u32[]{:S(2)}) collective-permute-start(bf16[96,384]{1,0:T(8,128)(2,1)S(1)} %get-tuple-element.44), channel_id=1, source_target_pairs={{0,7},{1,14},{2,5},{3,12},{4,3},{5,10},{6,1},{7,8},{8,15},{9,6},{1... | collective-permute-start | bytes 221192 | tf_op jit(solution)/shard_map/ppermute | solution.py:233
  33.6 0.0 collective-permute-done.11.after_ref.refs_0_
  33.6 2.6 %shard_map.90 = (bf16[384,768]{1,0:T(8,128)(2,1)}, bf16[384,768]{1,0:T(8,128)(2,1)}) custom-call(s32[6]{0:T(128)S(1)} %copy-done.4, bf16[384,768]{1,0:T(8,128)(2,1)S(1)} %bitcast.19, bf16[384,768]{1,0:T(8,128)(2,1)S(1)} %bitcast.20, bf16[2,96,384]{2,1,0:T(8,128)(2,1)S(1)} %collective-permute-done.11.after_ref.refs_0_, ...), custom_call_target="tpu_custom_call" | custom-call | flops 905969664 | bytes 2359296 | tf_op jit(solution)/shard_map/pallas_call | solution.py:239
  36.2 2.7 %collective-permute-start.16 = (bf16[96,384]{1,0:T(8,128)(2,1)S(1)}, bf16[96,384]{1,0:T(8,128)(2,1)S(1)}, u32[]{:S(2)}, u32[]{:S(2)}) collective-permute-start(bf16[96,384]{1,0:T(8,128)(2,1)S(1)} %slice_bitcast_fusion.2), channel_id=1, source_target_pairs={{0,1},{1,0},{2,3},{3,2},{4,5},{5,4},{6,7},{7,6},{8,9},{9,8},{10,11... | collective-permute-start | bytes 221192 | tf_op jit(solution)/shard_map/ppermute | solution.py:227
  38.9 0.1 collective-permute-start.15
  39.0 0.0 collective-permute-done.13.refs_2_
  39.0 0.8 %collective-permute-start.17 = (bf16[96,384]{1,0:T(8,128)(2,1)S(1)}, bf16[96,384]{1,0:T(8,128)(2,1)S(1)}, u32[]{:S(2)}, u32[]{:S(2)}) collective-permute-start(bf16[96,384]{1,0:T(8,128)(2,1)S(1)} %slice_bitcast_fusion), channel_id=1, source_target_pairs={{0,1},{1,0},{2,3},{3,2},{4,5},{5,4},{6,7},{7,6},{8,9},{9,8},{10,11... | collective-permute-start | bytes 221192 | tf_op jit(solution)/shard_map/ppermute | solution.py:227
  39.9 0.0 collective-permute-done.14.refs_3_
  39.9 0.0 collective-permute-done.18.refs_7_
  39.9 0.0 collective-permute-done.16.refs_5_
  39.9 0.4 collective-permute-done.15.refs_4_
  40.3 0.5 %collective-permute-done.17.refs_6_ = bf16[96,384]{1,0:T(8,128)(2,1)S(1)} collective-permute-done((bf16[96,384]{1,0:T(8,128)(2,1)S(1)}, bf16[96,384]{1,0:T(8,128)(2,1)S(1)}, u32[]{:S(2)}, u32[]{:S(2)}) %collective-permute-start.17) | collective-permute-done | bytes 73760 | tf_op jit(solution)/shard_map/ppermute | solution.py:227
  40.8 1.4 %shard_map.91 = bf16[6,96,384]{2,1,0:T(8,128)(2,1)} custom-call(s32[6]{0:T(128)S(1)} %copy-done.4, bf16[2,96,384]{2,1,0:T(8,128)(2,1)S(1)} %collective-permute-done.11.after_ref.refs_0_, bf16[2,96,384]{2,1,0:T(8,128)(2,1)S(1)} %collective-permute-done.12.refs_1_, bf16[2,96,384]{2,1,0:T(8,128)(2,1)S(1)} %collective-permute-done.13.refs_2_, ...), custom_call_target="tpu_custom_call" | custom-call | tf_op jit(solution)/shard_map/pallas_call | solution.py:239
  (14 shorter events, 0.0 us)
Async XLA Ops:
  0.6 2.9 %collective-permute-start = (bf16[6,96,768]{2,1,0:T(8,128)(2,1)}, bf16[6,96,768]{2,1,0:T(8,128)(2,1)S(1)}, u32[]{:S(2)}, u32[]{:S(2)}) collective-permute-start(bf16[6,96,768]{2,1,0:T(8,128)(2,1)} %bitcast.13), channel_id=1, source_target_pairs={{0,1},{1,0},{2,3},{3,2},{4,5},{5,4},{6,7},{7,6},{8,9},{9,8},{10,11... | collective-permute-start | bytes 2654216 | tf_op jit(solution)/shard_map/ppermute | solution.py:227
  1.1 8.1 %collective-permute-start.2 = (bf16[384,768]{1,0:T(8,128)(2,1)}, bf16[384,768]{1,0:T(8,128)(2,1)S(1)}, u32[]{:S(2)}, u32[]{:S(2)}) collective-permute-start(bf16[384,768]{1,0:T(8,128)(2,1)} %bitcast.17), channel_id=1, source_target_pairs={{0,1},{1,0},{2,3},{3,2},{4,5},{5,4},{6,7},{7,6},{8,9},{9,8},{10,11... | collective-permute-start | bytes 1769480 | tf_op jit(solution)/shard_map/ppermute | solution.py:227
  1.2 21.1 %collective-permute-start.8 = (bf16[768,384]{1,0:T(8,128)(2,1)}, bf16[768,384]{1,0:T(8,128)(2,1)S(1)}, u32[]{:S(2)}, u32[]{:S(2)}) collective-permute-start(bf16[768,384]{1,0:T(8,128)(2,1)} %bitcast.15), channel_id=1, source_target_pairs={{0,1},{1,0},{2,3},{3,2},{4,5},{5,4},{6,7},{7,6},{8,9},{9,8},{10,11... | collective-permute-start | bytes 1769480 | tf_op jit(solution)/shard_map/ppermute | solution.py:227
  1.7 1.2 %copy-start = (bf16[1,6,96,768]{3,2,1,0:T(8,128)(2,1)S(1)}, bf16[1,6,96,768]{3,2,1,0:T(8,128)(2,1)}, u32[]{:S(2)}) copy-start(bf16[1,6,96,768]{3,2,1,0:T(8,128)(2,1)} %param.6) | copy-start | bytes 2654212
  2.8 0.7 %copy-start.3 = (s32[6]{0:T(128)S(1)}, s32[6]{0:T(128)}, u32[]{:S(2)}) copy-start(s32[6]{0:T(128)} %owner_ref.5) | copy-start | bytes 76
  3.5 5.9 %copy-start.2 = (bf16[1,384,768]{2,1,0:T(8,128)(2,1)S(1)}, bf16[1,384,768]{2,1,0:T(8,128)(2,1)}, u32[]{:S(2)}) copy-start(bf16[1,384,768]{2,1,0:T(8,128)(2,1)} %param.10) | copy-start | bytes 1769476
  3.5 18.9 %copy-start.1 = (bf16[1,768,384]{2,1,0:T(8,128)(2,1)S(1)}, bf16[1,768,384]{2,1,0:T(8,128)(2,1)}, u32[]{:S(2)}) copy-start(bf16[1,768,384]{2,1,0:T(8,128)(2,1)} %param.11) | copy-start | bytes 1769476
  4.3 6.7 %collective-permute-start.1 = (bf16[96,768]{1,0:T(8,128)(2,1)S(1)}, bf16[96,768]{1,0:T(8,128)(2,1)S(1)}, u32[]{:S(2)}, u32[]{:S(2)}) collective-permute-start(bf16[96,768]{1,0:T(8,128)(2,1)S(1)} %get-tuple-element.24), channel_id=1, source_target_pairs={{0,4},{1,13},{2,6},{3,15},{4,0},{5,9},{6,2},{7,11},{8,12},{9,5},{1... | collective-permute-start | bytes 442376 | tf_op jit(solution)/shard_map/ppermute | solution.py:233
  7.1 9.0 %collective-permute-start.4 = (bf16[96,768]{1,0:T(8,128)(2,1)S(1)}, bf16[96,768]{1,0:T(8,128)(2,1)S(1)}, u32[]{:S(2)}, u32[]{:S(2)}) collective-permute-start(bf16[96,768]{1,0:T(8,128)(2,1)S(1)} %get-tuple-element.30), channel_id=1, source_target_pairs={{0,2},{1,11},{2,0},{3,9},{4,6},{5,15},{6,4},{7,13},{8,10},{9,3},{1... | collective-permute-start | bytes 442376 | tf_op jit(solution)/shard_map/ppermute | solution.py:233
  8.6 8.6 %collective-permute-start.6 = (bf16[96,768]{1,0:T(8,128)(2,1)S(1)}, bf16[96,768]{1,0:T(8,128)(2,1)S(1)}, u32[]{:S(2)}, u32[]{:S(2)}) collective-permute-start(bf16[96,768]{1,0:T(8,128)(2,1)S(1)} %get-tuple-element.31), channel_id=1, source_target_pairs={{0,0},{1,9},{2,2},{3,11},{4,4},{5,13},{6,6},{7,15},{8,8},{9,1},{10... | collective-permute-start | bytes 442376 | tf_op jit(solution)/shard_map/ppermute | solution.py:233
  9.3 11.6 %collective-permute-start.7 = (bf16[96,768]{1,0:T(8,128)(2,1)S(1)}, bf16[96,768]{1,0:T(8,128)(2,1)S(1)}, u32[]{:S(2)}, u32[]{:S(2)}) collective-permute-start(bf16[96,768]{1,0:T(8,128)(2,1)S(1)} %get-tuple-element.32), channel_id=1, source_target_pairs={{0,6},{1,15},{2,4},{3,13},{4,2},{5,11},{6,0},{7,9},{8,14},{9,7},{1... | collective-permute-start | bytes 442376 | tf_op jit(solution)/shard_map/ppermute | solution.py:233
  11.0 10.2 %collective-permute-start.3 = (bf16[96,768]{1,0:T(8,128)(2,1)S(1)}, bf16[96,768]{1,0:T(8,128)(2,1)S(1)}, u32[]{:S(2)}, u32[]{:S(2)}) collective-permute-start(bf16[96,768]{1,0:T(8,128)(2,1)S(1)} %collective-permute-done.1.refs_0_), channel_id=1, source_target_pairs={{0,1},{1,0},{2,3},{3,2},{4,5},{5,4},{6,7},{7,6},{8,9},{9,8},{10,11... | collective-permute-start | bytes 442376 | tf_op jit(solution)/shard_map/ppermute | solution.py:227
  16.1 5.1 %collective-permute-start.5 = (bf16[96,768]{1,0:T(8,128)(2,1)S(1)}, bf16[96,768]{1,0:T(8,128)(2,1)S(1)}, u32[]{:S(2)}, u32[]{:S(2)}) collective-permute-start(bf16[96,768]{1,0:T(8,128)(2,1)S(1)} %collective-permute-done.4.refs_2_.refs_1_), channel_id=1, source_target_pairs={{0,1},{1,0},{2,3},{3,2},{4,5},{5,4},{6,7},{7,6},{8,9},{9,8},{10,11... | collective-permute-start | bytes 442376 | tf_op jit(solution)/shard_map/ppermute | solution.py:227
  17.2 5.1 %collective-permute-start.10 = (bf16[96,768]{1,0:T(8,128)(2,1)S(1)}, bf16[96,768]{1,0:T(8,128)(2,1)S(1)}, u32[]{:S(2)}, u32[]{:S(2)}) collective-permute-start(bf16[96,768]{1,0:T(8,128)(2,1)S(1)} %collective-permute-done.6.refs_4_.refs_2_), channel_id=1, source_target_pairs={{0,1},{1,0},{2,3},{3,2},{4,5},{5,4},{6,7},{7,6},{8,9},{9,8},{10,11... | collective-permute-start | bytes 442376 | tf_op jit(solution)/shard_map/ppermute | solution.py:227
  20.8 1.5 %collective-permute-start.9 = (bf16[96,768]{1,0:T(8,128)(2,1)S(1)}, bf16[96,768]{1,0:T(8,128)(2,1)S(1)}, u32[]{:S(2)}, u32[]{:S(2)}) collective-permute-start(bf16[96,768]{1,0:T(8,128)(2,1)S(1)} %collective-permute-done.7.refs_5_.refs_3_), channel_id=1, source_target_pairs={{0,1},{1,0},{2,3},{3,2},{4,5},{5,4},{6,7},{7,6},{8,9},{9,8},{10,11... | collective-permute-start | bytes 442376 | tf_op jit(solution)/shard_map/ppermute | solution.py:227
  22.3 11.2 %copy-start.4 = (s32[6]{0:T(128)S(1)}, s32[6]{0:T(128)}, u32[]{:S(2)}) copy-start(s32[6]{0:T(128)} %owner_ref.5) | copy-start | bytes 76
  22.3 11.2 %copy-start.5 = (bf16[1,384,768]{2,1,0:T(8,128)(2,1)S(1)}, bf16[1,384,768]{2,1,0:T(8,128)(2,1)}, u32[]{:S(2)}) copy-start(bf16[1,384,768]{2,1,0:T(8,128)(2,1)} %param.8) | copy-start | bytes 1769476
  22.4 11.2 %copy-start.6 = (bf16[1,384,768]{2,1,0:T(8,128)(2,1)S(1)}, bf16[1,384,768]{2,1,0:T(8,128)(2,1)}, u32[]{:S(2)}) copy-start(bf16[1,384,768]{2,1,0:T(8,128)(2,1)} %param.9) | copy-start | bytes 1769476
  24.3 9.2 %collective-permute-start.11 = (bf16[2,96,384]{2,1,0:T(8,128)(2,1)S(1)}, bf16[2,96,384]{2,1,0:T(8,128)(2,1)S(1)}, u32[]{:S(2)}, u32[]{:S(2)}) collective-permute-start(bf16[2,96,384]{2,1,0:T(8,128)(2,1)S(1)} %get-tuple-element.35), channel_id=1, source_target_pairs={{0,4},{1,13},{2,6},{3,15},{4,0},{5,9},{6,2},{7,11},{8,12},{9,5},{1... | collective-permute-start | bytes 442376 | tf_op jit(solution)/shard_map/ppermute | solution.py:233
  26.6 9.6 %collective-permute-start.12 = (bf16[2,96,384]{2,1,0:T(8,128)(2,1)S(1)}, bf16[2,96,384]{2,1,0:T(8,128)(2,1)S(1)}, u32[]{:S(2)}, u32[]{:S(2)}) collective-permute-start(bf16[2,96,384]{2,1,0:T(8,128)(2,1)S(1)} %get-tuple-element.38), channel_id=1, source_target_pairs={{0,2},{1,11},{2,0},{3,9},{4,6},{5,15},{6,4},{7,13},{8,10},{9,3},{1... | collective-permute-start | bytes 442376 | tf_op jit(solution)/shard_map/ppermute | solution.py:233
  27.6 11.4 %collective-permute-start.13 = (bf16[2,96,384]{2,1,0:T(8,128)(2,1)S(1)}, bf16[2,96,384]{2,1,0:T(8,128)(2,1)S(1)}, u32[]{:S(2)}, u32[]{:S(2)}) collective-permute-start(bf16[2,96,384]{2,1,0:T(8,128)(2,1)S(1)} %get-tuple-element.42), channel_id=1, source_target_pairs={{0,0},{1,9},{2,2},{3,11},{4,4},{5,13},{6,6},{7,15},{8,8},{9,1},{10... | collective-permute-start | bytes 442376 | tf_op jit(solution)/shard_map/ppermute | solution.py:233
  28.3 11.6 %collective-permute-start.14 = (bf16[96,384]{1,0:T(8,128)(2,1)S(1)}, bf16[96,384]{1,0:T(8,128)(2,1)S(1)}, u32[]{:S(2)}, u32[]{:S(2)}) collective-permute-start(bf16[96,384]{1,0:T(8,128)(2,1)S(1)} %get-tuple-element.43), channel_id=1, source_target_pairs={{0,6},{1,15},{2,4},{3,13},{4,2},{5,11},{6,0},{7,9},{8,14},{9,7},{1... | collective-permute-start | bytes 221192 | tf_op jit(solution)/shard_map/ppermute | solution.py:233
  28.9 11.0 %collective-permute-start.18 = (bf16[96,384]{1,0:T(8,128)(2,1)S(1)}, bf16[96,384]{1,0:T(8,128)(2,1)S(1)}, u32[]{:S(2)}, u32[]{:S(2)}) collective-permute-start(bf16[96,384]{1,0:T(8,128)(2,1)S(1)} %get-tuple-element.44), channel_id=1, source_target_pairs={{0,7},{1,14},{2,5},{3,12},{4,3},{5,10},{6,1},{7,8},{8,15},{9,6},{1... | collective-permute-start | bytes 221192 | tf_op jit(solution)/shard_map/ppermute | solution.py:233
  36.2 3.7 %collective-permute-start.16 = (bf16[96,384]{1,0:T(8,128)(2,1)S(1)}, bf16[96,384]{1,0:T(8,128)(2,1)S(1)}, u32[]{:S(2)}, u32[]{:S(2)}) collective-permute-start(bf16[96,384]{1,0:T(8,128)(2,1)S(1)} %slice_bitcast_fusion.2), channel_id=1, source_target_pairs={{0,1},{1,0},{2,3},{3,2},{4,5},{5,4},{6,7},{7,6},{8,9},{9,8},{10,11... | collective-permute-start | bytes 221192 | tf_op jit(solution)/shard_map/ppermute | solution.py:227
  38.9 1.3 %collective-permute-start.15 = (bf16[96,384]{1,0:T(8,128)(2,1)S(1)}, bf16[96,384]{1,0:T(8,128)(2,1)S(1)}, u32[]{:S(2)}, u32[]{:S(2)}) collective-permute-start(bf16[96,384]{1,0:T(8,128)(2,1)S(1)} %slice_bitcast_fusion.1), channel_id=1, source_target_pairs={{0,1},{1,0},{2,3},{3,2},{4,5},{5,4},{6,7},{7,6},{8,9},{9,8},{10,11... | collective-permute-start | bytes 221192 | tf_op jit(solution)/shard_map/ppermute | solution.py:227
  39.0 1.8 %collective-permute-start.17 = (bf16[96,384]{1,0:T(8,128)(2,1)S(1)}, bf16[96,384]{1,0:T(8,128)(2,1)S(1)}, u32[]{:S(2)}, u32[]{:S(2)}) collective-permute-start(bf16[96,384]{1,0:T(8,128)(2,1)S(1)} %slice_bitcast_fusion), channel_id=1, source_target_pairs={{0,1},{1,0},{2,3},{3,2},{4,5},{5,4},{6,7},{7,6},{8,9},{9,8},{10,11... | collective-permute-start | bytes 221192 | tf_op jit(solution)/shard_map/ppermute | solution.py:227

commit v10 on v9

--- a/solution.py
+++ b/solution.py
@@ -8,7 +8,6 @@
 from jax.sharding import PartitionSpec as P
 
 VMEM = pl.BlockSpec(memory_space=pltpu.VMEM)
-SMEM = pl.BlockSpec(memory_space=pltpu.SMEM)
 ANY = pl.BlockSpec(memory_space=pl.ANY)
 LIGHT = pl.CostEstimate(flops=0, bytes_accessed=0, transcendentals=0)
 ORDER = {2: (1, 0), 4: (2, 1, 0, 3)}
@@ -69,8 +68,8 @@
 
 def block_of(owner_ref, owner):
     block = jnp.int32(-1)
-    for b in range(owner_ref.shape[0]):
-        block = jnp.where(owner_ref[b] == owner, b, block)
+    for b in range(owner_ref.shape[1]):
+        block = jnp.where(owner_ref[0, b] == owner, b, block)
     return block
 
 
@@ -80,7 +79,8 @@
 
 def squares(value):
     wide = value.astype(jnp.float32)
-    return jnp.sum(jnp.sum(wide * wide, axis=0, keepdims=True), axis=1, keepdims=True)
+    rows = jnp.sum((wide * wide).reshape(-1, 8, wide.shape[1]), axis=0)
+    return jnp.sum(jnp.sum(rows, axis=0, keepdims=True), axis=1, keepdims=True)
 
 
 def fetch_kernel(gradient_ref, after_ref, out_ref):
@@ -94,8 +94,10 @@
         out_ref[...] = total.astype(out_ref.dtype)
 
 
-def order_kernel(codes, slots, own_ref, other_ref, *refs):
-    out_refs, rows_ref = refs[:-1], refs[-1]
+def order_kernel(codes, slots, own_ref, other_ref, own_right_ref, other_right_ref, *refs):
+    *out_refs, right_ref, rows_ref = refs
+    right_ref[:, :own_right_ref.shape[1]] = own_right_ref[...]
+    right_ref[:, own_right_ref.shape[1]:] = other_right_ref[...]
     half, full = own_ref.shape
     rounds = len(codes[0])
     slab = half // rounds
@@ -134,27 +136,27 @@
     grad_sq_ref[...] = jnp.broadcast_to(squares(stacked_ref[...]), grad_sq_ref.shape)
 
 
-def finish_kernel(count, left_ref, total_ref, begun_sq_ref, own_ref, other_ref, *refs):
+def finish_kernel(count, left_ref, total_ref, begun_sq_ref, right_ref, *refs):
     slabs = refs[:count]
     *whole_refs, keep_ref, pass_ref, stacked_ref, side_ref, both_ref = refs[count:]
     slab = slabs[0].shape[0]
+    half, full = both_ref.shape
     for n, ref in enumerate(slabs):
         stacked_ref[n * slab:(n + 1) * slab, :] = ref[...]
     last = stacked_ref[...]
     side = total_ref[...] + jnp.dot(left_ref[...], last, preferred_element_type=jnp.float32)
     side_ref[...] = side.astype(side_ref.dtype)
     grad_sq = begun_sq_ref[0:1, 0:1] + squares(last)
-    half = own_ref.shape[1]
-    side_sq = jnp.zeros((1, 1), jnp.float32)
-    for n, ref in enumerate((own_ref, other_ref)):
-        both = jnp.dot(side_ref[...], ref[...], preferred_element_type=jnp.float32)
-        both_ref[n] = both[:half]
-        side_sq += squares(both)
-    graft = jnp.sqrt(grad_sq / (side_sq + 1e-06))
+    both = jnp.dot(side_ref[...], right_ref[...], preferred_element_type=jnp.float32)
+    both_ref[...] = both[:half]
+    graft = jnp.sqrt(grad_sq / (squares(both) + 1e-06))
+    columns = (slice(None, full // 2), slice(full // 2, None))
     for k, out_ref in enumerate(whole_refs):
-        out_ref[...] = (both_ref[:, k * slab:(k + 1) * slab] * graft).astype(out_ref.dtype)
+        for n in range(2):
+            piece = both_ref[k * slab:(k + 1) * slab, columns[n]] * graft
+            out_ref[n] = piece.astype(out_ref.dtype)
     for n, out_ref in enumerate((keep_ref, pass_ref)):
-        out_ref[...] = (both_ref[n, half - slab:] * graft).astype(out_ref.dtype)
+        out_ref[...] = (both_ref[half - slab:, columns[n]] * graft).astype(out_ref.dtype)
 
 
 def gram_kernel(codes, owner_ref, left_ref, right_ref, after_ref, *refs):
@@ -241,6 +243,7 @@
             cost_estimate=cost_estimate, **options
         )(*args)
 
+    block_owner = block_owner.reshape(1, blocks)
     other_gradient = other_core(gradients[0])
     fetched = call(
         fetch_kernel, shape((blocks, slab, width)), [VMEM, ANY], gradients[0], block_owner,
@@ -248,17 +251,19 @@
     )
     *outgoing, = call(
         functools.partial(pick_kernel, codes), [shape((slab, width))] * rounds,
-        [SMEM, VMEM, VMEM], block_owner, fetched, other_gradient, out_specs=[VMEM] * rounds,
+        [VMEM, VMEM, VMEM], block_owner, fetched, other_gradient, out_specs=[VMEM] * rounds,
     )
     mine = [trade(outgoing[k], k) for k in range(rounds)]
     other_left, other_right = other_core(left_root[0]), other_core(right_root[0])
-    left_sooner, left_last = call(
+    left_sooner, left_last, right = call(
         functools.partial(order_kernel, codes, slots),
-        [shape((2 * half_rows, len(group) * slab)) for group in slots], [VMEM, VMEM],
-        left_root[0], other_left, out_specs=[VMEM, VMEM],
+        [shape((2 * half_rows, len(group) * slab)) for group in slots] + [shape((width, width))],
+        [VMEM] * 4, left_root[0], other_left, right_root[0], other_right, out_specs=[VMEM] * 3,
         scratch_shapes=[pltpu.VMEM((2 * half_rows, width), jnp.bfloat16)],
     )
-    mine[0], left_sooner, left_last = lax.optimization_barrier((mine[0], left_sooner, left_last))
+    mine[0], left_sooner, left_last, right = lax.optimization_barrier(
+        (mine[0], left_sooner, left_last, right)
+    )
     theirs = [other_core(x) for x in mine]
     sooner = [(theirs if other else mine)[k] for k, other in slots[0]]
     begun, begun_sq = call(
@@ -270,13 +275,13 @@
     *whole, keep, cross = call(
         functools.partial(finish_kernel, len(after)),
         [shape((2, slab, width // 2))] * last + [shape((slab, width // 2))] * 2,
-        [VMEM] * (5 + len(after)),
-        left_last, begun, begun_sq, right_root[0], other_right, *[theirs[k] for k, _ in after],
+        [VMEM] * (4 + len(after)),
+        left_last, begun, begun_sq, right, *[theirs[k] for k, _ in after],
         out_specs=[VMEM] * (last + 2),
         scratch_shapes=[
             pltpu.VMEM((len(after) * slab, width), jnp.bfloat16),
             pltpu.VMEM((2 * half_rows, width), jnp.bfloat16),
-            pltpu.VMEM((2, half_rows, width // 2), jnp.float32),
+            pltpu.VMEM((half_rows, width), jnp.float32),
         ],
     )
     returned = [trade(x, k) for k, x in enumerate(whole)] + [trade(keep, last)]
@@ -284,7 +289,7 @@
     left_new, right_new = call(
         functools.partial(gram_kernel, codes),
         [shape(left_gram.shape[1:]), shape(right_gram.shape[1:])],
-        [SMEM, VMEM, VMEM, ANY] + [VMEM] * (2 * rounds),
+        [VMEM, VMEM, VMEM, ANY] + [VMEM] * (2 * rounds),
         block_owner, left_gram[0], right_gram[0], returned[0], *mine, *theirs,
         out_specs=[VMEM, VMEM],
         scratch_shapes=[pltpu.VMEM((width, width), jnp.bfloat16)],
@@ -297,7 +302,7 @@
     passed = [other_core(x[1]) for x in returned[:last]] + [crossed]
     update = call(
         functools.partial(place_kernel, codes), shape((blocks, slab, width // 2)),
-        [SMEM] + [ANY] * (2 * rounds), block_owner, *returned, *passed,
+        [VMEM] + [ANY] * (2 * rounds), block_owner, *returned, *passed,
         out_specs=ANY, scratch_shapes=[pltpu.SemaphoreType.DMA((2 * rounds,))],
     )
     return (left_new[None], right_new[None], update)

time: 42.4 us -> 41.2 us (0.972)
  Pallas kernels: 9.3 us -> 7.78 us
  starting transfers between devices: 29.2 us -> 29.7 us
    pallas_call x7, Pallas kernels: 9.3 us -> 7.78 us  [call(): pl.pallas_call(kernel, out_shape=out_shape, in_specs=in_specs, compiler_p...]
  transfers between devices with their start and end apart: 19 -> 19, of which waited for: 2 -> 2; matrix products, arithmetic and copies ran while one was open for 0% -> 0% of each run, Pallas kernels for 14% -> 13%
where the time goes in v10:
time: 41.2 us; the launch traced here: 41 us
  starting transfers between devices  29.7 us (72%)
  Pallas kernels  7.78 us (19%)
  local copies, waits for them, and re-layouts  1.87 us (5%)
  waiting for transfers between devices  0.94 us (2%)
  between operations  0.79 us (2%)
    ppermute x10, starting transfers between devices, other_core(): return lax.ppermute(x, 'replica', [(0, 1), (1, 0)])  15.3 us
    ppermute x9, starting transfers between devices, trade(): return lax.ppermute(x, ('shard', 'replica'), pairs)  14.3 us
    pallas_call x7, Pallas kernels, call(): pl.pallas_call(kernel, out_shape=out_shape, in_specs=in_specs, compiler_p...  7.78 us
    unnamed x14, local copies, waits for them, and re-layouts  1.85 us
    ppermute x10, waiting for transfers between devices, other_core(): return lax.ppermute(x, 'replica', [(0, 1), (1, 0)])  0.92 us
  transfers between devices with their start and end apart: 19, of which 2 were waited for; matrix products, arithmetic and copies ran while one was open for 0% of the time, Pallas kernels for 13%

profile of v10, /device:TPU:0, one launch (start us, length us, event | category | flops | bytes accessed | tf_op | source)
XLA Modules:
  0.0 41.0 jit_solution(932161499841916258)
XLA Ops:
  0.6 0.5 %collective-permute-start = (bf16[6,96,768]{2,1,0:T(8,128)(2,1)}, bf16[6,96,768]{2,1,0:T(8,128)(2,1)S(1)}, u32[]{:S(2)}, u32[]{:S(2)}) collective-permute-start(bf16[6,96,768]{2,1,0:T(8,128)(2,1)} %bitcast.14), channel_id=1, source_target_pairs={{0,1},{1,0},{2,3},{3,2},{4,5},{5,4},{6,7},{7,6},{8,9},{9,8},{10,11... | collective-permute-start | bytes 2654216 | tf_op jit(solution)/shard_map/ppermute | solution.py:229
  1.1 0.1 collective-permute-start.2
  1.2 0.4 %collective-permute-start.3 = (bf16[768,384]{1,0:T(8,128)(2,1)}, bf16[768,384]{1,0:T(8,128)(2,1)S(1)}, u32[]{:S(2)}, u32[]{:S(2)}) collective-permute-start(bf16[768,384]{1,0:T(8,128)(2,1)} %bitcast.18), channel_id=1, source_target_pairs={{0,1},{1,0},{2,3},{3,2},{4,5},{5,4},{6,7},{7,6},{8,9},{9,8},{10,11... | collective-permute-start | bytes 1769480 | tf_op jit(solution)/shard_map/ppermute | solution.py:229
  1.7 1.2 %copy-done = bf16[1,6,96,768]{3,2,1,0:T(8,128)(2,1)S(1)} copy-done((bf16[1,6,96,768]{3,2,1,0:T(8,128)(2,1)S(1)}, bf16[1,6,96,768]{3,2,1,0:T(8,128)(2,1)}, u32[]{:S(2)}) %copy-start) | copy-done | bytes 884760
  2.8 0.7 %copy-done.3 = s32[6]{0:T(128)S(1)} copy-done((s32[6]{0:T(128)S(1)}, s32[6]{0:T(128)}, u32[]{:S(2)}) %copy-start.3) | copy-done | bytes 48
  3.5 0.1 shard_map.85.mine_ref
  3.5 0.0 collective-permute-done.theirs_ref
  3.6 0.3 shard_map.86
  3.9 2.9 %collective-permute-start.1 = (bf16[96,768]{1,0:T(8,128)(2,1)S(1)}, bf16[96,768]{1,0:T(8,128)(2,1)S(1)}, u32[]{:S(2)}, u32[]{:S(2)}) collective-permute-start(bf16[96,768]{1,0:T(8,128)(2,1)S(1)} %get-tuple-element.26), channel_id=1, source_target_pairs={{0,4},{1,13},{2,6},{3,15},{4,0},{5,9},{6,2},{7,11},{8,12},{9,5},{1... | collective-permute-start | bytes 442376 | tf_op jit(solution)/shard_map/ppermute | solution.py:235
  6.7 1.5 %collective-permute-start.5 = (bf16[96,768]{1,0:T(8,128)(2,1)S(1)}, bf16[96,768]{1,0:T(8,128)(2,1)S(1)}, u32[]{:S(2)}, u32[]{:S(2)}) collective-permute-start(bf16[96,768]{1,0:T(8,128)(2,1)S(1)} %get-tuple-element.33), channel_id=1, source_target_pairs={{0,2},{1,11},{2,0},{3,9},{4,6},{5,15},{6,4},{7,13},{8,10},{9,3},{1... | collective-permute-start | bytes 442376 | tf_op jit(solution)/shard_map/ppermute | solution.py:235
  8.2 0.7 %collective-permute-start.7 = (bf16[96,768]{1,0:T(8,128)(2,1)S(1)}, bf16[96,768]{1,0:T(8,128)(2,1)S(1)}, u32[]{:S(2)}, u32[]{:S(2)}) collective-permute-start(bf16[96,768]{1,0:T(8,128)(2,1)S(1)} %get-tuple-element.34), channel_id=1, source_target_pairs={{0,0},{1,9},{2,2},{3,11},{4,4},{5,13},{6,6},{7,15},{8,8},{9,1},{10... | collective-permute-start | bytes 442376 | tf_op jit(solution)/shard_map/ppermute | solution.py:235
  8.9 0.0 collective-permute-done.2.other_ref
  8.9 0.1 collective-permute-start.8
  9.0 0.0 collective-permute-done.3.other_right_ref
  9.0 1.7 %shard_map.87 = (bf16[768,576]{1,0:T(8,128)(2,1)S(1)}, bf16[768,192]{1,0:T(8,128)(2,1)S(1)}, bf16[768,768]{1,0:T(8,128)(2,1)S(1)}) custom-call(bf16[384,768]{1,0:T(8,128)(2,1)S(1)} %bitcast.17, bf16[384,768]{1,0:T(8,128)(2,1)S(1)} %collective-permute-done.2.other_ref, bf16[768,384]{1,0:T(8,128)(2,1)S(1)} %bitcast.19, ...), custom_call_target="tpu_custom_call" | custom-call | tf_op jit(solution)/shard_map/pallas_call | solution.py:241
  10.7 0.0 collective-permute-done.1.refs_0_
  10.7 5.1 %collective-permute-start.4 = (bf16[96,768]{1,0:T(8,128)(2,1)S(1)}, bf16[96,768]{1,0:T(8,128)(2,1)S(1)}, u32[]{:S(2)}, u32[]{:S(2)}) collective-permute-start(bf16[96,768]{1,0:T(8,128)(2,1)S(1)} %collective-permute-done.1.refs_0_), channel_id=1, source_target_pairs={{0,1},{1,0},{2,3},{3,2},{4,5},{5,4},{6,7},{7,6},{8,9},{9,8},{10,11... | collective-permute-start | bytes 442376 | tf_op jit(solution)/shard_map/ppermute | solution.py:229
  15.9 0.0 collective-permute-done.5.refs_2_.refs_1_
  15.9 1.0 %collective-permute-start.6 = (bf16[96,768]{1,0:T(8,128)(2,1)S(1)}, bf16[96,768]{1,0:T(8,128)(2,1)S(1)}, u32[]{:S(2)}, u32[]{:S(2)}) collective-permute-start(bf16[96,768]{1,0:T(8,128)(2,1)S(1)} %collective-permute-done.5.refs_2_.refs_1_), channel_id=1, source_target_pairs={{0,1},{1,0},{2,3},{3,2},{4,5},{5,4},{6,7},{7,6},{8,9},{9,8},{10,11... | collective-permute-start | bytes 442376 | tf_op jit(solution)/shard_map/ppermute | solution.py:229
  16.8 0.0 collective-permute-done.7.refs_4_.refs_2_
  16.9 3.6 %collective-permute-start.10 = (bf16[96,768]{1,0:T(8,128)(2,1)S(1)}, bf16[96,768]{1,0:T(8,128)(2,1)S(1)}, u32[]{:S(2)}, u32[]{:S(2)}) collective-permute-start(bf16[96,768]{1,0:T(8,128)(2,1)S(1)} %collective-permute-done.7.refs_4_.refs_2_), channel_id=1, source_target_pairs={{0,1},{1,0},{2,3},{3,2},{4,5},{5,4},{6,7},{7,6},{8,9},{9,8},{10,11... | collective-permute-start | bytes 442376 | tf_op jit(solution)/shard_map/ppermute | solution.py:229
  20.4 0.0 collective-permute-done.8.refs_5_.refs_3_
  20.4 0.4 collective-permute-start.9
  20.8 0.0 collective-permute-done.4.refs_1_.refs_4_
  20.8 0.0 collective-permute-done.6.refs_3_.refs_5_
  20.8 1.1 %shard_map.88 = (f32[768,768]{1,0:T(8,128)S(1)}, f32[8,128]{1,0:T(8,128)S(1)}) custom-call(bf16[768,576]{1,0:T(8,128)(2,1)S(1)} %get-tuple-element.31.left_ref, bf16[96,768]{1,0:T(8,128)(2,1)S(1)} %collective-permute-done.1.refs_0_, bf16[96,768]{1,0:T(8,128)(2,1)S(1)} %collective-permute-done.4.refs_1_.refs_4_, ...), custom_call_target="tpu_custom_call" | custom-call | tf_op jit(solution)/shard_map/pallas_call | solution.py:241
  21.9 0.0 copy-start.4
  22.0 0.0 copy-start.5
  22.0 0.0 copy-start.6
  22.0 0.0 collective-permute-done.10.refs_1_.refs_6_
  22.0 0.0 collective-permute-done.9.refs_0_.refs_7_
  22.0 1.6 %shard_map.89 = (bf16[2,96,384]{2,1,0:T(8,128)(2,1)S(1)}, bf16[2,96,384]{2,1,0:T(8,128)(2,1)S(1)}, bf16[2,96,384]{2,1,0:T(8,128)(2,1)S(1)}, bf16[96,384]{1,0:T(8,128)(2,1)S(1)}, bf16[96,384]{1,0:T(8,128)(2,1)S(1)}) custom-call(bf16[768,192]{1,0:T(8,128)(2,1)S(1)} %get-tuple-element.30.left_ref, f32[768,768]{1,0:T(8,128)S(1)} %get-tuple-element.36.total_ref, ...), custom_call_target="tpu_custom_call" | custom-call | tf_op jit(solution)/shard_map/pallas_call | solution.py:241
  23.6 2.3 %collective-permute-start.11 = (bf16[2,96,384]{2,1,0:T(8,128)(2,1)S(1)}, bf16[2,96,384]{2,1,0:T(8,128)(2,1)S(1)}, u32[]{:S(2)}, u32[]{:S(2)}) collective-permute-start(bf16[2,96,384]{2,1,0:T(8,128)(2,1)S(1)} %get-tuple-element.39), channel_id=1, source_target_pairs={{0,4},{1,13},{2,6},{3,15},{4,0},{5,9},{6,2},{7,11},{8,12},{9,5},{1... | collective-permute-start | bytes 442376 | tf_op jit(solution)/shard_map/ppermute | solution.py:235
  25.9 1.0 %collective-permute-start.12 = (bf16[2,96,384]{2,1,0:T(8,128)(2,1)S(1)}, bf16[2,96,384]{2,1,0:T(8,128)(2,1)S(1)}, u32[]{:S(2)}, u32[]{:S(2)}) collective-permute-start(bf16[2,96,384]{2,1,0:T(8,128)(2,1)S(1)} %get-tuple-element.42), channel_id=1, source_target_pairs={{0,2},{1,11},{2,0},{3,9},{4,6},{5,15},{6,4},{7,13},{8,10},{9,3},{1... | collective-permute-start | bytes 442376 | tf_op jit(solution)/shard_map/ppermute | solution.py:235
  26.9 0.7 %collective-permute-start.13 = (bf16[2,96,384]{2,1,0:T(8,128)(2,1)S(1)}, bf16[2,96,384]{2,1,0:T(8,128)(2,1)S(1)}, u32[]{:S(2)}, u32[]{:S(2)}) collective-permute-start(bf16[2,96,384]{2,1,0:T(8,128)(2,1)S(1)} %get-tuple-element.46), channel_id=1, source_target_pairs={{0,0},{1,9},{2,2},{3,11},{4,4},{5,13},{6,6},{7,15},{8,8},{9,1},{10... | collective-permute-start | bytes 442376 | tf_op jit(solution)/shard_map/ppermute | solution.py:235
  27.6 0.6 %collective-permute-start.14 = (bf16[96,384]{1,0:T(8,128)(2,1)S(1)}, bf16[96,384]{1,0:T(8,128)(2,1)S(1)}, u32[]{:S(2)}, u32[]{:S(2)}) collective-permute-start(bf16[96,384]{1,0:T(8,128)(2,1)S(1)} %get-tuple-element.47), channel_id=1, source_target_pairs={{0,6},{1,15},{2,4},{3,13},{4,2},{5,11},{6,0},{7,9},{8,14},{9,7},{1... | collective-permute-start | bytes 221192 | tf_op jit(solution)/shard_map/ppermute | solution.py:235
  28.2 4.7 %collective-permute-start.18 = (bf16[96,384]{1,0:T(8,128)(2,1)S(1)}, bf16[96,384]{1,0:T(8,128)(2,1)S(1)}, u32[]{:S(2)}, u32[]{:S(2)}) collective-permute-start(bf16[96,384]{1,0:T(8,128)(2,1)S(1)} %get-tuple-element.48), channel_id=1, source_target_pairs={{0,7},{1,14},{2,5},{3,12},{4,3},{5,10},{6,1},{7,8},{8,15},{9,6},{1... | collective-permute-start | bytes 221192 | tf_op jit(solution)/shard_map/ppermute | solution.py:235
  32.8 0.0 collective-permute-done.11.after_ref.refs_0_
  32.9 2.1 %shard_map.90 = (bf16[384,768]{1,0:T(8,128)(2,1)}, bf16[384,768]{1,0:T(8,128)(2,1)}) custom-call(s32[1,6]{1,0:T(1,128)S(1)} %bitcast.22, bf16[384,768]{1,0:T(8,128)(2,1)S(1)} %bitcast.24, bf16[384,768]{1,0:T(8,128)(2,1)S(1)} %bitcast.25, bf16[2,96,384]{2,1,0:T(8,128)(2,1)S(1)} %collective-permute-done.11.after_ref.refs_0_, ...), custom_call_target="tpu_custom_call" | custom-call | flops 905969664 | bytes 2359296 | tf_op jit(solution)/shard_map/pallas_call | solution.py:241
  34.9 0.0 collective-permute-done.12.refs_1_
  35.0 3.2 %collective-permute-start.16 = (bf16[96,384]{1,0:T(8,128)(2,1)S(1)}, bf16[96,384]{1,0:T(8,128)(2,1)S(1)}, u32[]{:S(2)}, u32[]{:S(2)}) collective-permute-start(bf16[96,384]{1,0:T(8,128)(2,1)S(1)} %slice_bitcast_fusion.2), channel_id=1, source_target_pairs={{0,1},{1,0},{2,3},{3,2},{4,5},{5,4},{6,7},{7,6},{8,9},{9,8},{10,11... | collective-permute-start | bytes 221192 | tf_op jit(solution)/shard_map/ppermute | solution.py:229
  38.2 0.1 collective-permute-start.15
  38.3 0.9 %collective-permute-start.17 = (bf16[96,384]{1,0:T(8,128)(2,1)S(1)}, bf16[96,384]{1,0:T(8,128)(2,1)S(1)}, u32[]{:S(2)}, u32[]{:S(2)}) collective-permute-start(bf16[96,384]{1,0:T(8,128)(2,1)S(1)} %slice_bitcast_fusion), channel_id=1, source_target_pairs={{0,1},{1,0},{2,3},{3,2},{4,5},{5,4},{6,7},{7,6},{8,9},{9,8},{10,11... | collective-permute-start | bytes 221192 | tf_op jit(solution)/shard_map/ppermute | solution.py:229
  39.2 0.0 collective-permute-done.14.refs_3_
  39.2 0.0 collective-permute-done.18.refs_7_
  39.2 0.3 collective-permute-done.15.refs_4_
  39.5 0.6 %collective-permute-done.17.refs_6_ = bf16[96,384]{1,0:T(8,128)(2,1)S(1)} collective-permute-done((bf16[96,384]{1,0:T(8,128)(2,1)S(1)}, bf16[96,384]{1,0:T(8,128)(2,1)S(1)}, u32[]{:S(2)}, u32[]{:S(2)}) %collective-permute-start.17) | collective-permute-done | bytes 73760 | tf_op jit(solution)/shard_map/ppermute | solution.py:229
  40.1 1.0 %shard_map.91 = bf16[6,96,384]{2,1,0:T(8,128)(2,1)} custom-call(s32[1,6]{1,0:T(1,128)S(1)} %bitcast.23, bf16[2,96,384]{2,1,0:T(8,128)(2,1)S(1)} %collective-permute-done.11.after_ref.refs_0_, bf16[2,96,384]{2,1,0:T(8,128)(2,1)S(1)} %collective-permute-done.12.refs_1_, bf16[2,96,384]{2,1,0:T(8,128)(2,1)S(1)} %collective-permute-done.13.refs_2_, ...), custom_call_target="tpu_custom_call" | custom-call | tf_op jit(solution)/shard_map/pallas_call | solution.py:241
  (14 shorter events, 0.0 us)
Async XLA Ops:
  0.6 2.9 %collective-permute-start = (bf16[6,96,768]{2,1,0:T(8,128)(2,1)}, bf16[6,96,768]{2,1,0:T(8,128)(2,1)S(1)}, u32[]{:S(2)}, u32[]{:S(2)}) collective-permute-start(bf16[6,96,768]{2,1,0:T(8,128)(2,1)} %bitcast.14), channel_id=1, source_target_pairs={{0,1},{1,0},{2,3},{3,2},{4,5},{5,4},{6,7},{7,6},{8,9},{9,8},{10,11... | collective-permute-start | bytes 2654216 | tf_op jit(solution)/shard_map/ppermute | solution.py:229
  1.1 7.8 %collective-permute-start.2 = (bf16[384,768]{1,0:T(8,128)(2,1)}, bf16[384,768]{1,0:T(8,128)(2,1)S(1)}, u32[]{:S(2)}, u32[]{:S(2)}) collective-permute-start(bf16[384,768]{1,0:T(8,128)(2,1)} %bitcast.16), channel_id=1, source_target_pairs={{0,1},{1,0},{2,3},{3,2},{4,5},{5,4},{6,7},{7,6},{8,9},{9,8},{10,11... | collective-permute-start | bytes 1769480 | tf_op jit(solution)/shard_map/ppermute | solution.py:229
  1.2 7.8 %collective-permute-start.3 = (bf16[768,384]{1,0:T(8,128)(2,1)}, bf16[768,384]{1,0:T(8,128)(2,1)S(1)}, u32[]{:S(2)}, u32[]{:S(2)}) collective-permute-start(bf16[768,384]{1,0:T(8,128)(2,1)} %bitcast.18), channel_id=1, source_target_pairs={{0,1},{1,0},{2,3},{3,2},{4,5},{5,4},{6,7},{7,6},{8,9},{9,8},{10,11... | collective-permute-start | bytes 1769480 | tf_op jit(solution)/shard_map/ppermute | solution.py:229
  1.7 1.2 %copy-start = (bf16[1,6,96,768]{3,2,1,0:T(8,128)(2,1)S(1)}, bf16[1,6,96,768]{3,2,1,0:T(8,128)(2,1)}, u32[]{:S(2)}) copy-start(bf16[1,6,96,768]{3,2,1,0:T(8,128)(2,1)} %param.6) | copy-start | bytes 2654212
  2.8 0.7 %copy-start.3 = (s32[6]{0:T(128)S(1)}, s32[6]{0:T(128)}, u32[]{:S(2)}) copy-start(s32[6]{0:T(128)} %param.7) | copy-start | bytes 76
  3.5 5.5 %copy-start.1 = (bf16[1,384,768]{2,1,0:T(8,128)(2,1)S(1)}, bf16[1,384,768]{2,1,0:T(8,128)(2,1)}, u32[]{:S(2)}) copy-start(bf16[1,384,768]{2,1,0:T(8,128)(2,1)} %param.10) | copy-start | bytes 1769476
  3.5 5.5 %copy-start.2 = (bf16[1,768,384]{2,1,0:T(8,128)(2,1)S(1)}, bf16[1,768,384]{2,1,0:T(8,128)(2,1)}, u32[]{:S(2)}) copy-start(bf16[1,768,384]{2,1,0:T(8,128)(2,1)} %param.11) | copy-start | bytes 1769476
  3.9 6.8 %collective-permute-start.1 = (bf16[96,768]{1,0:T(8,128)(2,1)S(1)}, bf16[96,768]{1,0:T(8,128)(2,1)S(1)}, u32[]{:S(2)}, u32[]{:S(2)}) collective-permute-start(bf16[96,768]{1,0:T(8,128)(2,1)S(1)} %get-tuple-element.26), channel_id=1, source_target_pairs={{0,4},{1,13},{2,6},{3,15},{4,0},{5,9},{6,2},{7,11},{8,12},{9,5},{1... | collective-permute-start | bytes 442376 | tf_op jit(solution)/shard_map/ppermute | solution.py:235
  6.7 9.1 %collective-permute-start.5 = (bf16[96,768]{1,0:T(8,128)(2,1)S(1)}, bf16[96,768]{1,0:T(8,128)(2,1)S(1)}, u32[]{:S(2)}, u32[]{:S(2)}) collective-permute-start(bf16[96,768]{1,0:T(8,128)(2,1)S(1)} %get-tuple-element.33), channel_id=1, source_target_pairs={{0,2},{1,11},{2,0},{3,9},{4,6},{5,15},{6,4},{7,13},{8,10},{9,3},{1... | collective-permute-start | bytes 442376 | tf_op jit(solution)/shard_map/ppermute | solution.py:235
  8.2 8.6 %collective-permute-start.7 = (bf16[96,768]{1,0:T(8,128)(2,1)S(1)}, bf16[96,768]{1,0:T(8,128)(2,1)S(1)}, u32[]{:S(2)}, u32[]{:S(2)}) collective-permute-start(bf16[96,768]{1,0:T(8,128)(2,1)S(1)} %get-tuple-element.34), channel_id=1, source_target_pairs={{0,0},{1,9},{2,2},{3,11},{4,4},{5,13},{6,6},{7,15},{8,8},{9,1},{10... | collective-permute-start | bytes 442376 | tf_op jit(solution)/shard_map/ppermute | solution.py:235
  8.9 11.5 %collective-permute-start.8 = (bf16[96,768]{1,0:T(8,128)(2,1)S(1)}, bf16[96,768]{1,0:T(8,128)(2,1)S(1)}, u32[]{:S(2)}, u32[]{:S(2)}) collective-permute-start(bf16[96,768]{1,0:T(8,128)(2,1)S(1)} %get-tuple-element.35), channel_id=1, source_target_pairs={{0,6},{1,15},{2,4},{3,13},{4,2},{5,11},{6,0},{7,9},{8,14},{9,7},{1... | collective-permute-start | bytes 442376 | tf_op jit(solution)/shard_map/ppermute | solution.py:235
  10.7 10.1 %collective-permute-start.4 = (bf16[96,768]{1,0:T(8,128)(2,1)S(1)}, bf16[96,768]{1,0:T(8,128)(2,1)S(1)}, u32[]{:S(2)}, u32[]{:S(2)}) collective-permute-start(bf16[96,768]{1,0:T(8,128)(2,1)S(1)} %collective-permute-done.1.refs_0_), channel_id=1, source_target_pairs={{0,1},{1,0},{2,3},{3,2},{4,5},{5,4},{6,7},{7,6},{8,9},{9,8},{10,11... | collective-permute-start | bytes 442376 | tf_op jit(solution)/shard_map/ppermute | solution.py:229
  15.9 5.0 %collective-permute-start.6 = (bf16[96,768]{1,0:T(8,128)(2,1)S(1)}, bf16[96,768]{1,0:T(8,128)(2,1)S(1)}, u32[]{:S(2)}, u32[]{:S(2)}) collective-permute-start(bf16[96,768]{1,0:T(8,128)(2,1)S(1)} %collective-permute-done.5.refs_2_.refs_1_), channel_id=1, source_target_pairs={{0,1},{1,0},{2,3},{3,2},{4,5},{5,4},{6,7},{7,6},{8,9},{9,8},{10,11... | collective-permute-start | bytes 442376 | tf_op jit(solution)/shard_map/ppermute | solution.py:229
  16.9 5.1 %collective-permute-start.10 = (bf16[96,768]{1,0:T(8,128)(2,1)S(1)}, bf16[96,768]{1,0:T(8,128)(2,1)S(1)}, u32[]{:S(2)}, u32[]{:S(2)}) collective-permute-start(bf16[96,768]{1,0:T(8,128)(2,1)S(1)} %collective-permute-done.7.refs_4_.refs_2_), channel_id=1, source_target_pairs={{0,1},{1,0},{2,3},{3,2},{4,5},{5,4},{6,7},{7,6},{8,9},{9,8},{10,11... | collective-permute-start | bytes 442376 | tf_op jit(solution)/shard_map/ppermute | solution.py:229
  20.4 1.5 %collective-permute-start.9 = (bf16[96,768]{1,0:T(8,128)(2,1)S(1)}, bf16[96,768]{1,0:T(8,128)(2,1)S(1)}, u32[]{:S(2)}, u32[]{:S(2)}) collective-permute-start(bf16[96,768]{1,0:T(8,128)(2,1)S(1)} %collective-permute-done.8.refs_5_.refs_3_), channel_id=1, source_target_pairs={{0,1},{1,0},{2,3},{3,2},{4,5},{5,4},{6,7},{7,6},{8,9},{9,8},{10,11... | collective-permute-start | bytes 442376 | tf_op jit(solution)/shard_map/ppermute | solution.py:229
  21.9 10.9 %copy-start.4 = (s32[6]{0:T(128)S(1)}, s32[6]{0:T(128)}, u32[]{:S(2)}) copy-start(s32[6]{0:T(128)} %param.7) | copy-start | bytes 76
  22.0 10.9 %copy-start.5 = (bf16[1,384,768]{2,1,0:T(8,128)(2,1)S(1)}, bf16[1,384,768]{2,1,0:T(8,128)(2,1)}, u32[]{:S(2)}) copy-start(bf16[1,384,768]{2,1,0:T(8,128)(2,1)} %param.8) | copy-start | bytes 1769476
  22.0 10.9 %copy-start.6 = (bf16[1,384,768]{2,1,0:T(8,128)(2,1)S(1)}, bf16[1,384,768]{2,1,0:T(8,128)(2,1)}, u32[]{:S(2)}) copy-start(bf16[1,384,768]{2,1,0:T(8,128)(2,1)} %param.9) | copy-start | bytes 1769476
  23.6 9.2 %collective-permute-start.11 = (bf16[2,96,384]{2,1,0:T(8,128)(2,1)S(1)}, bf16[2,96,384]{2,1,0:T(8,128)(2,1)S(1)}, u32[]{:S(2)}, u32[]{:S(2)}) collective-permute-start(bf16[2,96,384]{2,1,0:T(8,128)(2,1)S(1)} %get-tuple-element.39), channel_id=1, source_target_pairs={{0,4},{1,13},{2,6},{3,15},{4,0},{5,9},{6,2},{7,11},{8,12},{9,5},{1... | collective-permute-start | bytes 442376 | tf_op jit(solution)/shard_map/ppermute | solution.py:235
  25.9 9.1 %collective-permute-start.12 = (bf16[2,96,384]{2,1,0:T(8,128)(2,1)S(1)}, bf16[2,96,384]{2,1,0:T(8,128)(2,1)S(1)}, u32[]{:S(2)}, u32[]{:S(2)}) collective-permute-start(bf16[2,96,384]{2,1,0:T(8,128)(2,1)S(1)} %get-tuple-element.42), channel_id=1, source_target_pairs={{0,2},{1,11},{2,0},{3,9},{4,6},{5,15},{6,4},{7,13},{8,10},{9,3},{1... | collective-permute-start | bytes 442376 | tf_op jit(solution)/shard_map/ppermute | solution.py:235
  26.9 11.4 %collective-permute-start.13 = (bf16[2,96,384]{2,1,0:T(8,128)(2,1)S(1)}, bf16[2,96,384]{2,1,0:T(8,128)(2,1)S(1)}, u32[]{:S(2)}, u32[]{:S(2)}) collective-permute-start(bf16[2,96,384]{2,1,0:T(8,128)(2,1)S(1)} %get-tuple-element.46), channel_id=1, source_target_pairs={{0,0},{1,9},{2,2},{3,11},{4,4},{5,13},{6,6},{7,15},{8,8},{9,1},{10... | collective-permute-start | bytes 442376 | tf_op jit(solution)/shard_map/ppermute | solution.py:235
  27.6 11.6 %collective-permute-start.14 = (bf16[96,384]{1,0:T(8,128)(2,1)S(1)}, bf16[96,384]{1,0:T(8,128)(2,1)S(1)}, u32[]{:S(2)}, u32[]{:S(2)}) collective-permute-start(bf16[96,384]{1,0:T(8,128)(2,1)S(1)} %get-tuple-element.47), channel_id=1, source_target_pairs={{0,6},{1,15},{2,4},{3,13},{4,2},{5,11},{6,0},{7,9},{8,14},{9,7},{1... | collective-permute-start | bytes 221192 | tf_op jit(solution)/shard_map/ppermute | solution.py:235
  28.2 11.0 %collective-permute-start.18 = (bf16[96,384]{1,0:T(8,128)(2,1)S(1)}, bf16[96,384]{1,0:T(8,128)(2,1)S(1)}, u32[]{:S(2)}, u32[]{:S(2)}) collective-permute-start(bf16[96,384]{1,0:T(8,128)(2,1)S(1)} %get-tuple-element.48), channel_id=1, source_target_pairs={{0,7},{1,14},{2,5},{3,12},{4,3},{5,10},{6,1},{7,8},{8,15},{9,6},{1... | collective-permute-start | bytes 221192 | tf_op jit(solution)/shard_map/ppermute | solution.py:235
  35.0 4.2 %collective-permute-start.16 = (bf16[96,384]{1,0:T(8,128)(2,1)S(1)}, bf16[96,384]{1,0:T(8,128)(2,1)S(1)}, u32[]{:S(2)}, u32[]{:S(2)}) collective-permute-start(bf16[96,384]{1,0:T(8,128)(2,1)S(1)} %slice_bitcast_fusion.2), channel_id=1, source_target_pairs={{0,1},{1,0},{2,3},{3,2},{4,5},{5,4},{6,7},{7,6},{8,9},{9,8},{10,11... | collective-permute-start | bytes 221192 | tf_op jit(solution)/shard_map/ppermute | solution.py:229
  38.2 1.3 %collective-permute-start.15 = (bf16[96,384]{1,0:T(8,128)(2,1)S(1)}, bf16[96,384]{1,0:T(8,128)(2,1)S(1)}, u32[]{:S(2)}, u32[]{:S(2)}) collective-permute-start(bf16[96,384]{1,0:T(8,128)(2,1)S(1)} %slice_bitcast_fusion.1), channel_id=1, source_target_pairs={{0,1},{1,0},{2,3},{3,2},{4,5},{5,4},{6,7},{7,6},{8,9},{9,8},{10,11... | collective-permute-start | bytes 221192 | tf_op jit(solution)/shard_map/ppermute | solution.py:229
  38.3 1.8 %collective-permute-start.17 = (bf16[96,384]{1,0:T(8,128)(2,1)S(1)}, bf16[96,384]{1,0:T(8,128)(2,1)S(1)}, u32[]{:S(2)}, u32[]{:S(2)}) collective-permute-start(bf16[96,384]{1,0:T(8,128)(2,1)S(1)} %slice_bitcast_fusion), channel_id=1, source_target_pairs={{0,1},{1,0},{2,3},{3,2},{4,5},{5,4},{6,7},{7,6},{8,9},{9,8},{10,11... | collective-permute-start | bytes 221192 | tf_op jit(solution)/shard_map/ppermute | solution.py:229

commit v11 on v10

v11 whole, which is shorter than its diff:
```python
import functools

import jax
import jax.numpy as jnp
from jax import lax
from jax.experimental import pallas as pl
from jax.experimental.pallas import tpu as pltpu
from jax.sharding import PartitionSpec as P

VMEM = pl.BlockSpec(memory_space=pltpu.VMEM)
ANY = pl.BlockSpec(memory_space=pl.ANY)
LIGHT = pl.CostEstimate(flops=0, bytes_accessed=0, transcendentals=0)
OUT = ((2, 6), (1, 5), (0, 4), (3, 7))
BACK = ((2, 4), (3, 5), (1, 7))
SHARED, SELF = (6, 6), (0, 0)
PARAMS = pltpu.CompilerParams(vmem_limit_bytes=24 * 1024 * 1024)


def per_device(gradients, block_owner, left_gram, right_gram, left_root, right_root):
    owners = lax.axis_size("shard")
    half_rows = left_gram.shape[1]
    full_width = left_gram.shape[2]
    first_row = lax.axis_index("replica") * half_rows
    owner_index = lax.broadcasted_iota(jnp.int32, (owners, block_owner.shape[0]), 0)
    owner_onehot = (owner_index == block_owner[None, :]).astype(jnp.bfloat16)
    outgoing = jnp.einsum(
        "ob,brc->orc", owner_onehot, gradients[0], preferred_element_type=jnp.float32
    )
    arrived = lax.all_to_all(
        outgoing.astype(jnp.bfloat16), "shard", split_axis=0, concat_axis=0, tiled=True
    )
    total = lax.psum(arrived.astype(jnp.float32).astype(jnp.bfloat16), "replica")
    summed_block = total.reshape(full_width, full_width)
    own_rows = lax.dynamic_slice_in_dim(summed_block, first_row, half_rows, 0)
    own_cols = lax.dynamic_slice_in_dim(summed_block, first_row, half_rows, 1)
    left_term = lax.dot_general(
        own_rows, summed_block, (((1,), (1,)), ((), ())), preferred_element_type=jnp.float32
    )
    right_term = lax.dot_general(
        own_cols, summed_block, (((0,), (0,)), ((), ())), preferred_element_type=jnp.float32
    )
    left_new = (0.99 * left_gram[0].astype(jnp.float32) + 0.01 * left_term).astype(jnp.bfloat16)
    right_new = (0.99 * right_gram[0].astype(jnp.float32) + 0.01 * right_term).astype(jnp.bfloat16)
    partial_side = jnp.dot(left_root[0], summed_block, preferred_element_type=jnp.float32).astype(
        jnp.bfloat16
    )
    left_side = lax.all_gather(partial_side, "replica", axis=0, tiled=True)
    both_sides = jnp.dot(left_side, right_root[0], preferred_element_type=jnp.float32)
    side_squares = lax.psum(jnp.sum(both_sides * both_sides), "replica")
    grad_squares = jnp.sum(jnp.square(summed_block.astype(jnp.float32)))
    graft = jnp.sqrt(grad_squares / (side_squares + 1e-06))
    scaled = (
        (both_sides * graft).astype(jnp.bfloat16).reshape(owners, full_width // owners, half_rows)
    )
    returned = lax.all_to_all(scaled, "shard", split_axis=0, concat_axis=0, tiled=True)
    update = jnp.take(returned, block_owner, axis=0)
    return (left_new[None], right_new[None], update)


def turned(rounds):
    return tuple(codes[::-1] for codes in rounds)


def partner(codes):
    code = jnp.where(lax.axis_index("replica") == 0, codes[0], codes[1])
    return lax.axis_index("shard") ^ code


def block_of(owner_ref, owner):
    block = jnp.int32(-1)
    for b in range(owner_ref.shape[1]):
        block = jnp.where(owner_ref[0, b] == owner, b, block)
    return block


def squares(value):
    wide = value.astype(jnp.float32)
    rows = jnp.sum((wide * wide).reshape(-1, 8, wide.shape[1]), axis=0)
    return jnp.sum(jnp.sum(rows, axis=0, keepdims=True), axis=1, keepdims=True)


def fetch_kernel(gradient_ref, after_ref, out_ref):
    out_ref[...] = gradient_ref[...]


def pick_kernel(owner_ref, mine_ref, theirs_ref, *out_refs):
    for codes, out_ref in zip(OUT, out_refs):
        b = jnp.maximum(block_of(owner_ref, partner(codes)), 0)
        total = mine_ref[b].astype(jnp.float32) + theirs_ref[b].astype(jnp.float32)
        out_ref[...] = total.astype(out_ref.dtype)


def order_kernel(rows, columns, own_ref, other_ref, own_right_ref, other_right_ref, *refs):
    *out_refs, right_ref, rows_ref = refs
    right_ref[:, :own_right_ref.shape[1]] = own_right_ref[...]
    right_ref[:, own_right_ref.shape[1]:] = other_right_ref[...]
    half, full = own_ref.shape
    slab = full // len(rows)
    core = lax.axis_index("replica")
    for n, codes in enumerate(rows):
        start = partner(codes) * slab
        row = pl.multiple_of(lax.rem(start, half), slab)
        for ref, near in ((own_ref, True), (other_ref, False)):

            @pl.when((lax.div(start, half) == core) == near)
            def _(ref=ref):
                rows_ref[n * slab:(n + 1) * slab, :] = ref[pl.ds(row, slab), :]

    for out_ref, group in zip(out_refs, columns):
        column = lax.broadcasted_iota(jnp.int32, (1, len(group) * slab), 1)
        source = column
        for n, codes in enumerate(group):
            inside = (column >= n * slab) & (column < (n + 1) * slab)
            source = jnp.where(inside, column + (partner(codes) - n) * slab, source)
        row_index = lax.broadcasted_iota(jnp.int32, (full, len(group) * slab), 0)
        choose = (row_index == source).astype(jnp.float32).astype(rows_ref.dtype)
        out_ref[...] = jnp.dot(
            rows_ref[...], choose, preferred_element_type=jnp.float32
        ).astype(out_ref.dtype)


def begin_kernel(left_ref, *refs):
    *slabs, total_ref, grad_sq_ref, stacked_ref = refs
    slab = slabs[0].shape[0]
    for n, ref in enumerate(slabs):
        stacked_ref[n * slab:(n + 1) * slab, :] = ref[...]
    total_ref[...] = jnp.dot(
        left_ref[...], stacked_ref[...], preferred_element_type=jnp.float32
    )
    grad_sq_ref[...] = jnp.broadcast_to(squares(stacked_ref[...]), grad_sq_ref.shape)


def finish_kernel(count, left_ref, total_ref, begun_sq_ref, right_ref, *refs):
    slabs = refs[:count]
    *out_refs, stacked_ref, side_ref, both_ref = refs[count:]
    slab = slabs[0].shape[0]
    used, full = both_ref.shape
    for n, ref in enumerate(slabs):
        stacked_ref[n * slab:(n + 1) * slab, :] = ref[...]
    last = stacked_ref[...]
    side = total_ref[...] + jnp.dot(left_ref[...], last, preferred_element_type=jnp.float32)
    side_ref[...] = side.astype(side_ref.dtype)
    grad_sq = begun_sq_ref[0:1, 0:1] + squares(last)
    both = jnp.dot(side_ref[...], right_ref[...], preferred_element_type=jnp.float32)
    both_ref[...] = both[:used]
    graft = jnp.sqrt(grad_sq / (squares(both) + 1e-06))
    for k, out_ref in enumerate(out_refs):
        rows = slice(k * slab, (k + 1) * slab)
        if len(out_ref.shape) == 2:
            out_ref[...] = (both_ref[rows, :full // 2] * graft).astype(out_ref.dtype)
        else:
            out_ref[0] = (both_ref[rows, :full // 2] * graft).astype(out_ref.dtype)
            out_ref[1] = (both_ref[rows, full // 2:] * graft).astype(out_ref.dtype)


def gram_kernel(owner_ref, left_ref, right_ref, after_ref, *refs):
    *slabs, left_out, right_out, summed_ref = refs
    slab = slabs[0].shape[0]
    for codes, ref in zip(OUT + turned(OUT), slabs):
        row = pl.multiple_of(partner(codes) * slab, slab)
        summed_ref[pl.ds(row, slab), :] = ref[...]
    half = left_ref.shape[0]
    first = pl.multiple_of(lax.axis_index("replica") * half, 128)
    present = block_of(owner_ref, lax.axis_index("shard")) >= 0
    share = jnp.where(present, 0.01, 0.0).astype(jnp.float32)
    summed = summed_ref[...]
    left_term = lax.dot_general(
        summed_ref[pl.ds(first, half), :], summed, (((1,), (1,)), ((), ())),
        preferred_element_type=jnp.float32,
    )
    left_out[...] = (0.99 * left_ref[...].astype(jnp.float32) + share * left_term).astype(
        left_out.dtype
    )
    right_term = lax.dot_general(
        summed_ref[:, pl.ds(first, half)], summed, (((0,), (0,)), ((), ())),
        preferred_element_type=jnp.float32,
    )
    right_out[...] = (0.99 * right_ref[...].astype(jnp.float32) + share * right_term).astype(
        right_out.dtype
    )


def place_kernel(owner_ref, *refs):
    *slabs, out_ref, sem = refs
    pending = []
    for n, codes in enumerate(BACK + turned(BACK) + (SELF, SHARED)):
        block = block_of(owner_ref, partner(codes))
        source = slabs[n] if len(slabs[n].shape) == 2 else slabs[n].at[0]
        copy = pltpu.make_async_copy(source, out_ref.at[jnp.maximum(block, 0)], sem.at[n])

        @pl.when(block >= 0)
        def _(copy=copy):
            copy.start()

        pending.append((block, copy))
    for block, copy in pending:

        @pl.when(block >= 0)
        def _(copy=copy):
            copy.wait()


def per_device_paired(gradients, block_owner, left_gram, right_gram, left_root, right_root):
    owners = lax.axis_size("shard")
    rounds = len(OUT)
    blocks, slab, width = gradients.shape[1:]
    half_rows = left_gram.shape[1]
    rows = BACK + (SHARED, SELF) + turned(BACK)
    theirs_last = (rounds - 1, rounds - 2)
    sooner = OUT + turned(OUT)[:rounds - 2]
    columns = (sooner, tuple(turned(OUT)[k] for k in theirs_last))

    def other_core(x):
        return lax.ppermute(x, "replica", [(0, 1), (1, 0)])

    def trade(x, codes):
        pairs = [(s * 2 + r, (s ^ codes[r]) * 2 + r) for s in range(owners) for r in range(2)]
        return lax.ppermute(x, ("shard", "replica"), pairs)

    def shape(dims, dtype=jnp.bfloat16):
        return jax.ShapeDtypeStruct(dims, dtype)

    def call(kernel, out_shape, in_specs, *args, params=PARAMS, cost_estimate=LIGHT, **options):
        return pl.pallas_call(
            kernel, out_shape=out_shape, in_specs=in_specs, compiler_params=params,
            cost_estimate=cost_estimate, **options
        )(*args)

    block_owner = block_owner.reshape(1, blocks)
    other_gradient = other_core(gradients[0])
    fetched = call(
        fetch_kernel, shape((blocks, slab, width)), [VMEM, ANY], gradients[0], block_owner,
        out_specs=VMEM,
    )
    *outgoing, = call(
        pick_kernel, [shape((slab, width))] * rounds,
        [VMEM, VMEM, VMEM], block_owner, fetched, other_gradient, out_specs=[VMEM] * rounds,
    )
    mine = [trade(x, codes) for x, codes in zip(outgoing, OUT)]
    other_left, other_right = other_core(left_root[0]), other_core(right_root[0])
    left_sooner, left_last, right = call(
        functools.partial(order_kernel, rows, columns),
        [shape((width, len(group) * slab)) for group in columns] + [shape((width, width))],
        [VMEM] * 4, left_root[0], other_left, right_root[0], other_right, out_specs=[VMEM] * 3,
        scratch_shapes=[pltpu.VMEM((width, width), jnp.bfloat16)],
    )
    mine[0], left_sooner, left_last, right = lax.optimization_barrier(
        (mine[0], left_sooner, left_last, right)
    )
    theirs = [other_core(x) for x in mine]
    begun, begun_sq = call(
        begin_kernel,
        [shape((width, width), jnp.float32), shape((8, 128), jnp.float32)],
        [VMEM] * (1 + len(sooner)), left_sooner, *mine, *theirs[:rounds - 2],
        out_specs=[VMEM, VMEM],
        scratch_shapes=[pltpu.VMEM((len(sooner) * slab, width), jnp.bfloat16)],
    )
    half_slab = shape((slab, width // 2))
    *whole, shared, own = call(
        functools.partial(finish_kernel, len(theirs_last)),
        [shape((2, slab, width // 2))] * len(BACK) + [half_slab] * 2,
        [VMEM] * (4 + len(theirs_last)),
        left_last, begun, begun_sq, right, *[theirs[k] for k in theirs_last],
        out_specs=[VMEM] * (len(BACK) + 2),
        scratch_shapes=[
            pltpu.VMEM((len(theirs_last) * slab, width), jnp.bfloat16),
            pltpu.VMEM((width, width), jnp.bfloat16),
            pltpu.VMEM(((len(BACK) + 2) * slab, width), jnp.float32),
        ],
    )
    returned = [trade(x, codes) for x, codes in zip(whole, BACK)]
    shared = trade(shared, SHARED)
    left_new, right_new = call(
        gram_kernel, [shape(left_gram.shape[1:]), shape(right_gram.shape[1:])],
        [VMEM, VMEM, VMEM, ANY] + [VMEM] * (2 * rounds),
        block_owner, left_gram[0], right_gram[0], returned[0], *mine, *theirs,
        out_specs=[VMEM, VMEM],
        scratch_shapes=[pltpu.VMEM((width, width), jnp.bfloat16)],
        cost_estimate=pl.CostEstimate(
            flops=4 * half_rows * width * width, bytes_accessed=8 * half_rows * width,
            transcendentals=0,
        ),
    )
    left_new, right_new, returned[0] = lax.optimization_barrier(
        (left_new, right_new, returned[0])
    )
    passed = [other_core(x[1]) for x in returned]
    update = call(
        place_kernel, shape((blocks, slab, width // 2)), [VMEM] + [ANY] * owners,
        block_owner, *returned, *passed, own, shared,
        out_specs=ANY, scratch_shapes=[pltpu.SemaphoreType.DMA((owners,))],
    )
    return (left_new[None], right_new[None], update)


def solution(mesh):
    owners = mesh.shape["shard"]
    paired = mesh.shape["replica"] == 2 and owners == 2 * len(OUT)
    return jax.shard_map(
        per_device_paired if paired else per_device,
        mesh=mesh,
        in_specs=(
            P("replica", "groups", "shard", None),
            P("groups"),
            P(("groups", "shard"), "replica", None),
            P(("groups", "shard"), "replica", None),
            P(("groups", "shard"), "replica", None),
            P(("groups", "shard"), None, "replica"),
        ),
        out_specs=(
            P(("groups", "shard"), "replica", None),
            P(("groups", "shard"), "replica", None),
            P("groups", "shard", "replica"),
        ),
        check_vma=False,
    )
```

time: 41.2 us -> 40.2 us (0.976)
  starting transfers between devices: 29.7 us -> 28 us
  waiting for transfers between devices: 0.94 us -> 1.48 us
    ppermute x9 -> x8, starting transfers between devices: 14.3 us -> 11.4 us  [trade(): return lax.ppermute(x, ('shard', 'replica'), pairs)]
    ppermute x10, starting transfers between devices: 15.3 us -> 16.5 us  [other_core(): return lax.ppermute(x, 'replica', [(0, 1), (1, 0)])]
    ppermute x9 -> x8, waiting for transfers between devices: 0.02 us -> 0.56 us  [trade(): return lax.ppermute(x, ('shard', 'replica'), pairs)]
  transfers between devices with their start and end apart: 19 -> 18, of which waited for: 2 -> 3; matrix products, arithmetic and copies ran while one was open for 0% -> 0% of each run, Pallas kernels for 13% -> 13%
where the time goes in v11:
time: 40.2 us; the launch traced here: 39.9 us
  starting transfers between devices  28 us (70%)
  Pallas kernels  7.81 us (19%)
  local copies, waits for them, and re-layouts  1.87 us (5%)
  waiting for transfers between devices  1.48 us (4%)
  between operations  0.77 us (2%)
    ppermute x10, starting transfers between devices, other_core(): return lax.ppermute(x, 'replica', [(0, 1), (1, 0)])  16.5 us
    ppermute x8, starting transfers between devices, trade(): return lax.ppermute(x, ('shard', 'replica'), pairs)  11.4 us
    pallas_call x7, Pallas kernels, call(): pl.pallas_call(kernel, out_shape=out_shape, in_specs=in_specs, compiler_p...  7.81 us
    unnamed x14, local copies, waits for them, and re-layouts  1.85 us
    ppermute x10, waiting for transfers between devices, other_core(): return lax.ppermute(x, 'replica', [(0, 1), (1, 0)])  0.92 us
  transfers between devices with their start and end apart: 18, of which 3 were waited for; matrix products, arithmetic and copies ran while one was open for 0% of the time, Pallas kernels for 13%

profile of v11, /device:TPU:0, one launch (start us, length us, event | category | flops | bytes accessed | tf_op | source)
XLA Modules:
  0.0 39.9 jit_solution(2921361858775412902)
XLA Ops:
  0.6 0.5 %collective-permute-start = (bf16[6,96,768]{2,1,0:T(8,128)(2,1)}, bf16[6,96,768]{2,1,0:T(8,128)(2,1)S(1)}, u32[]{:S(2)}, u32[]{:S(2)}) collective-permute-start(bf16[6,96,768]{2,1,0:T(8,128)(2,1)} %bitcast.14), channel_id=1, source_target_pairs={{0,1},{1,0},{2,3},{3,2},{4,5},{5,4},{6,7},{7,6},{8,9},{9,8},{10,11... | collective-permute-start | bytes 2654216 | tf_op jit(solution)/shard_map/ppermute | solution.py:214
  1.1 0.1 collective-permute-start.2
  1.2 0.4 %collective-permute-start.3 = (bf16[768,384]{1,0:T(8,128)(2,1)}, bf16[768,384]{1,0:T(8,128)(2,1)S(1)}, u32[]{:S(2)}, u32[]{:S(2)}) collective-permute-start(bf16[768,384]{1,0:T(8,128)(2,1)} %bitcast.18), channel_id=1, source_target_pairs={{0,1},{1,0},{2,3},{3,2},{4,5},{5,4},{6,7},{7,6},{8,9},{9,8},{10,11... | collective-permute-start | bytes 1769480 | tf_op jit(solution)/shard_map/ppermute | solution.py:214
  1.7 1.2 %copy-done = bf16[1,6,96,768]{3,2,1,0:T(8,128)(2,1)S(1)} copy-done((bf16[1,6,96,768]{3,2,1,0:T(8,128)(2,1)S(1)}, bf16[1,6,96,768]{3,2,1,0:T(8,128)(2,1)}, u32[]{:S(2)}) %copy-start) | copy-done | bytes 884760
  2.8 0.7 %copy-done.3 = s32[6]{0:T(128)S(1)} copy-done((s32[6]{0:T(128)S(1)}, s32[6]{0:T(128)}, u32[]{:S(2)}) %copy-start.3) | copy-done | bytes 48
  3.5 0.1 shard_map.85.mine_ref
  3.5 0.0 collective-permute-done.theirs_ref
  3.6 0.3 shard_map.86
  3.9 2.9 %collective-permute-start.1 = (bf16[96,768]{1,0:T(8,128)(2,1)S(1)}, bf16[96,768]{1,0:T(8,128)(2,1)S(1)}, u32[]{:S(2)}, u32[]{:S(2)}) collective-permute-start(bf16[96,768]{1,0:T(8,128)(2,1)S(1)} %get-tuple-element.26), channel_id=1, source_target_pairs={{0,4},{1,13},{2,6},{3,15},{4,0},{5,9},{6,2},{7,11},{8,12},{9,5},{1... | collective-permute-start | bytes 442376 | tf_op jit(solution)/shard_map/ppermute | solution.py:218
  6.7 1.5 %collective-permute-start.4 = (bf16[96,768]{1,0:T(8,128)(2,1)S(1)}, bf16[96,768]{1,0:T(8,128)(2,1)S(1)}, u32[]{:S(2)}, u32[]{:S(2)}) collective-permute-start(bf16[96,768]{1,0:T(8,128)(2,1)S(1)} %get-tuple-element.33), channel_id=1, source_target_pairs={{0,2},{1,11},{2,0},{3,9},{4,6},{5,15},{6,4},{7,13},{8,10},{9,3},{1... | collective-permute-start | bytes 442376 | tf_op jit(solution)/shard_map/ppermute | solution.py:218
  8.2 0.7 %collective-permute-start.5 = (bf16[96,768]{1,0:T(8,128)(2,1)S(1)}, bf16[96,768]{1,0:T(8,128)(2,1)S(1)}, u32[]{:S(2)}, u32[]{:S(2)}) collective-permute-start(bf16[96,768]{1,0:T(8,128)(2,1)S(1)} %get-tuple-element.34), channel_id=1, source_target_pairs={{0,0},{1,9},{2,2},{3,11},{4,4},{5,13},{6,6},{7,15},{8,8},{9,1},{10... | collective-permute-start | bytes 442376 | tf_op jit(solution)/shard_map/ppermute | solution.py:218
  8.9 0.0 collective-permute-done.2.other_ref
  8.9 0.1 collective-permute-start.6
  9.0 0.0 collective-permute-done.3.other_right_ref
  9.0 1.7 %shard_map.87 = (bf16[768,576]{1,0:T(8,128)(2,1)S(1)}, bf16[768,192]{1,0:T(8,128)(2,1)S(1)}, bf16[768,768]{1,0:T(8,128)(2,1)S(1)}) custom-call(bf16[384,768]{1,0:T(8,128)(2,1)S(1)} %bitcast.17, bf16[384,768]{1,0:T(8,128)(2,1)S(1)} %collective-permute-done.2.other_ref, bf16[768,384]{1,0:T(8,128)(2,1)S(1)} %bitcast.19, ...), custom_call_target="tpu_custom_call" | custom-call | tf_op jit(solution)/shard_map/pallas_call | solution.py:224
  10.8 0.0 collective-permute-done.1.refs_0_
  10.8 5.1 %collective-permute-start.7 = (bf16[96,768]{1,0:T(8,128)(2,1)S(1)}, bf16[96,768]{1,0:T(8,128)(2,1)S(1)}, u32[]{:S(2)}, u32[]{:S(2)}) collective-permute-start(bf16[96,768]{1,0:T(8,128)(2,1)S(1)} %collective-permute-done.1.refs_0_), channel_id=1, source_target_pairs={{0,1},{1,0},{2,3},{3,2},{4,5},{5,4},{6,7},{7,6},{8,9},{9,8},{10,11... | collective-permute-start | bytes 442376 | tf_op jit(solution)/shard_map/ppermute | solution.py:214
  15.9 0.0 collective-permute-done.4.refs_1_
  15.9 0.9 %collective-permute-start.8 = (bf16[96,768]{1,0:T(8,128)(2,1)S(1)}, bf16[96,768]{1,0:T(8,128)(2,1)S(1)}, u32[]{:S(2)}, u32[]{:S(2)}) collective-permute-start(bf16[96,768]{1,0:T(8,128)(2,1)S(1)} %collective-permute-done.4.refs_1_), channel_id=1, source_target_pairs={{0,1},{1,0},{2,3},{3,2},{4,5},{5,4},{6,7},{7,6},{8,9},{9,8},{10,11... | collective-permute-start | bytes 442376 | tf_op jit(solution)/shard_map/ppermute | solution.py:214
  16.8 0.0 collective-permute-done.5.refs_2_
  16.9 3.6 %collective-permute-start.10 = (bf16[96,768]{1,0:T(8,128)(2,1)S(1)}, bf16[96,768]{1,0:T(8,128)(2,1)S(1)}, u32[]{:S(2)}, u32[]{:S(2)}) collective-permute-start(bf16[96,768]{1,0:T(8,128)(2,1)S(1)} %collective-permute-done.5.refs_2_), channel_id=1, source_target_pairs={{0,1},{1,0},{2,3},{3,2},{4,5},{5,4},{6,7},{7,6},{8,9},{9,8},{10,11... | collective-permute-start | bytes 442376 | tf_op jit(solution)/shard_map/ppermute | solution.py:214
  20.4 0.0 collective-permute-done.6.refs_3_
  20.4 0.4 collective-permute-start.9
  20.8 0.0 collective-permute-done.7.refs_4_
  20.8 0.0 collective-permute-done.8.refs_5_
  20.8 1.1 %shard_map.88 = (f32[768,768]{1,0:T(8,128)S(1)}, f32[8,128]{1,0:T(8,128)S(1)}) custom-call(bf16[768,576]{1,0:T(8,128)(2,1)S(1)} %get-tuple-element.31.left_ref, bf16[96,768]{1,0:T(8,128)(2,1)S(1)} %collective-permute-done.1.refs_0_, bf16[96,768]{1,0:T(8,128)(2,1)S(1)} %collective-permute-done.4.refs_1_, bf16[96,768]{1,0:T(8,128)(2,1)S(1)} %collective-permute-done.5.refs_2_, ...), custom_call_target="tpu_custom_call" | custom-call | tf_op jit(solution)/shard_map/pallas_call | solution.py:224
  21.9 0.0 copy-start.4
  22.0 0.0 copy-start.5
  22.0 0.0 copy-start.6
  22.0 0.0 collective-permute-done.10.refs_1_.refs_6_
  22.0 0.0 collective-permute-done.9.refs_0_.refs_7_
  22.0 1.6 %shard_map.89 = (bf16[2,96,384]{2,1,0:T(8,128)(2,1)S(1)}, bf16[2,96,384]{2,1,0:T(8,128)(2,1)S(1)}, bf16[2,96,384]{2,1,0:T(8,128)(2,1)S(1)}, bf16[96,384]{1,0:T(8,128)(2,1)S(1)}, bf16[96,384]{1,0:T(8,128)(2,1)S(1)}) custom-call(bf16[768,192]{1,0:T(8,128)(2,1)S(1)} %get-tuple-element.30.left_ref, f32[768,768]{1,0:T(8,128)S(1)} %get-tuple-element.36.total_ref, ...), custom_call_target="tpu_custom_call" | custom-call | tf_op jit(solution)/shard_map/pallas_call | solution.py:224
  23.6 2.3 %collective-permute-start.11 = (bf16[2,96,384]{2,1,0:T(8,128)(2,1)S(1)}, bf16[2,96,384]{2,1,0:T(8,128)(2,1)S(1)}, u32[]{:S(2)}, u32[]{:S(2)}) collective-permute-start(bf16[2,96,384]{2,1,0:T(8,128)(2,1)S(1)} %get-tuple-element.39), channel_id=1, source_target_pairs={{0,4},{1,9},{2,6},{3,11},{4,0},{5,13},{6,2},{7,15},{8,12},{9,1},{1... | collective-permute-start | bytes 442376 | tf_op jit(solution)/shard_map/ppermute | solution.py:218
  25.9 0.5 %collective-permute-start.12 = (bf16[2,96,384]{2,1,0:T(8,128)(2,1)S(1)}, bf16[2,96,384]{2,1,0:T(8,128)(2,1)S(1)}, u32[]{:S(2)}, u32[]{:S(2)}) collective-permute-start(bf16[2,96,384]{2,1,0:T(8,128)(2,1)S(1)} %get-tuple-element.45), channel_id=1, source_target_pairs={{0,6},{1,11},{2,4},{3,9},{4,2},{5,15},{6,0},{7,13},{8,14},{9,3},{1... | collective-permute-start | bytes 442376 | tf_op jit(solution)/shard_map/ppermute | solution.py:218
  26.4 1.0 %collective-permute-start.13 = (bf16[2,96,384]{2,1,0:T(8,128)(2,1)S(1)}, bf16[2,96,384]{2,1,0:T(8,128)(2,1)S(1)}, u32[]{:S(2)}, u32[]{:S(2)}) collective-permute-start(bf16[2,96,384]{2,1,0:T(8,128)(2,1)S(1)} %get-tuple-element.46), channel_id=1, source_target_pairs={{0,2},{1,15},{2,0},{3,13},{4,6},{5,11},{6,4},{7,9},{8,10},{9,7},{1... | collective-permute-start | bytes 442376 | tf_op jit(solution)/shard_map/ppermute | solution.py:218
  27.4 2.5 %collective-permute-start.17 = (bf16[96,384]{1,0:T(8,128)(2,1)S(1)}, bf16[96,384]{1,0:T(8,128)(2,1)S(1)}, u32[]{:S(2)}, u32[]{:S(2)}) collective-permute-start(bf16[96,384]{1,0:T(8,128)(2,1)S(1)} %get-tuple-element.48), channel_id=1, source_target_pairs={{0,12},{1,13},{2,14},{3,15},{4,8},{5,9},{6,10},{7,11},{8,4},{9,5},... | collective-permute-start | bytes 221192 | tf_op jit(solution)/shard_map/ppermute | solution.py:218
  29.9 0.2 collective-permute-done.11.after_ref.refs_0_
  30.1 2.1 %shard_map.90 = (bf16[384,768]{1,0:T(8,128)(2,1)}, bf16[384,768]{1,0:T(8,128)(2,1)}) custom-call(s32[1,6]{1,0:T(1,128)S(1)} %bitcast.22, bf16[384,768]{1,0:T(8,128)(2,1)S(1)} %bitcast.24, bf16[384,768]{1,0:T(8,128)(2,1)S(1)} %bitcast.25, bf16[2,96,384]{2,1,0:T(8,128)(2,1)S(1)} %collective-permute-done.11.after_ref.refs_0_, ...), custom_call_target="tpu_custom_call" | custom-call | flops 905969664 | bytes 2359296 | tf_op jit(solution)/shard_map/pallas_call | solution.py:224
  32.2 1.2 %collective-permute-start.14 = (bf16[96,384]{1,0:T(8,128)(2,1)S(1)}, bf16[96,384]{1,0:T(8,128)(2,1)S(1)}, u32[]{:S(2)}, u32[]{:S(2)}) collective-permute-start(bf16[96,384]{1,0:T(8,128)(2,1)S(1)} %slice_bitcast_fusion.2), channel_id=1, source_target_pairs={{0,1},{1,0},{2,3},{3,2},{4,5},{5,4},{6,7},{7,6},{8,9},{9,8},{10,11... | collective-permute-start | bytes 221192 | tf_op jit(solution)/shard_map/ppermute | solution.py:214
  33.4 0.4 collective-permute-done.12.refs_1_
  33.7 2.1 %collective-permute-start.15 = (bf16[96,384]{1,0:T(8,128)(2,1)S(1)}, bf16[96,384]{1,0:T(8,128)(2,1)S(1)}, u32[]{:S(2)}, u32[]{:S(2)}) collective-permute-start(bf16[96,384]{1,0:T(8,128)(2,1)S(1)} %slice_bitcast_fusion.1), channel_id=1, source_target_pairs={{0,1},{1,0},{2,3},{3,2},{4,5},{5,4},{6,7},{7,6},{8,9},{9,8},{10,11... | collective-permute-start | bytes 221192 | tf_op jit(solution)/shard_map/ppermute | solution.py:214
  35.9 0.0 collective-permute-done.13.refs_2_
  35.9 2.2 %collective-permute-start.16 = (bf16[96,384]{1,0:T(8,128)(2,1)S(1)}, bf16[96,384]{1,0:T(8,128)(2,1)S(1)}, u32[]{:S(2)}, u32[]{:S(2)}) collective-permute-start(bf16[96,384]{1,0:T(8,128)(2,1)S(1)} %slice_bitcast_fusion), channel_id=1, source_target_pairs={{0,1},{1,0},{2,3},{3,2},{4,5},{5,4},{6,7},{7,6},{8,9},{9,8},{10,11... | collective-permute-start | bytes 221192 | tf_op jit(solution)/shard_map/ppermute | solution.py:214
  38.0 0.0 collective-permute-done.17.refs_7_
  38.0 0.0 collective-permute-done.14.refs_3_
  38.1 0.0 collective-permute-done.15.refs_4_
  38.1 0.9 %collective-permute-done.16.refs_5_ = bf16[96,384]{1,0:T(8,128)(2,1)S(1)} collective-permute-done((bf16[96,384]{1,0:T(8,128)(2,1)S(1)}, bf16[96,384]{1,0:T(8,128)(2,1)S(1)}, u32[]{:S(2)}, u32[]{:S(2)}) %collective-permute-start.16) | collective-permute-done | bytes 73760 | tf_op jit(solution)/shard_map/ppermute | solution.py:214
  39.0 0.9 %shard_map.91 = bf16[6,96,384]{2,1,0:T(8,128)(2,1)} custom-call(s32[1,6]{1,0:T(1,128)S(1)} %bitcast.23, bf16[2,96,384]{2,1,0:T(8,128)(2,1)S(1)} %collective-permute-done.11.after_ref.refs_0_, bf16[2,96,384]{2,1,0:T(8,128)(2,1)S(1)} %collective-permute-done.12.refs_1_, bf16[2,96,384]{2,1,0:T(8,128)(2,1)S(1)} %collective-permute-done.13.refs_2_, ...), custom_call_target="tpu_custom_call" | custom-call | tf_op jit(solution)/shard_map/pallas_call | solution.py:224
  (12 shorter events, 0.0 us)
Async XLA Ops:
  0.6 2.9 %collective-permute-start = (bf16[6,96,768]{2,1,0:T(8,128)(2,1)}, bf16[6,96,768]{2,1,0:T(8,128)(2,1)S(1)}, u32[]{:S(2)}, u32[]{:S(2)}) collective-permute-start(bf16[6,96,768]{2,1,0:T(8,128)(2,1)} %bitcast.14), channel_id=1, source_target_pairs={{0,1},{1,0},{2,3},{3,2},{4,5},{5,4},{6,7},{7,6},{8,9},{9,8},{10,11... | collective-permute-start | bytes 2654216 | tf_op jit(solution)/shard_map/ppermute | solution.py:214
  1.1 7.8 %collective-permute-start.2 = (bf16[384,768]{1,0:T(8,128)(2,1)}, bf16[384,768]{1,0:T(8,128)(2,1)S(1)}, u32[]{:S(2)}, u32[]{:S(2)}) collective-permute-start(bf16[384,768]{1,0:T(8,128)(2,1)} %bitcast.16), channel_id=1, source_target_pairs={{0,1},{1,0},{2,3},{3,2},{4,5},{5,4},{6,7},{7,6},{8,9},{9,8},{10,11... | collective-permute-start | bytes 1769480 | tf_op jit(solution)/shard_map/ppermute | solution.py:214
  1.2 7.8 %collective-permute-start.3 = (bf16[768,384]{1,0:T(8,128)(2,1)}, bf16[768,384]{1,0:T(8,128)(2,1)S(1)}, u32[]{:S(2)}, u32[]{:S(2)}) collective-permute-start(bf16[768,384]{1,0:T(8,128)(2,1)} %bitcast.18), channel_id=1, source_target_pairs={{0,1},{1,0},{2,3},{3,2},{4,5},{5,4},{6,7},{7,6},{8,9},{9,8},{10,11... | collective-permute-start | bytes 1769480 | tf_op jit(solution)/shard_map/ppermute | solution.py:214
  1.7 1.2 %copy-start = (bf16[1,6,96,768]{3,2,1,0:T(8,128)(2,1)S(1)}, bf16[1,6,96,768]{3,2,1,0:T(8,128)(2,1)}, u32[]{:S(2)}) copy-start(bf16[1,6,96,768]{3,2,1,0:T(8,128)(2,1)} %param.6) | copy-start | bytes 2654212
  2.8 0.7 %copy-start.3 = (s32[6]{0:T(128)S(1)}, s32[6]{0:T(128)}, u32[]{:S(2)}) copy-start(s32[6]{0:T(128)} %param.7) | copy-start | bytes 76
  3.5 5.5 %copy-start.1 = (bf16[1,384,768]{2,1,0:T(8,128)(2,1)S(1)}, bf16[1,384,768]{2,1,0:T(8,128)(2,1)}, u32[]{:S(2)}) copy-start(bf16[1,384,768]{2,1,0:T(8,128)(2,1)} %param.10) | copy-start | bytes 1769476
  3.5 5.5 %copy-start.2 = (bf16[1,768,384]{2,1,0:T(8,128)(2,1)S(1)}, bf16[1,768,384]{2,1,0:T(8,128)(2,1)}, u32[]{:S(2)}) copy-start(bf16[1,768,384]{2,1,0:T(8,128)(2,1)} %param.11) | copy-start | bytes 1769476
  3.9 6.9 %collective-permute-start.1 = (bf16[96,768]{1,0:T(8,128)(2,1)S(1)}, bf16[96,768]{1,0:T(8,128)(2,1)S(1)}, u32[]{:S(2)}, u32[]{:S(2)}) collective-permute-start(bf16[96,768]{1,0:T(8,128)(2,1)S(1)} %get-tuple-element.26), channel_id=1, source_target_pairs={{0,4},{1,13},{2,6},{3,15},{4,0},{5,9},{6,2},{7,11},{8,12},{9,5},{1... | collective-permute-start | bytes 442376 | tf_op jit(solution)/shard_map/ppermute | solution.py:218
  6.7 9.2 %collective-permute-start.4 = (bf16[96,768]{1,0:T(8,128)(2,1)S(1)}, bf16[96,768]{1,0:T(8,128)(2,1)S(1)}, u32[]{:S(2)}, u32[]{:S(2)}) collective-permute-start(bf16[96,768]{1,0:T(8,128)(2,1)S(1)} %get-tuple-element.33), channel_id=1, source_target_pairs={{0,2},{1,11},{2,0},{3,9},{4,6},{5,15},{6,4},{7,13},{8,10},{9,3},{1... | collective-permute-start | bytes 442376 | tf_op jit(solution)/shard_map/ppermute | solution.py:218
  8.2 8.6 %collective-permute-start.5 = (bf16[96,768]{1,0:T(8,128)(2,1)S(1)}, bf16[96,768]{1,0:T(8,128)(2,1)S(1)}, u32[]{:S(2)}, u32[]{:S(2)}) collective-permute-start(bf16[96,768]{1,0:T(8,128)(2,1)S(1)} %get-tuple-element.34), channel_id=1, source_target_pairs={{0,0},{1,9},{2,2},{3,11},{4,4},{5,13},{6,6},{7,15},{8,8},{9,1},{10... | collective-permute-start | bytes 442376 | tf_op jit(solution)/shard_map/ppermute | solution.py:218
  8.9 11.5 %collective-permute-start.6 = (bf16[96,768]{1,0:T(8,128)(2,1)S(1)}, bf16[96,768]{1,0:T(8,128)(2,1)S(1)}, u32[]{:S(2)}, u32[]{:S(2)}) collective-permute-start(bf16[96,768]{1,0:T(8,128)(2,1)S(1)} %get-tuple-element.35), channel_id=1, source_target_pairs={{0,6},{1,15},{2,4},{3,13},{4,2},{5,11},{6,0},{7,9},{8,14},{9,7},{1... | collective-permute-start | bytes 442376 | tf_op jit(solution)/shard_map/ppermute | solution.py:218
  10.8 10.1 %collective-permute-start.7 = (bf16[96,768]{1,0:T(8,128)(2,1)S(1)}, bf16[96,768]{1,0:T(8,128)(2,1)S(1)}, u32[]{:S(2)}, u32[]{:S(2)}) collective-permute-start(bf16[96,768]{1,0:T(8,128)(2,1)S(1)} %collective-permute-done.1.refs_0_), channel_id=1, source_target_pairs={{0,1},{1,0},{2,3},{3,2},{4,5},{5,4},{6,7},{7,6},{8,9},{9,8},{10,11... | collective-permute-start | bytes 442376 | tf_op jit(solution)/shard_map/ppermute | solution.py:214
  15.9 4.9 %collective-permute-start.8 = (bf16[96,768]{1,0:T(8,128)(2,1)S(1)}, bf16[96,768]{1,0:T(8,128)(2,1)S(1)}, u32[]{:S(2)}, u32[]{:S(2)}) collective-permute-start(bf16[96,768]{1,0:T(8,128)(2,1)S(1)} %collective-permute-done.4.refs_1_), channel_id=1, source_target_pairs={{0,1},{1,0},{2,3},{3,2},{4,5},{5,4},{6,7},{7,6},{8,9},{9,8},{10,11... | collective-permute-start | bytes 442376 | tf_op jit(solution)/shard_map/ppermute | solution.py:214
  16.9 5.1 %collective-permute-start.10 = (bf16[96,768]{1,0:T(8,128)(2,1)S(1)}, bf16[96,768]{1,0:T(8,128)(2,1)S(1)}, u32[]{:S(2)}, u32[]{:S(2)}) collective-permute-start(bf16[96,768]{1,0:T(8,128)(2,1)S(1)} %collective-permute-done.5.refs_2_), channel_id=1, source_target_pairs={{0,1},{1,0},{2,3},{3,2},{4,5},{5,4},{6,7},{7,6},{8,9},{9,8},{10,11... | collective-permute-start | bytes 442376 | tf_op jit(solution)/shard_map/ppermute | solution.py:214
  20.4 1.5 %collective-permute-start.9 = (bf16[96,768]{1,0:T(8,128)(2,1)S(1)}, bf16[96,768]{1,0:T(8,128)(2,1)S(1)}, u32[]{:S(2)}, u32[]{:S(2)}) collective-permute-start(bf16[96,768]{1,0:T(8,128)(2,1)S(1)} %collective-permute-done.6.refs_3_), channel_id=1, source_target_pairs={{0,1},{1,0},{2,3},{3,2},{4,5},{5,4},{6,7},{7,6},{8,9},{9,8},{10,11... | collective-permute-start | bytes 442376 | tf_op jit(solution)/shard_map/ppermute | solution.py:214
  21.9 8.2 %copy-start.4 = (s32[6]{0:T(128)S(1)}, s32[6]{0:T(128)}, u32[]{:S(2)}) copy-start(s32[6]{0:T(128)} %param.7) | copy-start | bytes 76
  22.0 8.2 %copy-start.5 = (bf16[1,384,768]{2,1,0:T(8,128)(2,1)S(1)}, bf16[1,384,768]{2,1,0:T(8,128)(2,1)}, u32[]{:S(2)}) copy-start(bf16[1,384,768]{2,1,0:T(8,128)(2,1)} %param.8) | copy-start | bytes 1769476
  22.0 8.1 %copy-start.6 = (bf16[1,384,768]{2,1,0:T(8,128)(2,1)S(1)}, bf16[1,384,768]{2,1,0:T(8,128)(2,1)}, u32[]{:S(2)}) copy-start(bf16[1,384,768]{2,1,0:T(8,128)(2,1)} %param.9) | copy-start | bytes 1769476
  23.6 6.5 %collective-permute-start.11 = (bf16[2,96,384]{2,1,0:T(8,128)(2,1)S(1)}, bf16[2,96,384]{2,1,0:T(8,128)(2,1)S(1)}, u32[]{:S(2)}, u32[]{:S(2)}) collective-permute-start(bf16[2,96,384]{2,1,0:T(8,128)(2,1)S(1)} %get-tuple-element.39), channel_id=1, source_target_pairs={{0,4},{1,9},{2,6},{3,11},{4,0},{5,13},{6,2},{7,15},{8,12},{9,1},{1... | collective-permute-start | bytes 442376 | tf_op jit(solution)/shard_map/ppermute | solution.py:218
  25.9 7.8 %collective-permute-start.12 = (bf16[2,96,384]{2,1,0:T(8,128)(2,1)S(1)}, bf16[2,96,384]{2,1,0:T(8,128)(2,1)S(1)}, u32[]{:S(2)}, u32[]{:S(2)}) collective-permute-start(bf16[2,96,384]{2,1,0:T(8,128)(2,1)S(1)} %get-tuple-element.45), channel_id=1, source_target_pairs={{0,6},{1,11},{2,4},{3,9},{4,2},{5,15},{6,0},{7,13},{8,14},{9,3},{1... | collective-permute-start | bytes 442376 | tf_op jit(solution)/shard_map/ppermute | solution.py:218
  26.4 9.5 %collective-permute-start.13 = (bf16[2,96,384]{2,1,0:T(8,128)(2,1)S(1)}, bf16[2,96,384]{2,1,0:T(8,128)(2,1)S(1)}, u32[]{:S(2)}, u32[]{:S(2)}) collective-permute-start(bf16[2,96,384]{2,1,0:T(8,128)(2,1)S(1)} %get-tuple-element.46), channel_id=1, source_target_pairs={{0,2},{1,15},{2,0},{3,13},{4,6},{5,11},{6,4},{7,9},{8,10},{9,7},{1... | collective-permute-start | bytes 442376 | tf_op jit(solution)/shard_map/ppermute | solution.py:218
  27.4 10.6 %collective-permute-start.17 = (bf16[96,384]{1,0:T(8,128)(2,1)S(1)}, bf16[96,384]{1,0:T(8,128)(2,1)S(1)}, u32[]{:S(2)}, u32[]{:S(2)}) collective-permute-start(bf16[96,384]{1,0:T(8,128)(2,1)S(1)} %get-tuple-element.48), channel_id=1, source_target_pairs={{0,12},{1,13},{2,14},{3,15},{4,8},{5,9},{6,10},{7,11},{8,4},{9,5},... | collective-permute-start | bytes 221192 | tf_op jit(solution)/shard_map/ppermute | solution.py:218
  32.2 5.9 %collective-permute-start.14 = (bf16[96,384]{1,0:T(8,128)(2,1)S(1)}, bf16[96,384]{1,0:T(8,128)(2,1)S(1)}, u32[]{:S(2)}, u32[]{:S(2)}) collective-permute-start(bf16[96,384]{1,0:T(8,128)(2,1)S(1)} %slice_bitcast_fusion.2), channel_id=1, source_target_pairs={{0,1},{1,0},{2,3},{3,2},{4,5},{5,4},{6,7},{7,6},{8,9},{9,8},{10,11... | collective-permute-start | bytes 221192 | tf_op jit(solution)/shard_map/ppermute | solution.py:214
  33.7 4.3 %collective-permute-start.15 = (bf16[96,384]{1,0:T(8,128)(2,1)S(1)}, bf16[96,384]{1,0:T(8,128)(2,1)S(1)}, u32[]{:S(2)}, u32[]{:S(2)}) collective-permute-start(bf16[96,384]{1,0:T(8,128)(2,1)S(1)} %slice_bitcast_fusion.1), channel_id=1, source_target_pairs={{0,1},{1,0},{2,3},{3,2},{4,5},{5,4},{6,7},{7,6},{8,9},{9,8},{10,11... | collective-permute-start | bytes 221192 | tf_op jit(solution)/shard_map/ppermute | solution.py:214
  35.9 3.1 %collective-permute-start.16 = (bf16[96,384]{1,0:T(8,128)(2,1)S(1)}, bf16[96,384]{1,0:T(8,128)(2,1)S(1)}, u32[]{:S(2)}, u32[]{:S(2)}) collective-permute-start(bf16[96,384]{1,0:T(8,128)(2,1)S(1)} %slice_bitcast_fusion), channel_id=1, source_target_pairs={{0,1},{1,0},{2,3},{3,2},{4,5},{5,4},{6,7},{7,6},{8,9},{9,8},{10,11... | collective-permute-start | bytes 221192 | tf_op jit(solution)/shard_map/ppermute | solution.py:214

commit v12 on v11

--- a/solution.py
+++ b/solution.py
@@ -269,11 +269,10 @@
         ],
     )
     returned = [trade(x, codes) for x, codes in zip(whole, BACK)]
-    shared = trade(shared, SHARED)
     left_new, right_new = call(
         gram_kernel, [shape(left_gram.shape[1:]), shape(right_gram.shape[1:])],
         [VMEM, VMEM, VMEM, ANY] + [VMEM] * (2 * rounds),
-        block_owner, left_gram[0], right_gram[0], returned[0], *mine, *theirs,
+        block_owner, left_gram[0], right_gram[0], own, *mine, *theirs,
         out_specs=[VMEM, VMEM],
         scratch_shapes=[pltpu.VMEM((width, width), jnp.bfloat16)],
         cost_estimate=pl.CostEstimate(
@@ -281,9 +280,10 @@
             transcendentals=0,
         ),
     )
-    left_new, right_new, returned[0] = lax.optimization_barrier(
-        (left_new, right_new, returned[0])
-    )
+    left_new, right_new, shared, returned[0] = lax.optimization_barrier(
+        (left_new, right_new, shared, returned[0])
+    )
+    shared = trade(shared, SHARED)
     passed = [other_core(x[1]) for x in returned]
     update = call(
         place_kernel, shape((blocks, slab, width // 2)), [VMEM] + [ANY] * owners,

time: 40.2 us -> 40.5 us (level)
  the two profiles are of different devices: /device:TPU:0 before, /device:TPU:21 now
where the time goes in v12:
time: 40.5 us; the launch traced here: 40.4 us
  waiting for transfers between devices  16.9 us (42%)
  starting transfers between devices  13 us (32%)
  Pallas kernels  7.81 us (19%)
  local copies, waits for them, and re-layouts  1.87 us (5%)
  between operations  0.79 us (2%)
    ppermute x8, waiting for transfers between devices, trade(): return lax.ppermute(x, ('shard', 'replica'), pairs)  15.8 us
    ppermute x8, starting transfers between devices, trade(): return lax.ppermute(x, ('shard', 'replica'), pairs)  10.2 us
    pallas_call x7, Pallas kernels, call(): pl.pallas_call(kernel, out_shape=out_shape, in_specs=in_specs, compiler_p...  7.81 us
    ppermute x10, starting transfers between devices, other_core(): return lax.ppermute(x, 'replica', [(0, 1), (1, 0)])  2.73 us
    unnamed x14, local copies, waits for them, and re-layouts  1.85 us
    ppermute x10, waiting for transfers between devices, other_core(): return lax.ppermute(x, 'replica', [(0, 1), (1, 0)])  1.17 us
  transfers between devices with their start and end apart: 18, of which 9 were waited for; matrix products, arithmetic and copies ran while one was open for 0% of the time, Pallas kernels for 13%

profile of v12, /device:TPU:21, one launch (start us, length us, event | category | flops | bytes accessed | tf_op | source)
XLA Modules:
  0.0 40.4 jit_solution(15117921719316404145)
XLA Ops:
  0.6 0.7 %collective-permute-start = (bf16[6,96,768]{2,1,0:T(8,128)(2,1)}, bf16[6,96,768]{2,1,0:T(8,128)(2,1)S(1)}, u32[]{:S(2)}, u32[]{:S(2)}) collective-permute-start(bf16[6,96,768]{2,1,0:T(8,128)(2,1)} %bitcast.14), channel_id=1, source_target_pairs={{0,1},{1,0},{2,3},{3,2},{4,5},{5,4},{6,7},{7,6},{8,9},{9,8},{10,11... | collective-permute-start | bytes 2654216 | tf_op jit(solution)/shard_map/ppermute | solution.py:214
  1.4 0.1 collective-permute-start.2
  1.4 0.4 %collective-permute-start.3 = (bf16[768,384]{1,0:T(8,128)(2,1)}, bf16[768,384]{1,0:T(8,128)(2,1)S(1)}, u32[]{:S(2)}, u32[]{:S(2)}) collective-permute-start(bf16[768,384]{1,0:T(8,128)(2,1)} %bitcast.18), channel_id=1, source_target_pairs={{0,1},{1,0},{2,3},{3,2},{4,5},{5,4},{6,7},{7,6},{8,9},{9,8},{10,11... | collective-permute-start | bytes 1769480 | tf_op jit(solution)/shard_map/ppermute | solution.py:214
  1.9 1.2 %copy-done = bf16[1,6,96,768]{3,2,1,0:T(8,128)(2,1)S(1)} copy-done((bf16[1,6,96,768]{3,2,1,0:T(8,128)(2,1)S(1)}, bf16[1,6,96,768]{3,2,1,0:T(8,128)(2,1)}, u32[]{:S(2)}) %copy-start) | copy-done | bytes 884760
  3.1 0.7 %copy-done.3 = s32[6]{0:T(128)S(1)} copy-done((s32[6]{0:T(128)S(1)}, s32[6]{0:T(128)}, u32[]{:S(2)}) %copy-start.3) | copy-done | bytes 48
  3.7 0.1 shard_map.85.mine_ref
  3.8 0.0 collective-permute-done.theirs_ref
  3.8 0.3 shard_map.86
  4.1 0.2 collective-permute-start.1
  4.3 4.1 %collective-permute-start.4 = (bf16[96,768]{1,0:T(8,128)(2,1)S(1)}, bf16[96,768]{1,0:T(8,128)(2,1)S(1)}, u32[]{:S(2)}, u32[]{:S(2)}) collective-permute-start(bf16[96,768]{1,0:T(8,128)(2,1)S(1)} %get-tuple-element.34), channel_id=1, source_target_pairs={{0,2},{1,11},{2,0},{3,9},{4,6},{5,15},{6,4},{7,13},{8,10},{9,3},{1... | collective-permute-start | bytes 442376 | tf_op jit(solution)/shard_map/ppermute | solution.py:218
  8.5 1.9 %collective-permute-start.5 = (bf16[96,768]{1,0:T(8,128)(2,1)S(1)}, bf16[96,768]{1,0:T(8,128)(2,1)S(1)}, u32[]{:S(2)}, u32[]{:S(2)}) collective-permute-start(bf16[96,768]{1,0:T(8,128)(2,1)S(1)} %get-tuple-element.35), channel_id=1, source_target_pairs={{0,0},{1,9},{2,2},{3,11},{4,4},{5,13},{6,6},{7,15},{8,8},{9,1},{10... | collective-permute-start | bytes 442376 | tf_op jit(solution)/shard_map/ppermute | solution.py:218
  10.4 0.0 collective-permute-done.2.other_ref
  10.4 0.5 %collective-permute-start.6 = (bf16[96,768]{1,0:T(8,128)(2,1)S(1)}, bf16[96,768]{1,0:T(8,128)(2,1)S(1)}, u32[]{:S(2)}, u32[]{:S(2)}) collective-permute-start(bf16[96,768]{1,0:T(8,128)(2,1)S(1)} %get-tuple-element.36), channel_id=1, source_target_pairs={{0,6},{1,15},{2,4},{3,13},{4,2},{5,11},{6,0},{7,9},{8,14},{9,7},{1... | collective-permute-start | bytes 442376 | tf_op jit(solution)/shard_map/ppermute | solution.py:218
  10.9 0.0 collective-permute-done.3.other_right_ref
  10.9 1.7 %shard_map.87 = (bf16[768,576]{1,0:T(8,128)(2,1)S(1)}, bf16[768,192]{1,0:T(8,128)(2,1)S(1)}, bf16[768,768]{1,0:T(8,128)(2,1)S(1)}) custom-call(bf16[384,768]{1,0:T(8,128)(2,1)S(1)} %bitcast.17, bf16[384,768]{1,0:T(8,128)(2,1)S(1)} %collective-permute-done.2.other_ref, bf16[768,384]{1,0:T(8,128)(2,1)S(1)} %bitcast.19, ...), custom_call_target="tpu_custom_call" | custom-call | tf_op jit(solution)/shard_map/pallas_call | solution.py:224
  12.6 0.0 collective-permute-done.1.refs_0_
  12.6 0.1 collective-permute-start.7
  12.7 1.9 %collective-permute-done.4.refs_1_ = bf16[96,768]{1,0:T(8,128)(2,1)S(1)} collective-permute-done((bf16[96,768]{1,0:T(8,128)(2,1)S(1)}, bf16[96,768]{1,0:T(8,128)(2,1)S(1)}, u32[]{:S(2)}, u32[]{:S(2)}) %collective-permute-start.4) | collective-permute-done | bytes 147488 | tf_op jit(solution)/shard_map/ppermute | solution.py:218
  14.6 0.0 collective-permute-start.8
  14.6 1.8 %collective-permute-done.5.refs_2_ = bf16[96,768]{1,0:T(8,128)(2,1)S(1)} collective-permute-done((bf16[96,768]{1,0:T(8,128)(2,1)S(1)}, bf16[96,768]{1,0:T(8,128)(2,1)S(1)}, u32[]{:S(2)}, u32[]{:S(2)}) %collective-permute-start.5) | collective-permute-done | bytes 147488 | tf_op jit(solution)/shard_map/ppermute | solution.py:218
  16.4 0.0 collective-permute-start.10
  16.4 3.8 %collective-permute-done.6.refs_3_ = bf16[96,768]{1,0:T(8,128)(2,1)S(1)} collective-permute-done((bf16[96,768]{1,0:T(8,128)(2,1)S(1)}, bf16[96,768]{1,0:T(8,128)(2,1)S(1)}, u32[]{:S(2)}, u32[]{:S(2)}) %collective-permute-start.6) | collective-permute-done | bytes 147488 | tf_op jit(solution)/shard_map/ppermute | solution.py:218
  20.2 0.0 collective-permute-start.9
  20.2 0.0 collective-permute-done.7.refs_4_
  20.2 0.0 collective-permute-done.8.refs_5_
  20.2 1.1 %shard_map.88 = (f32[768,768]{1,0:T(8,128)S(1)}, f32[8,128]{1,0:T(8,128)S(1)}) custom-call(bf16[768,576]{1,0:T(8,128)(2,1)S(1)} %get-tuple-element.32.left_ref, bf16[96,768]{1,0:T(8,128)(2,1)S(1)} %collective-permute-done.1.refs_0_, bf16[96,768]{1,0:T(8,128)(2,1)S(1)} %collective-permute-done.4.refs_1_, bf16[96,768]{1,0:T(8,128)(2,1)S(1)} %collective-permute-done.5.refs_2_, ...), custom_call_target="tpu_custom_call" | custom-call | tf_op jit(solution)/shard_map/pallas_call | solution.py:224
  21.3 0.0 copy-start.4
  21.3 0.0 copy-start.5
  21.3 0.0 copy-start.6
  21.3 0.0 collective-permute-done.10.refs_1_.refs_6_
  21.4 0.2 collective-permute-done.9.refs_0_.refs_7_
  21.6 1.6 %shard_map.89 = (bf16[2,96,384]{2,1,0:T(8,128)(2,1)S(1)}, bf16[2,96,384]{2,1,0:T(8,128)(2,1)S(1)}, bf16[2,96,384]{2,1,0:T(8,128)(2,1)S(1)}, bf16[96,384]{1,0:T(8,128)(2,1)S(1)}, bf16[96,384]{1,0:T(8,128)(2,1)S(1)}) custom-call(bf16[768,192]{1,0:T(8,128)(2,1)S(1)} %get-tuple-element.31.left_ref, f32[768,768]{1,0:T(8,128)S(1)} %get-tuple-element.37.total_ref, ...), custom_call_target="tpu_custom_call" | custom-call | tf_op jit(solution)/shard_map/pallas_call | solution.py:224
  23.2 0.1 collective-permute-start.11
  23.3 2.7 %collective-permute-start.12 = (bf16[2,96,384]{2,1,0:T(8,128)(2,1)S(1)}, bf16[2,96,384]{2,1,0:T(8,128)(2,1)S(1)}, u32[]{:S(2)}, u32[]{:S(2)}) collective-permute-start(bf16[2,96,384]{2,1,0:T(8,128)(2,1)S(1)} %get-tuple-element.48), channel_id=1, source_target_pairs={{0,6},{1,11},{2,4},{3,9},{4,2},{5,15},{6,0},{7,13},{8,14},{9,3},{1... | collective-permute-start | bytes 442376 | tf_op jit(solution)/shard_map/ppermute | solution.py:218
  26.0 0.7 %collective-permute-start.13 = (bf16[2,96,384]{2,1,0:T(8,128)(2,1)S(1)}, bf16[2,96,384]{2,1,0:T(8,128)(2,1)S(1)}, u32[]{:S(2)}, u32[]{:S(2)}) collective-permute-start(bf16[2,96,384]{2,1,0:T(8,128)(2,1)S(1)} %get-tuple-element.49), channel_id=1, source_target_pairs={{0,2},{1,15},{2,0},{3,13},{4,6},{5,11},{6,4},{7,9},{8,10},{9,7},{1... | collective-permute-start | bytes 442376 | tf_op jit(solution)/shard_map/ppermute | solution.py:218
  26.7 2.1 %shard_map.90 = (bf16[384,768]{1,0:T(8,128)(2,1)}, bf16[384,768]{1,0:T(8,128)(2,1)}) custom-call(s32[1,6]{1,0:T(1,128)S(1)} %bitcast.22, bf16[384,768]{1,0:T(8,128)(2,1)S(1)} %bitcast.24, bf16[384,768]{1,0:T(8,128)(2,1)S(1)} %bitcast.25, bf16[96,384]{1,0:T(8,128)(2,1)S(1)} %get-tuple-element.40.after_ref.refs_6_, ...), custom_call_target="tpu_custom_call" | custom-call | flops 905969664 | bytes 2359296 | tf_op jit(solution)/shard_map/pallas_call | solution.py:224
  28.7 1.0 %collective-permute-done.11.refs_0_ = bf16[2,96,384]{2,1,0:T(8,128)(2,1)S(1)} collective-permute-done((bf16[2,96,384]{2,1,0:T(8,128)(2,1)S(1)}, bf16[2,96,384]{2,1,0:T(8,128)(2,1)S(1)}, u32[]{:S(2)}, u32[]{:S(2)}) %collective-permute-start.11) | collective-permute-done | bytes 147488 | tf_op jit(solution)/shard_map/ppermute | solution.py:218
  29.7 0.6 %collective-permute-start.14 = (bf16[96,384]{1,0:T(8,128)(2,1)S(1)}, bf16[96,384]{1,0:T(8,128)(2,1)S(1)}, u32[]{:S(2)}, u32[]{:S(2)}) collective-permute-start(bf16[96,384]{1,0:T(8,128)(2,1)S(1)} %slice_bitcast_fusion.2), channel_id=1, source_target_pairs={{0,1},{1,0},{2,3},{3,2},{4,5},{5,4},{6,7},{7,6},{8,9},{9,8},{10,11... | collective-permute-start | bytes 221192 | tf_op jit(solution)/shard_map/ppermute | solution.py:214
  30.3 0.0 collective-permute-start.17
  30.3 3.6 %collective-permute-done.12.refs_1_ = bf16[2,96,384]{2,1,0:T(8,128)(2,1)S(1)} collective-permute-done((bf16[2,96,384]{2,1,0:T(8,128)(2,1)S(1)}, bf16[2,96,384]{2,1,0:T(8,128)(2,1)S(1)}, u32[]{:S(2)}, u32[]{:S(2)}) %collective-permute-start.12) | collective-permute-done | bytes 147488 | tf_op jit(solution)/shard_map/ppermute | solution.py:218
  33.9 0.7 %collective-permute-start.15 = (bf16[96,384]{1,0:T(8,128)(2,1)S(1)}, bf16[96,384]{1,0:T(8,128)(2,1)S(1)}, u32[]{:S(2)}, u32[]{:S(2)}) collective-permute-start(bf16[96,384]{1,0:T(8,128)(2,1)S(1)} %slice_bitcast_fusion.1), channel_id=1, source_target_pairs={{0,1},{1,0},{2,3},{3,2},{4,5},{5,4},{6,7},{7,6},{8,9},{9,8},{10,11... | collective-permute-start | bytes 221192 | tf_op jit(solution)/shard_map/ppermute | solution.py:214
  34.7 3.4 %collective-permute-done.13.refs_2_ = bf16[2,96,384]{2,1,0:T(8,128)(2,1)S(1)} collective-permute-done((bf16[2,96,384]{2,1,0:T(8,128)(2,1)S(1)}, bf16[2,96,384]{2,1,0:T(8,128)(2,1)S(1)}, u32[]{:S(2)}, u32[]{:S(2)}) %collective-permute-start.13) | collective-permute-done | bytes 147488 | tf_op jit(solution)/shard_map/ppermute | solution.py:218
  38.1 0.1 collective-permute-start.16
  38.2 0.0 collective-permute-done.14.refs_3_
  38.2 0.3 collective-permute-done.17.refs_7_
  38.5 0.0 collective-permute-done.15.refs_4_
  38.5 0.9 %collective-permute-done.16.refs_5_ = bf16[96,384]{1,0:T(8,128)(2,1)S(1)} collective-permute-done((bf16[96,384]{1,0:T(8,128)(2,1)S(1)}, bf16[96,384]{1,0:T(8,128)(2,1)S(1)}, u32[]{:S(2)}, u32[]{:S(2)}) %collective-permute-start.16) | collective-permute-done | bytes 73760 | tf_op jit(solution)/shard_map/ppermute | solution.py:214
  39.4 0.9 %shard_map.91 = bf16[6,96,384]{2,1,0:T(8,128)(2,1)} custom-call(s32[1,6]{1,0:T(1,128)S(1)} %bitcast.23, bf16[2,96,384]{2,1,0:T(8,128)(2,1)S(1)} %collective-permute-done.11.refs_0_, bf16[2,96,384]{2,1,0:T(8,128)(2,1)S(1)} %collective-permute-done.12.refs_1_, bf16[2,96,384]{2,1,0:T(8,128)(2,1)S(1)} %collective-permute-done.13.refs_2_, ...), custom_call_target="tpu_custom_call" | custom-call | tf_op jit(solution)/shard_map/pallas_call | solution.py:224
  (12 shorter events, 0.0 us)
Async XLA Ops:
  0.6 3.1 %collective-permute-start = (bf16[6,96,768]{2,1,0:T(8,128)(2,1)}, bf16[6,96,768]{2,1,0:T(8,128)(2,1)S(1)}, u32[]{:S(2)}, u32[]{:S(2)}) collective-permute-start(bf16[6,96,768]{2,1,0:T(8,128)(2,1)} %bitcast.14), channel_id=1, source_target_pairs={{0,1},{1,0},{2,3},{3,2},{4,5},{5,4},{6,7},{7,6},{8,9},{9,8},{10,11... | collective-permute-start | bytes 2654216 | tf_op jit(solution)/shard_map/ppermute | solution.py:214
  1.4 9.0 %collective-permute-start.2 = (bf16[384,768]{1,0:T(8,128)(2,1)}, bf16[384,768]{1,0:T(8,128)(2,1)S(1)}, u32[]{:S(2)}, u32[]{:S(2)}) collective-permute-start(bf16[384,768]{1,0:T(8,128)(2,1)} %bitcast.16), channel_id=1, source_target_pairs={{0,1},{1,0},{2,3},{3,2},{4,5},{5,4},{6,7},{7,6},{8,9},{9,8},{10,11... | collective-permute-start | bytes 1769480 | tf_op jit(solution)/shard_map/ppermute | solution.py:214
  1.4 9.4 %collective-permute-start.3 = (bf16[768,384]{1,0:T(8,128)(2,1)}, bf16[768,384]{1,0:T(8,128)(2,1)S(1)}, u32[]{:S(2)}, u32[]{:S(2)}) collective-permute-start(bf16[768,384]{1,0:T(8,128)(2,1)} %bitcast.18), channel_id=1, source_target_pairs={{0,1},{1,0},{2,3},{3,2},{4,5},{5,4},{6,7},{7,6},{8,9},{9,8},{10,11... | collective-permute-start | bytes 1769480 | tf_op jit(solution)/shard_map/ppermute | solution.py:214
  1.9 1.2 %copy-start = (bf16[1,6,96,768]{3,2,1,0:T(8,128)(2,1)S(1)}, bf16[1,6,96,768]{3,2,1,0:T(8,128)(2,1)}, u32[]{:S(2)}) copy-start(bf16[1,6,96,768]{3,2,1,0:T(8,128)(2,1)} %param.6) | copy-start | bytes 2654212
  3.0 0.7 %copy-start.3 = (s32[6]{0:T(128)S(1)}, s32[6]{0:T(128)}, u32[]{:S(2)}) copy-start(s32[6]{0:T(128)} %param.7) | copy-start | bytes 76
  3.7 7.2 %copy-start.1 = (bf16[1,384,768]{2,1,0:T(8,128)(2,1)S(1)}, bf16[1,384,768]{2,1,0:T(8,128)(2,1)}, u32[]{:S(2)}) copy-start(bf16[1,384,768]{2,1,0:T(8,128)(2,1)} %param.10) | copy-start | bytes 1769476
  3.7 7.2 %copy-start.2 = (bf16[1,768,384]{2,1,0:T(8,128)(2,1)S(1)}, bf16[1,768,384]{2,1,0:T(8,128)(2,1)}, u32[]{:S(2)}) copy-start(bf16[1,768,384]{2,1,0:T(8,128)(2,1)} %param.11) | copy-start | bytes 1769476
  4.1 8.5 %collective-permute-start.1 = (bf16[96,768]{1,0:T(8,128)(2,1)S(1)}, bf16[96,768]{1,0:T(8,128)(2,1)S(1)}, u32[]{:S(2)}, u32[]{:S(2)}) collective-permute-start(bf16[96,768]{1,0:T(8,128)(2,1)S(1)} %get-tuple-element.27), channel_id=1, source_target_pairs={{0,4},{1,13},{2,6},{3,15},{4,0},{5,9},{6,2},{7,11},{8,12},{9,5},{1... | collective-permute-start | bytes 442376 | tf_op jit(solution)/shard_map/ppermute | solution.py:218
  4.3 10.3 %collective-permute-start.4 = (bf16[96,768]{1,0:T(8,128)(2,1)S(1)}, bf16[96,768]{1,0:T(8,128)(2,1)S(1)}, u32[]{:S(2)}, u32[]{:S(2)}) collective-permute-start(bf16[96,768]{1,0:T(8,128)(2,1)S(1)} %get-tuple-element.34), channel_id=1, source_target_pairs={{0,2},{1,11},{2,0},{3,9},{4,6},{5,15},{6,4},{7,13},{8,10},{9,3},{1... | collective-permute-start | bytes 442376 | tf_op jit(solution)/shard_map/ppermute | solution.py:218
  8.5 7.9 %collective-permute-start.5 = (bf16[96,768]{1,0:T(8,128)(2,1)S(1)}, bf16[96,768]{1,0:T(8,128)(2,1)S(1)}, u32[]{:S(2)}, u32[]{:S(2)}) collective-permute-start(bf16[96,768]{1,0:T(8,128)(2,1)S(1)} %get-tuple-element.35), channel_id=1, source_target_pairs={{0,0},{1,9},{2,2},{3,11},{4,4},{5,13},{6,6},{7,15},{8,8},{9,1},{10... | collective-permute-start | bytes 442376 | tf_op jit(solution)/shard_map/ppermute | solution.py:218
  10.4 9.8 %collective-permute-start.6 = (bf16[96,768]{1,0:T(8,128)(2,1)S(1)}, bf16[96,768]{1,0:T(8,128)(2,1)S(1)}, u32[]{:S(2)}, u32[]{:S(2)}) collective-permute-start(bf16[96,768]{1,0:T(8,128)(2,1)S(1)} %get-tuple-element.36), channel_id=1, source_target_pairs={{0,6},{1,15},{2,4},{3,13},{4,2},{5,11},{6,0},{7,9},{8,14},{9,7},{1... | collective-permute-start | bytes 442376 | tf_op jit(solution)/shard_map/ppermute | solution.py:218
  12.6 7.6 %collective-permute-start.7 = (bf16[96,768]{1,0:T(8,128)(2,1)S(1)}, bf16[96,768]{1,0:T(8,128)(2,1)S(1)}, u32[]{:S(2)}, u32[]{:S(2)}) collective-permute-start(bf16[96,768]{1,0:T(8,128)(2,1)S(1)} %collective-permute-done.1.refs_0_), channel_id=1, source_target_pairs={{0,1},{1,0},{2,3},{3,2},{4,5},{5,4},{6,7},{7,6},{8,9},{9,8},{10,11... | collective-permute-start | bytes 442376 | tf_op jit(solution)/shard_map/ppermute | solution.py:214
  14.6 5.6 %collective-permute-start.8 = (bf16[96,768]{1,0:T(8,128)(2,1)S(1)}, bf16[96,768]{1,0:T(8,128)(2,1)S(1)}, u32[]{:S(2)}, u32[]{:S(2)}) collective-permute-start(bf16[96,768]{1,0:T(8,128)(2,1)S(1)} %collective-permute-done.4.refs_1_), channel_id=1, source_target_pairs={{0,1},{1,0},{2,3},{3,2},{4,5},{5,4},{6,7},{7,6},{8,9},{9,8},{10,11... | collective-permute-start | bytes 442376 | tf_op jit(solution)/shard_map/ppermute | solution.py:214
  16.4 4.9 %collective-permute-start.10 = (bf16[96,768]{1,0:T(8,128)(2,1)S(1)}, bf16[96,768]{1,0:T(8,128)(2,1)S(1)}, u32[]{:S(2)}, u32[]{:S(2)}) collective-permute-start(bf16[96,768]{1,0:T(8,128)(2,1)S(1)} %collective-permute-done.5.refs_2_), channel_id=1, source_target_pairs={{0,1},{1,0},{2,3},{3,2},{4,5},{5,4},{6,7},{7,6},{8,9},{9,8},{10,11... | collective-permute-start | bytes 442376 | tf_op jit(solution)/shard_map/ppermute | solution.py:214
  20.2 1.4 %collective-permute-start.9 = (bf16[96,768]{1,0:T(8,128)(2,1)S(1)}, bf16[96,768]{1,0:T(8,128)(2,1)S(1)}, u32[]{:S(2)}, u32[]{:S(2)}) collective-permute-start(bf16[96,768]{1,0:T(8,128)(2,1)S(1)} %collective-permute-done.6.refs_3_), channel_id=1, source_target_pairs={{0,1},{1,0},{2,3},{3,2},{4,5},{5,4},{6,7},{7,6},{8,9},{9,8},{10,11... | collective-permute-start | bytes 442376 | tf_op jit(solution)/shard_map/ppermute | solution.py:214
  21.3 5.4 %copy-start.4 = (s32[6]{0:T(128)S(1)}, s32[6]{0:T(128)}, u32[]{:S(2)}) copy-start(s32[6]{0:T(128)} %param.7) | copy-start | bytes 76
  21.3 5.4 %copy-start.5 = (bf16[1,384,768]{2,1,0:T(8,128)(2,1)S(1)}, bf16[1,384,768]{2,1,0:T(8,128)(2,1)}, u32[]{:S(2)}) copy-start(bf16[1,384,768]{2,1,0:T(8,128)(2,1)} %param.8) | copy-start | bytes 1769476
  21.3 5.3 %copy-start.6 = (bf16[1,384,768]{2,1,0:T(8,128)(2,1)S(1)}, bf16[1,384,768]{2,1,0:T(8,128)(2,1)}, u32[]{:S(2)}) copy-start(bf16[1,384,768]{2,1,0:T(8,128)(2,1)} %param.9) | copy-start | bytes 1769476
  23.2 6.5 %collective-permute-start.11 = (bf16[2,96,384]{2,1,0:T(8,128)(2,1)S(1)}, bf16[2,96,384]{2,1,0:T(8,128)(2,1)S(1)}, u32[]{:S(2)}, u32[]{:S(2)}) collective-permute-start(bf16[2,96,384]{2,1,0:T(8,128)(2,1)S(1)} %get-tuple-element.44), channel_id=1, source_target_pairs={{0,4},{1,9},{2,6},{3,11},{4,0},{5,13},{6,2},{7,15},{8,12},{9,1},{1... | collective-permute-start | bytes 442376 | tf_op jit(solution)/shard_map/ppermute | solution.py:218
  23.3 10.7 %collective-permute-start.12 = (bf16[2,96,384]{2,1,0:T(8,128)(2,1)S(1)}, bf16[2,96,384]{2,1,0:T(8,128)(2,1)S(1)}, u32[]{:S(2)}, u32[]{:S(2)}) collective-permute-start(bf16[2,96,384]{2,1,0:T(8,128)(2,1)S(1)} %get-tuple-element.48), channel_id=1, source_target_pairs={{0,6},{1,11},{2,4},{3,9},{4,2},{5,15},{6,0},{7,13},{8,14},{9,3},{1... | collective-permute-start | bytes 442376 | tf_op jit(solution)/shard_map/ppermute | solution.py:218
  26.0 12.1 %collective-permute-start.13 = (bf16[2,96,384]{2,1,0:T(8,128)(2,1)S(1)}, bf16[2,96,384]{2,1,0:T(8,128)(2,1)S(1)}, u32[]{:S(2)}, u32[]{:S(2)}) collective-permute-start(bf16[2,96,384]{2,1,0:T(8,128)(2,1)S(1)} %get-tuple-element.49), channel_id=1, source_target_pairs={{0,2},{1,15},{2,0},{3,13},{4,6},{5,11},{6,4},{7,9},{8,10},{9,7},{1... | collective-permute-start | bytes 442376 | tf_op jit(solution)/shard_map/ppermute | solution.py:218
  29.7 8.4 %collective-permute-start.14 = (bf16[96,384]{1,0:T(8,128)(2,1)S(1)}, bf16[96,384]{1,0:T(8,128)(2,1)S(1)}, u32[]{:S(2)}, u32[]{:S(2)}) collective-permute-start(bf16[96,384]{1,0:T(8,128)(2,1)S(1)} %slice_bitcast_fusion.2), channel_id=1, source_target_pairs={{0,1},{1,0},{2,3},{3,2},{4,5},{5,4},{6,7},{7,6},{8,9},{9,8},{10,11... | collective-permute-start | bytes 221192 | tf_op jit(solution)/shard_map/ppermute | solution.py:214
  30.3 8.1 %collective-permute-start.17 = (bf16[96,384]{1,0:T(8,128)(2,1)S(1)}, bf16[96,384]{1,0:T(8,128)(2,1)S(1)}, u32[]{:S(2)}, u32[]{:S(2)}) collective-permute-start(bf16[96,384]{1,0:T(8,128)(2,1)S(1)} %get-tuple-element.50), channel_id=1, source_target_pairs={{0,12},{1,13},{2,14},{3,15},{4,8},{5,9},{6,10},{7,11},{8,4},{9,5},... | collective-permute-start | bytes 221192 | tf_op jit(solution)/shard_map/ppermute | solution.py:218
  33.9 4.5 %collective-permute-start.15 = (bf16[96,384]{1,0:T(8,128)(2,1)S(1)}, bf16[96,384]{1,0:T(8,128)(2,1)S(1)}, u32[]{:S(2)}, u32[]{:S(2)}) collective-permute-start(bf16[96,384]{1,0:T(8,128)(2,1)S(1)} %slice_bitcast_fusion.1), channel_id=1, source_target_pairs={{0,1},{1,0},{2,3},{3,2},{4,5},{5,4},{6,7},{7,6},{8,9},{9,8},{10,11... | collective-permute-start | bytes 221192 | tf_op jit(solution)/shard_map/ppermute | solution.py:214
  38.1 1.3 %collective-permute-start.16 = (bf16[96,384]{1,0:T(8,128)(2,1)S(1)}, bf16[96,384]{1,0:T(8,128)(2,1)S(1)}, u32[]{:S(2)}, u32[]{:S(2)}) collective-permute-start(bf16[96,384]{1,0:T(8,128)(2,1)S(1)} %slice_bitcast_fusion), channel_id=1, source_target_pairs={{0,1},{1,0},{2,3},{3,2},{4,5},{5,4},{6,7},{7,6},{8,9},{9,8},{10,11... | collective-permute-start | bytes 221192 | tf_op jit(solution)/shard_map/ppermute | solution.py:214

commit v13 on v11

--- a/solution.py
+++ b/solution.py
@@ -11,8 +11,8 @@
 ANY = pl.BlockSpec(memory_space=pl.ANY)
 LIGHT = pl.CostEstimate(flops=0, bytes_accessed=0, transcendentals=0)
 OUT = ((2, 6), (1, 5), (0, 4), (3, 7))
-BACK = ((2, 4), (3, 5), (1, 7))
-SHARED, SELF = (6, 6), (0, 0)
+BACK = ((2, 4), (3, 5), (1, 6))
+SHARED, SELF = (7, 7), (0, 0)
 PARAMS = pltpu.CompilerParams(vmem_limit_bytes=24 * 1024 * 1024)
 
 

time: 40.2 us -> 39.9 us (level)
    ppermute x10, starting transfers between devices: 16.5 us -> 15.9 us  [other_core(): return lax.ppermute(x, 'replica', [(0, 1), (1, 0)])]
where the time goes in v13:
time: 39.9 us; the launch traced here: 39.7 us
  starting transfers between devices  27.7 us (69%)
  Pallas kernels  7.81 us (20%)
  local copies, waits for them, and re-layouts  1.87 us (5%)
  waiting for transfers between devices  1.46 us (4%)
  between operations  0.78 us (2%)
    ppermute x10, starting transfers between devices, other_core(): return lax.ppermute(x, 'replica', [(0, 1), (1, 0)])  15.9 us
    ppermute x8, starting transfers between devices, trade(): return lax.ppermute(x, ('shard', 'replica'), pairs)  11.8 us
    pallas_call x7, Pallas kernels, call(): pl.pallas_call(kernel, out_shape=out_shape, in_specs=in_specs, compiler_p...  7.81 us
    unnamed x14, local copies, waits for them, and re-layouts  1.85 us
    ppermute x8, waiting for transfers between devices, trade(): return lax.ppermute(x, ('shard', 'replica'), pairs)  0.93 us
  transfers between devices with their start and end apart: 18, of which 3 were waited for; matrix products, arithmetic and copies ran while one was open for 0% of the time, Pallas kernels for 13%

profile of v13, /device:TPU:0, one launch (start us, length us, event | category | flops | bytes accessed | tf_op | source)
XLA Modules:
  0.0 39.7 jit_solution(15454102221378872143)
XLA Ops:
  0.6 0.5 %collective-permute-start = (bf16[6,96,768]{2,1,0:T(8,128)(2,1)}, bf16[6,96,768]{2,1,0:T(8,128)(2,1)S(1)}, u32[]{:S(2)}, u32[]{:S(2)}) collective-permute-start(bf16[6,96,768]{2,1,0:T(8,128)(2,1)} %bitcast.14), channel_id=1, source_target_pairs={{0,1},{1,0},{2,3},{3,2},{4,5},{5,4},{6,7},{7,6},{8,9},{9,8},{10,11... | collective-permute-start | bytes 2654216 | tf_op jit(solution)/shard_map/ppermute | solution.py:214
  1.1 0.1 collective-permute-start.2
  1.2 0.4 %collective-permute-start.3 = (bf16[768,384]{1,0:T(8,128)(2,1)}, bf16[768,384]{1,0:T(8,128)(2,1)S(1)}, u32[]{:S(2)}, u32[]{:S(2)}) collective-permute-start(bf16[768,384]{1,0:T(8,128)(2,1)} %bitcast.18), channel_id=1, source_target_pairs={{0,1},{1,0},{2,3},{3,2},{4,5},{5,4},{6,7},{7,6},{8,9},{9,8},{10,11... | collective-permute-start | bytes 1769480 | tf_op jit(solution)/shard_map/ppermute | solution.py:214
  1.7 1.2 %copy-done = bf16[1,6,96,768]{3,2,1,0:T(8,128)(2,1)S(1)} copy-done((bf16[1,6,96,768]{3,2,1,0:T(8,128)(2,1)S(1)}, bf16[1,6,96,768]{3,2,1,0:T(8,128)(2,1)}, u32[]{:S(2)}) %copy-start) | copy-done | bytes 884760
  2.8 0.7 %copy-done.3 = s32[6]{0:T(128)S(1)} copy-done((s32[6]{0:T(128)S(1)}, s32[6]{0:T(128)}, u32[]{:S(2)}) %copy-start.3) | copy-done | bytes 48
  3.5 0.1 shard_map.85.mine_ref
  3.5 0.0 collective-permute-done.theirs_ref
  3.6 0.3 shard_map.86
  3.9 2.9 %collective-permute-start.1 = (bf16[96,768]{1,0:T(8,128)(2,1)S(1)}, bf16[96,768]{1,0:T(8,128)(2,1)S(1)}, u32[]{:S(2)}, u32[]{:S(2)}) collective-permute-start(bf16[96,768]{1,0:T(8,128)(2,1)S(1)} %get-tuple-element.26), channel_id=1, source_target_pairs={{0,4},{1,13},{2,6},{3,15},{4,0},{5,9},{6,2},{7,11},{8,12},{9,5},{1... | collective-permute-start | bytes 442376 | tf_op jit(solution)/shard_map/ppermute | solution.py:218
  6.7 1.5 %collective-permute-start.4 = (bf16[96,768]{1,0:T(8,128)(2,1)S(1)}, bf16[96,768]{1,0:T(8,128)(2,1)S(1)}, u32[]{:S(2)}, u32[]{:S(2)}) collective-permute-start(bf16[96,768]{1,0:T(8,128)(2,1)S(1)} %get-tuple-element.33), channel_id=1, source_target_pairs={{0,2},{1,11},{2,0},{3,9},{4,6},{5,15},{6,4},{7,13},{8,10},{9,3},{1... | collective-permute-start | bytes 442376 | tf_op jit(solution)/shard_map/ppermute | solution.py:218
  8.2 0.7 %collective-permute-start.5 = (bf16[96,768]{1,0:T(8,128)(2,1)S(1)}, bf16[96,768]{1,0:T(8,128)(2,1)S(1)}, u32[]{:S(2)}, u32[]{:S(2)}) collective-permute-start(bf16[96,768]{1,0:T(8,128)(2,1)S(1)} %get-tuple-element.34), channel_id=1, source_target_pairs={{0,0},{1,9},{2,2},{3,11},{4,4},{5,13},{6,6},{7,15},{8,8},{9,1},{10... | collective-permute-start | bytes 442376 | tf_op jit(solution)/shard_map/ppermute | solution.py:218
  8.9 0.0 collective-permute-done.2.other_ref
  8.9 0.1 collective-permute-start.6
  9.0 0.0 collective-permute-done.3.other_right_ref
  9.0 1.7 %shard_map.87 = (bf16[768,576]{1,0:T(8,128)(2,1)S(1)}, bf16[768,192]{1,0:T(8,128)(2,1)S(1)}, bf16[768,768]{1,0:T(8,128)(2,1)S(1)}) custom-call(bf16[384,768]{1,0:T(8,128)(2,1)S(1)} %bitcast.17, bf16[384,768]{1,0:T(8,128)(2,1)S(1)} %collective-permute-done.2.other_ref, bf16[768,384]{1,0:T(8,128)(2,1)S(1)} %bitcast.19, ...), custom_call_target="tpu_custom_call" | custom-call | tf_op jit(solution)/shard_map/pallas_call | solution.py:224
  10.8 0.0 collective-permute-done.1.refs_0_
  10.8 5.1 %collective-permute-start.7 = (bf16[96,768]{1,0:T(8,128)(2,1)S(1)}, bf16[96,768]{1,0:T(8,128)(2,1)S(1)}, u32[]{:S(2)}, u32[]{:S(2)}) collective-permute-start(bf16[96,768]{1,0:T(8,128)(2,1)S(1)} %collective-permute-done.1.refs_0_), channel_id=1, source_target_pairs={{0,1},{1,0},{2,3},{3,2},{4,5},{5,4},{6,7},{7,6},{8,9},{9,8},{10,11... | collective-permute-start | bytes 442376 | tf_op jit(solution)/shard_map/ppermute | solution.py:214
  15.9 0.0 collective-permute-done.4.refs_1_
  15.9 0.9 %collective-permute-start.8 = (bf16[96,768]{1,0:T(8,128)(2,1)S(1)}, bf16[96,768]{1,0:T(8,128)(2,1)S(1)}, u32[]{:S(2)}, u32[]{:S(2)}) collective-permute-start(bf16[96,768]{1,0:T(8,128)(2,1)S(1)} %collective-permute-done.4.refs_1_), channel_id=1, source_target_pairs={{0,1},{1,0},{2,3},{3,2},{4,5},{5,4},{6,7},{7,6},{8,9},{9,8},{10,11... | collective-permute-start | bytes 442376 | tf_op jit(solution)/shard_map/ppermute | solution.py:214
  16.8 0.0 collective-permute-done.5.refs_2_
  16.9 3.6 %collective-permute-start.10 = (bf16[96,768]{1,0:T(8,128)(2,1)S(1)}, bf16[96,768]{1,0:T(8,128)(2,1)S(1)}, u32[]{:S(2)}, u32[]{:S(2)}) collective-permute-start(bf16[96,768]{1,0:T(8,128)(2,1)S(1)} %collective-permute-done.5.refs_2_), channel_id=1, source_target_pairs={{0,1},{1,0},{2,3},{3,2},{4,5},{5,4},{6,7},{7,6},{8,9},{9,8},{10,11... | collective-permute-start | bytes 442376 | tf_op jit(solution)/shard_map/ppermute | solution.py:214
  20.4 0.0 collective-permute-done.6.refs_3_
  20.4 0.4 collective-permute-start.9
  20.8 0.0 collective-permute-done.7.refs_4_
  20.8 0.0 collective-permute-done.8.refs_5_
  20.8 1.1 %shard_map.88 = (f32[768,768]{1,0:T(8,128)S(1)}, f32[8,128]{1,0:T(8,128)S(1)}) custom-call(bf16[768,576]{1,0:T(8,128)(2,1)S(1)} %get-tuple-element.31.left_ref, bf16[96,768]{1,0:T(8,128)(2,1)S(1)} %collective-permute-done.1.refs_0_, bf16[96,768]{1,0:T(8,128)(2,1)S(1)} %collective-permute-done.4.refs_1_, bf16[96,768]{1,0:T(8,128)(2,1)S(1)} %collective-permute-done.5.refs_2_, ...), custom_call_target="tpu_custom_call" | custom-call | tf_op jit(solution)/shard_map/pallas_call | solution.py:224
  21.9 0.0 copy-start.4
  22.0 0.0 copy-start.5
  22.0 0.0 copy-start.6
  22.0 0.0 collective-permute-done.10.refs_1_.refs_6_
  22.0 0.0 collective-permute-done.9.refs_0_.refs_7_
  22.0 1.6 %shard_map.89 = (bf16[2,96,384]{2,1,0:T(8,128)(2,1)S(1)}, bf16[2,96,384]{2,1,0:T(8,128)(2,1)S(1)}, bf16[2,96,384]{2,1,0:T(8,128)(2,1)S(1)}, bf16[96,384]{1,0:T(8,128)(2,1)S(1)}, bf16[96,384]{1,0:T(8,128)(2,1)S(1)}) custom-call(bf16[768,192]{1,0:T(8,128)(2,1)S(1)} %get-tuple-element.30.left_ref, f32[768,768]{1,0:T(8,128)S(1)} %get-tuple-element.36.total_ref, ...), custom_call_target="tpu_custom_call" | custom-call | tf_op jit(solution)/shard_map/pallas_call | solution.py:224
  23.6 2.3 %collective-permute-start.11 = (bf16[2,96,384]{2,1,0:T(8,128)(2,1)S(1)}, bf16[2,96,384]{2,1,0:T(8,128)(2,1)S(1)}, u32[]{:S(2)}, u32[]{:S(2)}) collective-permute-start(bf16[2,96,384]{2,1,0:T(8,128)(2,1)S(1)} %get-tuple-element.39), channel_id=1, source_target_pairs={{0,4},{1,9},{2,6},{3,11},{4,0},{5,13},{6,2},{7,15},{8,12},{9,1},{1... | collective-permute-start | bytes 442376 | tf_op jit(solution)/shard_map/ppermute | solution.py:218
  25.9 0.5 %collective-permute-start.12 = (bf16[2,96,384]{2,1,0:T(8,128)(2,1)S(1)}, bf16[2,96,384]{2,1,0:T(8,128)(2,1)S(1)}, u32[]{:S(2)}, u32[]{:S(2)}) collective-permute-start(bf16[2,96,384]{2,1,0:T(8,128)(2,1)S(1)} %get-tuple-element.45), channel_id=1, source_target_pairs={{0,6},{1,11},{2,4},{3,9},{4,2},{5,15},{6,0},{7,13},{8,14},{9,3},{1... | collective-permute-start | bytes 442376 | tf_op jit(solution)/shard_map/ppermute | solution.py:218
  26.4 1.0 %collective-permute-start.13 = (bf16[2,96,384]{2,1,0:T(8,128)(2,1)S(1)}, bf16[2,96,384]{2,1,0:T(8,128)(2,1)S(1)}, u32[]{:S(2)}, u32[]{:S(2)}) collective-permute-start(bf16[2,96,384]{2,1,0:T(8,128)(2,1)S(1)} %get-tuple-element.46), channel_id=1, source_target_pairs={{0,2},{1,13},{2,0},{3,15},{4,6},{5,9},{6,4},{7,11},{8,10},{9,5},{1... | collective-permute-start | bytes 442376 | tf_op jit(solution)/shard_map/ppermute | solution.py:218
  27.4 2.9 %collective-permute-start.17 = (bf16[96,384]{1,0:T(8,128)(2,1)S(1)}, bf16[96,384]{1,0:T(8,128)(2,1)S(1)}, u32[]{:S(2)}, u32[]{:S(2)}) collective-permute-start(bf16[96,384]{1,0:T(8,128)(2,1)S(1)} %get-tuple-element.48), channel_id=1, source_target_pairs={{0,14},{1,15},{2,12},{3,13},{4,10},{5,11},{6,8},{7,9},{8,6},{9,7},... | collective-permute-start | bytes 221192 | tf_op jit(solution)/shard_map/ppermute | solution.py:218
  30.3 0.0 collective-permute-done.11.after_ref.refs_0_
  30.3 2.1 %shard_map.90 = (bf16[384,768]{1,0:T(8,128)(2,1)}, bf16[384,768]{1,0:T(8,128)(2,1)}) custom-call(s32[1,6]{1,0:T(1,128)S(1)} %bitcast.22, bf16[384,768]{1,0:T(8,128)(2,1)S(1)} %bitcast.24, bf16[384,768]{1,0:T(8,128)(2,1)S(1)} %bitcast.25, bf16[2,96,384]{2,1,0:T(8,128)(2,1)S(1)} %collective-permute-done.11.after_ref.refs_0_, ...), custom_call_target="tpu_custom_call" | custom-call | flops 905969664 | bytes 2359296 | tf_op jit(solution)/shard_map/pallas_call | solution.py:224
  32.4 1.0 %collective-permute-start.14 = (bf16[96,384]{1,0:T(8,128)(2,1)S(1)}, bf16[96,384]{1,0:T(8,128)(2,1)S(1)}, u32[]{:S(2)}, u32[]{:S(2)}) collective-permute-start(bf16[96,384]{1,0:T(8,128)(2,1)S(1)} %slice_bitcast_fusion.2), channel_id=1, source_target_pairs={{0,1},{1,0},{2,3},{3,2},{4,5},{5,4},{6,7},{7,6},{8,9},{9,8},{10,11... | collective-permute-start | bytes 221192 | tf_op jit(solution)/shard_map/ppermute | solution.py:214
  33.4 0.5 %collective-permute-done.12.refs_1_ = bf16[2,96,384]{2,1,0:T(8,128)(2,1)S(1)} collective-permute-done((bf16[2,96,384]{2,1,0:T(8,128)(2,1)S(1)}, bf16[2,96,384]{2,1,0:T(8,128)(2,1)S(1)}, u32[]{:S(2)}, u32[]{:S(2)}) %collective-permute-start.12) | collective-permute-done | bytes 147488 | tf_op jit(solution)/shard_map/ppermute | solution.py:218
  33.9 1.5 %collective-permute-start.15 = (bf16[96,384]{1,0:T(8,128)(2,1)S(1)}, bf16[96,384]{1,0:T(8,128)(2,1)S(1)}, u32[]{:S(2)}, u32[]{:S(2)}) collective-permute-start(bf16[96,384]{1,0:T(8,128)(2,1)S(1)} %slice_bitcast_fusion.1), channel_id=1, source_target_pairs={{0,1},{1,0},{2,3},{3,2},{4,5},{5,4},{6,7},{7,6},{8,9},{9,8},{10,11... | collective-permute-start | bytes 221192 | tf_op jit(solution)/shard_map/ppermute | solution.py:214
  35.4 0.0 collective-permute-done.13.refs_2_
  35.4 2.4 %collective-permute-start.16 = (bf16[96,384]{1,0:T(8,128)(2,1)S(1)}, bf16[96,384]{1,0:T(8,128)(2,1)S(1)}, u32[]{:S(2)}, u32[]{:S(2)}) collective-permute-start(bf16[96,384]{1,0:T(8,128)(2,1)S(1)} %slice_bitcast_fusion), channel_id=1, source_target_pairs={{0,1},{1,0},{2,3},{3,2},{4,5},{5,4},{6,7},{7,6},{8,9},{9,8},{10,11... | collective-permute-start | bytes 221192 | tf_op jit(solution)/shard_map/ppermute | solution.py:214
  37.8 0.4 %collective-permute-done.17.refs_7_ = bf16[96,384]{1,0:T(8,128)(2,1)S(1)} collective-permute-done((bf16[96,384]{1,0:T(8,128)(2,1)S(1)}, bf16[96,384]{1,0:T(8,128)(2,1)S(1)}, u32[]{:S(2)}, u32[]{:S(2)}) %collective-permute-start.17) | collective-permute-done | bytes 73760 | tf_op jit(solution)/shard_map/ppermute | solution.py:218
  38.2 0.0 collective-permute-done.14.refs_3_
  38.2 0.0 collective-permute-done.15.refs_4_
  38.2 0.5 %collective-permute-done.16.refs_5_ = bf16[96,384]{1,0:T(8,128)(2,1)S(1)} collective-permute-done((bf16[96,384]{1,0:T(8,128)(2,1)S(1)}, bf16[96,384]{1,0:T(8,128)(2,1)S(1)}, u32[]{:S(2)}, u32[]{:S(2)}) %collective-permute-start.16) | collective-permute-done | bytes 73760 | tf_op jit(solution)/shard_map/ppermute | solution.py:214
  38.7 0.9 %shard_map.91 = bf16[6,96,384]{2,1,0:T(8,128)(2,1)} custom-call(s32[1,6]{1,0:T(1,128)S(1)} %bitcast.23, bf16[2,96,384]{2,1,0:T(8,128)(2,1)S(1)} %collective-permute-done.11.after_ref.refs_0_, bf16[2,96,384]{2,1,0:T(8,128)(2,1)S(1)} %collective-permute-done.12.refs_1_, bf16[2,96,384]{2,1,0:T(8,128)(2,1)S(1)} %collective-permute-done.13.refs_2_, ...), custom_call_target="tpu_custom_call" | custom-call | tf_op jit(solution)/shard_map/pallas_call | solution.py:224
  (12 shorter events, 0.0 us)
Async XLA Ops:
  0.6 2.9 %collective-permute-start = (bf16[6,96,768]{2,1,0:T(8,128)(2,1)}, bf16[6,96,768]{2,1,0:T(8,128)(2,1)S(1)}, u32[]{:S(2)}, u32[]{:S(2)}) collective-permute-start(bf16[6,96,768]{2,1,0:T(8,128)(2,1)} %bitcast.14), channel_id=1, source_target_pairs={{0,1},{1,0},{2,3},{3,2},{4,5},{5,4},{6,7},{7,6},{8,9},{9,8},{10,11... | collective-permute-start | bytes 2654216 | tf_op jit(solution)/shard_map/ppermute | solution.py:214
  1.1 7.8 %collective-permute-start.2 = (bf16[384,768]{1,0:T(8,128)(2,1)}, bf16[384,768]{1,0:T(8,128)(2,1)S(1)}, u32[]{:S(2)}, u32[]{:S(2)}) collective-permute-start(bf16[384,768]{1,0:T(8,128)(2,1)} %bitcast.16), channel_id=1, source_target_pairs={{0,1},{1,0},{2,3},{3,2},{4,5},{5,4},{6,7},{7,6},{8,9},{9,8},{10,11... | collective-permute-start | bytes 1769480 | tf_op jit(solution)/shard_map/ppermute | solution.py:214
  1.2 7.8 %collective-permute-start.3 = (bf16[768,384]{1,0:T(8,128)(2,1)}, bf16[768,384]{1,0:T(8,128)(2,1)S(1)}, u32[]{:S(2)}, u32[]{:S(2)}) collective-permute-start(bf16[768,384]{1,0:T(8,128)(2,1)} %bitcast.18), channel_id=1, source_target_pairs={{0,1},{1,0},{2,3},{3,2},{4,5},{5,4},{6,7},{7,6},{8,9},{9,8},{10,11... | collective-permute-start | bytes 1769480 | tf_op jit(solution)/shard_map/ppermute | solution.py:214
  1.7 1.2 %copy-start = (bf16[1,6,96,768]{3,2,1,0:T(8,128)(2,1)S(1)}, bf16[1,6,96,768]{3,2,1,0:T(8,128)(2,1)}, u32[]{:S(2)}) copy-start(bf16[1,6,96,768]{3,2,1,0:T(8,128)(2,1)} %param.6) | copy-start | bytes 2654212
  2.8 0.7 %copy-start.3 = (s32[6]{0:T(128)S(1)}, s32[6]{0:T(128)}, u32[]{:S(2)}) copy-start(s32[6]{0:T(128)} %param.7) | copy-start | bytes 76
  3.5 5.5 %copy-start.1 = (bf16[1,384,768]{2,1,0:T(8,128)(2,1)S(1)}, bf16[1,384,768]{2,1,0:T(8,128)(2,1)}, u32[]{:S(2)}) copy-start(bf16[1,384,768]{2,1,0:T(8,128)(2,1)} %param.10) | copy-start | bytes 1769476
  3.5 5.5 %copy-start.2 = (bf16[1,768,384]{2,1,0:T(8,128)(2,1)S(1)}, bf16[1,768,384]{2,1,0:T(8,128)(2,1)}, u32[]{:S(2)}) copy-start(bf16[1,768,384]{2,1,0:T(8,128)(2,1)} %param.11) | copy-start | bytes 1769476
  3.9 6.9 %collective-permute-start.1 = (bf16[96,768]{1,0:T(8,128)(2,1)S(1)}, bf16[96,768]{1,0:T(8,128)(2,1)S(1)}, u32[]{:S(2)}, u32[]{:S(2)}) collective-permute-start(bf16[96,768]{1,0:T(8,128)(2,1)S(1)} %get-tuple-element.26), channel_id=1, source_target_pairs={{0,4},{1,13},{2,6},{3,15},{4,0},{5,9},{6,2},{7,11},{8,12},{9,5},{1... | collective-permute-start | bytes 442376 | tf_op jit(solution)/shard_map/ppermute | solution.py:218
  6.7 9.2 %collective-permute-start.4 = (bf16[96,768]{1,0:T(8,128)(2,1)S(1)}, bf16[96,768]{1,0:T(8,128)(2,1)S(1)}, u32[]{:S(2)}, u32[]{:S(2)}) collective-permute-start(bf16[96,768]{1,0:T(8,128)(2,1)S(1)} %get-tuple-element.33), channel_id=1, source_target_pairs={{0,2},{1,11},{2,0},{3,9},{4,6},{5,15},{6,4},{7,13},{8,10},{9,3},{1... | collective-permute-start | bytes 442376 | tf_op jit(solution)/shard_map/ppermute | solution.py:218
  8.2 8.6 %collective-permute-start.5 = (bf16[96,768]{1,0:T(8,128)(2,1)S(1)}, bf16[96,768]{1,0:T(8,128)(2,1)S(1)}, u32[]{:S(2)}, u32[]{:S(2)}) collective-permute-start(bf16[96,768]{1,0:T(8,128)(2,1)S(1)} %get-tuple-element.34), channel_id=1, source_target_pairs={{0,0},{1,9},{2,2},{3,11},{4,4},{5,13},{6,6},{7,15},{8,8},{9,1},{10... | collective-permute-start | bytes 442376 | tf_op jit(solution)/shard_map/ppermute | solution.py:218
  8.9 11.5 %collective-permute-start.6 = (bf16[96,768]{1,0:T(8,128)(2,1)S(1)}, bf16[96,768]{1,0:T(8,128)(2,1)S(1)}, u32[]{:S(2)}, u32[]{:S(2)}) collective-permute-start(bf16[96,768]{1,0:T(8,128)(2,1)S(1)} %get-tuple-element.35), channel_id=1, source_target_pairs={{0,6},{1,15},{2,4},{3,13},{4,2},{5,11},{6,0},{7,9},{8,14},{9,7},{1... | collective-permute-start | bytes 442376 | tf_op jit(solution)/shard_map/ppermute | solution.py:218
  10.8 10.1 %collective-permute-start.7 = (bf16[96,768]{1,0:T(8,128)(2,1)S(1)}, bf16[96,768]{1,0:T(8,128)(2,1)S(1)}, u32[]{:S(2)}, u32[]{:S(2)}) collective-permute-start(bf16[96,768]{1,0:T(8,128)(2,1)S(1)} %collective-permute-done.1.refs_0_), channel_id=1, source_target_pairs={{0,1},{1,0},{2,3},{3,2},{4,5},{5,4},{6,7},{7,6},{8,9},{9,8},{10,11... | collective-permute-start | bytes 442376 | tf_op jit(solution)/shard_map/ppermute | solution.py:214
  15.9 4.9 %collective-permute-start.8 = (bf16[96,768]{1,0:T(8,128)(2,1)S(1)}, bf16[96,768]{1,0:T(8,128)(2,1)S(1)}, u32[]{:S(2)}, u32[]{:S(2)}) collective-permute-start(bf16[96,768]{1,0:T(8,128)(2,1)S(1)} %collective-permute-done.4.refs_1_), channel_id=1, source_target_pairs={{0,1},{1,0},{2,3},{3,2},{4,5},{5,4},{6,7},{7,6},{8,9},{9,8},{10,11... | collective-permute-start | bytes 442376 | tf_op jit(solution)/shard_map/ppermute | solution.py:214
  16.9 5.1 %collective-permute-start.10 = (bf16[96,768]{1,0:T(8,128)(2,1)S(1)}, bf16[96,768]{1,0:T(8,128)(2,1)S(1)}, u32[]{:S(2)}, u32[]{:S(2)}) collective-permute-start(bf16[96,768]{1,0:T(8,128)(2,1)S(1)} %collective-permute-done.5.refs_2_), channel_id=1, source_target_pairs={{0,1},{1,0},{2,3},{3,2},{4,5},{5,4},{6,7},{7,6},{8,9},{9,8},{10,11... | collective-permute-start | bytes 442376 | tf_op jit(solution)/shard_map/ppermute | solution.py:214
  20.4 1.5 %collective-permute-start.9 = (bf16[96,768]{1,0:T(8,128)(2,1)S(1)}, bf16[96,768]{1,0:T(8,128)(2,1)S(1)}, u32[]{:S(2)}, u32[]{:S(2)}) collective-permute-start(bf16[96,768]{1,0:T(8,128)(2,1)S(1)} %collective-permute-done.6.refs_3_), channel_id=1, source_target_pairs={{0,1},{1,0},{2,3},{3,2},{4,5},{5,4},{6,7},{7,6},{8,9},{9,8},{10,11... | collective-permute-start | bytes 442376 | tf_op jit(solution)/shard_map/ppermute | solution.py:214
  21.9 8.4 %copy-start.4 = (s32[6]{0:T(128)S(1)}, s32[6]{0:T(128)}, u32[]{:S(2)}) copy-start(s32[6]{0:T(128)} %param.7) | copy-start | bytes 76
  22.0 8.4 %copy-start.5 = (bf16[1,384,768]{2,1,0:T(8,128)(2,1)S(1)}, bf16[1,384,768]{2,1,0:T(8,128)(2,1)}, u32[]{:S(2)}) copy-start(bf16[1,384,768]{2,1,0:T(8,128)(2,1)} %param.8) | copy-start | bytes 1769476
  22.0 8.3 %copy-start.6 = (bf16[1,384,768]{2,1,0:T(8,128)(2,1)S(1)}, bf16[1,384,768]{2,1,0:T(8,128)(2,1)}, u32[]{:S(2)}) copy-start(bf16[1,384,768]{2,1,0:T(8,128)(2,1)} %param.9) | copy-start | bytes 1769476
  23.6 6.7 %collective-permute-start.11 = (bf16[2,96,384]{2,1,0:T(8,128)(2,1)S(1)}, bf16[2,96,384]{2,1,0:T(8,128)(2,1)S(1)}, u32[]{:S(2)}, u32[]{:S(2)}) collective-permute-start(bf16[2,96,384]{2,1,0:T(8,128)(2,1)S(1)} %get-tuple-element.39), channel_id=1, source_target_pairs={{0,4},{1,9},{2,6},{3,11},{4,0},{5,13},{6,2},{7,15},{8,12},{9,1},{1... | collective-permute-start | bytes 442376 | tf_op jit(solution)/shard_map/ppermute | solution.py:218
  25.9 8.0 %collective-permute-start.12 = (bf16[2,96,384]{2,1,0:T(8,128)(2,1)S(1)}, bf16[2,96,384]{2,1,0:T(8,128)(2,1)S(1)}, u32[]{:S(2)}, u32[]{:S(2)}) collective-permute-start(bf16[2,96,384]{2,1,0:T(8,128)(2,1)S(1)} %get-tuple-element.45), channel_id=1, source_target_pairs={{0,6},{1,11},{2,4},{3,9},{4,2},{5,15},{6,0},{7,13},{8,14},{9,3},{1... | collective-permute-start | bytes 442376 | tf_op jit(solution)/shard_map/ppermute | solution.py:218
  26.4 9.0 %collective-permute-start.13 = (bf16[2,96,384]{2,1,0:T(8,128)(2,1)S(1)}, bf16[2,96,384]{2,1,0:T(8,128)(2,1)S(1)}, u32[]{:S(2)}, u32[]{:S(2)}) collective-permute-start(bf16[2,96,384]{2,1,0:T(8,128)(2,1)S(1)} %get-tuple-element.46), channel_id=1, source_target_pairs={{0,2},{1,13},{2,0},{3,15},{4,6},{5,9},{6,4},{7,11},{8,10},{9,5},{1... | collective-permute-start | bytes 442376 | tf_op jit(solution)/shard_map/ppermute | solution.py:218
  27.4 10.8 %collective-permute-start.17 = (bf16[96,384]{1,0:T(8,128)(2,1)S(1)}, bf16[96,384]{1,0:T(8,128)(2,1)S(1)}, u32[]{:S(2)}, u32[]{:S(2)}) collective-permute-start(bf16[96,384]{1,0:T(8,128)(2,1)S(1)} %get-tuple-element.48), channel_id=1, source_target_pairs={{0,14},{1,15},{2,12},{3,13},{4,10},{5,11},{6,8},{7,9},{8,6},{9,7},... | collective-permute-start | bytes 221192 | tf_op jit(solution)/shard_map/ppermute | solution.py:218
  32.4 5.8 %collective-permute-start.14 = (bf16[96,384]{1,0:T(8,128)(2,1)S(1)}, bf16[96,384]{1,0:T(8,128)(2,1)S(1)}, u32[]{:S(2)}, u32[]{:S(2)}) collective-permute-start(bf16[96,384]{1,0:T(8,128)(2,1)S(1)} %slice_bitcast_fusion.2), channel_id=1, source_target_pairs={{0,1},{1,0},{2,3},{3,2},{4,5},{5,4},{6,7},{7,6},{8,9},{9,8},{10,11... | collective-permute-start | bytes 221192 | tf_op jit(solution)/shard_map/ppermute | solution.py:214
  33.9 4.3 %collective-permute-start.15 = (bf16[96,384]{1,0:T(8,128)(2,1)S(1)}, bf16[96,384]{1,0:T(8,128)(2,1)S(1)}, u32[]{:S(2)}, u32[]{:S(2)}) collective-permute-start(bf16[96,384]{1,0:T(8,128)(2,1)S(1)} %slice_bitcast_fusion.1), channel_id=1, source_target_pairs={{0,1},{1,0},{2,3},{3,2},{4,5},{5,4},{6,7},{7,6},{8,9},{9,8},{10,11... | collective-permute-start | bytes 221192 | tf_op jit(solution)/shard_map/ppermute | solution.py:214
  35.4 3.3 %collective-permute-start.16 = (bf16[96,384]{1,0:T(8,128)(2,1)S(1)}, bf16[96,384]{1,0:T(8,128)(2,1)S(1)}, u32[]{:S(2)}, u32[]{:S(2)}) collective-permute-start(bf16[96,384]{1,0:T(8,128)(2,1)S(1)} %slice_bitcast_fusion), channel_id=1, source_target_pairs={{0,1},{1,0},{2,3},{3,2},{4,5},{5,4},{6,7},{7,6},{8,9},{9,8},{10,11... | collective-permute-start | bytes 221192 | tf_op jit(solution)/shard_map/ppermute | solution.py:214

commit v14 on v13

--- a/solution.py
+++ b/solution.py
@@ -11,7 +11,7 @@
 ANY = pl.BlockSpec(memory_space=pl.ANY)
 LIGHT = pl.CostEstimate(flops=0, bytes_accessed=0, transcendentals=0)
 OUT = ((2, 6), (1, 5), (0, 4), (3, 7))
-BACK = ((2, 4), (3, 5), (1, 6))
+BACK = ((2, 6), (3, 5), (1, 4))
 SHARED, SELF = (7, 7), (0, 0)
 PARAMS = pltpu.CompilerParams(vmem_limit_bytes=24 * 1024 * 1024)
 

time: 39.9 us -> 41.9 us (1.050)
  starting transfers between devices: 27.7 us -> 29.6 us
    ppermute x10, starting transfers between devices: 15.9 us -> 17.8 us  [other_core(): return lax.ppermute(x, 'replica', [(0, 1), (1, 0)])]
where the time goes in v14:
time: 41.9 us; the launch traced here: 41.7 us
  starting transfers between devices  29.6 us (71%)
  Pallas kernels  7.8 us (19%)
  local copies, waits for them, and re-layouts  1.87 us (4%)
  waiting for transfers between devices  1.69 us (4%)
  between operations  0.78 us (2%)
    ppermute x10, starting transfers between devices, other_core(): return lax.ppermute(x, 'replica', [(0, 1), (1, 0)])  17.8 us
    ppermute x8, starting transfers between devices, trade(): return lax.ppermute(x, ('shard', 'replica'), pairs)  11.8 us
    pallas_call x7, Pallas kernels, call(): pl.pallas_call(kernel, out_shape=out_shape, in_specs=in_specs, compiler_p...  7.8 us
    unnamed x14, local copies, waits for them, and re-layouts  1.85 us
    ppermute x10, waiting for transfers between devices, other_core(): return lax.ppermute(x, 'replica', [(0, 1), (1, 0)])  0.92 us
  transfers between devices with their start and end apart: 18, of which 3 were waited for; matrix products, arithmetic and copies ran while one was open for 0% of the time, Pallas kernels for 13%

profile of v14, /device:TPU:0, one launch (start us, length us, event | category | flops | bytes accessed | tf_op | source)
XLA Modules:
  0.0 41.7 jit_solution(15518497546210936227)
XLA Ops:
  0.6 0.5 %collective-permute-start = (bf16[6,96,768]{2,1,0:T(8,128)(2,1)}, bf16[6,96,768]{2,1,0:T(8,128)(2,1)S(1)}, u32[]{:S(2)}, u32[]{:S(2)}) collective-permute-start(bf16[6,96,768]{2,1,0:T(8,128)(2,1)} %bitcast.14), channel_id=1, source_target_pairs={{0,1},{1,0},{2,3},{3,2},{4,5},{5,4},{6,7},{7,6},{8,9},{9,8},{10,11... | collective-permute-start | bytes 2654216 | tf_op jit(solution)/shard_map/ppermute | solution.py:214
  1.1 0.1 collective-permute-start.2
  1.2 0.4 %collective-permute-start.3 = (bf16[768,384]{1,0:T(8,128)(2,1)}, bf16[768,384]{1,0:T(8,128)(2,1)S(1)}, u32[]{:S(2)}, u32[]{:S(2)}) collective-permute-start(bf16[768,384]{1,0:T(8,128)(2,1)} %bitcast.18), channel_id=1, source_target_pairs={{0,1},{1,0},{2,3},{3,2},{4,5},{5,4},{6,7},{7,6},{8,9},{9,8},{10,11... | collective-permute-start | bytes 1769480 | tf_op jit(solution)/shard_map/ppermute | solution.py:214
  1.7 1.2 %copy-done = bf16[1,6,96,768]{3,2,1,0:T(8,128)(2,1)S(1)} copy-done((bf16[1,6,96,768]{3,2,1,0:T(8,128)(2,1)S(1)}, bf16[1,6,96,768]{3,2,1,0:T(8,128)(2,1)}, u32[]{:S(2)}) %copy-start) | copy-done | bytes 884760
  2.8 0.7 %copy-done.3 = s32[6]{0:T(128)S(1)} copy-done((s32[6]{0:T(128)S(1)}, s32[6]{0:T(128)}, u32[]{:S(2)}) %copy-start.3) | copy-done | bytes 48
  3.5 0.1 shard_map.85.mine_ref
  3.5 0.0 collective-permute-done.theirs_ref
  3.6 0.3 shard_map.86
  3.9 2.9 %collective-permute-start.1 = (bf16[96,768]{1,0:T(8,128)(2,1)S(1)}, bf16[96,768]{1,0:T(8,128)(2,1)S(1)}, u32[]{:S(2)}, u32[]{:S(2)}) collective-permute-start(bf16[96,768]{1,0:T(8,128)(2,1)S(1)} %get-tuple-element.26), channel_id=1, source_target_pairs={{0,4},{1,13},{2,6},{3,15},{4,0},{5,9},{6,2},{7,11},{8,12},{9,5},{1... | collective-permute-start | bytes 442376 | tf_op jit(solution)/shard_map/ppermute | solution.py:218
  6.7 1.5 %collective-permute-start.4 = (bf16[96,768]{1,0:T(8,128)(2,1)S(1)}, bf16[96,768]{1,0:T(8,128)(2,1)S(1)}, u32[]{:S(2)}, u32[]{:S(2)}) collective-permute-start(bf16[96,768]{1,0:T(8,128)(2,1)S(1)} %get-tuple-element.33), channel_id=1, source_target_pairs={{0,2},{1,11},{2,0},{3,9},{4,6},{5,15},{6,4},{7,13},{8,10},{9,3},{1... | collective-permute-start | bytes 442376 | tf_op jit(solution)/shard_map/ppermute | solution.py:218
  8.2 0.7 %collective-permute-start.5 = (bf16[96,768]{1,0:T(8,128)(2,1)S(1)}, bf16[96,768]{1,0:T(8,128)(2,1)S(1)}, u32[]{:S(2)}, u32[]{:S(2)}) collective-permute-start(bf16[96,768]{1,0:T(8,128)(2,1)S(1)} %get-tuple-element.34), channel_id=1, source_target_pairs={{0,0},{1,9},{2,2},{3,11},{4,4},{5,13},{6,6},{7,15},{8,8},{9,1},{10... | collective-permute-start | bytes 442376 | tf_op jit(solution)/shard_map/ppermute | solution.py:218
  8.9 0.0 collective-permute-done.2.other_ref
  8.9 0.1 collective-permute-start.6
  9.0 0.0 collective-permute-done.3.other_right_ref
  9.0 1.7 %shard_map.87 = (bf16[768,576]{1,0:T(8,128)(2,1)S(1)}, bf16[768,192]{1,0:T(8,128)(2,1)S(1)}, bf16[768,768]{1,0:T(8,128)(2,1)S(1)}) custom-call(bf16[384,768]{1,0:T(8,128)(2,1)S(1)} %bitcast.17, bf16[384,768]{1,0:T(8,128)(2,1)S(1)} %collective-permute-done.2.other_ref, bf16[768,384]{1,0:T(8,128)(2,1)S(1)} %bitcast.19, ...), custom_call_target="tpu_custom_call" | custom-call | tf_op jit(solution)/shard_map/pallas_call | solution.py:224
  10.7 0.0 collective-permute-done.1.refs_0_
  10.8 5.1 %collective-permute-start.7 = (bf16[96,768]{1,0:T(8,128)(2,1)S(1)}, bf16[96,768]{1,0:T(8,128)(2,1)S(1)}, u32[]{:S(2)}, u32[]{:S(2)}) collective-permute-start(bf16[96,768]{1,0:T(8,128)(2,1)S(1)} %collective-permute-done.1.refs_0_), channel_id=1, source_target_pairs={{0,1},{1,0},{2,3},{3,2},{4,5},{5,4},{6,7},{7,6},{8,9},{9,8},{10,11... | collective-permute-start | bytes 442376 | tf_op jit(solution)/shard_map/ppermute | solution.py:214
  15.9 0.0 collective-permute-done.4.refs_1_
  15.9 1.0 %collective-permute-start.8 = (bf16[96,768]{1,0:T(8,128)(2,1)S(1)}, bf16[96,768]{1,0:T(8,128)(2,1)S(1)}, u32[]{:S(2)}, u32[]{:S(2)}) collective-permute-start(bf16[96,768]{1,0:T(8,128)(2,1)S(1)} %collective-permute-done.4.refs_1_), channel_id=1, source_target_pairs={{0,1},{1,0},{2,3},{3,2},{4,5},{5,4},{6,7},{7,6},{8,9},{9,8},{10,11... | collective-permute-start | bytes 442376 | tf_op jit(solution)/shard_map/ppermute | solution.py:214
  16.8 0.0 collective-permute-done.5.refs_2_
  16.9 3.6 %collective-permute-start.10 = (bf16[96,768]{1,0:T(8,128)(2,1)S(1)}, bf16[96,768]{1,0:T(8,128)(2,1)S(1)}, u32[]{:S(2)}, u32[]{:S(2)}) collective-permute-start(bf16[96,768]{1,0:T(8,128)(2,1)S(1)} %collective-permute-done.5.refs_2_), channel_id=1, source_target_pairs={{0,1},{1,0},{2,3},{3,2},{4,5},{5,4},{6,7},{7,6},{8,9},{9,8},{10,11... | collective-permute-start | bytes 442376 | tf_op jit(solution)/shard_map/ppermute | solution.py:214
  20.4 0.0 collective-permute-done.6.refs_3_
  20.4 0.4 collective-permute-start.9
  20.8 0.0 collective-permute-done.7.refs_4_
  20.8 0.0 collective-permute-done.8.refs_5_
  20.8 1.1 %shard_map.88 = (f32[768,768]{1,0:T(8,128)S(1)}, f32[8,128]{1,0:T(8,128)S(1)}) custom-call(bf16[768,576]{1,0:T(8,128)(2,1)S(1)} %get-tuple-element.31.left_ref, bf16[96,768]{1,0:T(8,128)(2,1)S(1)} %collective-permute-done.1.refs_0_, bf16[96,768]{1,0:T(8,128)(2,1)S(1)} %collective-permute-done.4.refs_1_, bf16[96,768]{1,0:T(8,128)(2,1)S(1)} %collective-permute-done.5.refs_2_, ...), custom_call_target="tpu_custom_call" | custom-call | tf_op jit(solution)/shard_map/pallas_call | solution.py:224
  21.9 0.0 copy-start.4
  22.0 0.0 copy-start.5
  22.0 0.0 copy-start.6
  22.0 0.0 collective-permute-done.10.refs_1_.refs_6_
  22.0 0.0 collective-permute-done.9.refs_0_.refs_7_
  22.0 1.6 %shard_map.89 = (bf16[2,96,384]{2,1,0:T(8,128)(2,1)S(1)}, bf16[2,96,384]{2,1,0:T(8,128)(2,1)S(1)}, bf16[2,96,384]{2,1,0:T(8,128)(2,1)S(1)}, bf16[96,384]{1,0:T(8,128)(2,1)S(1)}, bf16[96,384]{1,0:T(8,128)(2,1)S(1)}) custom-call(bf16[768,192]{1,0:T(8,128)(2,1)S(1)} %get-tuple-element.30.left_ref, f32[768,768]{1,0:T(8,128)S(1)} %get-tuple-element.36.total_ref, ...), custom_call_target="tpu_custom_call" | custom-call | tf_op jit(solution)/shard_map/pallas_call | solution.py:224
  23.6 2.3 %collective-permute-start.11 = (bf16[2,96,384]{2,1,0:T(8,128)(2,1)S(1)}, bf16[2,96,384]{2,1,0:T(8,128)(2,1)S(1)}, u32[]{:S(2)}, u32[]{:S(2)}) collective-permute-start(bf16[2,96,384]{2,1,0:T(8,128)(2,1)S(1)} %get-tuple-element.39), channel_id=1, source_target_pairs={{0,4},{1,13},{2,6},{3,15},{4,0},{5,9},{6,2},{7,11},{8,12},{9,5},{1... | collective-permute-start | bytes 442376 | tf_op jit(solution)/shard_map/ppermute | solution.py:218
  25.9 0.5 %collective-permute-start.12 = (bf16[2,96,384]{2,1,0:T(8,128)(2,1)S(1)}, bf16[2,96,384]{2,1,0:T(8,128)(2,1)S(1)}, u32[]{:S(2)}, u32[]{:S(2)}) collective-permute-start(bf16[2,96,384]{2,1,0:T(8,128)(2,1)S(1)} %get-tuple-element.45), channel_id=1, source_target_pairs={{0,6},{1,11},{2,4},{3,9},{4,2},{5,15},{6,0},{7,13},{8,14},{9,3},{1... | collective-permute-start | bytes 442376 | tf_op jit(solution)/shard_map/ppermute | solution.py:218
  26.4 1.0 %collective-permute-start.13 = (bf16[2,96,384]{2,1,0:T(8,128)(2,1)S(1)}, bf16[2,96,384]{2,1,0:T(8,128)(2,1)S(1)}, u32[]{:S(2)}, u32[]{:S(2)}) collective-permute-start(bf16[2,96,384]{2,1,0:T(8,128)(2,1)S(1)} %get-tuple-element.46), channel_id=1, source_target_pairs={{0,2},{1,9},{2,0},{3,11},{4,6},{5,13},{6,4},{7,15},{8,10},{9,1},{1... | collective-permute-start | bytes 442376 | tf_op jit(solution)/shard_map/ppermute | solution.py:218
  27.4 2.9 %collective-permute-start.17 = (bf16[96,384]{1,0:T(8,128)(2,1)S(1)}, bf16[96,384]{1,0:T(8,128)(2,1)S(1)}, u32[]{:S(2)}, u32[]{:S(2)}) collective-permute-start(bf16[96,384]{1,0:T(8,128)(2,1)S(1)} %get-tuple-element.48), channel_id=1, source_target_pairs={{0,14},{1,15},{2,12},{3,13},{4,10},{5,11},{6,8},{7,9},{8,6},{9,7},... | collective-permute-start | bytes 221192 | tf_op jit(solution)/shard_map/ppermute | solution.py:218
  30.3 0.3 collective-permute-done.11.after_ref.refs_0_
  30.6 2.1 %shard_map.90 = (bf16[384,768]{1,0:T(8,128)(2,1)}, bf16[384,768]{1,0:T(8,128)(2,1)}) custom-call(s32[1,6]{1,0:T(1,128)S(1)} %bitcast.22, bf16[384,768]{1,0:T(8,128)(2,1)S(1)} %bitcast.24, bf16[384,768]{1,0:T(8,128)(2,1)S(1)} %bitcast.25, bf16[2,96,384]{2,1,0:T(8,128)(2,1)S(1)} %collective-permute-done.11.after_ref.refs_0_, ...), custom_call_target="tpu_custom_call" | custom-call | flops 905969664 | bytes 2359296 | tf_op jit(solution)/shard_map/pallas_call | solution.py:224
  32.7 0.1 collective-permute-start.14
  32.8 0.5 %collective-permute-done.12.refs_1_ = bf16[2,96,384]{2,1,0:T(8,128)(2,1)S(1)} collective-permute-done((bf16[2,96,384]{2,1,0:T(8,128)(2,1)S(1)}, bf16[2,96,384]{2,1,0:T(8,128)(2,1)S(1)}, u32[]{:S(2)}, u32[]{:S(2)}) %collective-permute-start.12) | collective-permute-done | bytes 147488 | tf_op jit(solution)/shard_map/ppermute | solution.py:218
  33.2 5.5 %collective-permute-start.15 = (bf16[96,384]{1,0:T(8,128)(2,1)S(1)}, bf16[96,384]{1,0:T(8,128)(2,1)S(1)}, u32[]{:S(2)}, u32[]{:S(2)}) collective-permute-start(bf16[96,384]{1,0:T(8,128)(2,1)S(1)} %slice_bitcast_fusion.1), channel_id=1, source_target_pairs={{0,1},{1,0},{2,3},{3,2},{4,5},{5,4},{6,7},{7,6},{8,9},{9,8},{10,11... | collective-permute-start | bytes 221192 | tf_op jit(solution)/shard_map/ppermute | solution.py:214
  38.7 0.0 collective-permute-done.13.refs_2_
  38.8 1.1 %collective-permute-start.16 = (bf16[96,384]{1,0:T(8,128)(2,1)S(1)}, bf16[96,384]{1,0:T(8,128)(2,1)S(1)}, u32[]{:S(2)}, u32[]{:S(2)}) collective-permute-start(bf16[96,384]{1,0:T(8,128)(2,1)S(1)} %slice_bitcast_fusion), channel_id=1, source_target_pairs={{0,1},{1,0},{2,3},{3,2},{4,5},{5,4},{6,7},{7,6},{8,9},{9,8},{10,11... | collective-permute-start | bytes 221192 | tf_op jit(solution)/shard_map/ppermute | solution.py:214
  39.9 0.0 collective-permute-done.17.refs_7_
  39.9 0.0 collective-permute-done.14.refs_3_
  39.9 0.0 collective-permute-done.15.refs_4_
  39.9 0.9 %collective-permute-done.16.refs_5_ = bf16[96,384]{1,0:T(8,128)(2,1)S(1)} collective-permute-done((bf16[96,384]{1,0:T(8,128)(2,1)S(1)}, bf16[96,384]{1,0:T(8,128)(2,1)S(1)}, u32[]{:S(2)}, u32[]{:S(2)}) %collective-permute-start.16) | collective-permute-done | bytes 73760 | tf_op jit(solution)/shard_map/ppermute | solution.py:214
  40.8 0.9 %shard_map.91 = bf16[6,96,384]{2,1,0:T(8,128)(2,1)} custom-call(s32[1,6]{1,0:T(1,128)S(1)} %bitcast.23, bf16[2,96,384]{2,1,0:T(8,128)(2,1)S(1)} %collective-permute-done.11.after_ref.refs_0_, bf16[2,96,384]{2,1,0:T(8,128)(2,1)S(1)} %collective-permute-done.12.refs_1_, bf16[2,96,384]{2,1,0:T(8,128)(2,1)S(1)} %collective-permute-done.13.refs_2_, ...), custom_call_target="tpu_custom_call" | custom-call | tf_op jit(solution)/shard_map/pallas_call | solution.py:224
  (12 shorter events, 0.0 us)
Async XLA Ops:
  0.6 2.9 %collective-permute-start = (bf16[6,96,768]{2,1,0:T(8,128)(2,1)}, bf16[6,96,768]{2,1,0:T(8,128)(2,1)S(1)}, u32[]{:S(2)}, u32[]{:S(2)}) collective-permute-start(bf16[6,96,768]{2,1,0:T(8,128)(2,1)} %bitcast.14), channel_id=1, source_target_pairs={{0,1},{1,0},{2,3},{3,2},{4,5},{5,4},{6,7},{7,6},{8,9},{9,8},{10,11... | collective-permute-start | bytes 2654216 | tf_op jit(solution)/shard_map/ppermute | solution.py:214
  1.1 7.8 %collective-permute-start.2 = (bf16[384,768]{1,0:T(8,128)(2,1)}, bf16[384,768]{1,0:T(8,128)(2,1)S(1)}, u32[]{:S(2)}, u32[]{:S(2)}) collective-permute-start(bf16[384,768]{1,0:T(8,128)(2,1)} %bitcast.16), channel_id=1, source_target_pairs={{0,1},{1,0},{2,3},{3,2},{4,5},{5,4},{6,7},{7,6},{8,9},{9,8},{10,11... | collective-permute-start | bytes 1769480 | tf_op jit(solution)/shard_map/ppermute | solution.py:214
  1.2 7.8 %collective-permute-start.3 = (bf16[768,384]{1,0:T(8,128)(2,1)}, bf16[768,384]{1,0:T(8,128)(2,1)S(1)}, u32[]{:S(2)}, u32[]{:S(2)}) collective-permute-start(bf16[768,384]{1,0:T(8,128)(2,1)} %bitcast.18), channel_id=1, source_target_pairs={{0,1},{1,0},{2,3},{3,2},{4,5},{5,4},{6,7},{7,6},{8,9},{9,8},{10,11... | collective-permute-start | bytes 1769480 | tf_op jit(solution)/shard_map/ppermute | solution.py:214
  1.7 1.2 %copy-start = (bf16[1,6,96,768]{3,2,1,0:T(8,128)(2,1)S(1)}, bf16[1,6,96,768]{3,2,1,0:T(8,128)(2,1)}, u32[]{:S(2)}) copy-start(bf16[1,6,96,768]{3,2,1,0:T(8,128)(2,1)} %param.6) | copy-start | bytes 2654212
  2.8 0.7 %copy-start.3 = (s32[6]{0:T(128)S(1)}, s32[6]{0:T(128)}, u32[]{:S(2)}) copy-start(s32[6]{0:T(128)} %param.7) | copy-start | bytes 76
  3.5 5.5 %copy-start.1 = (bf16[1,384,768]{2,1,0:T(8,128)(2,1)S(1)}, bf16[1,384,768]{2,1,0:T(8,128)(2,1)}, u32[]{:S(2)}) copy-start(bf16[1,384,768]{2,1,0:T(8,128)(2,1)} %param.10) | copy-start | bytes 1769476
  3.5 5.5 %copy-start.2 = (bf16[1,768,384]{2,1,0:T(8,128)(2,1)S(1)}, bf16[1,768,384]{2,1,0:T(8,128)(2,1)}, u32[]{:S(2)}) copy-start(bf16[1,768,384]{2,1,0:T(8,128)(2,1)} %param.11) | copy-start | bytes 1769476
  3.9 6.9 %collective-permute-start.1 = (bf16[96,768]{1,0:T(8,128)(2,1)S(1)}, bf16[96,768]{1,0:T(8,128)(2,1)S(1)}, u32[]{:S(2)}, u32[]{:S(2)}) collective-permute-start(bf16[96,768]{1,0:T(8,128)(2,1)S(1)} %get-tuple-element.26), channel_id=1, source_target_pairs={{0,4},{1,13},{2,6},{3,15},{4,0},{5,9},{6,2},{7,11},{8,12},{9,5},{1... | collective-permute-start | bytes 442376 | tf_op jit(solution)/shard_map/ppermute | solution.py:218
  6.7 9.2 %collective-permute-start.4 = (bf16[96,768]{1,0:T(8,128)(2,1)S(1)}, bf16[96,768]{1,0:T(8,128)(2,1)S(1)}, u32[]{:S(2)}, u32[]{:S(2)}) collective-permute-start(bf16[96,768]{1,0:T(8,128)(2,1)S(1)} %get-tuple-element.33), channel_id=1, source_target_pairs={{0,2},{1,11},{2,0},{3,9},{4,6},{5,15},{6,4},{7,13},{8,10},{9,3},{1... | collective-permute-start | bytes 442376 | tf_op jit(solution)/shard_map/ppermute | solution.py:218
  8.2 8.6 %collective-permute-start.5 = (bf16[96,768]{1,0:T(8,128)(2,1)S(1)}, bf16[96,768]{1,0:T(8,128)(2,1)S(1)}, u32[]{:S(2)}, u32[]{:S(2)}) collective-permute-start(bf16[96,768]{1,0:T(8,128)(2,1)S(1)} %get-tuple-element.34), channel_id=1, source_target_pairs={{0,0},{1,9},{2,2},{3,11},{4,4},{5,13},{6,6},{7,15},{8,8},{9,1},{10... | collective-permute-start | bytes 442376 | tf_op jit(solution)/shard_map/ppermute | solution.py:218
  8.9 11.5 %collective-permute-start.6 = (bf16[96,768]{1,0:T(8,128)(2,1)S(1)}, bf16[96,768]{1,0:T(8,128)(2,1)S(1)}, u32[]{:S(2)}, u32[]{:S(2)}) collective-permute-start(bf16[96,768]{1,0:T(8,128)(2,1)S(1)} %get-tuple-element.35), channel_id=1, source_target_pairs={{0,6},{1,15},{2,4},{3,13},{4,2},{5,11},{6,0},{7,9},{8,14},{9,7},{1... | collective-permute-start | bytes 442376 | tf_op jit(solution)/shard_map/ppermute | solution.py:218
  10.8 10.1 %collective-permute-start.7 = (bf16[96,768]{1,0:T(8,128)(2,1)S(1)}, bf16[96,768]{1,0:T(8,128)(2,1)S(1)}, u32[]{:S(2)}, u32[]{:S(2)}) collective-permute-start(bf16[96,768]{1,0:T(8,128)(2,1)S(1)} %collective-permute-done.1.refs_0_), channel_id=1, source_target_pairs={{0,1},{1,0},{2,3},{3,2},{4,5},{5,4},{6,7},{7,6},{8,9},{9,8},{10,11... | collective-permute-start | bytes 442376 | tf_op jit(solution)/shard_map/ppermute | solution.py:214
  15.9 4.9 %collective-permute-start.8 = (bf16[96,768]{1,0:T(8,128)(2,1)S(1)}, bf16[96,768]{1,0:T(8,128)(2,1)S(1)}, u32[]{:S(2)}, u32[]{:S(2)}) collective-permute-start(bf16[96,768]{1,0:T(8,128)(2,1)S(1)} %collective-permute-done.4.refs_1_), channel_id=1, source_target_pairs={{0,1},{1,0},{2,3},{3,2},{4,5},{5,4},{6,7},{7,6},{8,9},{9,8},{10,11... | collective-permute-start | bytes 442376 | tf_op jit(solution)/shard_map/ppermute | solution.py:214
  16.9 5.1 %collective-permute-start.10 = (bf16[96,768]{1,0:T(8,128)(2,1)S(1)}, bf16[96,768]{1,0:T(8,128)(2,1)S(1)}, u32[]{:S(2)}, u32[]{:S(2)}) collective-permute-start(bf16[96,768]{1,0:T(8,128)(2,1)S(1)} %collective-permute-done.5.refs_2_), channel_id=1, source_target_pairs={{0,1},{1,0},{2,3},{3,2},{4,5},{5,4},{6,7},{7,6},{8,9},{9,8},{10,11... | collective-permute-start | bytes 442376 | tf_op jit(solution)/shard_map/ppermute | solution.py:214
  20.4 1.5 %collective-permute-start.9 = (bf16[96,768]{1,0:T(8,128)(2,1)S(1)}, bf16[96,768]{1,0:T(8,128)(2,1)S(1)}, u32[]{:S(2)}, u32[]{:S(2)}) collective-permute-start(bf16[96,768]{1,0:T(8,128)(2,1)S(1)} %collective-permute-done.6.refs_3_), channel_id=1, source_target_pairs={{0,1},{1,0},{2,3},{3,2},{4,5},{5,4},{6,7},{7,6},{8,9},{9,8},{10,11... | collective-permute-start | bytes 442376 | tf_op jit(solution)/shard_map/ppermute | solution.py:214
  21.9 8.6 %copy-start.4 = (s32[6]{0:T(128)S(1)}, s32[6]{0:T(128)}, u32[]{:S(2)}) copy-start(s32[6]{0:T(128)} %param.7) | copy-start | bytes 76
  22.0 8.6 %copy-start.5 = (bf16[1,384,768]{2,1,0:T(8,128)(2,1)S(1)}, bf16[1,384,768]{2,1,0:T(8,128)(2,1)}, u32[]{:S(2)}) copy-start(bf16[1,384,768]{2,1,0:T(8,128)(2,1)} %param.8) | copy-start | bytes 1769476
  22.0 8.6 %copy-start.6 = (bf16[1,384,768]{2,1,0:T(8,128)(2,1)S(1)}, bf16[1,384,768]{2,1,0:T(8,128)(2,1)}, u32[]{:S(2)}) copy-start(bf16[1,384,768]{2,1,0:T(8,128)(2,1)} %param.9) | copy-start | bytes 1769476
  23.6 7.0 %collective-permute-start.11 = (bf16[2,96,384]{2,1,0:T(8,128)(2,1)S(1)}, bf16[2,96,384]{2,1,0:T(8,128)(2,1)S(1)}, u32[]{:S(2)}, u32[]{:S(2)}) collective-permute-start(bf16[2,96,384]{2,1,0:T(8,128)(2,1)S(1)} %get-tuple-element.39), channel_id=1, source_target_pairs={{0,4},{1,13},{2,6},{3,15},{4,0},{5,9},{6,2},{7,11},{8,12},{9,5},{1... | collective-permute-start | bytes 442376 | tf_op jit(solution)/shard_map/ppermute | solution.py:218
  25.9 7.3 %collective-permute-start.12 = (bf16[2,96,384]{2,1,0:T(8,128)(2,1)S(1)}, bf16[2,96,384]{2,1,0:T(8,128)(2,1)S(1)}, u32[]{:S(2)}, u32[]{:S(2)}) collective-permute-start(bf16[2,96,384]{2,1,0:T(8,128)(2,1)S(1)} %get-tuple-element.45), channel_id=1, source_target_pairs={{0,6},{1,11},{2,4},{3,9},{4,2},{5,15},{6,0},{7,13},{8,14},{9,3},{1... | collective-permute-start | bytes 442376 | tf_op jit(solution)/shard_map/ppermute | solution.py:218
  26.4 12.3 %collective-permute-start.13 = (bf16[2,96,384]{2,1,0:T(8,128)(2,1)S(1)}, bf16[2,96,384]{2,1,0:T(8,128)(2,1)S(1)}, u32[]{:S(2)}, u32[]{:S(2)}) collective-permute-start(bf16[2,96,384]{2,1,0:T(8,128)(2,1)S(1)} %get-tuple-element.46), channel_id=1, source_target_pairs={{0,2},{1,9},{2,0},{3,11},{4,6},{5,13},{6,4},{7,15},{8,10},{9,1},{1... | collective-permute-start | bytes 442376 | tf_op jit(solution)/shard_map/ppermute | solution.py:218
  27.4 12.4 %collective-permute-start.17 = (bf16[96,384]{1,0:T(8,128)(2,1)S(1)}, bf16[96,384]{1,0:T(8,128)(2,1)S(1)}, u32[]{:S(2)}, u32[]{:S(2)}) collective-permute-start(bf16[96,384]{1,0:T(8,128)(2,1)S(1)} %get-tuple-element.48), channel_id=1, source_target_pairs={{0,14},{1,15},{2,12},{3,13},{4,10},{5,11},{6,8},{7,9},{8,6},{9,7},... | collective-permute-start | bytes 221192 | tf_op jit(solution)/shard_map/ppermute | solution.py:218
  32.7 7.2 %collective-permute-start.14 = (bf16[96,384]{1,0:T(8,128)(2,1)S(1)}, bf16[96,384]{1,0:T(8,128)(2,1)S(1)}, u32[]{:S(2)}, u32[]{:S(2)}) collective-permute-start(bf16[96,384]{1,0:T(8,128)(2,1)S(1)} %slice_bitcast_fusion.2), channel_id=1, source_target_pairs={{0,1},{1,0},{2,3},{3,2},{4,5},{5,4},{6,7},{7,6},{8,9},{9,8},{10,11... | collective-permute-start | bytes 221192 | tf_op jit(solution)/shard_map/ppermute | solution.py:214
  33.2 6.6 %collective-permute-start.15 = (bf16[96,384]{1,0:T(8,128)(2,1)S(1)}, bf16[96,384]{1,0:T(8,128)(2,1)S(1)}, u32[]{:S(2)}, u32[]{:S(2)}) collective-permute-start(bf16[96,384]{1,0:T(8,128)(2,1)S(1)} %slice_bitcast_fusion.1), channel_id=1, source_target_pairs={{0,1},{1,0},{2,3},{3,2},{4,5},{5,4},{6,7},{7,6},{8,9},{9,8},{10,11... | collective-permute-start | bytes 221192 | tf_op jit(solution)/shard_map/ppermute | solution.py:214
  38.8 2.0 %collective-permute-start.16 = (bf16[96,384]{1,0:T(8,128)(2,1)S(1)}, bf16[96,384]{1,0:T(8,128)(2,1)S(1)}, u32[]{:S(2)}, u32[]{:S(2)}) collective-permute-start(bf16[96,384]{1,0:T(8,128)(2,1)S(1)} %slice_bitcast_fusion), channel_id=1, source_target_pairs={{0,1},{1,0},{2,3},{3,2},{4,5},{5,4},{6,7},{7,6},{8,9},{9,8},{10,11... | collective-permute-start | bytes 221192 | tf_op jit(solution)/shard_map/ppermute | solution.py:214

commit v15 on v13

--- a/solution.py
+++ b/solution.py
@@ -10,7 +10,7 @@
 VMEM = pl.BlockSpec(memory_space=pltpu.VMEM)
 ANY = pl.BlockSpec(memory_space=pl.ANY)
 LIGHT = pl.CostEstimate(flops=0, bytes_accessed=0, transcendentals=0)
-OUT = ((2, 6), (1, 5), (0, 4), (3, 7))
+OUT = ((2, 4), (1, 5), (0, 7), (3, 6))
 BACK = ((2, 4), (3, 5), (1, 6))
 SHARED, SELF = (7, 7), (0, 0)
 PARAMS = pltpu.CompilerParams(vmem_limit_bytes=24 * 1024 * 1024)

time: 39.9 us -> 41.5 us (1.040)
  starting transfers between devices: 27.7 us -> 29.3 us
    ppermute x8, starting transfers between devices: 11.8 us -> 13.4 us  [trade(): return lax.ppermute(x, ('shard', 'replica'), pairs)]
    ppermute x10, waiting for transfers between devices: 0.52 us -> 1.25 us  [other_core(): return lax.ppermute(x, 'replica', [(0, 1), (1, 0)])]
    ppermute x8, waiting for transfers between devices: 0.93 us -> 0.32 us  [trade(): return lax.ppermute(x, ('shard', 'replica'), pairs)]
where the time goes in v15:
time: 41.5 us; the launch traced here: 41.4 us
  starting transfers between devices  29.3 us (71%)
  Pallas kernels  7.82 us (19%)
  local copies, waits for them, and re-layouts  1.87 us (5%)
  waiting for transfers between devices  1.57 us (4%)
  between operations  0.77 us (2%)
    ppermute x10, starting transfers between devices, other_core(): return lax.ppermute(x, 'replica', [(0, 1), (1, 0)])  16 us
    ppermute x8, starting transfers between devices, trade(): return lax.ppermute(x, ('shard', 'replica'), pairs)  13.4 us
    pallas_call x7, Pallas kernels, call(): pl.pallas_call(kernel, out_shape=out_shape, in_specs=in_specs, compiler_p...  7.82 us
    unnamed x14, local copies, waits for them, and re-layouts  1.85 us
    ppermute x10, waiting for transfers between devices, other_core(): return lax.ppermute(x, 'replica', [(0, 1), (1, 0)])  1.25 us
  transfers between devices with their start and end apart: 18, of which 3 were waited for; matrix products, arithmetic and copies ran while one was open for 0% of the time, Pallas kernels for 13%

profile of v15, /device:TPU:0, one launch (start us, length us, event | category | flops | bytes accessed | tf_op | source)
XLA Modules:
  0.0 41.4 jit_solution(7676052920163851099)
XLA Ops:
  0.6 0.5 %collective-permute-start = (bf16[6,96,768]{2,1,0:T(8,128)(2,1)}, bf16[6,96,768]{2,1,0:T(8,128)(2,1)S(1)}, u32[]{:S(2)}, u32[]{:S(2)}) collective-permute-start(bf16[6,96,768]{2,1,0:T(8,128)(2,1)} %bitcast.14), channel_id=1, source_target_pairs={{0,1},{1,0},{2,3},{3,2},{4,5},{5,4},{6,7},{7,6},{8,9},{9,8},{10,11... | collective-permute-start | bytes 2654216 | tf_op jit(solution)/shard_map/ppermute | solution.py:214
  1.1 0.1 collective-permute-start.2
  1.2 0.4 %collective-permute-start.3 = (bf16[768,384]{1,0:T(8,128)(2,1)}, bf16[768,384]{1,0:T(8,128)(2,1)S(1)}, u32[]{:S(2)}, u32[]{:S(2)}) collective-permute-start(bf16[768,384]{1,0:T(8,128)(2,1)} %bitcast.18), channel_id=1, source_target_pairs={{0,1},{1,0},{2,3},{3,2},{4,5},{5,4},{6,7},{7,6},{8,9},{9,8},{10,11... | collective-permute-start | bytes 1769480 | tf_op jit(solution)/shard_map/ppermute | solution.py:214
  1.7 1.2 %copy-done = bf16[1,6,96,768]{3,2,1,0:T(8,128)(2,1)S(1)} copy-done((bf16[1,6,96,768]{3,2,1,0:T(8,128)(2,1)S(1)}, bf16[1,6,96,768]{3,2,1,0:T(8,128)(2,1)}, u32[]{:S(2)}) %copy-start) | copy-done | bytes 884760
  2.8 0.7 %copy-done.3 = s32[6]{0:T(128)S(1)} copy-done((s32[6]{0:T(128)S(1)}, s32[6]{0:T(128)}, u32[]{:S(2)}) %copy-start.3) | copy-done | bytes 48
  3.5 0.1 shard_map.85.mine_ref
  3.5 0.0 collective-permute-done.theirs_ref
  3.6 0.3 shard_map.86
  3.9 2.9 %collective-permute-start.1 = (bf16[96,768]{1,0:T(8,128)(2,1)S(1)}, bf16[96,768]{1,0:T(8,128)(2,1)S(1)}, u32[]{:S(2)}, u32[]{:S(2)}) collective-permute-start(bf16[96,768]{1,0:T(8,128)(2,1)S(1)} %get-tuple-element.26), channel_id=1, source_target_pairs={{0,4},{1,9},{2,6},{3,11},{4,0},{5,13},{6,2},{7,15},{8,12},{9,1},{1... | collective-permute-start | bytes 442376 | tf_op jit(solution)/shard_map/ppermute | solution.py:218
  6.7 1.5 %collective-permute-start.4 = (bf16[96,768]{1,0:T(8,128)(2,1)S(1)}, bf16[96,768]{1,0:T(8,128)(2,1)S(1)}, u32[]{:S(2)}, u32[]{:S(2)}) collective-permute-start(bf16[96,768]{1,0:T(8,128)(2,1)S(1)} %get-tuple-element.33), channel_id=1, source_target_pairs={{0,2},{1,11},{2,0},{3,9},{4,6},{5,15},{6,4},{7,13},{8,10},{9,3},{1... | collective-permute-start | bytes 442376 | tf_op jit(solution)/shard_map/ppermute | solution.py:218
  8.2 0.7 %collective-permute-start.5 = (bf16[96,768]{1,0:T(8,128)(2,1)S(1)}, bf16[96,768]{1,0:T(8,128)(2,1)S(1)}, u32[]{:S(2)}, u32[]{:S(2)}) collective-permute-start(bf16[96,768]{1,0:T(8,128)(2,1)S(1)} %get-tuple-element.34), channel_id=1, source_target_pairs={{0,0},{1,15},{2,2},{3,13},{4,4},{5,11},{6,6},{7,9},{8,8},{9,7},{10... | collective-permute-start | bytes 442376 | tf_op jit(solution)/shard_map/ppermute | solution.py:218
  8.9 0.0 collective-permute-done.2.other_ref
  8.9 0.1 collective-permute-start.6
  9.0 0.0 collective-permute-done.3.other_right_ref
  9.0 1.7 %shard_map.87 = (bf16[768,576]{1,0:T(8,128)(2,1)S(1)}, bf16[768,192]{1,0:T(8,128)(2,1)S(1)}, bf16[768,768]{1,0:T(8,128)(2,1)S(1)}) custom-call(bf16[384,768]{1,0:T(8,128)(2,1)S(1)} %bitcast.17, bf16[384,768]{1,0:T(8,128)(2,1)S(1)} %collective-permute-done.2.other_ref, bf16[768,384]{1,0:T(8,128)(2,1)S(1)} %bitcast.19, ...), custom_call_target="tpu_custom_call" | custom-call | tf_op jit(solution)/shard_map/pallas_call | solution.py:224
  10.7 0.3 collective-permute-done.1.refs_0_
  11.0 4.8 %collective-permute-start.7 = (bf16[96,768]{1,0:T(8,128)(2,1)S(1)}, bf16[96,768]{1,0:T(8,128)(2,1)S(1)}, u32[]{:S(2)}, u32[]{:S(2)}) collective-permute-start(bf16[96,768]{1,0:T(8,128)(2,1)S(1)} %collective-permute-done.1.refs_0_), channel_id=1, source_target_pairs={{0,1},{1,0},{2,3},{3,2},{4,5},{5,4},{6,7},{7,6},{8,9},{9,8},{10,11... | collective-permute-start | bytes 442376 | tf_op jit(solution)/shard_map/ppermute | solution.py:214
  15.9 0.0 collective-permute-done.4.refs_1_
  15.9 0.6 %collective-permute-start.8 = (bf16[96,768]{1,0:T(8,128)(2,1)S(1)}, bf16[96,768]{1,0:T(8,128)(2,1)S(1)}, u32[]{:S(2)}, u32[]{:S(2)}) collective-permute-start(bf16[96,768]{1,0:T(8,128)(2,1)S(1)} %collective-permute-done.4.refs_1_), channel_id=1, source_target_pairs={{0,1},{1,0},{2,3},{3,2},{4,5},{5,4},{6,7},{7,6},{8,9},{9,8},{10,11... | collective-permute-start | bytes 442376 | tf_op jit(solution)/shard_map/ppermute | solution.py:214
  16.4 0.0 collective-permute-done.5.refs_2_
  16.4 2.2 %collective-permute-start.10 = (bf16[96,768]{1,0:T(8,128)(2,1)S(1)}, bf16[96,768]{1,0:T(8,128)(2,1)S(1)}, u32[]{:S(2)}, u32[]{:S(2)}) collective-permute-start(bf16[96,768]{1,0:T(8,128)(2,1)S(1)} %collective-permute-done.5.refs_2_), channel_id=1, source_target_pairs={{0,1},{1,0},{2,3},{3,2},{4,5},{5,4},{6,7},{7,6},{8,9},{9,8},{10,11... | collective-permute-start | bytes 442376 | tf_op jit(solution)/shard_map/ppermute | solution.py:214
  18.6 0.0 collective-permute-done.6.refs_3_
  18.6 1.2 %collective-permute-start.9 = (bf16[96,768]{1,0:T(8,128)(2,1)S(1)}, bf16[96,768]{1,0:T(8,128)(2,1)S(1)}, u32[]{:S(2)}, u32[]{:S(2)}) collective-permute-start(bf16[96,768]{1,0:T(8,128)(2,1)S(1)} %collective-permute-done.6.refs_3_), channel_id=1, source_target_pairs={{0,1},{1,0},{2,3},{3,2},{4,5},{5,4},{6,7},{7,6},{8,9},{9,8},{10,11... | collective-permute-start | bytes 442376 | tf_op jit(solution)/shard_map/ppermute | solution.py:214
  19.8 0.0 collective-permute-done.7.refs_4_
  19.8 0.0 collective-permute-done.8.refs_5_
  19.8 1.1 %shard_map.88 = (f32[768,768]{1,0:T(8,128)S(1)}, f32[8,128]{1,0:T(8,128)S(1)}) custom-call(bf16[768,576]{1,0:T(8,128)(2,1)S(1)} %get-tuple-element.31.left_ref, bf16[96,768]{1,0:T(8,128)(2,1)S(1)} %collective-permute-done.1.refs_0_, bf16[96,768]{1,0:T(8,128)(2,1)S(1)} %collective-permute-done.4.refs_1_, bf16[96,768]{1,0:T(8,128)(2,1)S(1)} %collective-permute-done.5.refs_2_, ...), custom_call_target="tpu_custom_call" | custom-call | tf_op jit(solution)/shard_map/pallas_call | solution.py:224
  20.9 0.0 copy-start.4
  20.9 0.0 copy-start.5
  20.9 0.0 copy-start.6
  20.9 0.0 collective-permute-done.10.refs_1_.refs_6_
  21.0 0.0 collective-permute-done.9.refs_0_.refs_7_
  21.0 1.6 %shard_map.89 = (bf16[2,96,384]{2,1,0:T(8,128)(2,1)S(1)}, bf16[2,96,384]{2,1,0:T(8,128)(2,1)S(1)}, bf16[2,96,384]{2,1,0:T(8,128)(2,1)S(1)}, bf16[96,384]{1,0:T(8,128)(2,1)S(1)}, bf16[96,384]{1,0:T(8,128)(2,1)S(1)}) custom-call(bf16[768,192]{1,0:T(8,128)(2,1)S(1)} %get-tuple-element.30.left_ref, f32[768,768]{1,0:T(8,128)S(1)} %get-tuple-element.36.total_ref, ...), custom_call_target="tpu_custom_call" | custom-call | tf_op jit(solution)/shard_map/pallas_call | solution.py:224
  22.6 2.7 %collective-permute-start.11 = (bf16[2,96,384]{2,1,0:T(8,128)(2,1)S(1)}, bf16[2,96,384]{2,1,0:T(8,128)(2,1)S(1)}, u32[]{:S(2)}, u32[]{:S(2)}) collective-permute-start(bf16[2,96,384]{2,1,0:T(8,128)(2,1)S(1)} %get-tuple-element.39), channel_id=1, source_target_pairs={{0,4},{1,9},{2,6},{3,11},{4,0},{5,13},{6,2},{7,15},{8,12},{9,1},{1... | collective-permute-start | bytes 442376 | tf_op jit(solution)/shard_map/ppermute | solution.py:218
  25.3 1.0 %collective-permute-start.12 = (bf16[2,96,384]{2,1,0:T(8,128)(2,1)S(1)}, bf16[2,96,384]{2,1,0:T(8,128)(2,1)S(1)}, u32[]{:S(2)}, u32[]{:S(2)}) collective-permute-start(bf16[2,96,384]{2,1,0:T(8,128)(2,1)S(1)} %get-tuple-element.45), channel_id=1, source_target_pairs={{0,6},{1,11},{2,4},{3,9},{4,2},{5,15},{6,0},{7,13},{8,14},{9,3},{1... | collective-permute-start | bytes 442376 | tf_op jit(solution)/shard_map/ppermute | solution.py:218
  26.3 0.5 %collective-permute-start.13 = (bf16[2,96,384]{2,1,0:T(8,128)(2,1)S(1)}, bf16[2,96,384]{2,1,0:T(8,128)(2,1)S(1)}, u32[]{:S(2)}, u32[]{:S(2)}) collective-permute-start(bf16[2,96,384]{2,1,0:T(8,128)(2,1)S(1)} %get-tuple-element.46), channel_id=1, source_target_pairs={{0,2},{1,13},{2,0},{3,15},{4,6},{5,9},{6,4},{7,11},{8,10},{9,5},{1... | collective-permute-start | bytes 442376 | tf_op jit(solution)/shard_map/ppermute | solution.py:218
  26.8 4.0 %collective-permute-start.17 = (bf16[96,384]{1,0:T(8,128)(2,1)S(1)}, bf16[96,384]{1,0:T(8,128)(2,1)S(1)}, u32[]{:S(2)}, u32[]{:S(2)}) collective-permute-start(bf16[96,384]{1,0:T(8,128)(2,1)S(1)} %get-tuple-element.48), channel_id=1, source_target_pairs={{0,14},{1,15},{2,12},{3,13},{4,10},{5,11},{6,8},{7,9},{8,6},{9,7},... | collective-permute-start | bytes 221192 | tf_op jit(solution)/shard_map/ppermute | solution.py:218
  30.8 0.0 collective-permute-done.11.after_ref.refs_0_
  30.9 2.1 %shard_map.90 = (bf16[384,768]{1,0:T(8,128)(2,1)}, bf16[384,768]{1,0:T(8,128)(2,1)}) custom-call(s32[1,6]{1,0:T(1,128)S(1)} %bitcast.22, bf16[384,768]{1,0:T(8,128)(2,1)S(1)} %bitcast.24, bf16[384,768]{1,0:T(8,128)(2,1)S(1)} %bitcast.25, bf16[2,96,384]{2,1,0:T(8,128)(2,1)S(1)} %collective-permute-done.11.after_ref.refs_0_, ...), custom_call_target="tpu_custom_call" | custom-call | flops 905969664 | bytes 2359296 | tf_op jit(solution)/shard_map/pallas_call | solution.py:224
  33.0 1.3 %collective-permute-start.14 = (bf16[96,384]{1,0:T(8,128)(2,1)S(1)}, bf16[96,384]{1,0:T(8,128)(2,1)S(1)}, u32[]{:S(2)}, u32[]{:S(2)}) collective-permute-start(bf16[96,384]{1,0:T(8,128)(2,1)S(1)} %slice_bitcast_fusion.2), channel_id=1, source_target_pairs={{0,1},{1,0},{2,3},{3,2},{4,5},{5,4},{6,7},{7,6},{8,9},{9,8},{10,11... | collective-permute-start | bytes 221192 | tf_op jit(solution)/shard_map/ppermute | solution.py:214
  34.3 0.0 collective-permute-done.12.refs_1_
  34.3 4.7 %collective-permute-start.15 = (bf16[96,384]{1,0:T(8,128)(2,1)S(1)}, bf16[96,384]{1,0:T(8,128)(2,1)S(1)}, u32[]{:S(2)}, u32[]{:S(2)}) collective-permute-start(bf16[96,384]{1,0:T(8,128)(2,1)S(1)} %slice_bitcast_fusion.1), channel_id=1, source_target_pairs={{0,1},{1,0},{2,3},{3,2},{4,5},{5,4},{6,7},{7,6},{8,9},{9,8},{10,11... | collective-permute-start | bytes 221192 | tf_op jit(solution)/shard_map/ppermute | solution.py:214
  39.1 0.0 collective-permute-done.13.refs_2_
  39.1 0.1 collective-permute-start.16
  39.2 0.0 collective-permute-done.17.refs_7_
  39.2 0.0 collective-permute-done.14.refs_3_
  39.2 0.8 %collective-permute-done.15.refs_4_ = bf16[96,384]{1,0:T(8,128)(2,1)S(1)} collective-permute-done((bf16[96,384]{1,0:T(8,128)(2,1)S(1)}, bf16[96,384]{1,0:T(8,128)(2,1)S(1)}, u32[]{:S(2)}, u32[]{:S(2)}) %collective-permute-start.15) | collective-permute-done | bytes 73760 | tf_op jit(solution)/shard_map/ppermute | solution.py:214
  40.0 0.4 %collective-permute-done.16.refs_5_ = bf16[96,384]{1,0:T(8,128)(2,1)S(1)} collective-permute-done((bf16[96,384]{1,0:T(8,128)(2,1)S(1)}, bf16[96,384]{1,0:T(8,128)(2,1)S(1)}, u32[]{:S(2)}, u32[]{:S(2)}) %collective-permute-start.16) | collective-permute-done | bytes 73760 | tf_op jit(solution)/shard_map/ppermute | solution.py:214
  40.4 0.9 %shard_map.91 = bf16[6,96,384]{2,1,0:T(8,128)(2,1)} custom-call(s32[1,6]{1,0:T(1,128)S(1)} %bitcast.23, bf16[2,96,384]{2,1,0:T(8,128)(2,1)S(1)} %collective-permute-done.11.after_ref.refs_0_, bf16[2,96,384]{2,1,0:T(8,128)(2,1)S(1)} %collective-permute-done.12.refs_1_, bf16[2,96,384]{2,1,0:T(8,128)(2,1)S(1)} %collective-permute-done.13.refs_2_, ...), custom_call_target="tpu_custom_call" | custom-call | tf_op jit(solution)/shard_map/pallas_call | solution.py:224
  (12 shorter events, 0.0 us)
Async XLA Ops:
  0.6 2.9 %collective-permute-start = (bf16[6,96,768]{2,1,0:T(8,128)(2,1)}, bf16[6,96,768]{2,1,0:T(8,128)(2,1)S(1)}, u32[]{:S(2)}, u32[]{:S(2)}) collective-permute-start(bf16[6,96,768]{2,1,0:T(8,128)(2,1)} %bitcast.14), channel_id=1, source_target_pairs={{0,1},{1,0},{2,3},{3,2},{4,5},{5,4},{6,7},{7,6},{8,9},{9,8},{10,11... | collective-permute-start | bytes 2654216 | tf_op jit(solution)/shard_map/ppermute | solution.py:214
  1.1 7.8 %collective-permute-start.2 = (bf16[384,768]{1,0:T(8,128)(2,1)}, bf16[384,768]{1,0:T(8,128)(2,1)S(1)}, u32[]{:S(2)}, u32[]{:S(2)}) collective-permute-start(bf16[384,768]{1,0:T(8,128)(2,1)} %bitcast.16), channel_id=1, source_target_pairs={{0,1},{1,0},{2,3},{3,2},{4,5},{5,4},{6,7},{7,6},{8,9},{9,8},{10,11... | collective-permute-start | bytes 1769480 | tf_op jit(solution)/shard_map/ppermute | solution.py:214
  1.2 7.8 %collective-permute-start.3 = (bf16[768,384]{1,0:T(8,128)(2,1)}, bf16[768,384]{1,0:T(8,128)(2,1)S(1)}, u32[]{:S(2)}, u32[]{:S(2)}) collective-permute-start(bf16[768,384]{1,0:T(8,128)(2,1)} %bitcast.18), channel_id=1, source_target_pairs={{0,1},{1,0},{2,3},{3,2},{4,5},{5,4},{6,7},{7,6},{8,9},{9,8},{10,11... | collective-permute-start | bytes 1769480 | tf_op jit(solution)/shard_map/ppermute | solution.py:214
  1.7 1.2 %copy-start = (bf16[1,6,96,768]{3,2,1,0:T(8,128)(2,1)S(1)}, bf16[1,6,96,768]{3,2,1,0:T(8,128)(2,1)}, u32[]{:S(2)}) copy-start(bf16[1,6,96,768]{3,2,1,0:T(8,128)(2,1)} %param.6) | copy-start | bytes 2654212
  2.8 0.7 %copy-start.3 = (s32[6]{0:T(128)S(1)}, s32[6]{0:T(128)}, u32[]{:S(2)}) copy-start(s32[6]{0:T(128)} %param.7) | copy-start | bytes 76
  3.5 5.5 %copy-start.1 = (bf16[1,384,768]{2,1,0:T(8,128)(2,1)S(1)}, bf16[1,384,768]{2,1,0:T(8,128)(2,1)}, u32[]{:S(2)}) copy-start(bf16[1,384,768]{2,1,0:T(8,128)(2,1)} %param.10) | copy-start | bytes 1769476
  3.5 5.5 %copy-start.2 = (bf16[1,768,384]{2,1,0:T(8,128)(2,1)S(1)}, bf16[1,768,384]{2,1,0:T(8,128)(2,1)}, u32[]{:S(2)}) copy-start(bf16[1,768,384]{2,1,0:T(8,128)(2,1)} %param.11) | copy-start | bytes 1769476
  3.9 7.2 %collective-permute-start.1 = (bf16[96,768]{1,0:T(8,128)(2,1)S(1)}, bf16[96,768]{1,0:T(8,128)(2,1)S(1)}, u32[]{:S(2)}, u32[]{:S(2)}) collective-permute-start(bf16[96,768]{1,0:T(8,128)(2,1)S(1)} %get-tuple-element.26), channel_id=1, source_target_pairs={{0,4},{1,9},{2,6},{3,11},{4,0},{5,13},{6,2},{7,15},{8,12},{9,1},{1... | collective-permute-start | bytes 442376 | tf_op jit(solution)/shard_map/ppermute | solution.py:218
  6.7 9.1 %collective-permute-start.4 = (bf16[96,768]{1,0:T(8,128)(2,1)S(1)}, bf16[96,768]{1,0:T(8,128)(2,1)S(1)}, u32[]{:S(2)}, u32[]{:S(2)}) collective-permute-start(bf16[96,768]{1,0:T(8,128)(2,1)S(1)} %get-tuple-element.33), channel_id=1, source_target_pairs={{0,2},{1,11},{2,0},{3,9},{4,6},{5,15},{6,4},{7,13},{8,10},{9,3},{1... | collective-permute-start | bytes 442376 | tf_op jit(solution)/shard_map/ppermute | solution.py:218
  8.2 8.2 %collective-permute-start.5 = (bf16[96,768]{1,0:T(8,128)(2,1)S(1)}, bf16[96,768]{1,0:T(8,128)(2,1)S(1)}, u32[]{:S(2)}, u32[]{:S(2)}) collective-permute-start(bf16[96,768]{1,0:T(8,128)(2,1)S(1)} %get-tuple-element.34), channel_id=1, source_target_pairs={{0,0},{1,15},{2,2},{3,13},{4,4},{5,11},{6,6},{7,9},{8,8},{9,7},{10... | collective-permute-start | bytes 442376 | tf_op jit(solution)/shard_map/ppermute | solution.py:218
  8.9 9.7 %collective-permute-start.6 = (bf16[96,768]{1,0:T(8,128)(2,1)S(1)}, bf16[96,768]{1,0:T(8,128)(2,1)S(1)}, u32[]{:S(2)}, u32[]{:S(2)}) collective-permute-start(bf16[96,768]{1,0:T(8,128)(2,1)S(1)} %get-tuple-element.35), channel_id=1, source_target_pairs={{0,6},{1,13},{2,4},{3,15},{4,2},{5,9},{6,0},{7,11},{8,14},{9,5},{1... | collective-permute-start | bytes 442376 | tf_op jit(solution)/shard_map/ppermute | solution.py:218
  11.0 8.8 %collective-permute-start.7 = (bf16[96,768]{1,0:T(8,128)(2,1)S(1)}, bf16[96,768]{1,0:T(8,128)(2,1)S(1)}, u32[]{:S(2)}, u32[]{:S(2)}) collective-permute-start(bf16[96,768]{1,0:T(8,128)(2,1)S(1)} %collective-permute-done.1.refs_0_), channel_id=1, source_target_pairs={{0,1},{1,0},{2,3},{3,2},{4,5},{5,4},{6,7},{7,6},{8,9},{9,8},{10,11... | collective-permute-start | bytes 442376 | tf_op jit(solution)/shard_map/ppermute | solution.py:214
  15.9 4.0 %collective-permute-start.8 = (bf16[96,768]{1,0:T(8,128)(2,1)S(1)}, bf16[96,768]{1,0:T(8,128)(2,1)S(1)}, u32[]{:S(2)}, u32[]{:S(2)}) collective-permute-start(bf16[96,768]{1,0:T(8,128)(2,1)S(1)} %collective-permute-done.4.refs_1_), channel_id=1, source_target_pairs={{0,1},{1,0},{2,3},{3,2},{4,5},{5,4},{6,7},{7,6},{8,9},{9,8},{10,11... | collective-permute-start | bytes 442376 | tf_op jit(solution)/shard_map/ppermute | solution.py:214
  16.4 4.5 %collective-permute-start.10 = (bf16[96,768]{1,0:T(8,128)(2,1)S(1)}, bf16[96,768]{1,0:T(8,128)(2,1)S(1)}, u32[]{:S(2)}, u32[]{:S(2)}) collective-permute-start(bf16[96,768]{1,0:T(8,128)(2,1)S(1)} %collective-permute-done.5.refs_2_), channel_id=1, source_target_pairs={{0,1},{1,0},{2,3},{3,2},{4,5},{5,4},{6,7},{7,6},{8,9},{9,8},{10,11... | collective-permute-start | bytes 442376 | tf_op jit(solution)/shard_map/ppermute | solution.py:214
  18.6 2.4 %collective-permute-start.9 = (bf16[96,768]{1,0:T(8,128)(2,1)S(1)}, bf16[96,768]{1,0:T(8,128)(2,1)S(1)}, u32[]{:S(2)}, u32[]{:S(2)}) collective-permute-start(bf16[96,768]{1,0:T(8,128)(2,1)S(1)} %collective-permute-done.6.refs_3_), channel_id=1, source_target_pairs={{0,1},{1,0},{2,3},{3,2},{4,5},{5,4},{6,7},{7,6},{8,9},{9,8},{10,11... | collective-permute-start | bytes 442376 | tf_op jit(solution)/shard_map/ppermute | solution.py:214
  20.9 9.9 %copy-start.4 = (s32[6]{0:T(128)S(1)}, s32[6]{0:T(128)}, u32[]{:S(2)}) copy-start(s32[6]{0:T(128)} %param.7) | copy-start | bytes 76
  20.9 9.9 %copy-start.5 = (bf16[1,384,768]{2,1,0:T(8,128)(2,1)S(1)}, bf16[1,384,768]{2,1,0:T(8,128)(2,1)}, u32[]{:S(2)}) copy-start(bf16[1,384,768]{2,1,0:T(8,128)(2,1)} %param.8) | copy-start | bytes 1769476
  20.9 9.9 %copy-start.6 = (bf16[1,384,768]{2,1,0:T(8,128)(2,1)S(1)}, bf16[1,384,768]{2,1,0:T(8,128)(2,1)}, u32[]{:S(2)}) copy-start(bf16[1,384,768]{2,1,0:T(8,128)(2,1)} %param.9) | copy-start | bytes 1769476
  22.6 8.2 %collective-permute-start.11 = (bf16[2,96,384]{2,1,0:T(8,128)(2,1)S(1)}, bf16[2,96,384]{2,1,0:T(8,128)(2,1)S(1)}, u32[]{:S(2)}, u32[]{:S(2)}) collective-permute-start(bf16[2,96,384]{2,1,0:T(8,128)(2,1)S(1)} %get-tuple-element.39), channel_id=1, source_target_pairs={{0,4},{1,9},{2,6},{3,11},{4,0},{5,13},{6,2},{7,15},{8,12},{9,1},{1... | collective-permute-start | bytes 442376 | tf_op jit(solution)/shard_map/ppermute | solution.py:218
  25.3 9.0 %collective-permute-start.12 = (bf16[2,96,384]{2,1,0:T(8,128)(2,1)S(1)}, bf16[2,96,384]{2,1,0:T(8,128)(2,1)S(1)}, u32[]{:S(2)}, u32[]{:S(2)}) collective-permute-start(bf16[2,96,384]{2,1,0:T(8,128)(2,1)S(1)} %get-tuple-element.45), channel_id=1, source_target_pairs={{0,6},{1,11},{2,4},{3,9},{4,2},{5,15},{6,0},{7,13},{8,14},{9,3},{1... | collective-permute-start | bytes 442376 | tf_op jit(solution)/shard_map/ppermute | solution.py:218
  26.3 12.8 %collective-permute-start.13 = (bf16[2,96,384]{2,1,0:T(8,128)(2,1)S(1)}, bf16[2,96,384]{2,1,0:T(8,128)(2,1)S(1)}, u32[]{:S(2)}, u32[]{:S(2)}) collective-permute-start(bf16[2,96,384]{2,1,0:T(8,128)(2,1)S(1)} %get-tuple-element.46), channel_id=1, source_target_pairs={{0,2},{1,13},{2,0},{3,15},{4,6},{5,9},{6,4},{7,11},{8,10},{9,5},{1... | collective-permute-start | bytes 442376 | tf_op jit(solution)/shard_map/ppermute | solution.py:218
  26.8 12.3 %collective-permute-start.17 = (bf16[96,384]{1,0:T(8,128)(2,1)S(1)}, bf16[96,384]{1,0:T(8,128)(2,1)S(1)}, u32[]{:S(2)}, u32[]{:S(2)}) collective-permute-start(bf16[96,384]{1,0:T(8,128)(2,1)S(1)} %get-tuple-element.48), channel_id=1, source_target_pairs={{0,14},{1,15},{2,12},{3,13},{4,10},{5,11},{6,8},{7,9},{8,6},{9,7},... | collective-permute-start | bytes 221192 | tf_op jit(solution)/shard_map/ppermute | solution.py:218
  33.0 6.2 %collective-permute-start.14 = (bf16[96,384]{1,0:T(8,128)(2,1)S(1)}, bf16[96,384]{1,0:T(8,128)(2,1)S(1)}, u32[]{:S(2)}, u32[]{:S(2)}) collective-permute-start(bf16[96,384]{1,0:T(8,128)(2,1)S(1)} %slice_bitcast_fusion.2), channel_id=1, source_target_pairs={{0,1},{1,0},{2,3},{3,2},{4,5},{5,4},{6,7},{7,6},{8,9},{9,8},{10,11... | collective-permute-start | bytes 221192 | tf_op jit(solution)/shard_map/ppermute | solution.py:214
  34.3 5.7 %collective-permute-start.15 = (bf16[96,384]{1,0:T(8,128)(2,1)S(1)}, bf16[96,384]{1,0:T(8,128)(2,1)S(1)}, u32[]{:S(2)}, u32[]{:S(2)}) collective-permute-start(bf16[96,384]{1,0:T(8,128)(2,1)S(1)} %slice_bitcast_fusion.1), channel_id=1, source_target_pairs={{0,1},{1,0},{2,3},{3,2},{4,5},{5,4},{6,7},{7,6},{8,9},{9,8},{10,11... | collective-permute-start | bytes 221192 | tf_op jit(solution)/shard_map/ppermute | solution.py:214
  39.1 1.3 %collective-permute-start.16 = (bf16[96,384]{1,0:T(8,128)(2,1)S(1)}, bf16[96,384]{1,0:T(8,128)(2,1)S(1)}, u32[]{:S(2)}, u32[]{:S(2)}) collective-permute-start(bf16[96,384]{1,0:T(8,128)(2,1)S(1)} %slice_bitcast_fusion), channel_id=1, source_target_pairs={{0,1},{1,0},{2,3},{3,2},{4,5},{5,4},{6,7},{7,6},{8,9},{9,8},{10,11... | collective-permute-start | bytes 221192 | tf_op jit(solution)/shard_map/ppermute | solution.py:214

commit v16 on v12

--- a/solution.py
+++ b/solution.py
@@ -11,8 +11,8 @@
 ANY = pl.BlockSpec(memory_space=pl.ANY)
 LIGHT = pl.CostEstimate(flops=0, bytes_accessed=0, transcendentals=0)
 OUT = ((2, 6), (1, 5), (0, 4), (3, 7))
-BACK = ((2, 4), (3, 5), (1, 7))
-SHARED, SELF = (6, 6), (0, 0)
+BACK = ((2, 4), (3, 5), (1, 6))
+SHARED, SELF = (7, 7), (0, 0)
 PARAMS = pltpu.CompilerParams(vmem_limit_bytes=24 * 1024 * 1024)
 
 

time: 40.5 us -> 40.1 us (level)
  the two profiles are of different devices: /device:TPU:21 before, /device:TPU:0 now
where the time goes in v16:
time: 40.1 us; the launch traced here: 39.9 us
  starting transfers between devices  26.6 us (66%)
  Pallas kernels  7.81 us (19%)
  waiting for transfers between devices  2.83 us (7%)
  local copies, waits for them, and re-layouts  1.87 us (5%)
  between operations  0.77 us (2%)
    ppermute x10, starting transfers between devices, other_core(): return lax.ppermute(x, 'replica', [(0, 1), (1, 0)])  14.6 us
    ppermute x8, starting transfers between devices, trade(): return lax.ppermute(x, ('shard', 'replica'), pairs)  12.1 us
    pallas_call x7, Pallas kernels, call(): pl.pallas_call(kernel, out_shape=out_shape, in_specs=in_specs, compiler_p...  7.81 us
    ppermute x8, waiting for transfers between devices, trade(): return lax.ppermute(x, ('shard', 'replica'), pairs)  2.8 us
    unnamed x14, local copies, waits for them, and re-layouts  1.85 us
  transfers between devices with their start and end apart: 18, of which 3 were waited for; matrix products, arithmetic and copies ran while one was open for 0% of the time, Pallas kernels for 13%

profile of v16, /device:TPU:0, one launch (start us, length us, event | category | flops | bytes accessed | tf_op | source)
XLA Modules:
  0.0 39.9 jit_solution(8731855625124373237)
XLA Ops:
  0.6 0.5 %collective-permute-start = (bf16[6,96,768]{2,1,0:T(8,128)(2,1)}, bf16[6,96,768]{2,1,0:T(8,128)(2,1)S(1)}, u32[]{:S(2)}, u32[]{:S(2)}) collective-permute-start(bf16[6,96,768]{2,1,0:T(8,128)(2,1)} %bitcast.14), channel_id=1, source_target_pairs={{0,1},{1,0},{2,3},{3,2},{4,5},{5,4},{6,7},{7,6},{8,9},{9,8},{10,11... | collective-permute-start | bytes 2654216 | tf_op jit(solution)/shard_map/ppermute | solution.py:214
  1.1 0.1 collective-permute-start.2
  1.2 0.4 %collective-permute-start.3 = (bf16[768,384]{1,0:T(8,128)(2,1)}, bf16[768,384]{1,0:T(8,128)(2,1)S(1)}, u32[]{:S(2)}, u32[]{:S(2)}) collective-permute-start(bf16[768,384]{1,0:T(8,128)(2,1)} %bitcast.18), channel_id=1, source_target_pairs={{0,1},{1,0},{2,3},{3,2},{4,5},{5,4},{6,7},{7,6},{8,9},{9,8},{10,11... | collective-permute-start | bytes 1769480 | tf_op jit(solution)/shard_map/ppermute | solution.py:214
  1.7 1.2 %copy-done = bf16[1,6,96,768]{3,2,1,0:T(8,128)(2,1)S(1)} copy-done((bf16[1,6,96,768]{3,2,1,0:T(8,128)(2,1)S(1)}, bf16[1,6,96,768]{3,2,1,0:T(8,128)(2,1)}, u32[]{:S(2)}) %copy-start) | copy-done | bytes 884760
  2.8 0.7 %copy-done.3 = s32[6]{0:T(128)S(1)} copy-done((s32[6]{0:T(128)S(1)}, s32[6]{0:T(128)}, u32[]{:S(2)}) %copy-start.3) | copy-done | bytes 48
  3.5 0.1 shard_map.85.mine_ref
  3.5 0.0 collective-permute-done.theirs_ref
  3.6 0.3 shard_map.86
  3.9 2.9 %collective-permute-start.1 = (bf16[96,768]{1,0:T(8,128)(2,1)S(1)}, bf16[96,768]{1,0:T(8,128)(2,1)S(1)}, u32[]{:S(2)}, u32[]{:S(2)}) collective-permute-start(bf16[96,768]{1,0:T(8,128)(2,1)S(1)} %get-tuple-element.27), channel_id=1, source_target_pairs={{0,4},{1,13},{2,6},{3,15},{4,0},{5,9},{6,2},{7,11},{8,12},{9,5},{1... | collective-permute-start | bytes 442376 | tf_op jit(solution)/shard_map/ppermute | solution.py:218
  6.7 1.5 %collective-permute-start.4 = (bf16[96,768]{1,0:T(8,128)(2,1)S(1)}, bf16[96,768]{1,0:T(8,128)(2,1)S(1)}, u32[]{:S(2)}, u32[]{:S(2)}) collective-permute-start(bf16[96,768]{1,0:T(8,128)(2,1)S(1)} %get-tuple-element.34), channel_id=1, source_target_pairs={{0,2},{1,11},{2,0},{3,9},{4,6},{5,15},{6,4},{7,13},{8,10},{9,3},{1... | collective-permute-start | bytes 442376 | tf_op jit(solution)/shard_map/ppermute | solution.py:218
  8.2 0.7 %collective-permute-start.5 = (bf16[96,768]{1,0:T(8,128)(2,1)S(1)}, bf16[96,768]{1,0:T(8,128)(2,1)S(1)}, u32[]{:S(2)}, u32[]{:S(2)}) collective-permute-start(bf16[96,768]{1,0:T(8,128)(2,1)S(1)} %get-tuple-element.35), channel_id=1, source_target_pairs={{0,0},{1,9},{2,2},{3,11},{4,4},{5,13},{6,6},{7,15},{8,8},{9,1},{10... | collective-permute-start | bytes 442376 | tf_op jit(solution)/shard_map/ppermute | solution.py:218
  8.9 0.0 collective-permute-done.2.other_ref
  8.9 0.1 collective-permute-start.6
  9.0 0.0 collective-permute-done.3.other_right_ref
  9.0 1.7 %shard_map.87 = (bf16[768,576]{1,0:T(8,128)(2,1)S(1)}, bf16[768,192]{1,0:T(8,128)(2,1)S(1)}, bf16[768,768]{1,0:T(8,128)(2,1)S(1)}) custom-call(bf16[384,768]{1,0:T(8,128)(2,1)S(1)} %bitcast.17, bf16[384,768]{1,0:T(8,128)(2,1)S(1)} %collective-permute-done.2.other_ref, bf16[768,384]{1,0:T(8,128)(2,1)S(1)} %bitcast.19, ...), custom_call_target="tpu_custom_call" | custom-call | tf_op jit(solution)/shard_map/pallas_call | solution.py:224
  10.8 0.0 collective-permute-done.1.refs_0_
  10.8 5.1 %collective-permute-start.7 = (bf16[96,768]{1,0:T(8,128)(2,1)S(1)}, bf16[96,768]{1,0:T(8,128)(2,1)S(1)}, u32[]{:S(2)}, u32[]{:S(2)}) collective-permute-start(bf16[96,768]{1,0:T(8,128)(2,1)S(1)} %collective-permute-done.1.refs_0_), channel_id=1, source_target_pairs={{0,1},{1,0},{2,3},{3,2},{4,5},{5,4},{6,7},{7,6},{8,9},{9,8},{10,11... | collective-permute-start | bytes 442376 | tf_op jit(solution)/shard_map/ppermute | solution.py:214
  15.9 0.0 collective-permute-done.4.refs_1_
  15.9 0.9 %collective-permute-start.8 = (bf16[96,768]{1,0:T(8,128)(2,1)S(1)}, bf16[96,768]{1,0:T(8,128)(2,1)S(1)}, u32[]{:S(2)}, u32[]{:S(2)}) collective-permute-start(bf16[96,768]{1,0:T(8,128)(2,1)S(1)} %collective-permute-done.4.refs_1_), channel_id=1, source_target_pairs={{0,1},{1,0},{2,3},{3,2},{4,5},{5,4},{6,7},{7,6},{8,9},{9,8},{10,11... | collective-permute-start | bytes 442376 | tf_op jit(solution)/shard_map/ppermute | solution.py:214
  16.8 0.0 collective-permute-done.5.refs_2_
  16.9 3.6 %collective-permute-start.10 = (bf16[96,768]{1,0:T(8,128)(2,1)S(1)}, bf16[96,768]{1,0:T(8,128)(2,1)S(1)}, u32[]{:S(2)}, u32[]{:S(2)}) collective-permute-start(bf16[96,768]{1,0:T(8,128)(2,1)S(1)} %collective-permute-done.5.refs_2_), channel_id=1, source_target_pairs={{0,1},{1,0},{2,3},{3,2},{4,5},{5,4},{6,7},{7,6},{8,9},{9,8},{10,11... | collective-permute-start | bytes 442376 | tf_op jit(solution)/shard_map/ppermute | solution.py:214
  20.4 0.0 collective-permute-done.6.refs_3_
  20.4 0.4 collective-permute-start.9
  20.8 0.0 collective-permute-done.7.refs_4_
  20.8 0.0 collective-permute-done.8.refs_5_
  20.8 1.1 %shard_map.88 = (f32[768,768]{1,0:T(8,128)S(1)}, f32[8,128]{1,0:T(8,128)S(1)}) custom-call(bf16[768,576]{1,0:T(8,128)(2,1)S(1)} %get-tuple-element.32.left_ref, bf16[96,768]{1,0:T(8,128)(2,1)S(1)} %collective-permute-done.1.refs_0_, bf16[96,768]{1,0:T(8,128)(2,1)S(1)} %collective-permute-done.4.refs_1_, bf16[96,768]{1,0:T(8,128)(2,1)S(1)} %collective-permute-done.5.refs_2_, ...), custom_call_target="tpu_custom_call" | custom-call | tf_op jit(solution)/shard_map/pallas_call | solution.py:224
  21.9 0.0 copy-start.4
  22.0 0.0 copy-start.5
  22.0 0.0 copy-start.6
  22.0 0.0 collective-permute-done.10.refs_1_.refs_6_
  22.0 0.0 collective-permute-done.9.refs_0_.refs_7_
  22.0 1.6 %shard_map.89 = (bf16[2,96,384]{2,1,0:T(8,128)(2,1)S(1)}, bf16[2,96,384]{2,1,0:T(8,128)(2,1)S(1)}, bf16[2,96,384]{2,1,0:T(8,128)(2,1)S(1)}, bf16[96,384]{1,0:T(8,128)(2,1)S(1)}, bf16[96,384]{1,0:T(8,128)(2,1)S(1)}) custom-call(bf16[768,192]{1,0:T(8,128)(2,1)S(1)} %get-tuple-element.31.left_ref, f32[768,768]{1,0:T(8,128)S(1)} %get-tuple-element.37.total_ref, ...), custom_call_target="tpu_custom_call" | custom-call | tf_op jit(solution)/shard_map/pallas_call | solution.py:224
  23.6 2.3 %collective-permute-start.11 = (bf16[2,96,384]{2,1,0:T(8,128)(2,1)S(1)}, bf16[2,96,384]{2,1,0:T(8,128)(2,1)S(1)}, u32[]{:S(2)}, u32[]{:S(2)}) collective-permute-start(bf16[2,96,384]{2,1,0:T(8,128)(2,1)S(1)} %get-tuple-element.44), channel_id=1, source_target_pairs={{0,4},{1,9},{2,6},{3,11},{4,0},{5,13},{6,2},{7,15},{8,12},{9,1},{1... | collective-permute-start | bytes 442376 | tf_op jit(solution)/shard_map/ppermute | solution.py:218
  25.9 0.5 %collective-permute-start.12 = (bf16[2,96,384]{2,1,0:T(8,128)(2,1)S(1)}, bf16[2,96,384]{2,1,0:T(8,128)(2,1)S(1)}, u32[]{:S(2)}, u32[]{:S(2)}) collective-permute-start(bf16[2,96,384]{2,1,0:T(8,128)(2,1)S(1)} %get-tuple-element.48), channel_id=1, source_target_pairs={{0,6},{1,11},{2,4},{3,9},{4,2},{5,15},{6,0},{7,13},{8,14},{9,3},{1... | collective-permute-start | bytes 442376 | tf_op jit(solution)/shard_map/ppermute | solution.py:218
  26.4 1.0 %collective-permute-start.13 = (bf16[2,96,384]{2,1,0:T(8,128)(2,1)S(1)}, bf16[2,96,384]{2,1,0:T(8,128)(2,1)S(1)}, u32[]{:S(2)}, u32[]{:S(2)}) collective-permute-start(bf16[2,96,384]{2,1,0:T(8,128)(2,1)S(1)} %get-tuple-element.49), channel_id=1, source_target_pairs={{0,2},{1,13},{2,0},{3,15},{4,6},{5,9},{6,4},{7,11},{8,10},{9,5},{1... | collective-permute-start | bytes 442376 | tf_op jit(solution)/shard_map/ppermute | solution.py:218
  27.4 2.1 %shard_map.90 = (bf16[384,768]{1,0:T(8,128)(2,1)}, bf16[384,768]{1,0:T(8,128)(2,1)}) custom-call(s32[1,6]{1,0:T(1,128)S(1)} %bitcast.22, bf16[384,768]{1,0:T(8,128)(2,1)S(1)} %bitcast.24, bf16[384,768]{1,0:T(8,128)(2,1)S(1)} %bitcast.25, bf16[96,384]{1,0:T(8,128)(2,1)S(1)} %get-tuple-element.40.after_ref.refs_6_, ...), custom_call_target="tpu_custom_call" | custom-call | flops 905969664 | bytes 2359296 | tf_op jit(solution)/shard_map/pallas_call | solution.py:224
  29.5 0.6 %collective-permute-done.11.refs_0_ = bf16[2,96,384]{2,1,0:T(8,128)(2,1)S(1)} collective-permute-done((bf16[2,96,384]{2,1,0:T(8,128)(2,1)S(1)}, bf16[2,96,384]{2,1,0:T(8,128)(2,1)S(1)}, u32[]{:S(2)}, u32[]{:S(2)}) %collective-permute-start.11) | collective-permute-done | bytes 147488 | tf_op jit(solution)/shard_map/ppermute | solution.py:218
  30.1 1.2 %collective-permute-start.14 = (bf16[96,384]{1,0:T(8,128)(2,1)S(1)}, bf16[96,384]{1,0:T(8,128)(2,1)S(1)}, u32[]{:S(2)}, u32[]{:S(2)}) collective-permute-start(bf16[96,384]{1,0:T(8,128)(2,1)S(1)} %slice_bitcast_fusion.2), channel_id=1, source_target_pairs={{0,1},{1,0},{2,3},{3,2},{4,5},{5,4},{6,7},{7,6},{8,9},{9,8},{10,11... | collective-permute-start | bytes 221192 | tf_op jit(solution)/shard_map/ppermute | solution.py:214
  31.3 3.1 %collective-permute-start.17 = (bf16[96,384]{1,0:T(8,128)(2,1)S(1)}, bf16[96,384]{1,0:T(8,128)(2,1)S(1)}, u32[]{:S(2)}, u32[]{:S(2)}) collective-permute-start(bf16[96,384]{1,0:T(8,128)(2,1)S(1)} %get-tuple-element.50), channel_id=1, source_target_pairs={{0,14},{1,15},{2,12},{3,13},{4,10},{5,11},{6,8},{7,9},{8,6},{9,7},... | collective-permute-start | bytes 221192 | tf_op jit(solution)/shard_map/ppermute | solution.py:218
  34.4 0.0 collective-permute-done.12.refs_1_
  34.4 0.2 collective-permute-start.15
  34.6 0.1 collective-permute-done.13.refs_2_
  34.7 2.1 %collective-permute-start.16 = (bf16[96,384]{1,0:T(8,128)(2,1)S(1)}, bf16[96,384]{1,0:T(8,128)(2,1)S(1)}, u32[]{:S(2)}, u32[]{:S(2)}) collective-permute-start(bf16[96,384]{1,0:T(8,128)(2,1)S(1)} %slice_bitcast_fusion), channel_id=1, source_target_pairs={{0,1},{1,0},{2,3},{3,2},{4,5},{5,4},{6,7},{7,6},{8,9},{9,8},{10,11... | collective-permute-start | bytes 221192 | tf_op jit(solution)/shard_map/ppermute | solution.py:214
  36.8 0.0 collective-permute-done.14.refs_3_
  36.8 2.1 %collective-permute-done.17.refs_7_ = bf16[96,384]{1,0:T(8,128)(2,1)S(1)} collective-permute-done((bf16[96,384]{1,0:T(8,128)(2,1)S(1)}, bf16[96,384]{1,0:T(8,128)(2,1)S(1)}, u32[]{:S(2)}, u32[]{:S(2)}) %collective-permute-start.17) | collective-permute-done | bytes 73760 | tf_op jit(solution)/shard_map/ppermute | solution.py:218
  38.9 0.0 collective-permute-done.15.refs_4_
  39.0 0.0 collective-permute-done.16.refs_5_
  39.0 0.9 %shard_map.91 = bf16[6,96,384]{2,1,0:T(8,128)(2,1)} custom-call(s32[1,6]{1,0:T(1,128)S(1)} %bitcast.23, bf16[2,96,384]{2,1,0:T(8,128)(2,1)S(1)} %collective-permute-done.11.refs_0_, bf16[2,96,384]{2,1,0:T(8,128)(2,1)S(1)} %collective-permute-done.12.refs_1_, bf16[2,96,384]{2,1,0:T(8,128)(2,1)S(1)} %collective-permute-done.13.refs_2_, ...), custom_call_target="tpu_custom_call" | custom-call | tf_op jit(solution)/shard_map/pallas_call | solution.py:224
  (12 shorter events, 0.0 us)
Async XLA Ops:
  0.6 2.9 %collective-permute-start = (bf16[6,96,768]{2,1,0:T(8,128)(2,1)}, bf16[6,96,768]{2,1,0:T(8,128)(2,1)S(1)}, u32[]{:S(2)}, u32[]{:S(2)}) collective-permute-start(bf16[6,96,768]{2,1,0:T(8,128)(2,1)} %bitcast.14), channel_id=1, source_target_pairs={{0,1},{1,0},{2,3},{3,2},{4,5},{5,4},{6,7},{7,6},{8,9},{9,8},{10,11... | collective-permute-start | bytes 2654216 | tf_op jit(solution)/shard_map/ppermute | solution.py:214
  1.1 7.8 %collective-permute-start.2 = (bf16[384,768]{1,0:T(8,128)(2,1)}, bf16[384,768]{1,0:T(8,128)(2,1)S(1)}, u32[]{:S(2)}, u32[]{:S(2)}) collective-permute-start(bf16[384,768]{1,0:T(8,128)(2,1)} %bitcast.16), channel_id=1, source_target_pairs={{0,1},{1,0},{2,3},{3,2},{4,5},{5,4},{6,7},{7,6},{8,9},{9,8},{10,11... | collective-permute-start | bytes 1769480 | tf_op jit(solution)/shard_map/ppermute | solution.py:214
  1.2 7.8 %collective-permute-start.3 = (bf16[768,384]{1,0:T(8,128)(2,1)}, bf16[768,384]{1,0:T(8,128)(2,1)S(1)}, u32[]{:S(2)}, u32[]{:S(2)}) collective-permute-start(bf16[768,384]{1,0:T(8,128)(2,1)} %bitcast.18), channel_id=1, source_target_pairs={{0,1},{1,0},{2,3},{3,2},{4,5},{5,4},{6,7},{7,6},{8,9},{9,8},{10,11... | collective-permute-start | bytes 1769480 | tf_op jit(solution)/shard_map/ppermute | solution.py:214
  1.7 1.2 %copy-start = (bf16[1,6,96,768]{3,2,1,0:T(8,128)(2,1)S(1)}, bf16[1,6,96,768]{3,2,1,0:T(8,128)(2,1)}, u32[]{:S(2)}) copy-start(bf16[1,6,96,768]{3,2,1,0:T(8,128)(2,1)} %param.6) | copy-start | bytes 2654212
  2.8 0.7 %copy-start.3 = (s32[6]{0:T(128)S(1)}, s32[6]{0:T(128)}, u32[]{:S(2)}) copy-start(s32[6]{0:T(128)} %param.7) | copy-start | bytes 76
  3.5 5.5 %copy-start.1 = (bf16[1,384,768]{2,1,0:T(8,128)(2,1)S(1)}, bf16[1,384,768]{2,1,0:T(8,128)(2,1)}, u32[]{:S(2)}) copy-start(bf16[1,384,768]{2,1,0:T(8,128)(2,1)} %param.10) | copy-start | bytes 1769476
  3.5 5.5 %copy-start.2 = (bf16[1,768,384]{2,1,0:T(8,128)(2,1)S(1)}, bf16[1,768,384]{2,1,0:T(8,128)(2,1)}, u32[]{:S(2)}) copy-start(bf16[1,768,384]{2,1,0:T(8,128)(2,1)} %param.11) | copy-start | bytes 1769476
  3.9 6.9 %collective-permute-start.1 = (bf16[96,768]{1,0:T(8,128)(2,1)S(1)}, bf16[96,768]{1,0:T(8,128)(2,1)S(1)}, u32[]{:S(2)}, u32[]{:S(2)}) collective-permute-start(bf16[96,768]{1,0:T(8,128)(2,1)S(1)} %get-tuple-element.27), channel_id=1, source_target_pairs={{0,4},{1,13},{2,6},{3,15},{4,0},{5,9},{6,2},{7,11},{8,12},{9,5},{1... | collective-permute-start | bytes 442376 | tf_op jit(solution)/shard_map/ppermute | solution.py:218
  6.7 9.2 %collective-permute-start.4 = (bf16[96,768]{1,0:T(8,128)(2,1)S(1)}, bf16[96,768]{1,0:T(8,128)(2,1)S(1)}, u32[]{:S(2)}, u32[]{:S(2)}) collective-permute-start(bf16[96,768]{1,0:T(8,128)(2,1)S(1)} %get-tuple-element.34), channel_id=1, source_target_pairs={{0,2},{1,11},{2,0},{3,9},{4,6},{5,15},{6,4},{7,13},{8,10},{9,3},{1... | collective-permute-start | bytes 442376 | tf_op jit(solution)/shard_map/ppermute | solution.py:218
  8.2 8.6 %collective-permute-start.5 = (bf16[96,768]{1,0:T(8,128)(2,1)S(1)}, bf16[96,768]{1,0:T(8,128)(2,1)S(1)}, u32[]{:S(2)}, u32[]{:S(2)}) collective-permute-start(bf16[96,768]{1,0:T(8,128)(2,1)S(1)} %get-tuple-element.35), channel_id=1, source_target_pairs={{0,0},{1,9},{2,2},{3,11},{4,4},{5,13},{6,6},{7,15},{8,8},{9,1},{10... | collective-permute-start | bytes 442376 | tf_op jit(solution)/shard_map/ppermute | solution.py:218
  8.9 11.5 %collective-permute-start.6 = (bf16[96,768]{1,0:T(8,128)(2,1)S(1)}, bf16[96,768]{1,0:T(8,128)(2,1)S(1)}, u32[]{:S(2)}, u32[]{:S(2)}) collective-permute-start(bf16[96,768]{1,0:T(8,128)(2,1)S(1)} %get-tuple-element.36), channel_id=1, source_target_pairs={{0,6},{1,15},{2,4},{3,13},{4,2},{5,11},{6,0},{7,9},{8,14},{9,7},{1... | collective-permute-start | bytes 442376 | tf_op jit(solution)/shard_map/ppermute | solution.py:218
  10.8 10.1 %collective-permute-start.7 = (bf16[96,768]{1,0:T(8,128)(2,1)S(1)}, bf16[96,768]{1,0:T(8,128)(2,1)S(1)}, u32[]{:S(2)}, u32[]{:S(2)}) collective-permute-start(bf16[96,768]{1,0:T(8,128)(2,1)S(1)} %collective-permute-done.1.refs_0_), channel_id=1, source_target_pairs={{0,1},{1,0},{2,3},{3,2},{4,5},{5,4},{6,7},{7,6},{8,9},{9,8},{10,11... | collective-permute-start | bytes 442376 | tf_op jit(solution)/shard_map/ppermute | solution.py:214
  15.9 4.9 %collective-permute-start.8 = (bf16[96,768]{1,0:T(8,128)(2,1)S(1)}, bf16[96,768]{1,0:T(8,128)(2,1)S(1)}, u32[]{:S(2)}, u32[]{:S(2)}) collective-permute-start(bf16[96,768]{1,0:T(8,128)(2,1)S(1)} %collective-permute-done.4.refs_1_), channel_id=1, source_target_pairs={{0,1},{1,0},{2,3},{3,2},{4,5},{5,4},{6,7},{7,6},{8,9},{9,8},{10,11... | collective-permute-start | bytes 442376 | tf_op jit(solution)/shard_map/ppermute | solution.py:214
  16.9 5.1 %collective-permute-start.10 = (bf16[96,768]{1,0:T(8,128)(2,1)S(1)}, bf16[96,768]{1,0:T(8,128)(2,1)S(1)}, u32[]{:S(2)}, u32[]{:S(2)}) collective-permute-start(bf16[96,768]{1,0:T(8,128)(2,1)S(1)} %collective-permute-done.5.refs_2_), channel_id=1, source_target_pairs={{0,1},{1,0},{2,3},{3,2},{4,5},{5,4},{6,7},{7,6},{8,9},{9,8},{10,11... | collective-permute-start | bytes 442376 | tf_op jit(solution)/shard_map/ppermute | solution.py:214
  20.4 1.5 %collective-permute-start.9 = (bf16[96,768]{1,0:T(8,128)(2,1)S(1)}, bf16[96,768]{1,0:T(8,128)(2,1)S(1)}, u32[]{:S(2)}, u32[]{:S(2)}) collective-permute-start(bf16[96,768]{1,0:T(8,128)(2,1)S(1)} %collective-permute-done.6.refs_3_), channel_id=1, source_target_pairs={{0,1},{1,0},{2,3},{3,2},{4,5},{5,4},{6,7},{7,6},{8,9},{9,8},{10,11... | collective-permute-start | bytes 442376 | tf_op jit(solution)/shard_map/ppermute | solution.py:214
  21.9 5.5 %copy-start.4 = (s32[6]{0:T(128)S(1)}, s32[6]{0:T(128)}, u32[]{:S(2)}) copy-start(s32[6]{0:T(128)} %param.7) | copy-start | bytes 76
  22.0 5.5 %copy-start.5 = (bf16[1,384,768]{2,1,0:T(8,128)(2,1)S(1)}, bf16[1,384,768]{2,1,0:T(8,128)(2,1)}, u32[]{:S(2)}) copy-start(bf16[1,384,768]{2,1,0:T(8,128)(2,1)} %param.8) | copy-start | bytes 1769476
  22.0 5.5 %copy-start.6 = (bf16[1,384,768]{2,1,0:T(8,128)(2,1)S(1)}, bf16[1,384,768]{2,1,0:T(8,128)(2,1)}, u32[]{:S(2)}) copy-start(bf16[1,384,768]{2,1,0:T(8,128)(2,1)} %param.9) | copy-start | bytes 1769476
  23.6 6.5 %collective-permute-start.11 = (bf16[2,96,384]{2,1,0:T(8,128)(2,1)S(1)}, bf16[2,96,384]{2,1,0:T(8,128)(2,1)S(1)}, u32[]{:S(2)}, u32[]{:S(2)}) collective-permute-start(bf16[2,96,384]{2,1,0:T(8,128)(2,1)S(1)} %get-tuple-element.44), channel_id=1, source_target_pairs={{0,4},{1,9},{2,6},{3,11},{4,0},{5,13},{6,2},{7,15},{8,12},{9,1},{1... | collective-permute-start | bytes 442376 | tf_op jit(solution)/shard_map/ppermute | solution.py:218
  25.9 8.5 %collective-permute-start.12 = (bf16[2,96,384]{2,1,0:T(8,128)(2,1)S(1)}, bf16[2,96,384]{2,1,0:T(8,128)(2,1)S(1)}, u32[]{:S(2)}, u32[]{:S(2)}) collective-permute-start(bf16[2,96,384]{2,1,0:T(8,128)(2,1)S(1)} %get-tuple-element.48), channel_id=1, source_target_pairs={{0,6},{1,11},{2,4},{3,9},{4,2},{5,15},{6,0},{7,13},{8,14},{9,3},{1... | collective-permute-start | bytes 442376 | tf_op jit(solution)/shard_map/ppermute | solution.py:218
  26.4 8.3 %collective-permute-start.13 = (bf16[2,96,384]{2,1,0:T(8,128)(2,1)S(1)}, bf16[2,96,384]{2,1,0:T(8,128)(2,1)S(1)}, u32[]{:S(2)}, u32[]{:S(2)}) collective-permute-start(bf16[2,96,384]{2,1,0:T(8,128)(2,1)S(1)} %get-tuple-element.49), channel_id=1, source_target_pairs={{0,2},{1,13},{2,0},{3,15},{4,6},{5,9},{6,4},{7,11},{8,10},{9,5},{1... | collective-permute-start | bytes 442376 | tf_op jit(solution)/shard_map/ppermute | solution.py:218
  30.1 6.7 %collective-permute-start.14 = (bf16[96,384]{1,0:T(8,128)(2,1)S(1)}, bf16[96,384]{1,0:T(8,128)(2,1)S(1)}, u32[]{:S(2)}, u32[]{:S(2)}) collective-permute-start(bf16[96,384]{1,0:T(8,128)(2,1)S(1)} %slice_bitcast_fusion.2), channel_id=1, source_target_pairs={{0,1},{1,0},{2,3},{3,2},{4,5},{5,4},{6,7},{7,6},{8,9},{9,8},{10,11... | collective-permute-start | bytes 221192 | tf_op jit(solution)/shard_map/ppermute | solution.py:214
  31.3 7.7 %collective-permute-start.17 = (bf16[96,384]{1,0:T(8,128)(2,1)S(1)}, bf16[96,384]{1,0:T(8,128)(2,1)S(1)}, u32[]{:S(2)}, u32[]{:S(2)}) collective-permute-start(bf16[96,384]{1,0:T(8,128)(2,1)S(1)} %get-tuple-element.50), channel_id=1, source_target_pairs={{0,14},{1,15},{2,12},{3,13},{4,10},{5,11},{6,8},{7,9},{8,6},{9,7},... | collective-permute-start | bytes 221192 | tf_op jit(solution)/shard_map/ppermute | solution.py:218
  34.4 4.5 %collective-permute-start.15 = (bf16[96,384]{1,0:T(8,128)(2,1)S(1)}, bf16[96,384]{1,0:T(8,128)(2,1)S(1)}, u32[]{:S(2)}, u32[]{:S(2)}) collective-permute-start(bf16[96,384]{1,0:T(8,128)(2,1)S(1)} %slice_bitcast_fusion.1), channel_id=1, source_target_pairs={{0,1},{1,0},{2,3},{3,2},{4,5},{5,4},{6,7},{7,6},{8,9},{9,8},{10,11... | collective-permute-start | bytes 221192 | tf_op jit(solution)/shard_map/ppermute | solution.py:214
  34.7 4.2 %collective-permute-start.16 = (bf16[96,384]{1,0:T(8,128)(2,1)S(1)}, bf16[96,384]{1,0:T(8,128)(2,1)S(1)}, u32[]{:S(2)}, u32[]{:S(2)}) collective-permute-start(bf16[96,384]{1,0:T(8,128)(2,1)S(1)} %slice_bitcast_fusion), channel_id=1, source_target_pairs={{0,1},{1,0},{2,3},{3,2},{4,5},{5,4},{6,7},{7,6},{8,9},{9,8},{10,11... | collective-permute-start | bytes 221192 | tf_op jit(solution)/shard_map/ppermute | solution.py:214

commit v17 on v13

--- a/solution.py
+++ b/solution.py
@@ -132,9 +132,9 @@
 
 def finish_kernel(count, left_ref, total_ref, begun_sq_ref, right_ref, *refs):
     slabs = refs[:count]
-    *out_refs, stacked_ref, side_ref, both_ref = refs[count:]
+    *out_refs, stacked_ref, side_ref = refs[count:]
     slab = slabs[0].shape[0]
-    used, full = both_ref.shape
+    full = right_ref.shape[1]
     for n, ref in enumerate(slabs):
         stacked_ref[n * slab:(n + 1) * slab, :] = ref[...]
     last = stacked_ref[...]
@@ -142,15 +142,14 @@
     side_ref[...] = side.astype(side_ref.dtype)
     grad_sq = begun_sq_ref[0:1, 0:1] + squares(last)
     both = jnp.dot(side_ref[...], right_ref[...], preferred_element_type=jnp.float32)
-    both_ref[...] = both[:used]
     graft = jnp.sqrt(grad_sq / (squares(both) + 1e-06))
     for k, out_ref in enumerate(out_refs):
         rows = slice(k * slab, (k + 1) * slab)
         if len(out_ref.shape) == 2:
-            out_ref[...] = (both_ref[rows, :full // 2] * graft).astype(out_ref.dtype)
+            out_ref[...] = (both[rows, :full // 2] * graft).astype(out_ref.dtype)
         else:
-            out_ref[0] = (both_ref[rows, :full // 2] * graft).astype(out_ref.dtype)
-            out_ref[1] = (both_ref[rows, full // 2:] * graft).astype(out_ref.dtype)
+            out_ref[0] = (both[rows, :full // 2] * graft).astype(out_ref.dtype)
+            out_ref[1] = (both[rows, full // 2:] * graft).astype(out_ref.dtype)
 
 
 def gram_kernel(owner_ref, left_ref, right_ref, after_ref, *refs):
@@ -265,7 +264,6 @@
         scratch_shapes=[
             pltpu.VMEM((len(theirs_last) * slab, width), jnp.bfloat16),
             pltpu.VMEM((width, width), jnp.bfloat16),
-            pltpu.VMEM(((len(BACK) + 2) * slab, width), jnp.float32),
         ],
     )
     returned = [trade(x, codes) for x, codes in zip(whole, BACK)]

time: 39.9 us -> 39.9 us (level)
  no operation moved by 1% of the time
where the time goes in v17:
time: 39.9 us; the launch traced here: 39.7 us
  starting transfers between devices  27.7 us (69%)
  Pallas kernels  7.82 us (20%)
  local copies, waits for them, and re-layouts  1.87 us (5%)
  waiting for transfers between devices  1.46 us (4%)
  between operations  0.78 us (2%)
    ppermute x10, starting transfers between devices, other_core(): return lax.ppermute(x, 'replica', [(0, 1), (1, 0)])  15.9 us
    ppermute x8, starting transfers between devices, trade(): return lax.ppermute(x, ('shard', 'replica'), pairs)  11.8 us
    pallas_call x7, Pallas kernels, call(): pl.pallas_call(kernel, out_shape=out_shape, in_specs=in_specs, compiler_p...  7.82 us
    unnamed x14, local copies, waits for them, and re-layouts  1.85 us
    ppermute x8, waiting for transfers between devices, trade(): return lax.ppermute(x, ('shard', 'replica'), pairs)  0.93 us
  transfers between devices with their start and end apart: 18, of which 3 were waited for; matrix products, arithmetic and copies ran while one was open for 0% of the time, Pallas kernels for 13%

profile of v17, /device:TPU:0, one launch (start us, length us, event | category | flops | bytes accessed | tf_op | source)
XLA Modules:
  0.0 39.7 jit_solution(15454102221378872143)
XLA Ops:
  0.6 0.5 %collective-permute-start = (bf16[6,96,768]{2,1,0:T(8,128)(2,1)}, bf16[6,96,768]{2,1,0:T(8,128)(2,1)S(1)}, u32[]{:S(2)}, u32[]{:S(2)}) collective-permute-start(bf16[6,96,768]{2,1,0:T(8,128)(2,1)} %bitcast.14), channel_id=1, source_target_pairs={{0,1},{1,0},{2,3},{3,2},{4,5},{5,4},{6,7},{7,6},{8,9},{9,8},{10,11... | collective-permute-start | bytes 2654216 | tf_op jit(solution)/shard_map/ppermute | solution.py:213
  1.1 0.1 collective-permute-start.2
  1.2 0.4 %collective-permute-start.3 = (bf16[768,384]{1,0:T(8,128)(2,1)}, bf16[768,384]{1,0:T(8,128)(2,1)S(1)}, u32[]{:S(2)}, u32[]{:S(2)}) collective-permute-start(bf16[768,384]{1,0:T(8,128)(2,1)} %bitcast.18), channel_id=1, source_target_pairs={{0,1},{1,0},{2,3},{3,2},{4,5},{5,4},{6,7},{7,6},{8,9},{9,8},{10,11... | collective-permute-start | bytes 1769480 | tf_op jit(solution)/shard_map/ppermute | solution.py:213
  1.7 1.2 %copy-done = bf16[1,6,96,768]{3,2,1,0:T(8,128)(2,1)S(1)} copy-done((bf16[1,6,96,768]{3,2,1,0:T(8,128)(2,1)S(1)}, bf16[1,6,96,768]{3,2,1,0:T(8,128)(2,1)}, u32[]{:S(2)}) %copy-start) | copy-done | bytes 884760
  2.8 0.7 %copy-done.3 = s32[6]{0:T(128)S(1)} copy-done((s32[6]{0:T(128)S(1)}, s32[6]{0:T(128)}, u32[]{:S(2)}) %copy-start.3) | copy-done | bytes 48
  3.5 0.1 shard_map.85.mine_ref
  3.5 0.0 collective-permute-done.theirs_ref
  3.6 0.3 shard_map.86
  3.9 2.9 %collective-permute-start.1 = (bf16[96,768]{1,0:T(8,128)(2,1)S(1)}, bf16[96,768]{1,0:T(8,128)(2,1)S(1)}, u32[]{:S(2)}, u32[]{:S(2)}) collective-permute-start(bf16[96,768]{1,0:T(8,128)(2,1)S(1)} %get-tuple-element.26), channel_id=1, source_target_pairs={{0,4},{1,13},{2,6},{3,15},{4,0},{5,9},{6,2},{7,11},{8,12},{9,5},{1... | collective-permute-start | bytes 442376 | tf_op jit(solution)/shard_map/ppermute | solution.py:217
  6.7 1.5 %collective-permute-start.4 = (bf16[96,768]{1,0:T(8,128)(2,1)S(1)}, bf16[96,768]{1,0:T(8,128)(2,1)S(1)}, u32[]{:S(2)}, u32[]{:S(2)}) collective-permute-start(bf16[96,768]{1,0:T(8,128)(2,1)S(1)} %get-tuple-element.33), channel_id=1, source_target_pairs={{0,2},{1,11},{2,0},{3,9},{4,6},{5,15},{6,4},{7,13},{8,10},{9,3},{1... | collective-permute-start | bytes 442376 | tf_op jit(solution)/shard_map/ppermute | solution.py:217
  8.2 0.7 %collective-permute-start.5 = (bf16[96,768]{1,0:T(8,128)(2,1)S(1)}, bf16[96,768]{1,0:T(8,128)(2,1)S(1)}, u32[]{:S(2)}, u32[]{:S(2)}) collective-permute-start(bf16[96,768]{1,0:T(8,128)(2,1)S(1)} %get-tuple-element.34), channel_id=1, source_target_pairs={{0,0},{1,9},{2,2},{3,11},{4,4},{5,13},{6,6},{7,15},{8,8},{9,1},{10... | collective-permute-start | bytes 442376 | tf_op jit(solution)/shard_map/ppermute | solution.py:217
  8.9 0.0 collective-permute-done.2.other_ref
  8.9 0.1 collective-permute-start.6
  9.0 0.0 collective-permute-done.3.other_right_ref
  9.0 1.7 %shard_map.87 = (bf16[768,576]{1,0:T(8,128)(2,1)S(1)}, bf16[768,192]{1,0:T(8,128)(2,1)S(1)}, bf16[768,768]{1,0:T(8,128)(2,1)S(1)}) custom-call(bf16[384,768]{1,0:T(8,128)(2,1)S(1)} %bitcast.17, bf16[384,768]{1,0:T(8,128)(2,1)S(1)} %collective-permute-done.2.other_ref, bf16[768,384]{1,0:T(8,128)(2,1)S(1)} %bitcast.19, ...), custom_call_target="tpu_custom_call" | custom-call | tf_op jit(solution)/shard_map/pallas_call | solution.py:223
  10.8 0.0 collective-permute-done.1.refs_0_
  10.8 5.1 %collective-permute-start.7 = (bf16[96,768]{1,0:T(8,128)(2,1)S(1)}, bf16[96,768]{1,0:T(8,128)(2,1)S(1)}, u32[]{:S(2)}, u32[]{:S(2)}) collective-permute-start(bf16[96,768]{1,0:T(8,128)(2,1)S(1)} %collective-permute-done.1.refs_0_), channel_id=1, source_target_pairs={{0,1},{1,0},{2,3},{3,2},{4,5},{5,4},{6,7},{7,6},{8,9},{9,8},{10,11... | collective-permute-start | bytes 442376 | tf_op jit(solution)/shard_map/ppermute | solution.py:213
  15.9 0.0 collective-permute-done.4.refs_1_
  15.9 0.9 %collective-permute-start.8 = (bf16[96,768]{1,0:T(8,128)(2,1)S(1)}, bf16[96,768]{1,0:T(8,128)(2,1)S(1)}, u32[]{:S(2)}, u32[]{:S(2)}) collective-permute-start(bf16[96,768]{1,0:T(8,128)(2,1)S(1)} %collective-permute-done.4.refs_1_), channel_id=1, source_target_pairs={{0,1},{1,0},{2,3},{3,2},{4,5},{5,4},{6,7},{7,6},{8,9},{9,8},{10,11... | collective-permute-start | bytes 442376 | tf_op jit(solution)/shard_map/ppermute | solution.py:213
  16.8 0.0 collective-permute-done.5.refs_2_
  16.9 3.6 %collective-permute-start.10 = (bf16[96,768]{1,0:T(8,128)(2,1)S(1)}, bf16[96,768]{1,0:T(8,128)(2,1)S(1)}, u32[]{:S(2)}, u32[]{:S(2)}) collective-permute-start(bf16[96,768]{1,0:T(8,128)(2,1)S(1)} %collective-permute-done.5.refs_2_), channel_id=1, source_target_pairs={{0,1},{1,0},{2,3},{3,2},{4,5},{5,4},{6,7},{7,6},{8,9},{9,8},{10,11... | collective-permute-start | bytes 442376 | tf_op jit(solution)/shard_map/ppermute | solution.py:213
  20.4 0.0 collective-permute-done.6.refs_3_
  20.4 0.4 collective-permute-start.9
  20.8 0.0 collective-permute-done.7.refs_4_
  20.8 0.0 collective-permute-done.8.refs_5_
  20.8 1.1 %shard_map.88 = (f32[768,768]{1,0:T(8,128)S(1)}, f32[8,128]{1,0:T(8,128)S(1)}) custom-call(bf16[768,576]{1,0:T(8,128)(2,1)S(1)} %get-tuple-element.31.left_ref, bf16[96,768]{1,0:T(8,128)(2,1)S(1)} %collective-permute-done.1.refs_0_, bf16[96,768]{1,0:T(8,128)(2,1)S(1)} %collective-permute-done.4.refs_1_, bf16[96,768]{1,0:T(8,128)(2,1)S(1)} %collective-permute-done.5.refs_2_, ...), custom_call_target="tpu_custom_call" | custom-call | tf_op jit(solution)/shard_map/pallas_call | solution.py:223
  21.9 0.0 copy-start.4
  22.0 0.0 copy-start.5
  22.0 0.0 copy-start.6
  22.0 0.0 collective-permute-done.10.refs_1_.refs_6_
  22.0 0.0 collective-permute-done.9.refs_0_.refs_7_
  22.0 1.6 %shard_map.89 = (bf16[2,96,384]{2,1,0:T(8,128)(2,1)S(1)}, bf16[2,96,384]{2,1,0:T(8,128)(2,1)S(1)}, bf16[2,96,384]{2,1,0:T(8,128)(2,1)S(1)}, bf16[96,384]{1,0:T(8,128)(2,1)S(1)}, bf16[96,384]{1,0:T(8,128)(2,1)S(1)}) custom-call(bf16[768,192]{1,0:T(8,128)(2,1)S(1)} %get-tuple-element.30.left_ref, f32[768,768]{1,0:T(8,128)S(1)} %get-tuple-element.36.total_ref, ...), custom_call_target="tpu_custom_call" | custom-call | tf_op jit(solution)/shard_map/pallas_call | solution.py:223
  23.6 2.3 %collective-permute-start.11 = (bf16[2,96,384]{2,1,0:T(8,128)(2,1)S(1)}, bf16[2,96,384]{2,1,0:T(8,128)(2,1)S(1)}, u32[]{:S(2)}, u32[]{:S(2)}) collective-permute-start(bf16[2,96,384]{2,1,0:T(8,128)(2,1)S(1)} %get-tuple-element.39), channel_id=1, source_target_pairs={{0,4},{1,9},{2,6},{3,11},{4,0},{5,13},{6,2},{7,15},{8,12},{9,1},{1... | collective-permute-start | bytes 442376 | tf_op jit(solution)/shard_map/ppermute | solution.py:217
  25.9 0.5 %collective-permute-start.12 = (bf16[2,96,384]{2,1,0:T(8,128)(2,1)S(1)}, bf16[2,96,384]{2,1,0:T(8,128)(2,1)S(1)}, u32[]{:S(2)}, u32[]{:S(2)}) collective-permute-start(bf16[2,96,384]{2,1,0:T(8,128)(2,1)S(1)} %get-tuple-element.45), channel_id=1, source_target_pairs={{0,6},{1,11},{2,4},{3,9},{4,2},{5,15},{6,0},{7,13},{8,14},{9,3},{1... | collective-permute-start | bytes 442376 | tf_op jit(solution)/shard_map/ppermute | solution.py:217
  26.4 1.0 %collective-permute-start.13 = (bf16[2,96,384]{2,1,0:T(8,128)(2,1)S(1)}, bf16[2,96,384]{2,1,0:T(8,128)(2,1)S(1)}, u32[]{:S(2)}, u32[]{:S(2)}) collective-permute-start(bf16[2,96,384]{2,1,0:T(8,128)(2,1)S(1)} %get-tuple-element.46), channel_id=1, source_target_pairs={{0,2},{1,13},{2,0},{3,15},{4,6},{5,9},{6,4},{7,11},{8,10},{9,5},{1... | collective-permute-start | bytes 442376 | tf_op jit(solution)/shard_map/ppermute | solution.py:217
  27.4 2.9 %collective-permute-start.17 = (bf16[96,384]{1,0:T(8,128)(2,1)S(1)}, bf16[96,384]{1,0:T(8,128)(2,1)S(1)}, u32[]{:S(2)}, u32[]{:S(2)}) collective-permute-start(bf16[96,384]{1,0:T(8,128)(2,1)S(1)} %get-tuple-element.48), channel_id=1, source_target_pairs={{0,14},{1,15},{2,12},{3,13},{4,10},{5,11},{6,8},{7,9},{8,6},{9,7},... | collective-permute-start | bytes 221192 | tf_op jit(solution)/shard_map/ppermute | solution.py:217
  30.3 0.0 collective-permute-done.11.after_ref.refs_0_
  30.3 2.1 %shard_map.90 = (bf16[384,768]{1,0:T(8,128)(2,1)}, bf16[384,768]{1,0:T(8,128)(2,1)}) custom-call(s32[1,6]{1,0:T(1,128)S(1)} %bitcast.22, bf16[384,768]{1,0:T(8,128)(2,1)S(1)} %bitcast.24, bf16[384,768]{1,0:T(8,128)(2,1)S(1)} %bitcast.25, bf16[2,96,384]{2,1,0:T(8,128)(2,1)S(1)} %collective-permute-done.11.after_ref.refs_0_, ...), custom_call_target="tpu_custom_call" | custom-call | flops 905969664 | bytes 2359296 | tf_op jit(solution)/shard_map/pallas_call | solution.py:223
  32.4 1.0 %collective-permute-start.14 = (bf16[96,384]{1,0:T(8,128)(2,1)S(1)}, bf16[96,384]{1,0:T(8,128)(2,1)S(1)}, u32[]{:S(2)}, u32[]{:S(2)}) collective-permute-start(bf16[96,384]{1,0:T(8,128)(2,1)S(1)} %slice_bitcast_fusion.2), channel_id=1, source_target_pairs={{0,1},{1,0},{2,3},{3,2},{4,5},{5,4},{6,7},{7,6},{8,9},{9,8},{10,11... | collective-permute-start | bytes 221192 | tf_op jit(solution)/shard_map/ppermute | solution.py:213
  33.4 0.5 %collective-permute-done.12.refs_1_ = bf16[2,96,384]{2,1,0:T(8,128)(2,1)S(1)} collective-permute-done((bf16[2,96,384]{2,1,0:T(8,128)(2,1)S(1)}, bf16[2,96,384]{2,1,0:T(8,128)(2,1)S(1)}, u32[]{:S(2)}, u32[]{:S(2)}) %collective-permute-start.12) | collective-permute-done | bytes 147488 | tf_op jit(solution)/shard_map/ppermute | solution.py:217
  33.9 1.5 %collective-permute-start.15 = (bf16[96,384]{1,0:T(8,128)(2,1)S(1)}, bf16[96,384]{1,0:T(8,128)(2,1)S(1)}, u32[]{:S(2)}, u32[]{:S(2)}) collective-permute-start(bf16[96,384]{1,0:T(8,128)(2,1)S(1)} %slice_bitcast_fusion.1), channel_id=1, source_target_pairs={{0,1},{1,0},{2,3},{3,2},{4,5},{5,4},{6,7},{7,6},{8,9},{9,8},{10,11... | collective-permute-start | bytes 221192 | tf_op jit(solution)/shard_map/ppermute | solution.py:213
  35.4 0.0 collective-permute-done.13.refs_2_
  35.4 2.4 %collective-permute-start.16 = (bf16[96,384]{1,0:T(8,128)(2,1)S(1)}, bf16[96,384]{1,0:T(8,128)(2,1)S(1)}, u32[]{:S(2)}, u32[]{:S(2)}) collective-permute-start(bf16[96,384]{1,0:T(8,128)(2,1)S(1)} %slice_bitcast_fusion), channel_id=1, source_target_pairs={{0,1},{1,0},{2,3},{3,2},{4,5},{5,4},{6,7},{7,6},{8,9},{9,8},{10,11... | collective-permute-start | bytes 221192 | tf_op jit(solution)/shard_map/ppermute | solution.py:213
  37.8 0.4 %collective-permute-done.17.refs_7_ = bf16[96,384]{1,0:T(8,128)(2,1)S(1)} collective-permute-done((bf16[96,384]{1,0:T(8,128)(2,1)S(1)}, bf16[96,384]{1,0:T(8,128)(2,1)S(1)}, u32[]{:S(2)}, u32[]{:S(2)}) %collective-permute-start.17) | collective-permute-done | bytes 73760 | tf_op jit(solution)/shard_map/ppermute | solution.py:217
  38.2 0.0 collective-permute-done.14.refs_3_
  38.2 0.0 collective-permute-done.15.refs_4_
  38.2 0.5 %collective-permute-done.16.refs_5_ = bf16[96,384]{1,0:T(8,128)(2,1)S(1)} collective-permute-done((bf16[96,384]{1,0:T(8,128)(2,1)S(1)}, bf16[96,384]{1,0:T(8,128)(2,1)S(1)}, u32[]{:S(2)}, u32[]{:S(2)}) %collective-permute-start.16) | collective-permute-done | bytes 73760 | tf_op jit(solution)/shard_map/ppermute | solution.py:213
  38.7 0.9 %shard_map.91 = bf16[6,96,384]{2,1,0:T(8,128)(2,1)} custom-call(s32[1,6]{1,0:T(1,128)S(1)} %bitcast.23, bf16[2,96,384]{2,1,0:T(8,128)(2,1)S(1)} %collective-permute-done.11.after_ref.refs_0_, bf16[2,96,384]{2,1,0:T(8,128)(2,1)S(1)} %collective-permute-done.12.refs_1_, bf16[2,96,384]{2,1,0:T(8,128)(2,1)S(1)} %collective-permute-done.13.refs_2_, ...), custom_call_target="tpu_custom_call" | custom-call | tf_op jit(solution)/shard_map/pallas_call | solution.py:223
  (12 shorter events, 0.0 us)
Async XLA Ops:
  0.6 2.9 %collective-permute-start = (bf16[6,96,768]{2,1,0:T(8,128)(2,1)}, bf16[6,96,768]{2,1,0:T(8,128)(2,1)S(1)}, u32[]{:S(2)}, u32[]{:S(2)}) collective-permute-start(bf16[6,96,768]{2,1,0:T(8,128)(2,1)} %bitcast.14), channel_id=1, source_target_pairs={{0,1},{1,0},{2,3},{3,2},{4,5},{5,4},{6,7},{7,6},{8,9},{9,8},{10,11... | collective-permute-start | bytes 2654216 | tf_op jit(solution)/shard_map/ppermute | solution.py:213
  1.1 7.8 %collective-permute-start.2 = (bf16[384,768]{1,0:T(8,128)(2,1)}, bf16[384,768]{1,0:T(8,128)(2,1)S(1)}, u32[]{:S(2)}, u32[]{:S(2)}) collective-permute-start(bf16[384,768]{1,0:T(8,128)(2,1)} %bitcast.16), channel_id=1, source_target_pairs={{0,1},{1,0},{2,3},{3,2},{4,5},{5,4},{6,7},{7,6},{8,9},{9,8},{10,11... | collective-permute-start | bytes 1769480 | tf_op jit(solution)/shard_map/ppermute | solution.py:213
  1.2 7.8 %collective-permute-start.3 = (bf16[768,384]{1,0:T(8,128)(2,1)}, bf16[768,384]{1,0:T(8,128)(2,1)S(1)}, u32[]{:S(2)}, u32[]{:S(2)}) collective-permute-start(bf16[768,384]{1,0:T(8,128)(2,1)} %bitcast.18), channel_id=1, source_target_pairs={{0,1},{1,0},{2,3},{3,2},{4,5},{5,4},{6,7},{7,6},{8,9},{9,8},{10,11... | collective-permute-start | bytes 1769480 | tf_op jit(solution)/shard_map/ppermute | solution.py:213
  1.7 1.2 %copy-start = (bf16[1,6,96,768]{3,2,1,0:T(8,128)(2,1)S(1)}, bf16[1,6,96,768]{3,2,1,0:T(8,128)(2,1)}, u32[]{:S(2)}) copy-start(bf16[1,6,96,768]{3,2,1,0:T(8,128)(2,1)} %param.6) | copy-start | bytes 2654212
  2.8 0.7 %copy-start.3 = (s32[6]{0:T(128)S(1)}, s32[6]{0:T(128)}, u32[]{:S(2)}) copy-start(s32[6]{0:T(128)} %param.7) | copy-start | bytes 76
  3.5 5.5 %copy-start.1 = (bf16[1,384,768]{2,1,0:T(8,128)(2,1)S(1)}, bf16[1,384,768]{2,1,0:T(8,128)(2,1)}, u32[]{:S(2)}) copy-start(bf16[1,384,768]{2,1,0:T(8,128)(2,1)} %param.10) | copy-start | bytes 1769476
  3.5 5.5 %copy-start.2 = (bf16[1,768,384]{2,1,0:T(8,128)(2,1)S(1)}, bf16[1,768,384]{2,1,0:T(8,128)(2,1)}, u32[]{:S(2)}) copy-start(bf16[1,768,384]{2,1,0:T(8,128)(2,1)} %param.11) | copy-start | bytes 1769476
  3.9 6.9 %collective-permute-start.1 = (bf16[96,768]{1,0:T(8,128)(2,1)S(1)}, bf16[96,768]{1,0:T(8,128)(2,1)S(1)}, u32[]{:S(2)}, u32[]{:S(2)}) collective-permute-start(bf16[96,768]{1,0:T(8,128)(2,1)S(1)} %get-tuple-element.26), channel_id=1, source_target_pairs={{0,4},{1,13},{2,6},{3,15},{4,0},{5,9},{6,2},{7,11},{8,12},{9,5},{1... | collective-permute-start | bytes 442376 | tf_op jit(solution)/shard_map/ppermute | solution.py:217
  6.7 9.2 %collective-permute-start.4 = (bf16[96,768]{1,0:T(8,128)(2,1)S(1)}, bf16[96,768]{1,0:T(8,128)(2,1)S(1)}, u32[]{:S(2)}, u32[]{:S(2)}) collective-permute-start(bf16[96,768]{1,0:T(8,128)(2,1)S(1)} %get-tuple-element.33), channel_id=1, source_target_pairs={{0,2},{1,11},{2,0},{3,9},{4,6},{5,15},{6,4},{7,13},{8,10},{9,3},{1... | collective-permute-start | bytes 442376 | tf_op jit(solution)/shard_map/ppermute | solution.py:217
  8.2 8.6 %collective-permute-start.5 = (bf16[96,768]{1,0:T(8,128)(2,1)S(1)}, bf16[96,768]{1,0:T(8,128)(2,1)S(1)}, u32[]{:S(2)}, u32[]{:S(2)}) collective-permute-start(bf16[96,768]{1,0:T(8,128)(2,1)S(1)} %get-tuple-element.34), channel_id=1, source_target_pairs={{0,0},{1,9},{2,2},{3,11},{4,4},{5,13},{6,6},{7,15},{8,8},{9,1},{10... | collective-permute-start | bytes 442376 | tf_op jit(solution)/shard_map/ppermute | solution.py:217
  8.9 11.5 %collective-permute-start.6 = (bf16[96,768]{1,0:T(8,128)(2,1)S(1)}, bf16[96,768]{1,0:T(8,128)(2,1)S(1)}, u32[]{:S(2)}, u32[]{:S(2)}) collective-permute-start(bf16[96,768]{1,0:T(8,128)(2,1)S(1)} %get-tuple-element.35), channel_id=1, source_target_pairs={{0,6},{1,15},{2,4},{3,13},{4,2},{5,11},{6,0},{7,9},{8,14},{9,7},{1... | collective-permute-start | bytes 442376 | tf_op jit(solution)/shard_map/ppermute | solution.py:217
  10.8 10.1 %collective-permute-start.7 = (bf16[96,768]{1,0:T(8,128)(2,1)S(1)}, bf16[96,768]{1,0:T(8,128)(2,1)S(1)}, u32[]{:S(2)}, u32[]{:S(2)}) collective-permute-start(bf16[96,768]{1,0:T(8,128)(2,1)S(1)} %collective-permute-done.1.refs_0_), channel_id=1, source_target_pairs={{0,1},{1,0},{2,3},{3,2},{4,5},{5,4},{6,7},{7,6},{8,9},{9,8},{10,11... | collective-permute-start | bytes 442376 | tf_op jit(solution)/shard_map/ppermute | solution.py:213
  15.9 4.9 %collective-permute-start.8 = (bf16[96,768]{1,0:T(8,128)(2,1)S(1)}, bf16[96,768]{1,0:T(8,128)(2,1)S(1)}, u32[]{:S(2)}, u32[]{:S(2)}) collective-permute-start(bf16[96,768]{1,0:T(8,128)(2,1)S(1)} %collective-permute-done.4.refs_1_), channel_id=1, source_target_pairs={{0,1},{1,0},{2,3},{3,2},{4,5},{5,4},{6,7},{7,6},{8,9},{9,8},{10,11... | collective-permute-start | bytes 442376 | tf_op jit(solution)/shard_map/ppermute | solution.py:213
  16.9 5.1 %collective-permute-start.10 = (bf16[96,768]{1,0:T(8,128)(2,1)S(1)}, bf16[96,768]{1,0:T(8,128)(2,1)S(1)}, u32[]{:S(2)}, u32[]{:S(2)}) collective-permute-start(bf16[96,768]{1,0:T(8,128)(2,1)S(1)} %collective-permute-done.5.refs_2_), channel_id=1, source_target_pairs={{0,1},{1,0},{2,3},{3,2},{4,5},{5,4},{6,7},{7,6},{8,9},{9,8},{10,11... | collective-permute-start | bytes 442376 | tf_op jit(solution)/shard_map/ppermute | solution.py:213
  20.4 1.5 %collective-permute-start.9 = (bf16[96,768]{1,0:T(8,128)(2,1)S(1)}, bf16[96,768]{1,0:T(8,128)(2,1)S(1)}, u32[]{:S(2)}, u32[]{:S(2)}) collective-permute-start(bf16[96,768]{1,0:T(8,128)(2,1)S(1)} %collective-permute-done.6.refs_3_), channel_id=1, source_target_pairs={{0,1},{1,0},{2,3},{3,2},{4,5},{5,4},{6,7},{7,6},{8,9},{9,8},{10,11... | collective-permute-start | bytes 442376 | tf_op jit(solution)/shard_map/ppermute | solution.py:213
  21.9 8.4 %copy-start.4 = (s32[6]{0:T(128)S(1)}, s32[6]{0:T(128)}, u32[]{:S(2)}) copy-start(s32[6]{0:T(128)} %param.7) | copy-start | bytes 76
  22.0 8.4 %copy-start.5 = (bf16[1,384,768]{2,1,0:T(8,128)(2,1)S(1)}, bf16[1,384,768]{2,1,0:T(8,128)(2,1)}, u32[]{:S(2)}) copy-start(bf16[1,384,768]{2,1,0:T(8,128)(2,1)} %param.8) | copy-start | bytes 1769476
  22.0 8.3 %copy-start.6 = (bf16[1,384,768]{2,1,0:T(8,128)(2,1)S(1)}, bf16[1,384,768]{2,1,0:T(8,128)(2,1)}, u32[]{:S(2)}) copy-start(bf16[1,384,768]{2,1,0:T(8,128)(2,1)} %param.9) | copy-start | bytes 1769476
  23.6 6.7 %collective-permute-start.11 = (bf16[2,96,384]{2,1,0:T(8,128)(2,1)S(1)}, bf16[2,96,384]{2,1,0:T(8,128)(2,1)S(1)}, u32[]{:S(2)}, u32[]{:S(2)}) collective-permute-start(bf16[2,96,384]{2,1,0:T(8,128)(2,1)S(1)} %get-tuple-element.39), channel_id=1, source_target_pairs={{0,4},{1,9},{2,6},{3,11},{4,0},{5,13},{6,2},{7,15},{8,12},{9,1},{1... | collective-permute-start | bytes 442376 | tf_op jit(solution)/shard_map/ppermute | solution.py:217
  25.9 8.0 %collective-permute-start.12 = (bf16[2,96,384]{2,1,0:T(8,128)(2,1)S(1)}, bf16[2,96,384]{2,1,0:T(8,128)(2,1)S(1)}, u32[]{:S(2)}, u32[]{:S(2)}) collective-permute-start(bf16[2,96,384]{2,1,0:T(8,128)(2,1)S(1)} %get-tuple-element.45), channel_id=1, source_target_pairs={{0,6},{1,11},{2,4},{3,9},{4,2},{5,15},{6,0},{7,13},{8,14},{9,3},{1... | collective-permute-start | bytes 442376 | tf_op jit(solution)/shard_map/ppermute | solution.py:217
  26.4 9.0 %collective-permute-start.13 = (bf16[2,96,384]{2,1,0:T(8,128)(2,1)S(1)}, bf16[2,96,384]{2,1,0:T(8,128)(2,1)S(1)}, u32[]{:S(2)}, u32[]{:S(2)}) collective-permute-start(bf16[2,96,384]{2,1,0:T(8,128)(2,1)S(1)} %get-tuple-element.46), channel_id=1, source_target_pairs={{0,2},{1,13},{2,0},{3,15},{4,6},{5,9},{6,4},{7,11},{8,10},{9,5},{1... | collective-permute-start | bytes 442376 | tf_op jit(solution)/shard_map/ppermute | solution.py:217
  27.4 10.8 %collective-permute-start.17 = (bf16[96,384]{1,0:T(8,128)(2,1)S(1)}, bf16[96,384]{1,0:T(8,128)(2,1)S(1)}, u32[]{:S(2)}, u32[]{:S(2)}) collective-permute-start(bf16[96,384]{1,0:T(8,128)(2,1)S(1)} %get-tuple-element.48), channel_id=1, source_target_pairs={{0,14},{1,15},{2,12},{3,13},{4,10},{5,11},{6,8},{7,9},{8,6},{9,7},... | collective-permute-start | bytes 221192 | tf_op jit(solution)/shard_map/ppermute | solution.py:217
  32.4 5.8 %collective-permute-start.14 = (bf16[96,384]{1,0:T(8,128)(2,1)S(1)}, bf16[96,384]{1,0:T(8,128)(2,1)S(1)}, u32[]{:S(2)}, u32[]{:S(2)}) collective-permute-start(bf16[96,384]{1,0:T(8,128)(2,1)S(1)} %slice_bitcast_fusion.2), channel_id=1, source_target_pairs={{0,1},{1,0},{2,3},{3,2},{4,5},{5,4},{6,7},{7,6},{8,9},{9,8},{10,11... | collective-permute-start | bytes 221192 | tf_op jit(solution)/shard_map/ppermute | solution.py:213
  33.9 4.3 %collective-permute-start.15 = (bf16[96,384]{1,0:T(8,128)(2,1)S(1)}, bf16[96,384]{1,0:T(8,128)(2,1)S(1)}, u32[]{:S(2)}, u32[]{:S(2)}) collective-permute-start(bf16[96,384]{1,0:T(8,128)(2,1)S(1)} %slice_bitcast_fusion.1), channel_id=1, source_target_pairs={{0,1},{1,0},{2,3},{3,2},{4,5},{5,4},{6,7},{7,6},{8,9},{9,8},{10,11... | collective-permute-start | bytes 221192 | tf_op jit(solution)/shard_map/ppermute | solution.py:213
  35.4 3.3 %collective-permute-start.16 = (bf16[96,384]{1,0:T(8,128)(2,1)S(1)}, bf16[96,384]{1,0:T(8,128)(2,1)S(1)}, u32[]{:S(2)}, u32[]{:S(2)}) collective-permute-start(bf16[96,384]{1,0:T(8,128)(2,1)S(1)} %slice_bitcast_fusion), channel_id=1, source_target_pairs={{0,1},{1,0},{2,3},{3,2},{4,5},{5,4},{6,7},{7,6},{8,9},{9,8},{10,11... | collective-permute-start | bytes 221192 | tf_op jit(solution)/shard_map/ppermute | solution.py:213
